TPU v7x, 128 devices: a whole 4x4x4 slice. The times are simulated.
128 devices in a mesh: dp: 16 (over z, y), tensor: 8 (over x, core).
Axes of the slice: x: 4, y: 4, z: 4, core: 2. Of those that a mesh axis runs over, the one named last changes fastest.
Arguments:
- query: bfloat16 [32, 128, 8192], P('dp', None, 'tensor'), may hold values from -6 to 6
- image: bfloat16 [32, 512, 8192], P('dp', None, 'tensor'), may hold values from -6 to 6
- tiles: int32 [32], replicated, may hold values from 0 to 4, as said below
- image_slot: int32 [32], replicated, may hold values from 0 to 31, as said below
- key_weight_matrix: bfloat16 [8192, 1024], P('dp', 'tensor'), may hold values from -0.0625 to 0.0625
- value_weight_matrix: bfloat16 [8192, 1024], P('dp', 'tensor'), may hold values from -0.0625 to 0.0625
- query_gain: float32 [128], replicated, may hold values from 0.5 to 2
- key_gain: float32 [128], replicated, may hold values from 0.5 to 2
- gate: float32 [1], replicated, may hold values from 0.3 to 1.5
- cotangent: bfloat16 [32, 128, 8192], P('dp', None, 'tensor'), may hold values from -6 to 6
Outputs:
- context: bfloat16 [32, 128, 8192], P('dp', None, 'tensor')
- d_query: bfloat16 [32, 128, 8192], P('dp', None, 'tensor')
- d_w_key: float32 [8192, 1024], P('dp', 'tensor')
- d_w_value: float32 [8192, 1024], P('dp', 'tensor')
Inputs may be any that keep to these rules, and one draw needn't show every extreme that they name: Some sample has 4 tiles and some has none. image_slot is a permutation of the samples. Sample s sits at dp index s // 2; the image rows image_slot[s] sit at the same dp index or at the one that differs from it by half the dp axis, and of the two samples at one dp index at most one has its image at the other index.
All inputs are finite; a program needn't handle non-finite values.
Results may differ from a plain program's by a relative error of at most 0.02.
Values may be sent and summed in bfloat16 or wider, within the bound.
No kernel may reach another device: no remote copies, remote signals or barrier semaphores. Data moves between devices by JAX's collectives and lax.ppermute only.
A program may use at most 128 MiB of HBM per device.

v0:
```python
import functools

import jax
import jax.numpy as jnp
from jax import lax
from jax.experimental import pallas as pl
from jax.experimental.pallas import tpu as pltpu
from jax.sharding import PartitionSpec as P

TILE = 128
RING = 4
EPS = 1e-06


def along_z(x, step):
    pairs = [(z * RING + y, (z + step) % RING * RING + y) for z in range(RING) for y in range(RING)]
    return lax.ppermute(x, "dp", pairs)


def by_core(x, step, z_core):
    pairs = []
    for z in range(RING):
        for y in range(RING):
            for i in range(RING):
                for c in range(2):
                    to_z, to_y = (z + step, y) if c == z_core else (z, y + step)
                    source = (z * RING + y) * 2 * RING + i * 2 + c
                    target = (to_z % RING * RING + to_y % RING) * 2 * RING + i * 2 + c
                    pairs.append((source, target))
    return lax.ppermute(x, ("dp", "tensor"), pairs)


def inner(x, step):
    return by_core(x, step, 0)


def outer(x, step):
    return by_core(x, step, 1)


def along_x(x, step):
    pairs = [(i * 2 + c, (i + step) % RING * 2 + c) for i in range(RING) for c in range(2)]
    return lax.ppermute(x, "tensor", pairs)


def other_core(x):
    return lax.ppermute(x, "tensor", [(i, i ^ 1) for i in range(2 * RING)])


def gathered(block, move):
    far, after, before = (move(block, step) for step in (2, 1, 3))
    return [block, after, far, before]


def scattered(parts, move):
    return [move(parts[step], step) for step in (2, 1, 3)]


def summed(blocks):
    total = blocks[0].astype(jnp.float32)
    for block in blocks[1:]:
        total = total + block.astype(jnp.float32)
    return total


def rms_factor(values):
    return lax.rsqrt(jnp.mean(values * values, axis=-1, keepdims=True) + EPS)


def norm_back(values, norm_multiplier, gain, grad):
    weighted = grad * gain
    inner = jnp.sum(weighted * values, axis=-1, keepdims=True)
    return (
        norm_multiplier * weighted
        - values * (norm_multiplier * norm_multiplier * norm_multiplier) * inner / values.shape[-1]
    )


def matmul(a, b, contract):
    return lax.dot_general(a, b, (contract, ((), ())), preferred_element_type=jnp.float32)


VMEM = pl.BlockSpec(memory_space=pltpu.VMEM)
SMEM = pl.BlockSpec(memory_space=pltpu.SMEM)
ANY = pl.BlockSpec(memory_space=pl.ANY)
HBM = pl.BlockSpec(memory_space=pltpu.HBM)
PARAMS = pltpu.CompilerParams(vmem_limit_bytes=16 * 1024 * 1024)


def route_kernel(tiles, slots, image_ref, key_ref, value_ref, near, far, chip, far_ref, near_ref, shard_ref, sems):
    rank, place = lax.axis_index("dp"), lax.axis_index("tensor")
    first = 2 * rank

    def sample_of(slot):
        found = lambda i, at: jnp.where(slots[i] == slot, i, at)
        return lax.fori_loop(0, slots.shape[0], found, 0)

    away = [sample_of(first + i) >> 1 != rank for i in range(2)]
    swaps = jnp.logical_or(away[0], away[1])
    far_slot = jnp.where(away[1], 1, 0)
    copies = []
    for i, (slot, target) in enumerate(((far_slot, far_ref), (1 - far_slot, near_ref))):
        copies.append(pltpu.make_async_copy(image_ref.at[slot], target, sems.at[i]))
        copies[i].start()
    head_dim = key_ref.shape[1]
    for i, source in enumerate((key_ref, value_ref)):
        target = shard_ref.at[:, pl.ds(i * head_dim, head_dim)]
        copies.append(pltpu.make_async_copy(source, target, sems.at[2 + i]))
        copies[2 + i].start()
    second_home = slots[first + 1]
    of_slot = jnp.where(second_home == first + far_slot, 1, 0)
    far_own = jnp.where(swaps, jnp.where(second_home >> 1 != rank, 1, 0), of_slot)
    near[0] = 1 - far_own
    near[1] = tiles[first + 1 - far_own]
    near[2] = 0
    far[0] = far_own
    far[1] = tiles[first + far_own]
    far[2] = jnp.where(swaps, 1, 0)
    chip[0] = rank // RING
    chip[1] = rank % RING
    chip[2] = place // 2
    chip[3] = place % 2
    for copy in copies:
        copy.wait()


def route(tiles, image_slot, image, key_weights, value_weights):
    rows = jax.ShapeDtypeStruct(image.shape[1:], image.dtype)
    count, head_dim = key_weights.shape
    weights = jax.ShapeDtypeStruct((count, 2 * head_dim), key_weights.dtype)
    numbers = lambda n: jax.ShapeDtypeStruct((n,), jnp.int32)
    return pl.pallas_call(
        route_kernel,
        in_specs=[SMEM, SMEM, HBM, HBM, HBM],
        out_specs=[SMEM, SMEM, SMEM, VMEM, VMEM, VMEM],
        out_shape=[numbers(3), numbers(3), numbers(4), rows, rows, weights],
        scratch_shapes=[pltpu.SemaphoreType.DMA((4,))],
        compiler_params=PARAMS,
        cost_estimate=pl.CostEstimate(flops=0, bytes_accessed=4 * image.size, transcendentals=0),
    )(tiles, image_slot, image, key_weights, value_weights)


def assemble_kernel(chip, *refs):
    pieces, out_ref, sems = refs[:RING], refs[RING], refs[RING + 1]
    rows, both = pieces[0].shape
    count = rows // RING
    z, y, x, core = chip[0], chip[1], chip[2], chip[3]
    copies = []
    for b in range(RING):
        for a in range(RING):
            from_z = (z - jnp.where(core == 0, a, b) + RING) % RING
            from_y = (y - jnp.where(core == 0, b, a) + RING) % RING
            o = (x - from_z + RING) % RING
            start = ((o * 2 + ((from_y >> 1) ^ core)) * 2 + from_y % 2) * count
            target = out_ref.at[pl.ds(pl.multiple_of(start, count), count)]
            source = pieces[b].at[pl.ds(a * count, count)]
            copies.append(pltpu.make_async_copy(source, target, sems.at[b, a]))
    for copy in copies:
        copy.start()
    for copy in copies:
        copy.wait()


def assemble(chip, pieces):
    rows, both = pieces[0].shape
    return pl.pallas_call(
        assemble_kernel,
        in_specs=[SMEM] + [ANY] * RING,
        out_specs=VMEM,
        out_shape=jax.ShapeDtypeStruct((RING * rows, both), pieces[0].dtype),
        scratch_shapes=[pltpu.SemaphoreType.DMA((RING, RING))],
        compiler_params=PARAMS,
        cost_estimate=pl.CostEstimate(
            flops=0, bytes_accessed=4 * RING * rows * both, transcendentals=0
        ),
    )(chip, *pieces)


def finish_kernel(total_ref, gain_ref, key_value_ref):
    head_dim = gain_ref.shape[1]
    raw = total_ref[:, :head_dim]
    keys = (raw * rms_factor(raw) * gain_ref[...]).astype(jnp.bfloat16)
    key_value_ref[:, :head_dim] = keys
    key_value_ref[:, head_dim:] = total_ref[:, head_dim:].astype(jnp.bfloat16)


def finish(total, gain):
    return pl.pallas_call(
        finish_kernel,
        in_specs=[VMEM] * 2,
        out_specs=VMEM,
        out_shape=jax.ShapeDtypeStruct(total.shape, jnp.bfloat16),
        compiler_params=PARAMS,
        cost_estimate=pl.CostEstimate(
            flops=3 * total.size, bytes_accessed=6 * total.size, transcendentals=total.shape[0]
        ),
    )(total, gain[None, :])


def turn_kernel(flag, total_ref, grad_ref, other_ref, gain_ref, out_ref):
    head_dim = gain_ref.shape[1]
    grad = jnp.where(flag[2] != 0, other_ref[...], grad_ref[...])
    raw = total_ref[:, :head_dim]
    d_raw = norm_back(raw, rms_factor(raw), gain_ref[...], grad[:, :head_dim].astype(jnp.float32))
    out_ref[:, :head_dim] = d_raw.astype(jnp.bfloat16)
    out_ref[:, head_dim:] = grad[:, head_dim:]


def turn(flag, total, grad, other, gain):
    return pl.pallas_call(
        turn_kernel,
        in_specs=[SMEM] + [VMEM] * 4,
        out_specs=VMEM,
        out_shape=jax.ShapeDtypeStruct(grad.shape, jnp.bfloat16),
        compiler_params=PARAMS,
        cost_estimate=pl.CostEstimate(
            flops=6 * grad.size, bytes_accessed=8 * grad.size, transcendentals=grad.shape[0]
        ),
    )(flag, total, grad, other, gain[None, :])


def first_part_kernel(*refs):
    sources, (grads_ref, out_ref) = refs[:-2], refs[-2:]
    depth = sources[0].shape[1]
    for k, source in enumerate(sources):
        out_ref[k * depth : (k + 1) * depth] = matmul(source[...], grads_ref[...], ((0,), (0,)))


def first_part(feats, grads):
    rows, depth = feats[0].shape
    both = grads.shape[1]
    return pl.pallas_call(
        first_part_kernel,
        in_specs=[VMEM] * (len(feats) + 1),
        out_specs=VMEM,
        out_shape=jax.ShapeDtypeStruct((len(feats) * depth, both), jnp.float32),
        compiler_params=PARAMS,
        cost_estimate=pl.CostEstimate(
            flops=2 * len(feats) * rows * depth * both,
            bytes_accessed=2 * len(feats) * rows * depth,
            transcendentals=0,
        ),
    )(*feats, grads)


def product_kernel(chip, *refs):
    sources, (grads_ref, part_ref), refs = refs[: 2 * RING], refs[2 * RING : 2 * RING + 2], refs[2 * RING + 2 :]
    outs, (held, sems) = refs[:RING], refs[RING:]
    depth = sources[0].shape[1]
    count = depth // 2
    z, y, x, core = chip[0], chip[1], chip[2], chip[3]
    for k, source in enumerate(sources):
        total = matmul(source[...], grads_ref[...], ((0,), (0,)))
        total = (total + part_ref[k * depth : (k + 1) * depth]).astype(held.dtype)
        by_z = (x - k // 2 - z + 2 * RING) % RING
        for h in range(2):
            by_y = (2 * (k % 2 ^ core) + h - y + RING) % RING
            outer_by = jnp.where(core == 0, by_y, by_z)
            inner_by = jnp.where(core == 0, by_z, by_y)
            start = pl.multiple_of(inner_by * count, count)
            held[outer_by, pl.ds(start, count)] = total[h * count : (h + 1) * count]
    copies = [pltpu.make_async_copy(held.at[k], outs[k], sems.at[k]) for k in range(RING)]
    for copy in copies:
        copy.start()
    for copy in copies:
        copy.wait()


def product(chip, feats, grads, part):
    rows, depth = feats[0].shape
    both = grads.shape[1]
    shape = (RING * depth // 2, both)
    return pl.pallas_call(
        product_kernel,
        in_specs=[SMEM] + [VMEM] * (len(feats) + 2),
        out_specs=[ANY] * RING,
        out_shape=[jax.ShapeDtypeStruct(shape, jnp.bfloat16)] * RING,
        scratch_shapes=[
            pltpu.VMEM((RING, *shape), jnp.bfloat16),
            pltpu.SemaphoreType.DMA((RING,)),
        ],
        compiler_params=PARAMS,
        cost_estimate=pl.CostEstimate(
            flops=2 * len(feats) * rows * depth * both,
            bytes_accessed=2 * len(feats) * rows * depth,
            transcendentals=0,
        ),
    )(chip, *feats, grads, part)


def attend_kernel(heads, index, ratio_ref, q_ref, cot_ref, kv_ref, away_ref, gain_ref, *refs):
    context_ref, d_query_ref, d_kv_ref, d_key_sum, d_value_sum = refs[-5:]
    step = pl.program_id(0)
    head_dim = gain_ref.shape[1]
    scale = head_dim ** (-0.5)
    count = index[1]
    ratio = ratio_ref[0]
    gain = gain_ref[...]
    key_value = jnp.where(index[2] != 0, away_ref[...], kv_ref[...])
    keys = key_value[:, :head_dim]
    vals = key_value[:, head_dim:]

    def stacked(ref):
        parts = [ref[0, :, h * head_dim : (h + 1) * head_dim] for h in range(heads)]
        return jnp.concatenate(parts, axis=0).astype(jnp.float32)

    def unstacked(ref, rows):
        text = rows.shape[0] // heads
        for h in range(heads):
            part = rows[h * text : (h + 1) * text]
            ref[0, :, h * head_dim : (h + 1) * head_dim] = part.astype(ref.dtype)

    @pl.when(step == 0)
    def _():
        d_key_sum[...] = jnp.zeros_like(d_key_sum)
        d_value_sum[...] = jnp.zeros_like(d_value_sum)

    q_raw = stacked(q_ref)
    q_factor = rms_factor(q_raw)
    q_norm = (q_raw * q_factor * gain).astype(jnp.bfloat16)
    raw = matmul(q_norm, keys, ((1,), (1,))) * scale
    place = lax.broadcasted_iota(jnp.int32, raw.shape, 1)
    expo = jnp.where(place < count * TILE, jnp.exp(raw), 0.0)
    total = jnp.sum(expo, axis=1, keepdims=True) + (count == 0).astype(jnp.float32)
    inverse = 1.0 / total
    weights_b = expo.astype(jnp.bfloat16)
    attended = matmul(weights_b, vals, ((1,), (0,))) * inverse
    unstacked(context_ref, ratio * attended)
    d_att = ratio * stacked(cot_ref)
    d_att_b = d_att.astype(jnp.bfloat16)
    scaled_b = (d_att * inverse).astype(jnp.bfloat16)
    delta = jnp.sum(d_att * attended, axis=1, keepdims=True)
    d_prob = matmul(d_att_b, vals, ((1,), (1,)))
    d_score = (expo * inverse * (d_prob - delta)).astype(jnp.bfloat16)
    d_qn = scale * matmul(d_score, keys, ((1,), (0,)))
    unstacked(d_query_ref, norm_back(q_raw, q_factor, gain, d_qn))
    d_key_sum[...] += matmul(d_score, q_norm, ((0,), (0,)))
    d_value_sum[...] += matmul(weights_b, scaled_b, ((0,), (0,)))

    @pl.when(step == pl.num_programs(0) - 1)
    def _():
        d_kv_ref[:, :head_dim] = (scale * d_key_sum[...]).astype(d_kv_ref.dtype)
        d_kv_ref[:, head_dim:] = d_value_sum[...].astype(d_kv_ref.dtype)


def attend(index, ratio, query, cot, key_value, away, gain, earlier, heads=2):
    rows, both = key_value.shape
    head_dim = both // 2
    text = query.shape[1]
    width = heads * head_dim
    block = pl.BlockSpec((1, text, width), lambda h, index: (index[0], 0, h))
    whole = lambda shape: pl.BlockSpec(shape, lambda h, index: (0, 0))
    in_specs = [
        pl.BlockSpec(memory_space=pltpu.SMEM),
        block,
        block,
        whole((rows, both)),
        whole((rows, both)),
        whole((1, head_dim)),
    ]
    aliases = {}
    if earlier:
        in_specs += [pl.BlockSpec(memory_space=pl.ANY)] * 2
        aliases = {7: 0, 8: 1}
    steps = query.shape[2] // width
    return pl.pallas_call(
        functools.partial(attend_kernel, heads),
        grid_spec=pltpu.PrefetchScalarGridSpec(
            num_scalar_prefetch=1,
            grid=(steps,),
            in_specs=in_specs,
            out_specs=[block, block, whole((rows, both))],
            scratch_shapes=[pltpu.VMEM((rows, head_dim), jnp.float32)] * 2,
        ),
        out_shape=[
            jax.ShapeDtypeStruct(query.shape, jnp.bfloat16),
            jax.ShapeDtypeStruct(query.shape, jnp.bfloat16),
            jax.ShapeDtypeStruct((rows, both), jnp.bfloat16),
        ],
        input_output_aliases=aliases,
        compiler_params=pltpu.CompilerParams(
            vmem_limit_bytes=24 * 1024 * 1024
        ),
        cost_estimate=pl.CostEstimate(
            flops=14 * steps * heads * text * rows * head_dim,
            bytes_accessed=8 * text * steps * width + 6 * rows * head_dim,
            transcendentals=steps * heads * text * rows,
        ),
    )(
        index,
        ratio,
        query,
        cot,
        key_value,
        away,
        gain[None, :],
        *earlier,
    )


def per_device(
    query,
    image,
    tiles,
    image_slot,
    key_weight_matrix,
    value_weight_matrix,
    query_gain,
    key_gain,
    gate,
    cotangent,
):
    ratio = jnp.tanh(gate)
    near_index, far_index, chip, far_own, near_own, shard = route(
        tiles, image_slot, image, key_weight_matrix, value_weight_matrix
    )

    def opposite(after, before):
        half = after.shape[0] // 2
        return along_x(after[:half], 1), along_x(before[half:], 3)

    far_x = [along_x(far_own, 1), along_x(far_own, 3)]
    pieces = gathered(jnp.concatenate(gathered(shard, inner), axis=0), outer)
    near_own, *far_x = lax.optimization_barrier((near_own, *far_x))
    far_halves = opposite(*far_x)
    near_x = [along_x(near_own, 1), along_x(near_own, 3)]
    weights = assemble(chip, pieces)
    near_halves = opposite(*near_x)

    def both_cores(own, after, before, halves):
        blocks = [own, after, jnp.concatenate(halves, axis=0), before]
        return [block for own in blocks for block in (own, other_core(own))]

    def project(feats):
        depth = feats[0].shape[1]
        total = None
        for o in (0, 1, 3, 2):
            for k in (2 * o, 2 * o + 1):
                part = matmul(feats[k], weights[k * depth : (k + 1) * depth], ((1,), (0,)))
                total = part if total is None else total + part
        return total

    shared = (ratio, query, cotangent)
    far_feats = both_cores(far_own, *far_x, far_halves)
    far_total = project(far_feats)
    far_key_value = finish(far_total, key_gain)
    away = along_z(far_key_value, RING // 2)
    *earlier, far_grad = attend(far_index, *shared, far_key_value, away, query_gain, ())
    back = along_z(far_grad, RING // 2)
    far_rows = turn(far_index, far_total, far_grad, back, key_gain)
    part = first_part(far_feats, far_rows)

    near_feats = both_cores(near_own, *near_x, near_halves)
    near_total = project(near_feats)
    near_key_value = finish(near_total, key_gain)
    context, d_query, near_grad = attend(
        near_index, *shared, near_key_value, near_key_value, query_gain, earlier
    )
    near_rows = turn(near_index, near_total, near_grad, near_grad, key_gain)

    blocks = product(chip, near_feats, near_rows, part)
    total = summed([blocks[0], *scattered(blocks, outer)])
    count = total.shape[0] // RING
    parts = [total[d * count : (d + 1) * count] for d in range(RING)]
    sent = [None] + [part.astype(jnp.bfloat16) for part in parts[1:]]
    share = summed([parts[0], *scattered(sent, inner)])
    head_dim = query_gain.shape[0]
    return (context, d_query, share[:, :head_dim], share[:, head_dim:])


def solution(mesh):
    placed = (
        P("dp", None, "tensor"),
        P("dp", None, "tensor"),
        P(),
        P(),
        P("dp", "tensor"),
        P("dp", "tensor"),
        P(),
        P(),
        P(),
        P("dp", None, "tensor"),
    )
    return jax.shard_map(
        per_device,
        mesh=mesh,
        in_specs=placed,
        out_specs=(
            P("dp", None, "tensor"),
            P("dp", None, "tensor"),
            P("dp", "tensor"),
            P("dp", "tensor"),
        ),
        check_vma=False,
    )
```

profile of v0, /device:TPU:4, one launch (start us, length us, event | category | flops | bytes accessed | tf_op | source)
XLA Modules:
  0.0 178.7 jit_solution(4633942636931719306)
XLA Ops:
  9.4 3.6 %collective-permute-start.3 = (bf16[512,256]{1,0:T(8,128)(2,1)S(1)}, bf16[512,256]{1,0:T(8,128)(2,1)S(1)}, u32[]{:S(2)}, u32[]{:S(2)}) collective-permute-start(bf16[512,256]{1,0:T(8,128)(2,1)S(1)} %get-tuple-element.28), channel_id=1, source_target_pairs={{0,64},{1,17},{2,66},{3,19},{4,68},{5,21},{6,70},{7,23},{8,72},{9,... | collective-permute-start | bytes 786440 | tf_op jit(solution)/shard_map/ppermute | solution.py:30
  16.1 4.1 %collective-permute-done.3 = bf16[512,256]{1,0:T(8,128)(2,1)S(1)} collective-permute-done((bf16[512,256]{1,0:T(8,128)(2,1)S(1)}, bf16[512,256]{1,0:T(8,128)(2,1)S(1)}, u32[]{:S(2)}, u32[]{:S(2)}) %collective-permute-start.3) | collective-permute-done | bytes 262176 | tf_op jit(solution)/shard_map/ppermute | solution.py:30
  22.2 2.9 %collective-permute-start.6 = (bf16[2048,256]{1,0:T(8,128)(2,1)S(1)}, bf16[2048,256]{1,0:T(8,128)(2,1)S(1)}, u32[]{:S(2)}, u32[]{:S(2)}) collective-permute-start(bf16[2048,256]{1,0:T(8,128)(2,1)S(1)} %constant_dynamic-update-slice_fusion.refs_0_), channel_id=1, source_target_pairs={{0,16},{1,65},{2,18},{3,67},{4,20},{5,69},{6,22},{7,71},{8,24},{9,... | collective-permute-start | bytes 3145736 | tf_op jit(solution)/shard_map/ppermute | solution.py:30
  26.5 9.8 %collective-permute-done.refs_2_ = bf16[512,1024]{1,0:T(8,128)(2,1)S(1)} collective-permute-done((bf16[512,1024]{1,0:T(8,128)(2,1)S(1)}, bf16[512,1024]{1,0:T(8,128)(2,1)S(1)}, u32[]{:S(2)}, u32[]{:S(2)}) %collective-permute-start) | collective-permute-done | bytes 1048608 | tf_op jit(solution)/shard_map/ppermute | solution.py:43
  40.5 8.7 %collective-permute-done.6.refs_2_ = bf16[2048,256]{1,0:T(8,128)(2,1)S(1)} collective-permute-done((bf16[2048,256]{1,0:T(8,128)(2,1)S(1)}, bf16[2048,256]{1,0:T(8,128)(2,1)S(1)}, u32[]{:S(2)}, u32[]{:S(2)}) %collective-permute-start.6) | collective-permute-done | bytes 1048608 | tf_op jit(solution)/shard_map/ppermute | solution.py:30
  53.9 20.1 %collective-permute-done.19 = bf16[256,1024]{1,0:T(8,128)(2,1)S(1)} collective-permute-done((bf16[256,1024]{1,0:T(8,128)(2,1)S(1)}, bf16[256,1024]{1,0:T(8,128)(2,1)S(1)}, u32[]{:S(2)}, u32[]{:S(2)}) %collective-permute-start.19) | collective-permute-done | bytes 524320 | tf_op jit(solution)/shard_map/ppermute | solution.py:43
  76.0 3.0 %collective-permute-start.13 = (bf16[256,1024]{1,0:T(8,128)(2,1)S(1)}, bf16[256,1024]{1,0:T(8,128)(2,1)S(1)}, u32[]{:S(2)}, u32[]{:S(2)}) collective-permute-start(bf16[256,1024]{1,0:T(8,128)(2,1)S(1)} %slice.89), channel_id=1, source_target_pairs={{0,2},{1,3},{2,4},{3,5},{4,6},{5,7},{6,0},{7,1},{8,10},{9,11},{10,... | collective-permute-start | bytes 1572872 | tf_op jit(solution)/shard_map/ppermute | solution.py:43
  82.2 8.2 %collective-permute-done.13 = bf16[256,1024]{1,0:T(8,128)(2,1)S(1)} collective-permute-done((bf16[256,1024]{1,0:T(8,128)(2,1)S(1)}, bf16[256,1024]{1,0:T(8,128)(2,1)S(1)}, u32[]{:S(2)}, u32[]{:S(2)}) %collective-permute-start.13) | collective-permute-done | bytes 524320 | tf_op jit(solution)/shard_map/ppermute | solution.py:43
  90.4 2.7 %collective-permute-done.14 = bf16[256,1024]{1,0:T(8,128)(2,1)S(1)} collective-permute-done((bf16[256,1024]{1,0:T(8,128)(2,1)S(1)}, bf16[256,1024]{1,0:T(8,128)(2,1)S(1)}, u32[]{:S(2)}, u32[]{:S(2)}) %collective-permute-start.14) | collective-permute-done | bytes 524320 | tf_op jit(solution)/shard_map/ppermute | solution.py:43
  94.7 4.2 %collective-permute-start.22 = (bf16[512,256]{1,0:T(8,128)(2,1)S(1)}, bf16[512,256]{1,0:T(8,128)(2,1)S(1)}, u32[]{:S(2)}, u32[]{:S(2)}) collective-permute-start(bf16[512,256]{1,0:T(8,128)(2,1)S(1)} %shard_map.132.kv_ref), channel_id=1, source_target_pairs={{0,64},{8,72},{16,80},{24,88},{32,96},{40,104},{48,112},{56,120},{... | collective-permute-start | bytes 786440 | tf_op jit(solution)/shard_map/ppermute | solution.py:17
  99.3 6.5 %collective-permute-done.22.away_ref = bf16[512,256]{1,0:T(8,128)(2,1)S(1)} collective-permute-done((bf16[512,256]{1,0:T(8,128)(2,1)S(1)}, bf16[512,256]{1,0:T(8,128)(2,1)S(1)}, u32[]{:S(2)}, u32[]{:S(2)}) %collective-permute-start.22) | collective-permute-done | bytes 262176 | tf_op jit(solution)/shard_map/ppermute | solution.py:17
  105.8 5.3 %shard_map.133 = (bf16[2,128,1024]{2,1,0:T(8,128)(2,1)}, bf16[2,128,1024]{2,1,0:T(8,128)(2,1)}, bf16[512,256]{1,0:T(8,128)(2,1)S(1)}) custom-call(s32[3]{0:T(128)S(1)} %get-tuple-element.29.index.flag, f32[1]{0:T(128)S(6)} %tanh.3.ratio_ref, bf16[2,128,1024]{2,1,0:T(8,128)(2,1)S(1)} %copy-done.6, bf16[2,128,1024]{2,1,0:T(8,128)(2,1)S(1)} %copy-done.7, ...), custom_call_target="tpu_custom_call" | custom-call | flops 939524096 | bytes 1441792 | tf_op jit(solution)/shard_map/pallas_call | solution.py:366
  111.2 3.3 %collective-permute-start.23 = (bf16[512,256]{1,0:T(8,128)(2,1)S(1)}, bf16[512,256]{1,0:T(8,128)(2,1)S(1)}, u32[]{:S(2)}, u32[]{:S(2)}) collective-permute-start(bf16[512,256]{1,0:T(8,128)(2,1)S(1)} %get-tuple-element.37.grad_ref), channel_id=1, source_target_pairs={{0,64},{8,72},{16,80},{24,88},{32,96},{40,104},{48,112},{56,120},{... | collective-permute-start | bytes 786440 | tf_op jit(solution)/shard_map/ppermute | solution.py:17
  114.9 5.9 %collective-permute-done.23.other_ref = bf16[512,256]{1,0:T(8,128)(2,1)S(1)} collective-permute-done((bf16[512,256]{1,0:T(8,128)(2,1)S(1)}, bf16[512,256]{1,0:T(8,128)(2,1)S(1)}, u32[]{:S(2)}, u32[]{:S(2)}) %collective-permute-start.23) | collective-permute-done | bytes 262176 | tf_op jit(solution)/shard_map/ppermute | solution.py:17
  123.0 2.6 %shard_map.137.refs_9_ = f32[8192,256]{1,0:T(8,128)S(1)} custom-call(bf16[512,1024]{1,0:T(8,128)(2,1)S(1)} %get-tuple-element.25.refs_0_, bf16[512,1024]{1,0:T(8,128)(2,1)S(1)} %collective-permute-done.16.refs_1_, bf16[512,1024]{1,0:T(8,128)(2,1)S(1)} %collective-permute-done.refs_2_, bf16[512,1024]{1,0:T(8,128)(2,1)S(1)} %collective-permute-done.17.refs_3_, ...), custom_call_target="tpu_custom_call" | custom-call | flops 2147483648 | bytes 8388608 | tf_op jit(solution)/shard_map/pallas_call | solution.py:232
  125.7 5.3 %shard_map.134 = (bf16[2,128,1024]{2,1,0:T(8,128)(2,1)}, bf16[2,128,1024]{2,1,0:T(8,128)(2,1)}, bf16[512,256]{1,0:T(8,128)(2,1)S(1)}) custom-call(s32[3]{0:T(128)S(1)} %get-tuple-element.23.index.flag, f32[1]{0:T(128)S(6)} %tanh.3.ratio_ref, bf16[2,128,1024]{2,1,0:T(8,128)(2,1)S(1)} %copy-done.6, ...), custom_call_target="tpu_custom_call", output_to_operand_aliasing={{0}: (7, {}), {1}: (8, {})} | custom-call | flops 939524096 | bytes 1441792 | tf_op jit(solution)/shard_map/pallas_call | solution.py:366
  131.8 3.8 %shard_map.138 = (bf16[2048,256]{1,0:T(8,128)(2,1)S(1)}, bf16[2048,256]{1,0:T(8,128)(2,1)S(1)}, bf16[2048,256]{1,0:T(8,128)(2,1)S(1)}, bf16[2048,256]{1,0:T(8,128)(2,1)S(1)}) custom-call(s32[4]{0:T(128)S(1)} %get-tuple-element.27.chip, bf16[512,1024]{1,0:T(8,128)(2,1)S(1)} %get-tuple-element.26.refs_0_, ...), custom_call_target="tpu_custom_call" | custom-call | flops 2147483648 | bytes 8388608 | tf_op jit(solution)/shard_map/pallas_call | solution.py:273
  135.6 6.7 %collective-permute-start.24 = (bf16[2048,256]{1,0:T(8,128)(2,1)S(1)}, bf16[2048,256]{1,0:T(8,128)(2,1)S(1)}, u32[]{:S(2)}, u32[]{:S(2)}) collective-permute-start(bf16[2048,256]{1,0:T(8,128)(2,1)S(1)} %get-tuple-element.39), channel_id=1, source_target_pairs={{0,16},{1,65},{2,18},{3,67},{4,20},{5,69},{6,22},{7,71},{8,24},{9,... | collective-permute-start | bytes 3145736 | tf_op jit(solution)/shard_map/ppermute | solution.py:30
  142.3 3.2 %collective-permute-start.26 = (bf16[2048,256]{1,0:T(8,128)(2,1)S(1)}, bf16[2048,256]{1,0:T(8,128)(2,1)S(1)}, u32[]{:S(2)}, u32[]{:S(2)}) collective-permute-start(bf16[2048,256]{1,0:T(8,128)(2,1)S(1)} %get-tuple-element.41), channel_id=1, source_target_pairs={{0,24},{1,97},{2,26},{3,99},{4,28},{5,101},{6,30},{7,103},{8,0},{9... | collective-permute-start | bytes 3145736 | tf_op jit(solution)/shard_map/ppermute | solution.py:30
  145.6 9.6 %collective-permute-done.24 = bf16[2048,256]{1,0:T(8,128)(2,1)S(1)} collective-permute-done((bf16[2048,256]{1,0:T(8,128)(2,1)S(1)}, bf16[2048,256]{1,0:T(8,128)(2,1)S(1)}, u32[]{:S(2)}, u32[]{:S(2)}) %collective-permute-start.24) | collective-permute-done | bytes 1048608 | tf_op jit(solution)/shard_map/ppermute | solution.py:30
  155.2 11.1 %collective-permute-done.25 = bf16[2048,256]{1,0:T(8,128)(2,1)S(1)} collective-permute-done((bf16[2048,256]{1,0:T(8,128)(2,1)S(1)}, bf16[2048,256]{1,0:T(8,128)(2,1)S(1)}, u32[]{:S(2)}, u32[]{:S(2)}) %collective-permute-start.25) | collective-permute-done | bytes 1048608 | tf_op jit(solution)/shard_map/ppermute | solution.py:30
  166.9 3.1 %collective-permute-start.27 = (bf16[512,256]{1,0:T(8,128)(2,1)S(1)}, bf16[512,256]{1,0:T(8,128)(2,1)S(1)}, u32[]{:S(2)}, u32[]{:S(2)}) collective-permute-start(bf16[512,256]{1,0:T(8,128)(2,1)S(1)} %get-tuple-element.44), channel_id=1, source_target_pairs={{0,64},{1,17},{2,66},{3,19},{4,68},{5,21},{6,70},{7,23},{8,72},{9,... | collective-permute-start | bytes 786440 | tf_op jit(solution)/shard_map/ppermute | solution.py:30
  170.1 3.2 %collective-permute-start.29 = (bf16[512,256]{1,0:T(8,128)(2,1)S(1)}, bf16[512,256]{1,0:T(8,128)(2,1)S(1)}, u32[]{:S(2)}, u32[]{:S(2)}) collective-permute-start(bf16[512,256]{1,0:T(8,128)(2,1)S(1)} %get-tuple-element.45), channel_id=1, source_target_pairs={{0,96},{1,25},{2,98},{3,27},{4,100},{5,29},{6,102},{7,31},{8,104},... | collective-permute-start | bytes 786440 | tf_op jit(solution)/shard_map/ppermute | solution.py:30
  174.9 2.8 %collective-permute-done.28 = bf16[512,256]{1,0:T(8,128)(2,1)S(1)} collective-permute-done((bf16[512,256]{1,0:T(8,128)(2,1)S(1)}, bf16[512,256]{1,0:T(8,128)(2,1)S(1)}, u32[]{:S(2)}, u32[]{:S(2)}) %collective-permute-start.28) | collective-permute-done | bytes 262176 | tf_op jit(solution)/shard_map/ppermute | solution.py:30
  (96 shorter events, 37.1 us)
Async XLA Ops:
  7.4 8.6 %collective-permute-start.2 = (bf16[512,256]{1,0:T(8,128)(2,1)S(1)}, bf16[512,256]{1,0:T(8,128)(2,1)S(1)}, u32[]{:S(2)}, u32[]{:S(2)}) collective-permute-start(bf16[512,256]{1,0:T(8,128)(2,1)S(1)} %get-tuple-element.28), channel_id=1, source_target_pairs={{0,32},{1,9},{2,34},{3,11},{4,36},{5,13},{6,38},{7,15},{8,40},{9,1... | collective-permute-start | bytes 786440 | tf_op jit(solution)/shard_map/ppermute | solution.py:30
  9.4 10.7 %collective-permute-start.3 = (bf16[512,256]{1,0:T(8,128)(2,1)S(1)}, bf16[512,256]{1,0:T(8,128)(2,1)S(1)}, u32[]{:S(2)}, u32[]{:S(2)}) collective-permute-start(bf16[512,256]{1,0:T(8,128)(2,1)S(1)} %get-tuple-element.28), channel_id=1, source_target_pairs={{0,64},{1,17},{2,66},{3,19},{4,68},{5,21},{6,70},{7,23},{8,72},{9,... | collective-permute-start | bytes 786440 | tf_op jit(solution)/shard_map/ppermute | solution.py:30
  13.0 23.3 %collective-permute-start = (bf16[512,1024]{1,0:T(8,128)(2,1)S(1)}, bf16[512,1024]{1,0:T(8,128)(2,1)S(1)}, u32[]{:S(2)}, u32[]{:S(2)}) collective-permute-start(bf16[512,1024]{1,0:T(8,128)(2,1)S(1)} %get-tuple-element.25.refs_0_), channel_id=1, source_target_pairs={{0,2},{1,3},{2,4},{3,5},{4,6},{5,7},{6,0},{7,1},{8,10},{9,11},{10,... | collective-permute-start | bytes 3145736 | tf_op jit(solution)/shard_map/ppermute | solution.py:43
  15.2 23.1 %collective-permute-start.1 = (bf16[512,1024]{1,0:T(8,128)(2,1)S(1)}, bf16[512,1024]{1,0:T(8,128)(2,1)S(1)}, u32[]{:S(2)}, u32[]{:S(2)}) collective-permute-start(bf16[512,1024]{1,0:T(8,128)(2,1)S(1)} %get-tuple-element.25.refs_0_), channel_id=1, source_target_pairs={{0,6},{1,7},{2,0},{3,1},{4,2},{5,3},{6,4},{7,5},{8,14},{9,15},{10,... | collective-permute-start | bytes 3145736 | tf_op jit(solution)/shard_map/ppermute | solution.py:43
  20.6 19.6 %collective-permute-start.5 = (bf16[2048,256]{1,0:T(8,128)(2,1)S(1)}, bf16[2048,256]{1,0:T(8,128)(2,1)S(1)}, u32[]{:S(2)}, u32[]{:S(2)}) collective-permute-start(bf16[2048,256]{1,0:T(8,128)(2,1)S(1)} %constant_dynamic-update-slice_fusion.refs_0_), channel_id=1, source_target_pairs={{0,8},{1,33},{2,10},{3,35},{4,12},{5,37},{6,14},{7,39},{8,16},{9,4... | collective-permute-start | bytes 3145736 | tf_op jit(solution)/shard_map/ppermute | solution.py:30
  22.2 26.9 %collective-permute-start.6 = (bf16[2048,256]{1,0:T(8,128)(2,1)S(1)}, bf16[2048,256]{1,0:T(8,128)(2,1)S(1)}, u32[]{:S(2)}, u32[]{:S(2)}) collective-permute-start(bf16[2048,256]{1,0:T(8,128)(2,1)S(1)} %constant_dynamic-update-slice_fusion.refs_0_), channel_id=1, source_target_pairs={{0,16},{1,65},{2,18},{3,67},{4,20},{5,69},{6,22},{7,71},{8,24},{9,... | collective-permute-start | bytes 3145736 | tf_op jit(solution)/shard_map/ppermute | solution.py:30
  25.1 24.8 %collective-permute-start.7 = (bf16[2048,256]{1,0:T(8,128)(2,1)S(1)}, bf16[2048,256]{1,0:T(8,128)(2,1)S(1)}, u32[]{:S(2)}, u32[]{:S(2)}) collective-permute-start(bf16[2048,256]{1,0:T(8,128)(2,1)S(1)} %constant_dynamic-update-slice_fusion.refs_0_), channel_id=1, source_target_pairs={{0,24},{1,97},{2,26},{3,99},{4,28},{5,101},{6,30},{7,103},{8,0},{9... | collective-permute-start | bytes 3145736 | tf_op jit(solution)/shard_map/ppermute | solution.py:30
  36.3 17.0 %collective-permute-start.16 = (bf16[512,1024]{1,0:T(8,128)(2,1)S(1)}, bf16[512,1024]{1,0:T(8,128)(2,1)S(1)}, u32[]{:S(2)}, u32[]{:S(2)}) collective-permute-start(bf16[512,1024]{1,0:T(8,128)(2,1)S(1)} %get-tuple-element.25.refs_0_), channel_id=1, source_target_pairs={{0,1},{1,0},{2,3},{3,2},{4,5},{5,4},{6,7},{7,6},{8,9},{9,8},{10,11... | collective-permute-start | bytes 3145736 | tf_op jit(solution)/shard_map/ppermute | solution.py:47
  38.4 37.0 %collective-permute-start.9 = (bf16[512,1024]{1,0:T(8,128)(2,1)S(1)}, bf16[512,1024]{1,0:T(8,128)(2,1)S(1)}, u32[]{:S(2)}, u32[]{:S(2)}) collective-permute-start(bf16[512,1024]{1,0:T(8,128)(2,1)S(1)} %get-tuple-element.26.refs_0_), channel_id=1, source_target_pairs={{0,2},{1,3},{2,4},{3,5},{4,6},{5,7},{6,0},{7,1},{8,10},{9,11},{10,... | collective-permute-start | bytes 3145736 | tf_op jit(solution)/shard_map/ppermute | solution.py:43
  40.2 35.9 %collective-permute-start.11 = (bf16[512,1024]{1,0:T(8,128)(2,1)S(1)}, bf16[512,1024]{1,0:T(8,128)(2,1)S(1)}, u32[]{:S(2)}, u32[]{:S(2)}) collective-permute-start(bf16[512,1024]{1,0:T(8,128)(2,1)S(1)} %get-tuple-element.26.refs_0_), channel_id=1, source_target_pairs={{0,6},{1,7},{2,0},{3,1},{4,2},{5,3},{6,4},{7,5},{8,14},{9,15},{10,... | collective-permute-start | bytes 3145736 | tf_op jit(solution)/shard_map/ppermute | solution.py:43
  49.2 24.8 %collective-permute-start.19 = (bf16[256,1024]{1,0:T(8,128)(2,1)S(1)}, bf16[256,1024]{1,0:T(8,128)(2,1)S(1)}, u32[]{:S(2)}, u32[]{:S(2)}) collective-permute-start(bf16[256,1024]{1,0:T(8,128)(2,1)S(1)} %slice.75), channel_id=1, source_target_pairs={{0,2},{1,3},{2,4},{3,5},{4,6},{5,7},{6,0},{7,1},{8,10},{9,11},{10,... | collective-permute-start | bytes 1572872 | tf_op jit(solution)/shard_map/ppermute | solution.py:43
  50.0 24.9 %collective-permute-start.20 = (bf16[256,1024]{1,0:T(8,128)(2,1)S(1)}, bf16[256,1024]{1,0:T(8,128)(2,1)S(1)}, u32[]{:S(2)}, u32[]{:S(2)}) collective-permute-start(bf16[256,1024]{1,0:T(8,128)(2,1)S(1)} %slice.76), channel_id=1, source_target_pairs={{0,6},{1,7},{2,0},{3,1},{4,2},{5,3},{6,4},{7,5},{8,14},{9,15},{10,... | collective-permute-start | bytes 1572872 | tf_op jit(solution)/shard_map/ppermute | solution.py:43
  53.4 26.1 %collective-permute-start.18 = (bf16[512,1024]{1,0:T(8,128)(2,1)S(1)}, bf16[512,1024]{1,0:T(8,128)(2,1)S(1)}, u32[]{:S(2)}, u32[]{:S(2)}) collective-permute-start(bf16[512,1024]{1,0:T(8,128)(2,1)S(1)} %collective-permute-done.1.refs_6_), channel_id=1, source_target_pairs={{0,1},{1,0},{2,3},{3,2},{4,5},{5,4},{6,7},{7,6},{8,9},{9,8},{10,11... | collective-permute-start | bytes 3145736 | tf_op jit(solution)/shard_map/ppermute | solution.py:47
  75.4 18.1 %collective-permute-start.21 = (bf16[512,1024]{1,0:T(8,128)(2,1)S(1)}, bf16[512,1024]{1,0:T(8,128)(2,1)S(1)}, u32[]{:S(2)}, u32[]{:S(2)}) collective-permute-start(bf16[512,1024]{1,0:T(8,128)(2,1)S(1)} %constant_dynamic-update-slice_fusion.6.refs_4_), channel_id=1, source_target_pairs={{0,1},{1,0},{2,3},{3,2},{4,5},{5,4},{6,7},{7,6},{8,9},{9,8},{10,11... | collective-permute-start | bytes 3145736 | tf_op jit(solution)/shard_map/ppermute | solution.py:47
  76.0 14.3 %collective-permute-start.13 = (bf16[256,1024]{1,0:T(8,128)(2,1)S(1)}, bf16[256,1024]{1,0:T(8,128)(2,1)S(1)}, u32[]{:S(2)}, u32[]{:S(2)}) collective-permute-start(bf16[256,1024]{1,0:T(8,128)(2,1)S(1)} %slice.89), channel_id=1, source_target_pairs={{0,2},{1,3},{2,4},{3,5},{4,6},{5,7},{6,0},{7,1},{8,10},{9,11},{10,... | collective-permute-start | bytes 1572872 | tf_op jit(solution)/shard_map/ppermute | solution.py:43
  79.5 13.6 %collective-permute-start.14 = (bf16[256,1024]{1,0:T(8,128)(2,1)S(1)}, bf16[256,1024]{1,0:T(8,128)(2,1)S(1)}, u32[]{:S(2)}, u32[]{:S(2)}) collective-permute-start(bf16[256,1024]{1,0:T(8,128)(2,1)S(1)} %slice.90), channel_id=1, source_target_pairs={{0,6},{1,7},{2,0},{3,1},{4,2},{5,3},{6,4},{7,5},{8,14},{9,15},{10,... | collective-permute-start | bytes 1572872 | tf_op jit(solution)/shard_map/ppermute | solution.py:43
  80.1 41.5 %collective-permute-start.10 = (bf16[512,1024]{1,0:T(8,128)(2,1)S(1)}, bf16[512,1024]{1,0:T(8,128)(2,1)S(1)}, u32[]{:S(2)}, u32[]{:S(2)}) collective-permute-start(bf16[512,1024]{1,0:T(8,128)(2,1)S(1)} %collective-permute-done.9.refs_2_), channel_id=1, source_target_pairs={{0,1},{1,0},{2,3},{3,2},{4,5},{5,4},{6,7},{7,6},{8,9},{9,8},{10,11... | collective-permute-start | bytes 3145736 | tf_op jit(solution)/shard_map/ppermute | solution.py:47
  80.6 41.9 %collective-permute-start.12 = (bf16[512,1024]{1,0:T(8,128)(2,1)S(1)}, bf16[512,1024]{1,0:T(8,128)(2,1)S(1)}, u32[]{:S(2)}, u32[]{:S(2)}) collective-permute-start(bf16[512,1024]{1,0:T(8,128)(2,1)S(1)} %collective-permute-done.11.refs_6_), channel_id=1, source_target_pairs={{0,1},{1,0},{2,3},{3,2},{4,5},{5,4},{6,7},{7,6},{8,9},{9,8},{10,11... | collective-permute-start | bytes 3145736 | tf_op jit(solution)/shard_map/ppermute | solution.py:47
  93.2 28.8 %collective-permute-start.15 = (bf16[512,1024]{1,0:T(8,128)(2,1)S(1)}, bf16[512,1024]{1,0:T(8,128)(2,1)S(1)}, u32[]{:S(2)}, u32[]{:S(2)}) collective-permute-start(bf16[512,1024]{1,0:T(8,128)(2,1)S(1)} %constant_dynamic-update-slice_fusion.4.refs_4_), channel_id=1, source_target_pairs={{0,1},{1,0},{2,3},{3,2},{4,5},{5,4},{6,7},{7,6},{8,9},{9,8},{10,11... | collective-permute-start | bytes 3145736 | tf_op jit(solution)/shard_map/ppermute | solution.py:47
  94.7 11.1 %collective-permute-start.22 = (bf16[512,256]{1,0:T(8,128)(2,1)S(1)}, bf16[512,256]{1,0:T(8,128)(2,1)S(1)}, u32[]{:S(2)}, u32[]{:S(2)}) collective-permute-start(bf16[512,256]{1,0:T(8,128)(2,1)S(1)} %shard_map.132.kv_ref), channel_id=1, source_target_pairs={{0,64},{8,72},{16,80},{24,88},{32,96},{40,104},{48,112},{56,120},{... | collective-permute-start | bytes 786440 | tf_op jit(solution)/shard_map/ppermute | solution.py:17
  111.2 9.6 %collective-permute-start.23 = (bf16[512,256]{1,0:T(8,128)(2,1)S(1)}, bf16[512,256]{1,0:T(8,128)(2,1)S(1)}, u32[]{:S(2)}, u32[]{:S(2)}) collective-permute-start(bf16[512,256]{1,0:T(8,128)(2,1)S(1)} %get-tuple-element.37.grad_ref), channel_id=1, source_target_pairs={{0,64},{8,72},{16,80},{24,88},{32,96},{40,104},{48,112},{56,120},{... | collective-permute-start | bytes 786440 | tf_op jit(solution)/shard_map/ppermute | solution.py:17
  135.6 19.6 %collective-permute-start.24 = (bf16[2048,256]{1,0:T(8,128)(2,1)S(1)}, bf16[2048,256]{1,0:T(8,128)(2,1)S(1)}, u32[]{:S(2)}, u32[]{:S(2)}) collective-permute-start(bf16[2048,256]{1,0:T(8,128)(2,1)S(1)} %get-tuple-element.39), channel_id=1, source_target_pairs={{0,16},{1,65},{2,18},{3,67},{4,20},{5,69},{6,22},{7,71},{8,24},{9,... | collective-permute-start | bytes 3145736 | tf_op jit(solution)/shard_map/ppermute | solution.py:30
  142.3 24.0 %collective-permute-start.25 = (bf16[2048,256]{1,0:T(8,128)(2,1)S(1)}, bf16[2048,256]{1,0:T(8,128)(2,1)S(1)}, u32[]{:S(2)}, u32[]{:S(2)}) collective-permute-start(bf16[2048,256]{1,0:T(8,128)(2,1)S(1)} %get-tuple-element.40), channel_id=1, source_target_pairs={{0,8},{1,33},{2,10},{3,35},{4,12},{5,37},{6,14},{7,39},{8,16},{9,4... | collective-permute-start | bytes 3145736 | tf_op jit(solution)/shard_map/ppermute | solution.py:30
  142.3 24.0 %collective-permute-start.26 = (bf16[2048,256]{1,0:T(8,128)(2,1)S(1)}, bf16[2048,256]{1,0:T(8,128)(2,1)S(1)}, u32[]{:S(2)}, u32[]{:S(2)}) collective-permute-start(bf16[2048,256]{1,0:T(8,128)(2,1)S(1)} %get-tuple-element.41), channel_id=1, source_target_pairs={{0,24},{1,97},{2,26},{3,99},{4,28},{5,101},{6,30},{7,103},{8,0},{9... | collective-permute-start | bytes 3145736 | tf_op jit(solution)/shard_map/ppermute | solution.py:30
  (15 other events, 83.1 us)
where the time goes:
time: 180 us; the launch traced here: 179 us
  waiting for transfers between devices  93.8 us (52%)
  starting transfers between devices  47 us (26%)
  Pallas kernels  22.2 us (12%)
  matrix products  7.29 us (4%)
  local copies, waits for them, and re-layouts  5.96 us (3%)
    ppermute x8, waiting for transfers between devices, along_x(): return lax.ppermute(x, 'tensor', pairs)  43 us
    ppermute x12, waiting for transfers between devices, by_core(): return lax.ppermute(x, ('dp', 'tensor'), pairs)  38.3 us
    ppermute x12, starting transfers between devices, by_core(): return lax.ppermute(x, ('dp', 'tensor'), pairs)  28.8 us
    ppermute x2, waiting for transfers between devices, along_z(): return lax.ppermute(x, 'dp', pairs)  12.4 us
    pallas_call x2, Pallas kernels, attend(): pl.pallas_call(functools.partial(attend_kernel, heads), grid_spec=pltpu.P...  10.6 us
    ppermute x8, starting transfers between devices, along_x(): return lax.ppermute(x, 'tensor', pairs)  9.19 us
    ppermute x2, starting transfers between devices, along_z(): return lax.ppermute(x, 'dp', pairs)  7.42 us
    dot_general x16, matrix products, matmul(): lax.dot_general(a, b, (contract, ((), ())), preferred_element_type=jnp.fl...  7.29 us
  transfers between devices with their start and end apart: 30, of which 15 were waited for; matrix products, arithmetic and copies ran while one was open for 4% of the time, Pallas kernels for 4%

commit v1 on v0

--- a/solution.py
+++ b/solution.py
@@ -135,7 +135,7 @@
         out_specs=[SMEM, SMEM, SMEM, VMEM, VMEM, VMEM],
         out_shape=[numbers(3), numbers(3), numbers(4), rows, rows, weights],
         scratch_shapes=[pltpu.SemaphoreType.DMA((4,))],
-        compiler_params=PARAMS,
+        compiler_params=pltpu.CompilerParams(vmem_limit_bytes=60 * 1024 * 1024),
         cost_estimate=pl.CostEstimate(flops=0, bytes_accessed=4 * image.size, transcendentals=0),
     )(tiles, image_slot, image, key_weights, value_weights)
 
@@ -245,7 +245,8 @@
 
 def product_kernel(chip, *refs):
     sources, (grads_ref, part_ref), refs = refs[: 2 * RING], refs[2 * RING : 2 * RING + 2], refs[2 * RING + 2 :]
-    outs, (held, sems) = refs[:RING], refs[RING:]
+    outs, (held, sems) = refs[: RING + 1], refs[RING + 1 :]
+    sems_of = [sems.at[i] for i in range(len(outs))]
     depth = sources[0].shape[1]
     count = depth // 2
     z, y, x, core = chip[0], chip[1], chip[2], chip[3]
@@ -259,7 +260,9 @@
             inner_by = jnp.where(core == 0, by_z, by_y)
             start = pl.multiple_of(inner_by * count, count)
             held[outer_by, pl.ds(start, count)] = total[h * count : (h + 1) * count]
-    copies = [pltpu.make_async_copy(held.at[k], outs[k], sems.at[k]) for k in range(RING)]
+    half = held.shape[1] // 2
+    parts = (held.at[0], held.at[1], held.at[2, pl.ds(0, half)], held.at[2, pl.ds(half, half)], held.at[3])
+    copies = [pltpu.make_async_copy(part, out, sem) for part, out, sem in zip(parts, outs, sems_of)]
     for copy in copies:
         copy.start()
     for copy in copies:
@@ -270,14 +273,16 @@
     rows, depth = feats[0].shape
     both = grads.shape[1]
     shape = (RING * depth // 2, both)
+    whole = jax.ShapeDtypeStruct(shape, jnp.bfloat16)
+    half = jax.ShapeDtypeStruct((shape[0] // 2, both), jnp.bfloat16)
     return pl.pallas_call(
         product_kernel,
         in_specs=[SMEM] + [VMEM] * (len(feats) + 2),
-        out_specs=[ANY] * RING,
-        out_shape=[jax.ShapeDtypeStruct(shape, jnp.bfloat16)] * RING,
+        out_specs=[ANY] * (RING + 1),
+        out_shape=[whole, whole, half, half, whole],
         scratch_shapes=[
             pltpu.VMEM((RING, *shape), jnp.bfloat16),
-            pltpu.SemaphoreType.DMA((RING,)),
+            pltpu.SemaphoreType.DMA((RING + 1,)),
         ],
         compiler_params=PARAMS,
         cost_estimate=pl.CostEstimate(
@@ -286,6 +291,31 @@
             transcendentals=0,
         ),
     )(chip, *feats, grads, part)
+
+
+def passed_kernel(after_ref, before_ref, upper_ref, lower_ref, to_after_ref, to_before_ref):
+    half = upper_ref.shape[0]
+
+    def added(block, piece):
+        return (block.astype(jnp.float32) + piece.astype(jnp.float32)).astype(jnp.bfloat16)
+
+    to_after_ref[:half] = added(after_ref[:half], upper_ref[...])
+    to_after_ref[half:] = after_ref[half:]
+    to_before_ref[:half] = before_ref[:half]
+    to_before_ref[half:] = added(before_ref[half:], lower_ref[...])
+
+
+def passed(after, before, upper, lower):
+    return pl.pallas_call(
+        passed_kernel,
+        in_specs=[VMEM] * 4,
+        out_specs=[VMEM] * 2,
+        out_shape=[jax.ShapeDtypeStruct(after.shape, after.dtype)] * 2,
+        compiler_params=PARAMS,
+        cost_estimate=pl.CostEstimate(
+            flops=after.size, bytes_accessed=10 * after.size, transcendentals=0
+        ),
+    )(after, before, upper, lower)
 
 
 def attend_kernel(heads, index, ratio_ref, q_ref, cot_ref, kv_ref, away_ref, gain_ref, *refs):
@@ -421,11 +451,10 @@
 
     far_x = [along_x(far_own, 1), along_x(far_own, 3)]
     pieces = gathered(jnp.concatenate(gathered(shard, inner), axis=0), outer)
-    near_own, *far_x = lax.optimization_barrier((near_own, *far_x))
     far_halves = opposite(*far_x)
+    near_own, *far_halves = lax.optimization_barrier((near_own, *far_halves))
     near_x = [along_x(near_own, 1), along_x(near_own, 3)]
     weights = assemble(chip, pieces)
-    near_halves = opposite(*near_x)
 
     def both_cores(own, after, before, halves):
         blocks = [own, after, jnp.concatenate(halves, axis=0), before]
@@ -444,6 +473,8 @@
     far_feats = both_cores(far_own, *far_x, far_halves)
     far_total = project(far_feats)
     far_key_value = finish(far_total, key_gain)
+    far_key_value, *near_x = lax.optimization_barrier((far_key_value, *near_x))
+    near_halves = opposite(*near_x)
     away = along_z(far_key_value, RING // 2)
     *earlier, far_grad = attend(far_index, *shared, far_key_value, away, query_gain, ())
     back = along_z(far_grad, RING // 2)
@@ -459,7 +490,9 @@
     near_rows = turn(near_index, near_total, near_grad, near_grad, key_gain)
 
     blocks = product(chip, near_feats, near_rows, part)
-    total = summed([blocks[0], *scattered(blocks, outer)])
+    own, after, upper, lower, before = blocks
+    after, before = passed(after, before, outer(upper, 1), outer(lower, 3))
+    total = summed([own, outer(after, 1), outer(before, 3)])
     count = total.shape[0] // RING
     parts = [total[d * count : (d + 1) * count] for d in range(RING)]
     sent = [None] + [part.astype(jnp.bfloat16) for part in parts[1:]]

time: 180 us -> 173 us (0.961)
  local copies, waits for them, and re-layouts: 5.96 us -> 2.41 us
  waiting for transfers between devices: 93.8 us -> 90.4 us
  starting transfers between devices: 47 us -> 43.9 us
  Pallas kernels: 22.2 us -> 24.8 us
    ppermute x8, waiting for transfers between devices: 43 us -> 31.7 us  [along_x(): return lax.ppermute(x, 'tensor', pairs)]
    ppermute x12 -> x13, waiting for transfers between devices: 38.3 us -> 46.2 us  [by_core(): return lax.ppermute(x, ('dp', 'tensor'), pairs)]
    unnamed x23, local copies, waits for them, and re-layouts: 4.85 us -> 1.31 us
    ppermute x12 -> x13, starting transfers between devices: 28.8 us -> 25.6 us  [by_core(): return lax.ppermute(x, ('dp', 'tensor'), pairs)]
    pallas_call x1, Pallas kernels: 2.08 us -> 4.37 us  [route(): pl.pallas_call(route_kernel, in_specs=[SMEM, SMEM, HBM, HBM, HBM], out_sp...]
  transfers between devices with their start and end apart: 30 -> 31, of which waited for: 15 -> 15; matrix products, arithmetic and copies ran while one was open for 4% -> 4% of each run, Pallas kernels for 4% -> 4%
where the time goes in v1:
time: 173 us; the launch traced here: 171 us
  waiting for transfers between devices  90.4 us (52%)
  starting transfers between devices  43.9 us (25%)
  Pallas kernels  24.8 us (14%)
  matrix products  7.28 us (4%)
  local copies, waits for them, and re-layouts  2.41 us (1%)
  between operations  1.85 us (1%)
    ppermute x13, waiting for transfers between devices, by_core(): return lax.ppermute(x, ('dp', 'tensor'), pairs)  46.2 us
    ppermute x8, waiting for transfers between devices, along_x(): return lax.ppermute(x, 'tensor', pairs)  31.7 us
    ppermute x13, starting transfers between devices, by_core(): return lax.ppermute(x, ('dp', 'tensor'), pairs)  25.6 us
    ppermute x2, waiting for transfers between devices, along_z(): return lax.ppermute(x, 'dp', pairs)  12.5 us
    pallas_call x2, Pallas kernels, attend(): pl.pallas_call(functools.partial(attend_kernel, heads), grid_spec=pltpu.P...  10.6 us
    ppermute x8, starting transfers between devices, along_x(): return lax.ppermute(x, 'tensor', pairs)  9.1 us
    ppermute x2, starting transfers between devices, along_z(): return lax.ppermute(x, 'dp', pairs)  8.14 us
    dot_general x16, matrix products, matmul(): lax.dot_general(a, b, (contract, ((), ())), preferred_element_type=jnp.fl...  7.28 us
  transfers between devices with their start and end apart: 31, of which 15 were waited for; matrix products, arithmetic and copies ran while one was open for 4% of the time, Pallas kernels for 4%

profile of v1, /device:TPU:4, one launch (start us, length us, event | category | flops | bytes accessed | tf_op | source)
XLA Modules:
  0.0 171.2 jit_solution(731332335590454147)
XLA Ops:
  0.6 4.4 %shard_map.129 = (s32[3]{0:T(128)}, s32[3]{0:T(128)}, s32[4]{0:T(128)}, bf16[512,1024]{1,0:T(8,128)(2,1)}, bf16[512,1024]{1,0:T(8,128)(2,1)}, /*index=5*/bf16[512,256]{1,0:T(8,128)(2,1)}) custom-call(s32[32]{0:T(128)} %tiles.1, s32[32]{0:T(128)} %slots.1, bf16[2,512,1024]{2,1,0:T(8,128)(2,1)} %image_ref.1, bf16[512,128]{1,0:T(8,128)(2,1)} %key_ref.1, ...), custom_call_target="tpu_custom_call" | custom-call | bytes 4194304 | tf_op jit(solution)/shard_map/pallas_call | solution.py:132
  8.2 3.6 %collective-permute-start.5 = (bf16[512,256]{1,0:T(8,128)(2,1)}, bf16[512,256]{1,0:T(8,128)(2,1)S(1)}, u32[]{:S(2)}, u32[]{:S(2)}) collective-permute-start(bf16[512,256]{1,0:T(8,128)(2,1)} %get-tuple-element.34), channel_id=1, source_target_pairs={{0,64},{1,17},{2,66},{3,19},{4,68},{5,21},{6,70},{7,23},{8,72},{9,... | collective-permute-start | bytes 786440 | tf_op jit(solution)/shard_map/ppermute | solution.py:30
  14.9 4.2 %collective-permute-done.5 = bf16[512,256]{1,0:T(8,128)(2,1)S(1)} collective-permute-done((bf16[512,256]{1,0:T(8,128)(2,1)}, bf16[512,256]{1,0:T(8,128)(2,1)S(1)}, u32[]{:S(2)}, u32[]{:S(2)}) %collective-permute-start.5) | collective-permute-done | bytes 262176 | tf_op jit(solution)/shard_map/ppermute | solution.py:30
  20.9 2.9 %collective-permute-start.8 = (bf16[2048,256]{1,0:T(8,128)(2,1)S(1)}, bf16[2048,256]{1,0:T(8,128)(2,1)S(1)}, u32[]{:S(2)}, u32[]{:S(2)}) collective-permute-start(bf16[2048,256]{1,0:T(8,128)(2,1)S(1)} %constant_dynamic-update-slice_fusion.refs_0_), channel_id=1, source_target_pairs={{0,16},{1,65},{2,18},{3,67},{4,20},{5,69},{6,22},{7,71},{8,24},{9,... | collective-permute-start | bytes 3145736 | tf_op jit(solution)/shard_map/ppermute | solution.py:30
  25.1 5.1 %collective-permute-done.refs_2_ = bf16[512,1024]{1,0:T(8,128)(2,1)S(1)} collective-permute-done((bf16[512,1024]{1,0:T(8,128)(2,1)}, bf16[512,1024]{1,0:T(8,128)(2,1)S(1)}, u32[]{:S(2)}, u32[]{:S(2)}) %collective-permute-start) | collective-permute-done | bytes 1048608 | tf_op jit(solution)/shard_map/ppermute | solution.py:43
  30.9 5.2 %collective-permute-done.2.refs_6_ = bf16[512,1024]{1,0:T(8,128)(2,1)S(1)} collective-permute-done((bf16[512,1024]{1,0:T(8,128)(2,1)}, bf16[512,1024]{1,0:T(8,128)(2,1)S(1)}, u32[]{:S(2)}, u32[]{:S(2)}) %collective-permute-start.2) | collective-permute-done | bytes 1048608 | tf_op jit(solution)/shard_map/ppermute | solution.py:43
  38.2 9.5 %collective-permute-done.8.refs_2_ = bf16[2048,256]{1,0:T(8,128)(2,1)S(1)} collective-permute-done((bf16[2048,256]{1,0:T(8,128)(2,1)S(1)}, bf16[2048,256]{1,0:T(8,128)(2,1)S(1)}, u32[]{:S(2)}, u32[]{:S(2)}) %collective-permute-start.8) | collective-permute-done | bytes 1048608 | tf_op jit(solution)/shard_map/ppermute | solution.py:30
  56.1 21.2 %collective-permute-done.15.refs_2_ = bf16[512,1024]{1,0:T(8,128)(2,1)S(1)} collective-permute-done((bf16[512,1024]{1,0:T(8,128)(2,1)S(1)}, bf16[512,1024]{1,0:T(8,128)(2,1)S(1)}, u32[]{:S(2)}, u32[]{:S(2)}) %collective-permute-start.15) | collective-permute-done | bytes 1048608 | tf_op jit(solution)/shard_map/ppermute | solution.py:43
  77.5 2.8 %collective-permute-start.19 = (bf16[256,1024]{1,0:T(8,128)(2,1)S(1)}, bf16[256,1024]{1,0:T(8,128)(2,1)S(1)}, u32[]{:S(2)}, u32[]{:S(2)}) collective-permute-start(bf16[256,1024]{1,0:T(8,128)(2,1)S(1)} %slice.75), channel_id=1, source_target_pairs={{0,2},{1,3},{2,4},{3,5},{4,6},{5,7},{6,0},{7,1},{8,10},{9,11},{10,... | collective-permute-start | bytes 1572872 | tf_op jit(solution)/shard_map/ppermute | solution.py:43
  80.9 4.9 %collective-permute-start.22 = (bf16[512,256]{1,0:T(8,128)(2,1)S(1)}, bf16[512,256]{1,0:T(8,128)(2,1)S(1)}, u32[]{:S(2)}, u32[]{:S(2)}) collective-permute-start(bf16[512,256]{1,0:T(8,128)(2,1)S(1)} %shard_map.131.kv_ref), channel_id=1, source_target_pairs={{0,64},{8,72},{16,80},{24,88},{32,96},{40,104},{48,112},{56,120},{... | collective-permute-start | bytes 786440 | tf_op jit(solution)/shard_map/ppermute | solution.py:17
  86.3 6.4 %collective-permute-done.22.away_ref = bf16[512,256]{1,0:T(8,128)(2,1)S(1)} collective-permute-done((bf16[512,256]{1,0:T(8,128)(2,1)S(1)}, bf16[512,256]{1,0:T(8,128)(2,1)S(1)}, u32[]{:S(2)}, u32[]{:S(2)}) %collective-permute-start.22) | collective-permute-done | bytes 262176 | tf_op jit(solution)/shard_map/ppermute | solution.py:17
  92.8 5.3 %shard_map.133 = (bf16[2,128,1024]{2,1,0:T(8,128)(2,1)}, bf16[2,128,1024]{2,1,0:T(8,128)(2,1)}, bf16[512,256]{1,0:T(8,128)(2,1)S(1)}) custom-call(s32[3]{0:T(128)S(1)} %copy-done.5, f32[1]{0:T(128)S(6)} %tanh.3.ratio_ref, bf16[2,128,1024]{2,1,0:T(8,128)(2,1)S(1)} %copy-done.6, bf16[2,128,1024]{2,1,0:T(8,128)(2,1)S(1)} %copy-done.7, ...), custom_call_target="tpu_custom_call" | custom-call | flops 939524096 | bytes 1441792 | tf_op jit(solution)/shard_map/pallas_call | solution.py:396
  98.1 3.2 %collective-permute-start.23 = (bf16[512,256]{1,0:T(8,128)(2,1)S(1)}, bf16[512,256]{1,0:T(8,128)(2,1)S(1)}, u32[]{:S(2)}, u32[]{:S(2)}) collective-permute-start(bf16[512,256]{1,0:T(8,128)(2,1)S(1)} %get-tuple-element.46.grad_ref), channel_id=1, source_target_pairs={{0,64},{8,72},{16,80},{24,88},{32,96},{40,104},{48,112},{56,120},{... | collective-permute-start | bytes 786440 | tf_op jit(solution)/shard_map/ppermute | solution.py:17
  102.2 6.1 %collective-permute-done.23.other_ref = bf16[512,256]{1,0:T(8,128)(2,1)S(1)} collective-permute-done((bf16[512,256]{1,0:T(8,128)(2,1)S(1)}, bf16[512,256]{1,0:T(8,128)(2,1)S(1)}, u32[]{:S(2)}, u32[]{:S(2)}) %collective-permute-start.23) | collective-permute-done | bytes 262176 | tf_op jit(solution)/shard_map/ppermute | solution.py:17
  111.5 2.6 %shard_map.137.refs_9_ = f32[8192,256]{1,0:T(8,128)S(1)} custom-call(bf16[512,1024]{1,0:T(8,128)(2,1)S(1)} %copy-done, bf16[512,1024]{1,0:T(8,128)(2,1)S(1)} %collective-permute-done.11.refs_1_, bf16[512,1024]{1,0:T(8,128)(2,1)S(1)} %collective-permute-done.refs_2_, bf16[512,1024]{1,0:T(8,128)(2,1)S(1)} %collective-permute-done.12.refs_3_, ...), custom_call_target="tpu_custom_call" | custom-call | flops 2147483648 | bytes 8388608 | tf_op jit(solution)/shard_map/pallas_call | solution.py:232
  114.2 5.3 %shard_map.134 = (bf16[2,128,1024]{2,1,0:T(8,128)(2,1)}, bf16[2,128,1024]{2,1,0:T(8,128)(2,1)}, bf16[512,256]{1,0:T(8,128)(2,1)S(1)}) custom-call(s32[3]{0:T(128)S(1)} %copy-done.4, f32[1]{0:T(128)S(6)} %tanh.3.ratio_ref, bf16[2,128,1024]{2,1,0:T(8,128)(2,1)S(1)} %copy-done.6, ...), custom_call_target="tpu_custom_call", output_to_operand_aliasing={{0}: (7, {}), {1}: (8, {})} | custom-call | flops 939524096 | bytes 1441792 | tf_op jit(solution)/shard_map/pallas_call | solution.py:396
  120.3 3.8 %shard_map.138 = (bf16[2048,256]{1,0:T(8,128)(2,1)S(1)}, bf16[2048,256]{1,0:T(8,128)(2,1)S(1)}, bf16[1024,256]{1,0:T(8,128)(2,1)S(1)}, bf16[1024,256]{1,0:T(8,128)(2,1)S(1)}, bf16[2048,256]{1,0:T(8,128)(2,1)S(1)}) custom-call(s32[4]{0:T(128)S(1)} %copy-done.3, bf16[512,1024]{1,0:T(8,128)(2,1)S(1)} %copy-done.1, ...), custom_call_target="tpu_custom_call" | custom-call | flops 2147483648 | bytes 8388608 | tf_op jit(solution)/shard_map/pallas_call | solution.py:278
  127.4 7.2 %collective-permute-done.24.upper_ref = bf16[1024,256]{1,0:T(8,128)(2,1)S(1)} collective-permute-done((bf16[1024,256]{1,0:T(8,128)(2,1)S(1)}, bf16[1024,256]{1,0:T(8,128)(2,1)S(1)}, u32[]{:S(2)}, u32[]{:S(2)}) %collective-permute-start.24) | collective-permute-done | bytes 524320 | tf_op jit(solution)/shard_map/ppermute | solution.py:30
  134.6 4.3 %collective-permute-done.25.lower_ref = bf16[1024,256]{1,0:T(8,128)(2,1)S(1)} collective-permute-done((bf16[1024,256]{1,0:T(8,128)(2,1)S(1)}, bf16[1024,256]{1,0:T(8,128)(2,1)S(1)}, u32[]{:S(2)}, u32[]{:S(2)}) %collective-permute-start.25) | collective-permute-done | bytes 524320 | tf_op jit(solution)/shard_map/ppermute | solution.py:30
  142.4 12.8 %collective-permute-done.26 = bf16[2048,256]{1,0:T(8,128)(2,1)S(1)} collective-permute-done((bf16[2048,256]{1,0:T(8,128)(2,1)S(1)}, bf16[2048,256]{1,0:T(8,128)(2,1)S(1)}, u32[]{:S(2)}, u32[]{:S(2)}) %collective-permute-start.26) | collective-permute-done | bytes 1048608 | tf_op jit(solution)/shard_map/ppermute | solution.py:30
  155.2 3.6 %collective-permute-done.27 = bf16[2048,256]{1,0:T(8,128)(2,1)S(1)} collective-permute-done((bf16[2048,256]{1,0:T(8,128)(2,1)S(1)}, bf16[2048,256]{1,0:T(8,128)(2,1)S(1)}, u32[]{:S(2)}, u32[]{:S(2)}) %collective-permute-start.27) | collective-permute-done | bytes 1048608 | tf_op jit(solution)/shard_map/ppermute | solution.py:30
  159.3 3.3 %collective-permute-start.28 = (bf16[512,256]{1,0:T(8,128)(2,1)S(1)}, bf16[512,256]{1,0:T(8,128)(2,1)S(1)}, u32[]{:S(2)}, u32[]{:S(2)}) collective-permute-start(bf16[512,256]{1,0:T(8,128)(2,1)S(1)} %get-tuple-element.56), channel_id=1, source_target_pairs={{0,64},{1,17},{2,66},{3,19},{4,68},{5,21},{6,70},{7,23},{8,72},{9,... | collective-permute-start | bytes 786440 | tf_op jit(solution)/shard_map/ppermute | solution.py:30
  162.6 3.2 %collective-permute-start.30 = (bf16[512,256]{1,0:T(8,128)(2,1)S(1)}, bf16[512,256]{1,0:T(8,128)(2,1)S(1)}, u32[]{:S(2)}, u32[]{:S(2)}) collective-permute-start(bf16[512,256]{1,0:T(8,128)(2,1)S(1)} %get-tuple-element.57), channel_id=1, source_target_pairs={{0,96},{1,25},{2,98},{3,27},{4,100},{5,29},{6,102},{7,31},{8,104},... | collective-permute-start | bytes 786440 | tf_op jit(solution)/shard_map/ppermute | solution.py:30
  167.3 3.0 %collective-permute-done.29 = bf16[512,256]{1,0:T(8,128)(2,1)S(1)} collective-permute-done((bf16[512,256]{1,0:T(8,128)(2,1)S(1)}, bf16[512,256]{1,0:T(8,128)(2,1)S(1)}, u32[]{:S(2)}, u32[]{:S(2)}) %collective-permute-start.29) | collective-permute-done | bytes 262176 | tf_op jit(solution)/shard_map/ppermute | solution.py:30
  (99 shorter events, 35.5 us)
Async XLA Ops:
  5.0 25.2 %collective-permute-start = (bf16[512,1024]{1,0:T(8,128)(2,1)}, bf16[512,1024]{1,0:T(8,128)(2,1)S(1)}, u32[]{:S(2)}, u32[]{:S(2)}) collective-permute-start(bf16[512,1024]{1,0:T(8,128)(2,1)} %get-tuple-element.31.refs_0_), channel_id=1, source_target_pairs={{0,2},{1,3},{2,4},{3,5},{4,6},{5,7},{6,0},{7,1},{8,10},{9,11},{10,... | collective-permute-start | bytes 3145736 | tf_op jit(solution)/shard_map/ppermute | solution.py:43
  6.3 8.6 %collective-permute-start.4 = (bf16[512,256]{1,0:T(8,128)(2,1)}, bf16[512,256]{1,0:T(8,128)(2,1)S(1)}, u32[]{:S(2)}, u32[]{:S(2)}) collective-permute-start(bf16[512,256]{1,0:T(8,128)(2,1)} %get-tuple-element.34), channel_id=1, source_target_pairs={{0,32},{1,9},{2,34},{3,11},{4,36},{5,13},{6,38},{7,15},{8,40},{9,1... | collective-permute-start | bytes 786440 | tf_op jit(solution)/shard_map/ppermute | solution.py:30
  8.2 10.9 %collective-permute-start.5 = (bf16[512,256]{1,0:T(8,128)(2,1)}, bf16[512,256]{1,0:T(8,128)(2,1)S(1)}, u32[]{:S(2)}, u32[]{:S(2)}) collective-permute-start(bf16[512,256]{1,0:T(8,128)(2,1)} %get-tuple-element.34), channel_id=1, source_target_pairs={{0,64},{1,17},{2,66},{3,19},{4,68},{5,21},{6,70},{7,23},{8,72},{9,... | collective-permute-start | bytes 786440 | tf_op jit(solution)/shard_map/ppermute | solution.py:30
  12.8 23.3 %collective-permute-start.2 = (bf16[512,1024]{1,0:T(8,128)(2,1)}, bf16[512,1024]{1,0:T(8,128)(2,1)S(1)}, u32[]{:S(2)}, u32[]{:S(2)}) collective-permute-start(bf16[512,1024]{1,0:T(8,128)(2,1)} %get-tuple-element.31.refs_0_), channel_id=1, source_target_pairs={{0,6},{1,7},{2,0},{3,1},{4,2},{5,3},{6,4},{7,5},{8,14},{9,15},{10,... | collective-permute-start | bytes 3145736 | tf_op jit(solution)/shard_map/ppermute | solution.py:43
  19.2 18.6 %collective-permute-start.7 = (bf16[2048,256]{1,0:T(8,128)(2,1)S(1)}, bf16[2048,256]{1,0:T(8,128)(2,1)S(1)}, u32[]{:S(2)}, u32[]{:S(2)}) collective-permute-start(bf16[2048,256]{1,0:T(8,128)(2,1)S(1)} %constant_dynamic-update-slice_fusion.refs_0_), channel_id=1, source_target_pairs={{0,8},{1,33},{2,10},{3,35},{4,12},{5,37},{6,14},{7,39},{8,16},{9,4... | collective-permute-start | bytes 3145736 | tf_op jit(solution)/shard_map/ppermute | solution.py:30
  20.9 26.9 %collective-permute-start.8 = (bf16[2048,256]{1,0:T(8,128)(2,1)S(1)}, bf16[2048,256]{1,0:T(8,128)(2,1)S(1)}, u32[]{:S(2)}, u32[]{:S(2)}) collective-permute-start(bf16[2048,256]{1,0:T(8,128)(2,1)S(1)} %constant_dynamic-update-slice_fusion.refs_0_), channel_id=1, source_target_pairs={{0,16},{1,65},{2,18},{3,67},{4,20},{5,69},{6,22},{7,71},{8,24},{9,... | collective-permute-start | bytes 3145736 | tf_op jit(solution)/shard_map/ppermute | solution.py:30
  23.8 24.0 %collective-permute-start.9 = (bf16[2048,256]{1,0:T(8,128)(2,1)S(1)}, bf16[2048,256]{1,0:T(8,128)(2,1)S(1)}, u32[]{:S(2)}, u32[]{:S(2)}) collective-permute-start(bf16[2048,256]{1,0:T(8,128)(2,1)S(1)} %constant_dynamic-update-slice_fusion.refs_0_), channel_id=1, source_target_pairs={{0,24},{1,97},{2,26},{3,99},{4,28},{5,101},{6,30},{7,103},{8,0},{9... | collective-permute-start | bytes 3145736 | tf_op jit(solution)/shard_map/ppermute | solution.py:30
  30.2 19.8 %collective-permute-start.11 = (bf16[512,1024]{1,0:T(8,128)(2,1)}, bf16[512,1024]{1,0:T(8,128)(2,1)S(1)}, u32[]{:S(2)}, u32[]{:S(2)}) collective-permute-start(bf16[512,1024]{1,0:T(8,128)(2,1)} %get-tuple-element.31.refs_0_), channel_id=1, source_target_pairs={{0,1},{1,0},{2,3},{3,2},{4,5},{5,4},{6,7},{7,6},{8,9},{9,8},{10,11... | collective-permute-start | bytes 3145736 | tf_op jit(solution)/shard_map/ppermute | solution.py:47
  36.1 14.4 %collective-permute-start.1 = (bf16[256,1024]{1,0:T(8,128)(2,1)S(1)}, bf16[256,1024]{1,0:T(8,128)(2,1)S(1)}, u32[]{:S(2)}, u32[]{:S(2)}) collective-permute-start(bf16[256,1024]{1,0:T(8,128)(2,1)S(1)} %slice.83), channel_id=1, source_target_pairs={{0,2},{1,3},{2,4},{3,5},{4,6},{5,7},{6,0},{7,1},{8,10},{9,11},{10,... | collective-permute-start | bytes 1572872 | tf_op jit(solution)/shard_map/ppermute | solution.py:43
  37.8 12.7 %collective-permute-start.3 = (bf16[256,1024]{1,0:T(8,128)(2,1)S(1)}, bf16[256,1024]{1,0:T(8,128)(2,1)S(1)}, u32[]{:S(2)}, u32[]{:S(2)}) collective-permute-start(bf16[256,1024]{1,0:T(8,128)(2,1)S(1)} %slice.84), channel_id=1, source_target_pairs={{0,6},{1,7},{2,0},{3,1},{4,2},{5,3},{6,4},{7,5},{8,14},{9,15},{10,... | collective-permute-start | bytes 1572872 | tf_op jit(solution)/shard_map/ppermute | solution.py:43
  51.8 25.5 %collective-permute-start.15 = (bf16[512,1024]{1,0:T(8,128)(2,1)S(1)}, bf16[512,1024]{1,0:T(8,128)(2,1)S(1)}, u32[]{:S(2)}, u32[]{:S(2)}) collective-permute-start(bf16[512,1024]{1,0:T(8,128)(2,1)S(1)} %copy-done.1), channel_id=1, source_target_pairs={{0,2},{1,3},{2,4},{3,5},{4,6},{5,7},{6,0},{7,1},{8,10},{9,11},{10,... | collective-permute-start | bytes 3145736 | tf_op jit(solution)/shard_map/ppermute | solution.py:43
  52.3 25.1 %collective-permute-start.16 = (bf16[512,1024]{1,0:T(8,128)(2,1)S(1)}, bf16[512,1024]{1,0:T(8,128)(2,1)S(1)}, u32[]{:S(2)}, u32[]{:S(2)}) collective-permute-start(bf16[512,1024]{1,0:T(8,128)(2,1)S(1)} %copy-done.1), channel_id=1, source_target_pairs={{0,6},{1,7},{2,0},{3,1},{4,2},{5,3},{6,4},{7,5},{8,14},{9,15},{10,... | collective-permute-start | bytes 3145736 | tf_op jit(solution)/shard_map/ppermute | solution.py:43
  54.3 47.4 %collective-permute-start.10 = (bf16[512,1024]{1,0:T(8,128)(2,1)S(1)}, bf16[512,1024]{1,0:T(8,128)(2,1)S(1)}, u32[]{:S(2)}, u32[]{:S(2)}) collective-permute-start(bf16[512,1024]{1,0:T(8,128)(2,1)S(1)} %copy-done.1), channel_id=1, source_target_pairs={{0,1},{1,0},{2,3},{3,2},{4,5},{5,4},{6,7},{7,6},{8,9},{9,8},{10,11... | collective-permute-start | bytes 3145736 | tf_op jit(solution)/shard_map/ppermute | solution.py:47
  77.5 20.6 %collective-permute-start.19 = (bf16[256,1024]{1,0:T(8,128)(2,1)S(1)}, bf16[256,1024]{1,0:T(8,128)(2,1)S(1)}, u32[]{:S(2)}, u32[]{:S(2)}) collective-permute-start(bf16[256,1024]{1,0:T(8,128)(2,1)S(1)} %slice.75), channel_id=1, source_target_pairs={{0,2},{1,3},{2,4},{3,5},{4,6},{5,7},{6,0},{7,1},{8,10},{9,11},{10,... | collective-permute-start | bytes 1572872 | tf_op jit(solution)/shard_map/ppermute | solution.py:43
  80.3 21.1 %collective-permute-start.20 = (bf16[256,1024]{1,0:T(8,128)(2,1)S(1)}, bf16[256,1024]{1,0:T(8,128)(2,1)S(1)}, u32[]{:S(2)}, u32[]{:S(2)}) collective-permute-start(bf16[256,1024]{1,0:T(8,128)(2,1)S(1)} %slice.76), channel_id=1, source_target_pairs={{0,6},{1,7},{2,0},{3,1},{4,2},{5,3},{6,4},{7,5},{8,14},{9,15},{10,... | collective-permute-start | bytes 1572872 | tf_op jit(solution)/shard_map/ppermute | solution.py:43
  80.8 28.7 %collective-permute-start.17 = (bf16[512,1024]{1,0:T(8,128)(2,1)S(1)}, bf16[512,1024]{1,0:T(8,128)(2,1)S(1)}, u32[]{:S(2)}, u32[]{:S(2)}) collective-permute-start(bf16[512,1024]{1,0:T(8,128)(2,1)S(1)} %collective-permute-done.15.refs_2_), channel_id=1, source_target_pairs={{0,1},{1,0},{2,3},{3,2},{4,5},{5,4},{6,7},{7,6},{8,9},{9,8},{10,11... | collective-permute-start | bytes 3145736 | tf_op jit(solution)/shard_map/ppermute | solution.py:47
  80.9 11.8 %collective-permute-start.22 = (bf16[512,256]{1,0:T(8,128)(2,1)S(1)}, bf16[512,256]{1,0:T(8,128)(2,1)S(1)}, u32[]{:S(2)}, u32[]{:S(2)}) collective-permute-start(bf16[512,256]{1,0:T(8,128)(2,1)S(1)} %shard_map.131.kv_ref), channel_id=1, source_target_pairs={{0,64},{8,72},{16,80},{24,88},{32,96},{40,104},{48,112},{56,120},{... | collective-permute-start | bytes 786440 | tf_op jit(solution)/shard_map/ppermute | solution.py:17
  92.7 17.3 %collective-permute-start.18 = (bf16[512,1024]{1,0:T(8,128)(2,1)S(1)}, bf16[512,1024]{1,0:T(8,128)(2,1)S(1)}, u32[]{:S(2)}, u32[]{:S(2)}) collective-permute-start(bf16[512,1024]{1,0:T(8,128)(2,1)S(1)} %collective-permute-done.16.refs_6_), channel_id=1, source_target_pairs={{0,1},{1,0},{2,3},{3,2},{4,5},{5,4},{6,7},{7,6},{8,9},{9,8},{10,11... | collective-permute-start | bytes 3145736 | tf_op jit(solution)/shard_map/ppermute | solution.py:47
  98.1 10.2 %collective-permute-start.23 = (bf16[512,256]{1,0:T(8,128)(2,1)S(1)}, bf16[512,256]{1,0:T(8,128)(2,1)S(1)}, u32[]{:S(2)}, u32[]{:S(2)}) collective-permute-start(bf16[512,256]{1,0:T(8,128)(2,1)S(1)} %get-tuple-element.46.grad_ref), channel_id=1, source_target_pairs={{0,64},{8,72},{16,80},{24,88},{32,96},{40,104},{48,112},{56,120},{... | collective-permute-start | bytes 786440 | tf_op jit(solution)/shard_map/ppermute | solution.py:17
  101.4 9.1 %collective-permute-start.21 = (bf16[512,1024]{1,0:T(8,128)(2,1)S(1)}, bf16[512,1024]{1,0:T(8,128)(2,1)S(1)}, u32[]{:S(2)}, u32[]{:S(2)}) collective-permute-start(bf16[512,1024]{1,0:T(8,128)(2,1)S(1)} %constant_dynamic-update-slice_fusion.6.refs_4_), channel_id=1, source_target_pairs={{0,1},{1,0},{2,3},{3,2},{4,5},{5,4},{6,7},{7,6},{8,9},{9,8},{10,11... | collective-permute-start | bytes 3145736 | tf_op jit(solution)/shard_map/ppermute | solution.py:47
  124.1 10.5 %collective-permute-start.24 = (bf16[1024,256]{1,0:T(8,128)(2,1)S(1)}, bf16[1024,256]{1,0:T(8,128)(2,1)S(1)}, u32[]{:S(2)}, u32[]{:S(2)}) collective-permute-start(bf16[1024,256]{1,0:T(8,128)(2,1)S(1)} %get-tuple-element.50), channel_id=1, source_target_pairs={{0,8},{1,33},{2,10},{3,35},{4,12},{5,37},{6,14},{7,39},{8,16},{9,4... | collective-permute-start | bytes 1572872 | tf_op jit(solution)/shard_map/ppermute | solution.py:30
  125.7 13.1 %collective-permute-start.25 = (bf16[1024,256]{1,0:T(8,128)(2,1)S(1)}, bf16[1024,256]{1,0:T(8,128)(2,1)S(1)}, u32[]{:S(2)}, u32[]{:S(2)}) collective-permute-start(bf16[1024,256]{1,0:T(8,128)(2,1)S(1)} %get-tuple-element.51), channel_id=1, source_target_pairs={{0,24},{1,97},{2,26},{3,99},{4,28},{5,101},{6,30},{7,103},{8,0},{9... | collective-permute-start | bytes 1572872 | tf_op jit(solution)/shard_map/ppermute | solution.py:30
  139.1 16.1 %collective-permute-start.26 = (bf16[2048,256]{1,0:T(8,128)(2,1)S(1)}, bf16[2048,256]{1,0:T(8,128)(2,1)S(1)}, u32[]{:S(2)}, u32[]{:S(2)}) collective-permute-start(bf16[2048,256]{1,0:T(8,128)(2,1)S(1)} %get-tuple-element.52), channel_id=1, source_target_pairs={{0,8},{1,33},{2,10},{3,35},{4,12},{5,37},{6,14},{7,39},{8,16},{9,4... | collective-permute-start | bytes 3145736 | tf_op jit(solution)/shard_map/ppermute | solution.py:30
  141.2 17.6 %collective-permute-start.27 = (bf16[2048,256]{1,0:T(8,128)(2,1)S(1)}, bf16[2048,256]{1,0:T(8,128)(2,1)S(1)}, u32[]{:S(2)}, u32[]{:S(2)}) collective-permute-start(bf16[2048,256]{1,0:T(8,128)(2,1)S(1)} %get-tuple-element.53), channel_id=1, source_target_pairs={{0,24},{1,97},{2,26},{3,99},{4,28},{5,101},{6,30},{7,103},{8,0},{9... | collective-permute-start | bytes 3145736 | tf_op jit(solution)/shard_map/ppermute | solution.py:30
  (16 other events, 246.5 us)

commit v2 on v1

--- a/solution.py
+++ b/solution.py
@@ -90,12 +90,10 @@
 def route_kernel(tiles, slots, image_ref, key_ref, value_ref, near, far, chip, far_ref, near_ref, shard_ref, sems):
     rank, place = lax.axis_index("dp"), lax.axis_index("tensor")
     first = 2 * rank
-
-    def sample_of(slot):
-        found = lambda i, at: jnp.where(slots[i] == slot, i, at)
-        return lax.fori_loop(0, slots.shape[0], found, 0)
-
-    away = [sample_of(first + i) >> 1 != rank for i in range(2)]
+    homes = (slots[first], slots[first + 1])
+    away = [
+        jnp.logical_and(homes[0] != first + i, homes[1] != first + i) for i in range(2)
+    ]
     swaps = jnp.logical_or(away[0], away[1])
     far_slot = jnp.where(away[1], 1, 0)
     copies = []
@@ -107,9 +105,8 @@
         target = shard_ref.at[:, pl.ds(i * head_dim, head_dim)]
         copies.append(pltpu.make_async_copy(source, target, sems.at[2 + i]))
         copies[2 + i].start()
-    second_home = slots[first + 1]
-    of_slot = jnp.where(second_home == first + far_slot, 1, 0)
-    far_own = jnp.where(swaps, jnp.where(second_home >> 1 != rank, 1, 0), of_slot)
+    of_slot = jnp.where(homes[1] == first + far_slot, 1, 0)
+    far_own = jnp.where(swaps, jnp.where(homes[1] >> 1 != rank, 1, 0), of_slot)
     near[0] = 1 - far_own
     near[1] = tiles[first + 1 - far_own]
     near[2] = 0
@@ -450,15 +447,20 @@
         return along_x(after[:half], 1), along_x(before[half:], 3)
 
     far_x = [along_x(far_own, 1), along_x(far_own, 3)]
+    far_other = other_core(far_own)
+    shard, far_other = lax.optimization_barrier((shard, far_other))
     pieces = gathered(jnp.concatenate(gathered(shard, inner), axis=0), outer)
     far_halves = opposite(*far_x)
     near_own, *far_halves = lax.optimization_barrier((near_own, *far_halves))
     near_x = [along_x(near_own, 1), along_x(near_own, 3)]
     weights = assemble(chip, pieces)
-
-    def both_cores(own, after, before, halves):
-        blocks = [own, after, jnp.concatenate(halves, axis=0), before]
-        return [block for own in blocks for block in (own, other_core(own))]
+    weights, *far_blocks = lax.optimization_barrier((weights, *far_x, *far_halves))
+
+    def both_cores(own, other, after, before, *halves):
+        feats = [own, other]
+        for block in (after, jnp.concatenate(halves, axis=0), before):
+            feats += [block, other_core(block)]
+        return feats
 
     def project(feats):
         depth = feats[0].shape[1]
@@ -470,10 +472,10 @@
         return total
 
     shared = (ratio, query, cotangent)
-    far_feats = both_cores(far_own, *far_x, far_halves)
+    far_feats = both_cores(far_own, far_other, *far_blocks)
     far_total = project(far_feats)
     far_key_value = finish(far_total, key_gain)
-    far_key_value, *near_x = lax.optimization_barrier((far_key_value, *near_x))
+    _, *near_x = lax.optimization_barrier((far_key_value, *near_x))
     near_halves = opposite(*near_x)
     away = along_z(far_key_value, RING // 2)
     *earlier, far_grad = attend(far_index, *shared, far_key_value, away, query_gain, ())
@@ -481,7 +483,7 @@
     far_rows = turn(far_index, far_total, far_grad, back, key_gain)
     part = first_part(far_feats, far_rows)
 
-    near_feats = both_cores(near_own, *near_x, near_halves)
+    near_feats = both_cores(near_own, other_core(near_own), *near_x, *near_halves)
     near_total = project(near_feats)
     near_key_value = finish(near_total, key_gain)
     context, d_query, near_grad = attend(

time: 173 us -> 169 us (0.977)
  the two profiles are of different devices: /device:TPU:4 before, /device:TPU:24 now
where the time goes in v2:
time: 169 us; the launch traced here: 168 us
  waiting for transfers between devices  82 us (49%)
  starting transfers between devices  50.2 us (30%)
  Pallas kernels  24.1 us (14%)
  matrix products  7.31 us (4%)
  local copies, waits for them, and re-layouts  2.27 us (1%)
  between operations  1.84 us (1%)
    ppermute x13, waiting for transfers between devices, by_core(): return lax.ppermute(x, ('dp', 'tensor'), pairs)  36.7 us
    ppermute x8, waiting for transfers between devices, along_x(): return lax.ppermute(x, 'tensor', pairs)  33.4 us
    ppermute x13, starting transfers between devices, by_core(): return lax.ppermute(x, ('dp', 'tensor'), pairs)  29.5 us
    pallas_call x2, Pallas kernels, attend(): pl.pallas_call(functools.partial(attend_kernel, heads), grid_spec=pltpu.P...  10.6 us
    ppermute x8, starting transfers between devices, along_x(): return lax.ppermute(x, 'tensor', pairs)  10.6 us
    ppermute x2, starting transfers between devices, along_z(): return lax.ppermute(x, 'dp', pairs)  8.59 us
    dot_general x16, matrix products, matmul(): lax.dot_general(a, b, (contract, ((), ())), preferred_element_type=jnp.fl...  7.31 us
    ppermute x2, waiting for transfers between devices, along_z(): return lax.ppermute(x, 'dp', pairs)  6.48 us
  transfers between devices with their start and end apart: 31, of which 17 were waited for; matrix products, arithmetic and copies ran while one was open for 5% of the time, Pallas kernels for 4%

profile of v2, /device:TPU:24, one launch (start us, length us, event | category | flops | bytes accessed | tf_op | source)
XLA Modules:
  0.0 168.3 jit_solution(13192798395799869154)
XLA Ops:
  0.6 3.7 %shard_map.129 = (s32[3]{0:T(128)}, s32[3]{0:T(128)}, s32[4]{0:T(128)}, bf16[512,1024]{1,0:T(8,128)(2,1)}, bf16[512,1024]{1,0:T(8,128)(2,1)}, /*index=5*/bf16[512,256]{1,0:T(8,128)(2,1)}) custom-call(s32[32]{0:T(128)} %tiles.1, s32[32]{0:T(128)} %slots.1, bf16[2,512,1024]{2,1,0:T(8,128)(2,1)} %image_ref.1, bf16[512,128]{1,0:T(8,128)(2,1)} %key_ref.1, ...), custom_call_target="tpu_custom_call" | custom-call | bytes 4194304 | tf_op jit(solution)/shard_map/pallas_call | solution.py:129
  4.5 2.9 %collective-permute-done.4.refs_1_ = bf16[512,1024]{1,0:T(8,128)(2,1)S(1)} collective-permute-done((bf16[512,1024]{1,0:T(8,128)(2,1)}, bf16[512,1024]{1,0:T(8,128)(2,1)S(1)}, u32[]{:S(2)}, u32[]{:S(2)}) %collective-permute-start.4) | collective-permute-done | bytes 1048608 | tf_op jit(solution)/shard_map/ppermute | solution.py:47
  9.2 2.8 %collective-permute-start.2 = (bf16[512,1024]{1,0:T(8,128)(2,1)}, bf16[512,1024]{1,0:T(8,128)(2,1)S(1)}, u32[]{:S(2)}, u32[]{:S(2)}) collective-permute-start(bf16[512,1024]{1,0:T(8,128)(2,1)} %get-tuple-element.37.refs_0_), channel_id=1, source_target_pairs={{0,6},{1,7},{2,0},{3,1},{4,2},{5,3},{6,4},{7,5},{8,14},{9,15},{10,... | collective-permute-start | bytes 3145736 | tf_op jit(solution)/shard_map/ppermute | solution.py:43
  12.0 3.6 %collective-permute-start.6 = (bf16[512,256]{1,0:T(8,128)(2,1)}, bf16[512,256]{1,0:T(8,128)(2,1)S(1)}, u32[]{:S(2)}, u32[]{:S(2)}) collective-permute-start(bf16[512,256]{1,0:T(8,128)(2,1)} %get-tuple-element.41), channel_id=1, source_target_pairs={{0,64},{1,17},{2,66},{3,19},{4,68},{5,21},{6,70},{7,23},{8,72},{9,... | collective-permute-start | bytes 786440 | tf_op jit(solution)/shard_map/ppermute | solution.py:30
  26.3 6.8 %collective-permute-done.2.refs_6_ = bf16[512,1024]{1,0:T(8,128)(2,1)S(1)} collective-permute-done((bf16[512,1024]{1,0:T(8,128)(2,1)}, bf16[512,1024]{1,0:T(8,128)(2,1)S(1)}, u32[]{:S(2)}, u32[]{:S(2)}) %collective-permute-start.2) | collective-permute-done | bytes 1048608 | tf_op jit(solution)/shard_map/ppermute | solution.py:43
  33.1 3.7 %collective-permute-start.3 = (bf16[256,1024]{1,0:T(8,128)(2,1)S(1)}, bf16[256,1024]{1,0:T(8,128)(2,1)S(1)}, u32[]{:S(2)}, u32[]{:S(2)}) collective-permute-start(bf16[256,1024]{1,0:T(8,128)(2,1)S(1)} %slice.84), channel_id=1, source_target_pairs={{0,6},{1,7},{2,0},{3,1},{4,2},{5,3},{6,4},{7,5},{8,14},{9,15},{10,... | collective-permute-start | bytes 1572872 | tf_op jit(solution)/shard_map/ppermute | solution.py:43
  37.6 7.8 %collective-permute-done.3 = bf16[256,1024]{1,0:T(8,128)(2,1)S(1)} collective-permute-done((bf16[256,1024]{1,0:T(8,128)(2,1)S(1)}, bf16[256,1024]{1,0:T(8,128)(2,1)S(1)}, u32[]{:S(2)}, u32[]{:S(2)}) %collective-permute-start.3) | collective-permute-done | bytes 524320 | tf_op jit(solution)/shard_map/ppermute | solution.py:43
  45.5 3.5 %collective-permute-done.1 = bf16[256,1024]{1,0:T(8,128)(2,1)S(1)} collective-permute-done((bf16[256,1024]{1,0:T(8,128)(2,1)S(1)}, bf16[256,1024]{1,0:T(8,128)(2,1)S(1)}, u32[]{:S(2)}, u32[]{:S(2)}) %collective-permute-start.1) | collective-permute-done | bytes 524320 | tf_op jit(solution)/shard_map/ppermute | solution.py:43
  59.7 11.0 %collective-permute-done.16.refs_6_ = bf16[512,1024]{1,0:T(8,128)(2,1)S(1)} collective-permute-done((bf16[512,1024]{1,0:T(8,128)(2,1)S(1)}, bf16[512,1024]{1,0:T(8,128)(2,1)S(1)}, u32[]{:S(2)}, u32[]{:S(2)}) %collective-permute-start.16) | collective-permute-done | bytes 1048608 | tf_op jit(solution)/shard_map/ppermute | solution.py:43
  74.7 4.2 %collective-permute-start.22 = (bf16[512,256]{1,0:T(8,128)(2,1)S(1)}, bf16[512,256]{1,0:T(8,128)(2,1)S(1)}, u32[]{:S(2)}, u32[]{:S(2)}) collective-permute-start(bf16[512,256]{1,0:T(8,128)(2,1)S(1)} %shard_map.131.kv_ref), channel_id=1, source_target_pairs={{0,64},{8,72},{16,80},{24,88},{32,96},{40,104},{48,112},{56,120},{... | collective-permute-start | bytes 786440 | tf_op jit(solution)/shard_map/ppermute | solution.py:17
  79.9 3.0 %collective-permute-done.19 = bf16[256,1024]{1,0:T(8,128)(2,1)S(1)} collective-permute-done((bf16[256,1024]{1,0:T(8,128)(2,1)S(1)}, bf16[256,1024]{1,0:T(8,128)(2,1)S(1)}, u32[]{:S(2)}, u32[]{:S(2)}) %collective-permute-start.19) | collective-permute-done | bytes 524320 | tf_op jit(solution)/shard_map/ppermute | solution.py:43
  83.6 5.3 %shard_map.133 = (bf16[2,128,1024]{2,1,0:T(8,128)(2,1)}, bf16[2,128,1024]{2,1,0:T(8,128)(2,1)}, bf16[512,256]{1,0:T(8,128)(2,1)S(1)}) custom-call(s32[3]{0:T(128)S(1)} %copy-done.5, f32[1]{0:T(128)S(6)} %tanh.3.ratio_ref, bf16[2,128,1024]{2,1,0:T(8,128)(2,1)S(1)} %copy-done.6, bf16[2,128,1024]{2,1,0:T(8,128)(2,1)S(1)} %copy-done.7, ...), custom_call_target="tpu_custom_call" | custom-call | flops 939524096 | bytes 1441792 | tf_op jit(solution)/shard_map/pallas_call | solution.py:393
  88.9 4.3 %collective-permute-start.23 = (bf16[512,256]{1,0:T(8,128)(2,1)S(1)}, bf16[512,256]{1,0:T(8,128)(2,1)S(1)}, u32[]{:S(2)}, u32[]{:S(2)}) collective-permute-start(bf16[512,256]{1,0:T(8,128)(2,1)S(1)} %get-tuple-element.58.grad_ref), channel_id=1, source_target_pairs={{0,64},{8,72},{16,80},{24,88},{32,96},{40,104},{48,112},{56,120},{... | collective-permute-start | bytes 786440 | tf_op jit(solution)/shard_map/ppermute | solution.py:17
  93.7 6.5 %collective-permute-done.23.other_ref = bf16[512,256]{1,0:T(8,128)(2,1)S(1)} collective-permute-done((bf16[512,256]{1,0:T(8,128)(2,1)S(1)}, bf16[512,256]{1,0:T(8,128)(2,1)S(1)}, u32[]{:S(2)}, u32[]{:S(2)}) %collective-permute-start.23) | collective-permute-done | bytes 262176 | tf_op jit(solution)/shard_map/ppermute | solution.py:17
  103.0 2.6 %shard_map.137.refs_9_ = f32[8192,256]{1,0:T(8,128)S(1)} custom-call(bf16[512,1024]{1,0:T(8,128)(2,1)S(1)} %copy-done, bf16[512,1024]{1,0:T(8,128)(2,1)S(1)} %collective-permute-done.4.refs_1_, bf16[512,1024]{1,0:T(8,128)(2,1)S(1)} %collective-permute-done.refs_2_, bf16[512,1024]{1,0:T(8,128)(2,1)S(1)} %collective-permute-done.12.refs_3_, ...), custom_call_target="tpu_custom_call" | custom-call | flops 2147483648 | bytes 8388608 | tf_op jit(solution)/shard_map/pallas_call | solution.py:229
  105.7 5.3 %shard_map.134 = (bf16[2,128,1024]{2,1,0:T(8,128)(2,1)}, bf16[2,128,1024]{2,1,0:T(8,128)(2,1)}, bf16[512,256]{1,0:T(8,128)(2,1)S(1)}) custom-call(s32[3]{0:T(128)S(1)} %copy-done.4, f32[1]{0:T(128)S(6)} %tanh.3.ratio_ref, bf16[2,128,1024]{2,1,0:T(8,128)(2,1)S(1)} %copy-done.6, ...), custom_call_target="tpu_custom_call", output_to_operand_aliasing={{0}: (7, {}), {1}: (8, {})} | custom-call | flops 939524096 | bytes 1441792 | tf_op jit(solution)/shard_map/pallas_call | solution.py:393
  111.7 3.8 %shard_map.138 = (bf16[2048,256]{1,0:T(8,128)(2,1)S(1)}, bf16[2048,256]{1,0:T(8,128)(2,1)S(1)}, bf16[1024,256]{1,0:T(8,128)(2,1)S(1)}, bf16[1024,256]{1,0:T(8,128)(2,1)S(1)}, bf16[2048,256]{1,0:T(8,128)(2,1)S(1)}) custom-call(s32[4]{0:T(128)S(1)} %copy-done.3, bf16[512,1024]{1,0:T(8,128)(2,1)S(1)} %copy-done.1, ...), custom_call_target="tpu_custom_call" | custom-call | flops 2147483648 | bytes 8388608 | tf_op jit(solution)/shard_map/pallas_call | solution.py:275
  115.6 5.4 %collective-permute-start.24 = (bf16[1024,256]{1,0:T(8,128)(2,1)S(1)}, bf16[1024,256]{1,0:T(8,128)(2,1)S(1)}, u32[]{:S(2)}, u32[]{:S(2)}) collective-permute-start(bf16[1024,256]{1,0:T(8,128)(2,1)S(1)} %get-tuple-element.62), channel_id=1, source_target_pairs={{0,8},{1,33},{2,10},{3,35},{4,12},{5,37},{6,14},{7,39},{8,16},{9,4... | collective-permute-start | bytes 1572872 | tf_op jit(solution)/shard_map/ppermute | solution.py:30
  120.9 6.7 %collective-permute-done.24.upper_ref = bf16[1024,256]{1,0:T(8,128)(2,1)S(1)} collective-permute-done((bf16[1024,256]{1,0:T(8,128)(2,1)S(1)}, bf16[1024,256]{1,0:T(8,128)(2,1)S(1)}, u32[]{:S(2)}, u32[]{:S(2)}) %collective-permute-start.24) | collective-permute-done | bytes 524320 | tf_op jit(solution)/shard_map/ppermute | solution.py:30
  127.6 3.7 %collective-permute-done.25.lower_ref = bf16[1024,256]{1,0:T(8,128)(2,1)S(1)} collective-permute-done((bf16[1024,256]{1,0:T(8,128)(2,1)S(1)}, bf16[1024,256]{1,0:T(8,128)(2,1)S(1)}, u32[]{:S(2)}, u32[]{:S(2)}) %collective-permute-start.25) | collective-permute-done | bytes 524320 | tf_op jit(solution)/shard_map/ppermute | solution.py:30
  133.7 12.8 %collective-permute-done.26 = bf16[2048,256]{1,0:T(8,128)(2,1)S(1)} collective-permute-done((bf16[2048,256]{1,0:T(8,128)(2,1)S(1)}, bf16[2048,256]{1,0:T(8,128)(2,1)S(1)}, u32[]{:S(2)}, u32[]{:S(2)}) %collective-permute-start.26) | collective-permute-done | bytes 1048608 | tf_op jit(solution)/shard_map/ppermute | solution.py:30
  148.5 3.3 %collective-permute-start.28 = (bf16[512,256]{1,0:T(8,128)(2,1)S(1)}, bf16[512,256]{1,0:T(8,128)(2,1)S(1)}, u32[]{:S(2)}, u32[]{:S(2)}) collective-permute-start(bf16[512,256]{1,0:T(8,128)(2,1)S(1)} %get-tuple-element.68), channel_id=1, source_target_pairs={{0,64},{1,17},{2,66},{3,19},{4,68},{5,21},{6,70},{7,23},{8,72},{9,... | collective-permute-start | bytes 786440 | tf_op jit(solution)/shard_map/ppermute | solution.py:30
  151.8 7.5 %collective-permute-start.30 = (bf16[512,256]{1,0:T(8,128)(2,1)S(1)}, bf16[512,256]{1,0:T(8,128)(2,1)S(1)}, u32[]{:S(2)}, u32[]{:S(2)}) collective-permute-start(bf16[512,256]{1,0:T(8,128)(2,1)S(1)} %get-tuple-element.69), channel_id=1, source_target_pairs={{0,96},{1,25},{2,98},{3,27},{4,100},{5,29},{6,102},{7,31},{8,104},... | collective-permute-start | bytes 786440 | tf_op jit(solution)/shard_map/ppermute | solution.py:30
  160.1 7.2 %collective-permute-done.30 = bf16[512,256]{1,0:T(8,128)(2,1)S(1)} collective-permute-done((bf16[512,256]{1,0:T(8,128)(2,1)S(1)}, bf16[512,256]{1,0:T(8,128)(2,1)S(1)}, u32[]{:S(2)}, u32[]{:S(2)}) %collective-permute-start.30) | collective-permute-done | bytes 262176 | tf_op jit(solution)/shard_map/ppermute | solution.py:30
  (99 shorter events, 39.2 us)
Async XLA Ops:
  7.3 10.3 %collective-permute-start.5 = (bf16[512,256]{1,0:T(8,128)(2,1)}, bf16[512,256]{1,0:T(8,128)(2,1)S(1)}, u32[]{:S(2)}, u32[]{:S(2)}) collective-permute-start(bf16[512,256]{1,0:T(8,128)(2,1)} %get-tuple-element.41), channel_id=1, source_target_pairs={{0,32},{1,9},{2,34},{3,11},{4,36},{5,13},{6,38},{7,15},{8,40},{9,1... | collective-permute-start | bytes 786440 | tf_op jit(solution)/shard_map/ppermute | solution.py:30
  9.2 23.9 %collective-permute-start.2 = (bf16[512,1024]{1,0:T(8,128)(2,1)}, bf16[512,1024]{1,0:T(8,128)(2,1)S(1)}, u32[]{:S(2)}, u32[]{:S(2)}) collective-permute-start(bf16[512,1024]{1,0:T(8,128)(2,1)} %get-tuple-element.37.refs_0_), channel_id=1, source_target_pairs={{0,6},{1,7},{2,0},{3,1},{4,2},{5,3},{6,4},{7,5},{8,14},{9,15},{10,... | collective-permute-start | bytes 3145736 | tf_op jit(solution)/shard_map/ppermute | solution.py:43
  12.0 24.8 %collective-permute-start = (bf16[512,1024]{1,0:T(8,128)(2,1)}, bf16[512,1024]{1,0:T(8,128)(2,1)S(1)}, u32[]{:S(2)}, u32[]{:S(2)}) collective-permute-start(bf16[512,1024]{1,0:T(8,128)(2,1)} %get-tuple-element.37.refs_0_), channel_id=1, source_target_pairs={{0,2},{1,3},{2,4},{3,5},{4,6},{5,7},{6,0},{7,1},{8,10},{9,11},{10,... | collective-permute-start | bytes 3145736 | tf_op jit(solution)/shard_map/ppermute | solution.py:43
  22.4 28.6 %collective-permute-start.10 = (bf16[2048,256]{1,0:T(8,128)(2,1)S(1)}, bf16[2048,256]{1,0:T(8,128)(2,1)S(1)}, u32[]{:S(2)}, u32[]{:S(2)}) collective-permute-start(bf16[2048,256]{1,0:T(8,128)(2,1)S(1)} %constant_dynamic-update-slice_fusion.refs_0_), channel_id=1, source_target_pairs={{0,24},{1,97},{2,26},{3,99},{4,28},{5,101},{6,30},{7,103},{8,0},{9... | collective-permute-start | bytes 3145736 | tf_op jit(solution)/shard_map/ppermute | solution.py:30
  23.2 27.8 %collective-permute-start.9 = (bf16[2048,256]{1,0:T(8,128)(2,1)S(1)}, bf16[2048,256]{1,0:T(8,128)(2,1)S(1)}, u32[]{:S(2)}, u32[]{:S(2)}) collective-permute-start(bf16[2048,256]{1,0:T(8,128)(2,1)S(1)} %constant_dynamic-update-slice_fusion.refs_0_), channel_id=1, source_target_pairs={{0,16},{1,65},{2,18},{3,67},{4,20},{5,69},{6,22},{7,71},{8,24},{9,... | collective-permute-start | bytes 3145736 | tf_op jit(solution)/shard_map/ppermute | solution.py:30
  24.1 26.9 %collective-permute-start.8 = (bf16[2048,256]{1,0:T(8,128)(2,1)S(1)}, bf16[2048,256]{1,0:T(8,128)(2,1)S(1)}, u32[]{:S(2)}, u32[]{:S(2)}) collective-permute-start(bf16[2048,256]{1,0:T(8,128)(2,1)S(1)} %constant_dynamic-update-slice_fusion.refs_0_), channel_id=1, source_target_pairs={{0,8},{1,33},{2,10},{3,35},{4,12},{5,37},{6,14},{7,39},{8,16},{9,4... | collective-permute-start | bytes 3145736 | tf_op jit(solution)/shard_map/ppermute | solution.py:30
  33.1 12.3 %collective-permute-start.3 = (bf16[256,1024]{1,0:T(8,128)(2,1)S(1)}, bf16[256,1024]{1,0:T(8,128)(2,1)S(1)}, u32[]{:S(2)}, u32[]{:S(2)}) collective-permute-start(bf16[256,1024]{1,0:T(8,128)(2,1)S(1)} %slice.84), channel_id=1, source_target_pairs={{0,6},{1,7},{2,0},{3,1},{4,2},{5,3},{6,4},{7,5},{8,14},{9,15},{10,... | collective-permute-start | bytes 1572872 | tf_op jit(solution)/shard_map/ppermute | solution.py:43
  36.8 12.1 %collective-permute-start.1 = (bf16[256,1024]{1,0:T(8,128)(2,1)S(1)}, bf16[256,1024]{1,0:T(8,128)(2,1)S(1)}, u32[]{:S(2)}, u32[]{:S(2)}) collective-permute-start(bf16[256,1024]{1,0:T(8,128)(2,1)S(1)} %slice.83), channel_id=1, source_target_pairs={{0,2},{1,3},{2,4},{3,5},{4,6},{5,7},{6,0},{7,1},{8,10},{9,11},{10,... | collective-permute-start | bytes 1572872 | tf_op jit(solution)/shard_map/ppermute | solution.py:43
  49.0 21.7 %collective-permute-start.16 = (bf16[512,1024]{1,0:T(8,128)(2,1)S(1)}, bf16[512,1024]{1,0:T(8,128)(2,1)S(1)}, u32[]{:S(2)}, u32[]{:S(2)}) collective-permute-start(bf16[512,1024]{1,0:T(8,128)(2,1)S(1)} %copy-done.1), channel_id=1, source_target_pairs={{0,6},{1,7},{2,0},{3,1},{4,2},{5,3},{6,4},{7,5},{8,14},{9,15},{10,... | collective-permute-start | bytes 3145736 | tf_op jit(solution)/shard_map/ppermute | solution.py:43
  49.2 22.8 %collective-permute-start.15 = (bf16[512,1024]{1,0:T(8,128)(2,1)S(1)}, bf16[512,1024]{1,0:T(8,128)(2,1)S(1)}, u32[]{:S(2)}, u32[]{:S(2)}) collective-permute-start(bf16[512,1024]{1,0:T(8,128)(2,1)S(1)} %copy-done.1), channel_id=1, source_target_pairs={{0,2},{1,3},{2,4},{3,5},{4,6},{5,7},{6,0},{7,1},{8,10},{9,11},{10,... | collective-permute-start | bytes 3145736 | tf_op jit(solution)/shard_map/ppermute | solution.py:43
  56.7 17.6 %collective-permute-start.11 = (bf16[512,1024]{1,0:T(8,128)(2,1)S(1)}, bf16[512,1024]{1,0:T(8,128)(2,1)S(1)}, u32[]{:S(2)}, u32[]{:S(2)}) collective-permute-start(bf16[512,1024]{1,0:T(8,128)(2,1)S(1)} %copy-done.1), channel_id=1, source_target_pairs={{0,1},{1,0},{2,3},{3,2},{4,5},{5,4},{6,7},{7,6},{8,9},{9,8},{10,11... | collective-permute-start | bytes 3145736 | tf_op jit(solution)/shard_map/ppermute | solution.py:47
  72.1 10.8 %collective-permute-start.20 = (bf16[256,1024]{1,0:T(8,128)(2,1)S(1)}, bf16[256,1024]{1,0:T(8,128)(2,1)S(1)}, u32[]{:S(2)}, u32[]{:S(2)}) collective-permute-start(bf16[256,1024]{1,0:T(8,128)(2,1)S(1)} %slice.76), channel_id=1, source_target_pairs={{0,6},{1,7},{2,0},{3,1},{4,2},{5,3},{6,4},{7,5},{8,14},{9,15},{10,... | collective-permute-start | bytes 1572872 | tf_op jit(solution)/shard_map/ppermute | solution.py:43
  72.5 10.4 %collective-permute-start.19 = (bf16[256,1024]{1,0:T(8,128)(2,1)S(1)}, bf16[256,1024]{1,0:T(8,128)(2,1)S(1)}, u32[]{:S(2)}, u32[]{:S(2)}) collective-permute-start(bf16[256,1024]{1,0:T(8,128)(2,1)S(1)} %slice.75), channel_id=1, source_target_pairs={{0,2},{1,3},{2,4},{3,5},{4,6},{5,7},{6,0},{7,1},{8,10},{9,11},{10,... | collective-permute-start | bytes 1572872 | tf_op jit(solution)/shard_map/ppermute | solution.py:43
  74.7 8.8 %collective-permute-start.22 = (bf16[512,256]{1,0:T(8,128)(2,1)S(1)}, bf16[512,256]{1,0:T(8,128)(2,1)S(1)}, u32[]{:S(2)}, u32[]{:S(2)}) collective-permute-start(bf16[512,256]{1,0:T(8,128)(2,1)S(1)} %shard_map.131.kv_ref), channel_id=1, source_target_pairs={{0,64},{8,72},{16,80},{24,88},{32,96},{40,104},{48,112},{56,120},{... | collective-permute-start | bytes 786440 | tf_op jit(solution)/shard_map/ppermute | solution.py:17
  78.9 22.1 %collective-permute-start.17 = (bf16[512,1024]{1,0:T(8,128)(2,1)S(1)}, bf16[512,1024]{1,0:T(8,128)(2,1)S(1)}, u32[]{:S(2)}, u32[]{:S(2)}) collective-permute-start(bf16[512,1024]{1,0:T(8,128)(2,1)S(1)} %collective-permute-done.15.refs_2_), channel_id=1, source_target_pairs={{0,1},{1,0},{2,3},{3,2},{4,5},{5,4},{6,7},{7,6},{8,9},{9,8},{10,11... | collective-permute-start | bytes 3145736 | tf_op jit(solution)/shard_map/ppermute | solution.py:47
  78.9 22.5 %collective-permute-start.18 = (bf16[512,1024]{1,0:T(8,128)(2,1)S(1)}, bf16[512,1024]{1,0:T(8,128)(2,1)S(1)}, u32[]{:S(2)}, u32[]{:S(2)}) collective-permute-start(bf16[512,1024]{1,0:T(8,128)(2,1)S(1)} %collective-permute-done.16.refs_6_), channel_id=1, source_target_pairs={{0,1},{1,0},{2,3},{3,2},{4,5},{5,4},{6,7},{7,6},{8,9},{9,8},{10,11... | collective-permute-start | bytes 3145736 | tf_op jit(solution)/shard_map/ppermute | solution.py:47
  83.0 19.0 %collective-permute-start.21 = (bf16[512,1024]{1,0:T(8,128)(2,1)S(1)}, bf16[512,1024]{1,0:T(8,128)(2,1)S(1)}, u32[]{:S(2)}, u32[]{:S(2)}) collective-permute-start(bf16[512,1024]{1,0:T(8,128)(2,1)S(1)} %constant_dynamic-update-slice_fusion.6.refs_4_), channel_id=1, source_target_pairs={{0,1},{1,0},{2,3},{3,2},{4,5},{5,4},{6,7},{7,6},{8,9},{9,8},{10,11... | collective-permute-start | bytes 3145736 | tf_op jit(solution)/shard_map/ppermute | solution.py:47
  88.9 11.3 %collective-permute-start.23 = (bf16[512,256]{1,0:T(8,128)(2,1)S(1)}, bf16[512,256]{1,0:T(8,128)(2,1)S(1)}, u32[]{:S(2)}, u32[]{:S(2)}) collective-permute-start(bf16[512,256]{1,0:T(8,128)(2,1)S(1)} %get-tuple-element.58.grad_ref), channel_id=1, source_target_pairs={{0,64},{8,72},{16,80},{24,88},{32,96},{40,104},{48,112},{56,120},{... | collective-permute-start | bytes 786440 | tf_op jit(solution)/shard_map/ppermute | solution.py:17
  115.6 12.1 %collective-permute-start.24 = (bf16[1024,256]{1,0:T(8,128)(2,1)S(1)}, bf16[1024,256]{1,0:T(8,128)(2,1)S(1)}, u32[]{:S(2)}, u32[]{:S(2)}) collective-permute-start(bf16[1024,256]{1,0:T(8,128)(2,1)S(1)} %get-tuple-element.62), channel_id=1, source_target_pairs={{0,8},{1,33},{2,10},{3,35},{4,12},{5,37},{6,14},{7,39},{8,16},{9,4... | collective-permute-start | bytes 1572872 | tf_op jit(solution)/shard_map/ppermute | solution.py:30
  120.9 10.4 %collective-permute-start.25 = (bf16[1024,256]{1,0:T(8,128)(2,1)S(1)}, bf16[1024,256]{1,0:T(8,128)(2,1)S(1)}, u32[]{:S(2)}, u32[]{:S(2)}) collective-permute-start(bf16[1024,256]{1,0:T(8,128)(2,1)S(1)} %get-tuple-element.63), channel_id=1, source_target_pairs={{0,24},{1,97},{2,26},{3,99},{4,28},{5,101},{6,30},{7,103},{8,0},{9... | collective-permute-start | bytes 1572872 | tf_op jit(solution)/shard_map/ppermute | solution.py:30
  131.6 14.9 %collective-permute-start.26 = (bf16[2048,256]{1,0:T(8,128)(2,1)S(1)}, bf16[2048,256]{1,0:T(8,128)(2,1)S(1)}, u32[]{:S(2)}, u32[]{:S(2)}) collective-permute-start(bf16[2048,256]{1,0:T(8,128)(2,1)S(1)} %get-tuple-element.64), channel_id=1, source_target_pairs={{0,8},{1,33},{2,10},{3,35},{4,12},{5,37},{6,14},{7,39},{8,16},{9,4... | collective-permute-start | bytes 3145736 | tf_op jit(solution)/shard_map/ppermute | solution.py:30
  132.1 16.0 %collective-permute-start.27 = (bf16[2048,256]{1,0:T(8,128)(2,1)S(1)}, bf16[2048,256]{1,0:T(8,128)(2,1)S(1)}, u32[]{:S(2)}, u32[]{:S(2)}) collective-permute-start(bf16[2048,256]{1,0:T(8,128)(2,1)S(1)} %get-tuple-element.65), channel_id=1, source_target_pairs={{0,24},{1,97},{2,26},{3,99},{4,28},{5,101},{6,30},{7,103},{8,0},{9... | collective-permute-start | bytes 3145736 | tf_op jit(solution)/shard_map/ppermute | solution.py:30
  148.5 11.6 %collective-permute-start.28 = (bf16[512,256]{1,0:T(8,128)(2,1)S(1)}, bf16[512,256]{1,0:T(8,128)(2,1)S(1)}, u32[]{:S(2)}, u32[]{:S(2)}) collective-permute-start(bf16[512,256]{1,0:T(8,128)(2,1)S(1)} %get-tuple-element.68), channel_id=1, source_target_pairs={{0,64},{1,17},{2,66},{3,19},{4,68},{5,21},{6,70},{7,23},{8,72},{9,... | collective-permute-start | bytes 786440 | tf_op jit(solution)/shard_map/ppermute | solution.py:30
  151.8 15.5 %collective-permute-start.30 = (bf16[512,256]{1,0:T(8,128)(2,1)S(1)}, bf16[512,256]{1,0:T(8,128)(2,1)S(1)}, u32[]{:S(2)}, u32[]{:S(2)}) collective-permute-start(bf16[512,256]{1,0:T(8,128)(2,1)S(1)} %get-tuple-element.69), channel_id=1, source_target_pairs={{0,96},{1,25},{2,98},{3,27},{4,100},{5,29},{6,102},{7,31},{8,104},... | collective-permute-start | bytes 786440 | tf_op jit(solution)/shard_map/ppermute | solution.py:30
  (16 other events, 184.4 us)

commit v3 on v2

--- a/solution.py
+++ b/solution.py
@@ -87,7 +87,10 @@
 PARAMS = pltpu.CompilerParams(vmem_limit_bytes=16 * 1024 * 1024)
 
 
-def route_kernel(tiles, slots, image_ref, key_ref, value_ref, near, far, chip, far_ref, near_ref, shard_ref, sems):
+NEAR, FAR, CHIP = 0, 3, 6
+
+
+def route_kernel(tiles, slots, image_ref, numbers, far_ref, near_ref, sems):
     rank, place = lax.axis_index("dp"), lax.axis_index("tensor")
     first = 2 * rank
     homes = (slots[first], slots[first + 1])
@@ -100,48 +103,66 @@
     for i, (slot, target) in enumerate(((far_slot, far_ref), (1 - far_slot, near_ref))):
         copies.append(pltpu.make_async_copy(image_ref.at[slot], target, sems.at[i]))
         copies[i].start()
-    head_dim = key_ref.shape[1]
-    for i, source in enumerate((key_ref, value_ref)):
-        target = shard_ref.at[:, pl.ds(i * head_dim, head_dim)]
-        copies.append(pltpu.make_async_copy(source, target, sems.at[2 + i]))
-        copies[2 + i].start()
     of_slot = jnp.where(homes[1] == first + far_slot, 1, 0)
     far_own = jnp.where(swaps, jnp.where(homes[1] >> 1 != rank, 1, 0), of_slot)
-    near[0] = 1 - far_own
-    near[1] = tiles[first + 1 - far_own]
-    near[2] = 0
-    far[0] = far_own
-    far[1] = tiles[first + far_own]
-    far[2] = jnp.where(swaps, 1, 0)
-    chip[0] = rank // RING
-    chip[1] = rank % RING
-    chip[2] = place // 2
-    chip[3] = place % 2
+    numbers[NEAR] = 1 - far_own
+    numbers[NEAR + 1] = tiles[first + 1 - far_own]
+    numbers[NEAR + 2] = 0
+    numbers[FAR] = far_own
+    numbers[FAR + 1] = tiles[first + far_own]
+    numbers[FAR + 2] = jnp.where(swaps, 1, 0)
+    numbers[CHIP] = rank // RING
+    numbers[CHIP + 1] = rank % RING
+    numbers[CHIP + 2] = place // 2
+    numbers[CHIP + 3] = place % 2
     for copy in copies:
         copy.wait()
 
 
-def route(tiles, image_slot, image, key_weights, value_weights):
+def route(tiles, image_slot, image):
     rows = jax.ShapeDtypeStruct(image.shape[1:], image.dtype)
-    count, head_dim = key_weights.shape
-    weights = jax.ShapeDtypeStruct((count, 2 * head_dim), key_weights.dtype)
-    numbers = lambda n: jax.ShapeDtypeStruct((n,), jnp.int32)
     return pl.pallas_call(
         route_kernel,
-        in_specs=[SMEM, SMEM, HBM, HBM, HBM],
-        out_specs=[SMEM, SMEM, SMEM, VMEM, VMEM, VMEM],
-        out_shape=[numbers(3), numbers(3), numbers(4), rows, rows, weights],
-        scratch_shapes=[pltpu.SemaphoreType.DMA((4,))],
+        in_specs=[SMEM, SMEM, HBM],
+        out_specs=[SMEM, VMEM, VMEM],
+        out_shape=[jax.ShapeDtypeStruct((CHIP + 4,), jnp.int32), rows, rows],
+        scratch_shapes=[pltpu.SemaphoreType.DMA((2,))],
         compiler_params=pltpu.CompilerParams(vmem_limit_bytes=60 * 1024 * 1024),
         cost_estimate=pl.CostEstimate(flops=0, bytes_accessed=4 * image.size, transcendentals=0),
-    )(tiles, image_slot, image, key_weights, value_weights)
+    )(tiles, image_slot, image)
+
+
+def lay_kernel(numbers, key_ref, value_ref, out_ref, sems):
+    head_dim = key_ref.shape[1]
+    copies = []
+    for i, source in enumerate((key_ref, value_ref)):
+        target = out_ref.at[:, pl.ds(i * head_dim, head_dim)]
+        copies.append(pltpu.make_async_copy(source, target, sems.at[i]))
+        copies[i].start()
+    for copy in copies:
+        copy.wait()
+
+
+def lay(numbers, key_weights, value_weights):
+    count, head_dim = key_weights.shape
+    return pl.pallas_call(
+        lay_kernel,
+        in_specs=[SMEM, ANY, ANY],
+        out_specs=VMEM,
+        out_shape=jax.ShapeDtypeStruct((count, 2 * head_dim), key_weights.dtype),
+        scratch_shapes=[pltpu.SemaphoreType.DMA((2,))],
+        compiler_params=PARAMS,
+        cost_estimate=pl.CostEstimate(
+            flops=0, bytes_accessed=8 * count * head_dim, transcendentals=0
+        ),
+    )(numbers, key_weights, value_weights)
 
 
 def assemble_kernel(chip, *refs):
     pieces, out_ref, sems = refs[:RING], refs[RING], refs[RING + 1]
     rows, both = pieces[0].shape
     count = rows // RING
-    z, y, x, core = chip[0], chip[1], chip[2], chip[3]
+    z, y, x, core = (chip[CHIP + i] for i in range(4))
     copies = []
     for b in range(RING):
         for a in range(RING):
@@ -194,18 +215,18 @@
     )(total, gain[None, :])
 
 
-def turn_kernel(flag, total_ref, grad_ref, other_ref, gain_ref, out_ref):
+def turn_kernel(base, numbers, total_ref, grad_ref, other_ref, gain_ref, out_ref):
     head_dim = gain_ref.shape[1]
-    grad = jnp.where(flag[2] != 0, other_ref[...], grad_ref[...])
+    grad = jnp.where(numbers[base + 2] != 0, other_ref[...], grad_ref[...])
     raw = total_ref[:, :head_dim]
     d_raw = norm_back(raw, rms_factor(raw), gain_ref[...], grad[:, :head_dim].astype(jnp.float32))
     out_ref[:, :head_dim] = d_raw.astype(jnp.bfloat16)
     out_ref[:, head_dim:] = grad[:, head_dim:]
 
 
-def turn(flag, total, grad, other, gain):
-    return pl.pallas_call(
-        turn_kernel,
+def turn(base, numbers, total, grad, other, gain):
+    return pl.pallas_call(
+        functools.partial(turn_kernel, base),
         in_specs=[SMEM] + [VMEM] * 4,
         out_specs=VMEM,
         out_shape=jax.ShapeDtypeStruct(grad.shape, jnp.bfloat16),
@@ -213,7 +234,7 @@
         cost_estimate=pl.CostEstimate(
             flops=6 * grad.size, bytes_accessed=8 * grad.size, transcendentals=grad.shape[0]
         ),
-    )(flag, total, grad, other, gain[None, :])
+    )(numbers, total, grad, other, gain[None, :])
 
 
 def first_part_kernel(*refs):
@@ -242,11 +263,11 @@
 
 def product_kernel(chip, *refs):
     sources, (grads_ref, part_ref), refs = refs[: 2 * RING], refs[2 * RING : 2 * RING + 2], refs[2 * RING + 2 :]
-    outs, (held, sems) = refs[: RING + 1], refs[RING + 1 :]
+    outs, (held, sems) = refs[: 2 * RING + 2], refs[2 * RING + 2 :]
     sems_of = [sems.at[i] for i in range(len(outs))]
     depth = sources[0].shape[1]
     count = depth // 2
-    z, y, x, core = chip[0], chip[1], chip[2], chip[3]
+    z, y, x, core = (chip[CHIP + i] for i in range(4))
     for k, source in enumerate(sources):
         total = matmul(source[...], grads_ref[...], ((0,), (0,)))
         total = (total + part_ref[k * depth : (k + 1) * depth]).astype(held.dtype)
@@ -257,8 +278,12 @@
             inner_by = jnp.where(core == 0, by_z, by_y)
             start = pl.multiple_of(inner_by * count, count)
             held[outer_by, pl.ds(start, count)] = total[h * count : (h + 1) * count]
-    half = held.shape[1] // 2
-    parts = (held.at[0], held.at[1], held.at[2, pl.ds(0, half)], held.at[2, pl.ds(half, half)], held.at[3])
+    half, head_dim = held.shape[1] // 2, held.shape[2] // 2
+    parts = []
+    for i in range(2):
+        columns = pl.ds(i * head_dim, head_dim)
+        parts += [held.at[2, pl.ds(0, half), columns], held.at[2, pl.ds(half, half), columns]]
+        parts += [held.at[k, :, columns] for k in (1, 3, 0)]
     copies = [pltpu.make_async_copy(part, out, sem) for part, out, sem in zip(parts, outs, sems_of)]
     for copy in copies:
         copy.start()
@@ -270,16 +295,16 @@
     rows, depth = feats[0].shape
     both = grads.shape[1]
     shape = (RING * depth // 2, both)
-    whole = jax.ShapeDtypeStruct(shape, jnp.bfloat16)
-    half = jax.ShapeDtypeStruct((shape[0] // 2, both), jnp.bfloat16)
+    whole = jax.ShapeDtypeStruct((shape[0], both // 2), jnp.bfloat16)
+    half = jax.ShapeDtypeStruct((shape[0] // 2, both // 2), jnp.bfloat16)
     return pl.pallas_call(
         product_kernel,
         in_specs=[SMEM] + [VMEM] * (len(feats) + 2),
-        out_specs=[ANY] * (RING + 1),
-        out_shape=[whole, whole, half, half, whole],
+        out_specs=[ANY] * (2 * RING + 2),
+        out_shape=[half, half, whole, whole, whole] * 2,
         scratch_shapes=[
             pltpu.VMEM((RING, *shape), jnp.bfloat16),
-            pltpu.SemaphoreType.DMA((RING + 1,)),
+            pltpu.SemaphoreType.DMA((2 * RING + 2,)),
         ],
         compiler_params=PARAMS,
         cost_estimate=pl.CostEstimate(
@@ -315,15 +340,15 @@
     )(after, before, upper, lower)
 
 
-def attend_kernel(heads, index, ratio_ref, q_ref, cot_ref, kv_ref, away_ref, gain_ref, *refs):
+def attend_kernel(heads, base, index, ratio_ref, q_ref, cot_ref, kv_ref, away_ref, gain_ref, *refs):
     context_ref, d_query_ref, d_kv_ref, d_key_sum, d_value_sum = refs[-5:]
     step = pl.program_id(0)
     head_dim = gain_ref.shape[1]
     scale = head_dim ** (-0.5)
-    count = index[1]
+    count = index[base + 1]
     ratio = ratio_ref[0]
     gain = gain_ref[...]
-    key_value = jnp.where(index[2] != 0, away_ref[...], kv_ref[...])
+    key_value = jnp.where(index[base + 2] != 0, away_ref[...], kv_ref[...])
     keys = key_value[:, :head_dim]
     vals = key_value[:, head_dim:]
 
@@ -370,12 +395,12 @@
         d_kv_ref[:, head_dim:] = d_value_sum[...].astype(d_kv_ref.dtype)
 
 
-def attend(index, ratio, query, cot, key_value, away, gain, earlier, heads=2):
+def attend(base, index, ratio, query, cot, key_value, away, gain, earlier, heads=2):
     rows, both = key_value.shape
     head_dim = both // 2
     text = query.shape[1]
     width = heads * head_dim
-    block = pl.BlockSpec((1, text, width), lambda h, index: (index[0], 0, h))
+    block = pl.BlockSpec((1, text, width), lambda h, index: (index[base], 0, h))
     whole = lambda shape: pl.BlockSpec(shape, lambda h, index: (0, 0))
     in_specs = [
         pl.BlockSpec(memory_space=pltpu.SMEM),
@@ -391,7 +416,7 @@
         aliases = {7: 0, 8: 1}
     steps = query.shape[2] // width
     return pl.pallas_call(
-        functools.partial(attend_kernel, heads),
+        functools.partial(attend_kernel, heads, base),
         grid_spec=pltpu.PrefetchScalarGridSpec(
             num_scalar_prefetch=1,
             grid=(steps,),
@@ -438,29 +463,26 @@
     cotangent,
 ):
     ratio = jnp.tanh(gate)
-    near_index, far_index, chip, far_own, near_own, shard = route(
-        tiles, image_slot, image, key_weight_matrix, value_weight_matrix
-    )
+    numbers, far_own, near_own = route(tiles, image_slot, image)
 
     def opposite(after, before):
         half = after.shape[0] // 2
         return along_x(after[:half], 1), along_x(before[half:], 3)
 
     far_x = [along_x(far_own, 1), along_x(far_own, 3)]
-    far_other = other_core(far_own)
-    shard, far_other = lax.optimization_barrier((shard, far_other))
+    shard = lay(numbers, key_weight_matrix, value_weight_matrix)
     pieces = gathered(jnp.concatenate(gathered(shard, inner), axis=0), outer)
     far_halves = opposite(*far_x)
     near_own, *far_halves = lax.optimization_barrier((near_own, *far_halves))
     near_x = [along_x(near_own, 1), along_x(near_own, 3)]
-    weights = assemble(chip, pieces)
+    weights = assemble(numbers, pieces)
     weights, *far_blocks = lax.optimization_barrier((weights, *far_x, *far_halves))
 
-    def both_cores(own, other, after, before, *halves):
-        feats = [own, other]
-        for block in (after, jnp.concatenate(halves, axis=0), before):
-            feats += [block, other_core(block)]
-        return feats
+    def other_cores(*blocks):
+        return [other_core(block) for block in blocks]
+
+    def paired(own, other, after, before, opposite, after_other, before_other, opposite_other):
+        return [own, other, after, after_other, opposite, opposite_other, before, before_other]
 
     def project(feats):
         depth = feats[0].shape[1]
@@ -471,36 +493,50 @@
                 total = part if total is None else total + part
         return total
 
-    shared = (ratio, query, cotangent)
-    far_feats = both_cores(far_own, far_other, *far_blocks)
+    shared = (numbers, ratio, query, cotangent)
+    after, before, *halves = far_blocks
+    blocks = [after, before, jnp.concatenate(halves, axis=0)]
+    far_feats = paired(far_own, other_core(far_own), *blocks, *other_cores(*blocks))
     far_total = project(far_feats)
     far_key_value = finish(far_total, key_gain)
-    _, *near_x = lax.optimization_barrier((far_key_value, *near_x))
-    near_halves = opposite(*near_x)
     away = along_z(far_key_value, RING // 2)
-    *earlier, far_grad = attend(far_index, *shared, far_key_value, away, query_gain, ())
+    _, *near_late = lax.optimization_barrier((away, *near_x))
+    near_halves = opposite(*near_late)
+    near_others = other_cores(*near_late)
+    away, _ = lax.optimization_barrier((away, near_others[0]))
+    *earlier, far_grad = attend(FAR, *shared, far_key_value, away, query_gain, ())
     back = along_z(far_grad, RING // 2)
-    far_rows = turn(far_index, far_total, far_grad, back, key_gain)
+    far_rows = turn(FAR, numbers, far_total, far_grad, back, key_gain)
     part = first_part(far_feats, far_rows)
 
-    near_feats = both_cores(near_own, other_core(near_own), *near_x, *near_halves)
+    blocks = [*near_x, jnp.concatenate(near_halves, axis=0)]
+    near_others.append(other_core(blocks[2]))
+    near_feats = paired(near_own, other_core(near_own), *blocks, *near_others)
     near_total = project(near_feats)
     near_key_value = finish(near_total, key_gain)
     context, d_query, near_grad = attend(
-        near_index, *shared, near_key_value, near_key_value, query_gain, earlier
+        NEAR, *shared, near_key_value, near_key_value, query_gain, earlier
     )
-    near_rows = turn(near_index, near_total, near_grad, near_grad, key_gain)
-
-    blocks = product(chip, near_feats, near_rows, part)
-    own, after, upper, lower, before = blocks
-    after, before = passed(after, before, outer(upper, 1), outer(lower, 3))
-    total = summed([own, outer(after, 1), outer(before, 3)])
-    count = total.shape[0] // RING
-    parts = [total[d * count : (d + 1) * count] for d in range(RING)]
-    sent = [None] + [part.astype(jnp.bfloat16) for part in parts[1:]]
-    share = summed([parts[0], *scattered(sent, inner)])
-    head_dim = query_gain.shape[0]
-    return (context, d_query, share[:, :head_dim], share[:, head_dim:])
+    near_rows = turn(NEAR, numbers, near_total, near_grad, near_grad, key_gain)
+
+    blocks = product(numbers, near_feats, near_rows, part)
+    chains = [blocks[: RING + 1], blocks[RING + 1 :]]
+    chains = [(chain, outer(chain[0], 1), outer(chain[1], 3)) for chain in chains]
+    halves = lax.optimization_barrier(tuple(half for chain in chains for half in chain[1:]))
+    chains = [
+        (chain[0], *passed(chain[0][2], chain[0][3], *halves[2 * i : 2 * i + 2]))
+        for i, chain in enumerate(chains)
+    ]
+    totals = [
+        summed([chain[4], outer(after, 1), outer(before, 3)]) for chain, after, before in chains
+    ]
+    shares = []
+    for total in totals:
+        count = total.shape[0] // RING
+        parts = [total[d * count : (d + 1) * count] for d in range(RING)]
+        sent = [None] + [part.astype(jnp.bfloat16) for part in parts[1:]]
+        shares.append(summed([parts[0], *scattered(sent, inner)]))
+    return (context, d_query, *shares)
 
 
 def solution(mesh):

time: 169 us -> 170 us (level)
  the two profiles are of different devices: /device:TPU:24 before, /device:TPU:4 now
where the time goes in v3:
time: 170 us; the launch traced here: 169 us
  starting transfers between devices  65.7 us (39%)
  waiting for transfers between devices  63.7 us (37%)
  Pallas kernels  25.1 us (15%)
  matrix products  7.3 us (4%)
  local copies, waits for them, and re-layouts  2.92 us (2%)
  other arithmetic  2.02 us (1%)
  between operations  1.82 us (1%)
    ppermute x20, starting transfers between devices, by_core(): return lax.ppermute(x, ('dp', 'tensor'), pairs)  38.8 us
    ppermute x8, waiting for transfers between devices, along_x(): return lax.ppermute(x, 'tensor', pairs)  28.7 us
    ppermute x20, waiting for transfers between devices, by_core(): return lax.ppermute(x, ('dp', 'tensor'), pairs)  27.2 us
    ppermute x2, starting transfers between devices, along_z(): return lax.ppermute(x, 'dp', pairs)  16.2 us
    pallas_call x2, Pallas kernels, attend(): pl.pallas_call(functools.partial(attend_kernel, heads, base), grid_spec=p...  10.6 us
    ppermute x8, starting transfers between devices, along_x(): return lax.ppermute(x, 'tensor', pairs)  9.11 us
    dot_general x16, matrix products, matmul(): lax.dot_general(a, b, (contract, ((), ())), preferred_element_type=jnp.fl...  7.3 us
    ppermute x2, waiting for transfers between devices, along_z(): return lax.ppermute(x, 'dp', pairs)  6.02 us
  transfers between devices with their start and end apart: 38, of which 18 were waited for; matrix products, arithmetic and copies ran while one was open for 5% of the time, Pallas kernels for 5%

profile of v3, /device:TPU:4, one launch (start us, length us, event | category | flops | bytes accessed | tf_op | source)
XLA Modules:
  0.0 168.6 jit_solution(10211333992779811580)
XLA Ops:
  0.6 3.6 %shard_map.129 = (s32[10]{0:T(128)}, bf16[512,1024]{1,0:T(8,128)(2,1)}, bf16[512,1024]{1,0:T(8,128)(2,1)}) custom-call(s32[32]{0:T(128)} %tiles.1, s32[32]{0:T(128)} %slots.1, bf16[2,512,1024]{2,1,0:T(8,128)(2,1)} %image_ref.1), custom_call_target="tpu_custom_call" | custom-call | bytes 4194304 | tf_op jit(solution)/shard_map/pallas_call | solution.py:124
  9.4 3.6 %collective-permute-start.5 = (bf16[512,256]{1,0:T(8,128)(2,1)S(1)}, bf16[512,256]{1,0:T(8,128)(2,1)S(1)}, u32[]{:S(2)}, u32[]{:S(2)}) collective-permute-start(bf16[512,256]{1,0:T(8,128)(2,1)S(1)} %shard_map.130), channel_id=1, source_target_pairs={{0,64},{1,17},{2,66},{3,19},{4,68},{5,21},{6,70},{7,23},{8,72},{9,... | collective-permute-start | bytes 786440 | tf_op jit(solution)/shard_map/ppermute | solution.py:30
  16.0 4.1 %collective-permute-done.5 = bf16[512,256]{1,0:T(8,128)(2,1)S(1)} collective-permute-done((bf16[512,256]{1,0:T(8,128)(2,1)S(1)}, bf16[512,256]{1,0:T(8,128)(2,1)S(1)}, u32[]{:S(2)}, u32[]{:S(2)}) %collective-permute-start.5) | collective-permute-done | bytes 262176 | tf_op jit(solution)/shard_map/ppermute | solution.py:30
  21.9 2.9 %collective-permute-start.8 = (bf16[2048,256]{1,0:T(8,128)(2,1)S(1)}, bf16[2048,256]{1,0:T(8,128)(2,1)S(1)}, u32[]{:S(2)}, u32[]{:S(2)}) collective-permute-start(bf16[2048,256]{1,0:T(8,128)(2,1)S(1)} %pad_maximum_fusion.refs_0_), channel_id=1, source_target_pairs={{0,16},{1,65},{2,18},{3,67},{4,20},{5,69},{6,22},{7,71},{8,24},{9,... | collective-permute-start | bytes 3145736 | tf_op jit(solution)/shard_map/ppermute | solution.py:30
  26.1 11.5 %collective-permute-done.refs_2_ = bf16[512,1024]{1,0:T(8,128)(2,1)S(1)} collective-permute-done((bf16[512,1024]{1,0:T(8,128)(2,1)}, bf16[512,1024]{1,0:T(8,128)(2,1)S(1)}, u32[]{:S(2)}, u32[]{:S(2)}) %collective-permute-start) | collective-permute-done | bytes 1048608 | tf_op jit(solution)/shard_map/ppermute | solution.py:43
  39.9 8.9 %collective-permute-done.8.refs_2_ = bf16[2048,256]{1,0:T(8,128)(2,1)S(1)} collective-permute-done((bf16[2048,256]{1,0:T(8,128)(2,1)S(1)}, bf16[2048,256]{1,0:T(8,128)(2,1)S(1)}, u32[]{:S(2)}, u32[]{:S(2)}) %collective-permute-start.8) | collective-permute-done | bytes 1048608 | tf_op jit(solution)/shard_map/ppermute | solution.py:30
  50.1 2.8 %collective-permute-start.11 = (bf16[512,1024]{1,0:T(8,128)(2,1)S(1)}, bf16[512,1024]{1,0:T(8,128)(2,1)S(1)}, u32[]{:S(2)}, u32[]{:S(2)}) collective-permute-start(bf16[512,1024]{1,0:T(8,128)(2,1)S(1)} %copy-done.1), channel_id=1, source_target_pairs={{0,2},{1,3},{2,4},{3,5},{4,6},{5,7},{6,0},{7,1},{8,10},{9,11},{10,... | collective-permute-start | bytes 3145736 | tf_op jit(solution)/shard_map/ppermute | solution.py:43
  59.1 6.2 %collective-permute-start.16 = (bf16[512,256]{1,0:T(8,128)(2,1)S(1)}, bf16[512,256]{1,0:T(8,128)(2,1)S(1)}, u32[]{:S(2)}, u32[]{:S(2)}) collective-permute-start(bf16[512,256]{1,0:T(8,128)(2,1)S(1)} %shard_map.132.kv_ref), channel_id=1, source_target_pairs={{0,64},{8,72},{16,80},{24,88},{32,96},{40,104},{48,112},{56,120},{... | collective-permute-start | bytes 786440 | tf_op jit(solution)/shard_map/ppermute | solution.py:17
  66.0 7.0 %collective-permute-done.11.refs_2_ = bf16[512,1024]{1,0:T(8,128)(2,1)S(1)} collective-permute-done((bf16[512,1024]{1,0:T(8,128)(2,1)S(1)}, bf16[512,1024]{1,0:T(8,128)(2,1)S(1)}, u32[]{:S(2)}, u32[]{:S(2)}) %collective-permute-start.11) | collective-permute-done | bytes 1048608 | tf_op jit(solution)/shard_map/ppermute | solution.py:43
  78.0 7.5 %collective-permute-done.20 = bf16[256,1024]{1,0:T(8,128)(2,1)S(1)} collective-permute-done((bf16[256,1024]{1,0:T(8,128)(2,1)S(1)}, bf16[256,1024]{1,0:T(8,128)(2,1)S(1)}, u32[]{:S(2)}, u32[]{:S(2)}) %collective-permute-start.20) | collective-permute-done | bytes 524320 | tf_op jit(solution)/shard_map/ppermute | solution.py:43
  88.5 5.3 %shard_map.134 = (bf16[2,128,1024]{2,1,0:T(8,128)(2,1)}, bf16[2,128,1024]{2,1,0:T(8,128)(2,1)}, bf16[512,256]{1,0:T(8,128)(2,1)S(1)}) custom-call(s32[10]{0:T(128)S(1)} %copy-done.5, f32[1]{0:T(128)S(6)} %tanh.3.ratio_ref, bf16[2,128,1024]{2,1,0:T(8,128)(2,1)S(1)} %copy-done.7, bf16[2,128,1024]{2,1,0:T(8,128)(2,1)S(1)} %copy-done.8, ...), custom_call_target="tpu_custom_call" | custom-call | flops 939524096 | bytes 1441792 | tf_op jit(solution)/shard_map/pallas_call | solution.py:418
  93.8 10.0 %collective-permute-start.23 = (bf16[512,256]{1,0:T(8,128)(2,1)S(1)}, bf16[512,256]{1,0:T(8,128)(2,1)S(1)}, u32[]{:S(2)}, u32[]{:S(2)}) collective-permute-start(bf16[512,256]{1,0:T(8,128)(2,1)S(1)} %get-tuple-element.61.grad_ref), channel_id=1, source_target_pairs={{0,64},{8,72},{16,80},{24,88},{32,96},{40,104},{48,112},{56,120},{... | collective-permute-start | bytes 786440 | tf_op jit(solution)/shard_map/ppermute | solution.py:17
  104.8 6.0 %collective-permute-done.23.other_ref = bf16[512,256]{1,0:T(8,128)(2,1)S(1)} collective-permute-done((bf16[512,256]{1,0:T(8,128)(2,1)S(1)}, bf16[512,256]{1,0:T(8,128)(2,1)S(1)}, u32[]{:S(2)}, u32[]{:S(2)}) %collective-permute-start.23) | collective-permute-done | bytes 262176 | tf_op jit(solution)/shard_map/ppermute | solution.py:17
  112.6 2.6 %shard_map.138.refs_9_ = f32[8192,256]{1,0:T(8,128)S(1)} custom-call(bf16[512,1024]{1,0:T(8,128)(2,1)S(1)} %copy-done, bf16[512,1024]{1,0:T(8,128)(2,1)S(1)} %collective-permute-done.12.refs_1_, bf16[512,1024]{1,0:T(8,128)(2,1)S(1)} %collective-permute-done.refs_2_, bf16[512,1024]{1,0:T(8,128)(2,1)S(1)} %collective-permute-done.13.refs_3_, ...), custom_call_target="tpu_custom_call" | custom-call | flops 2147483648 | bytes 8388608 | tf_op jit(solution)/shard_map/pallas_call | solution.py:250
  115.3 5.3 %shard_map.135 = (bf16[2,128,1024]{2,1,0:T(8,128)(2,1)}, bf16[2,128,1024]{2,1,0:T(8,128)(2,1)}, bf16[512,256]{1,0:T(8,128)(2,1)S(1)}) custom-call(s32[10]{0:T(128)S(1)} %copy-done.5, f32[1]{0:T(128)S(6)} %tanh.3.ratio_ref, bf16[2,128,1024]{2,1,0:T(8,128)(2,1)S(1)} %copy-done.7, ...), custom_call_target="tpu_custom_call", output_to_operand_aliasing={{0}: (7, {}), {1}: (8, {})} | custom-call | flops 939524096 | bytes 1441792 | tf_op jit(solution)/shard_map/pallas_call | solution.py:418
  121.4 4.3 %shard_map.139 = (bf16[1024,128]{1,0:T(8,128)(2,1)S(1)}, bf16[1024,128]{1,0:T(8,128)(2,1)S(1)}, bf16[2048,128]{1,0:T(8,128)(2,1)S(1)}, bf16[2048,128]{1,0:T(8,12...) custom-call(s32[10]{0:T(128)S(1)} %copy-done.5, ...), custom_call_target="tpu_custom_call" | custom-call | flops 2147483648 | bytes 8388608 | tf_op jit(solution)/shard_map/pallas_call | solution.py:300
  125.8 3.2 %collective-permute-start.25 = (bf16[1024,128]{1,0:T(8,128)(2,1)S(1)}, bf16[1024,128]{1,0:T(8,128)(2,1)S(1)}, u32[]{:S(2)}, u32[]{:S(2)}) collective-permute-start(bf16[1024,128]{1,0:T(8,128)(2,1)S(1)} %get-tuple-element.66), channel_id=1, source_target_pairs={{0,24},{1,97},{2,26},{3,99},{4,28},{5,101},{6,30},{7,103},{8,0},{9... | collective-permute-start | bytes 786440 | tf_op jit(solution)/shard_map/ppermute | solution.py:30
  129.0 3.2 %collective-permute-start.27 = (bf16[1024,128]{1,0:T(8,128)(2,1)S(1)}, bf16[1024,128]{1,0:T(8,128)(2,1)S(1)}, u32[]{:S(2)}, u32[]{:S(2)}) collective-permute-start(bf16[1024,128]{1,0:T(8,128)(2,1)S(1)} %get-tuple-element.68), channel_id=1, source_target_pairs={{0,24},{1,97},{2,26},{3,99},{4,28},{5,101},{6,30},{7,103},{8,0},{9... | collective-permute-start | bytes 786440 | tf_op jit(solution)/shard_map/ppermute | solution.py:30
  133.3 3.2 %collective-permute-done.26.upper_ref = bf16[1024,128]{1,0:T(8,128)(2,1)S(1)} collective-permute-done((bf16[1024,128]{1,0:T(8,128)(2,1)S(1)}, bf16[1024,128]{1,0:T(8,128)(2,1)S(1)}, u32[]{:S(2)}, u32[]{:S(2)}) %collective-permute-start.26) | collective-permute-done | bytes 262176 | tf_op jit(solution)/shard_map/ppermute | solution.py:30
  136.8 3.3 %collective-permute-start.34 = (bf16[2048,128]{1,0:T(8,128)(2,1)S(1)}, bf16[2048,128]{1,0:T(8,128)(2,1)S(1)}, u32[]{:S(2)}, u32[]{:S(2)}) collective-permute-start(bf16[2048,128]{1,0:T(8,128)(2,1)S(1)} %get-tuple-element.79), channel_id=1, source_target_pairs={{0,24},{1,97},{2,26},{3,99},{4,28},{5,101},{6,30},{7,103},{8,0},{9... | collective-permute-start | bytes 1572872 | tf_op jit(solution)/shard_map/ppermute | solution.py:30
  140.3 3.2 %collective-permute-start.29 = (bf16[2048,128]{1,0:T(8,128)(2,1)S(1)}, bf16[2048,128]{1,0:T(8,128)(2,1)S(1)}, u32[]{:S(2)}, u32[]{:S(2)}) collective-permute-start(bf16[2048,128]{1,0:T(8,128)(2,1)S(1)} %get-tuple-element.72), channel_id=1, source_target_pairs={{0,24},{1,97},{2,26},{3,99},{4,28},{5,101},{6,30},{7,103},{8,0},{9... | collective-permute-start | bytes 1572872 | tf_op jit(solution)/shard_map/ppermute | solution.py:30
  143.6 3.6 %collective-permute-done.33 = bf16[2048,128]{1,0:T(8,128)(2,1)S(1)} collective-permute-done((bf16[2048,128]{1,0:T(8,128)(2,1)S(1)}, bf16[2048,128]{1,0:T(8,128)(2,1)S(1)}, u32[]{:S(2)}, u32[]{:S(2)}) %collective-permute-start.33) | collective-permute-done | bytes 524320 | tf_op jit(solution)/shard_map/ppermute | solution.py:30
  148.5 3.3 %collective-permute-start.35 = (bf16[512,128]{1,0:T(8,128)(2,1)S(1)}, bf16[512,128]{1,0:T(8,128)(2,1)S(1)}, u32[]{:S(2)}, u32[]{:S(2)}) collective-permute-start(bf16[512,128]{1,0:T(8,128)(2,1)S(1)} %get-tuple-element.84), channel_id=1, source_target_pairs={{0,64},{1,17},{2,66},{3,19},{4,68},{5,21},{6,70},{7,23},{8,72},{9,... | collective-permute-start | bytes 393224 | tf_op jit(solution)/shard_map/ppermute | solution.py:30
  158.3 3.3 %collective-permute-start.30 = (bf16[512,128]{1,0:T(8,128)(2,1)S(1)}, bf16[512,128]{1,0:T(8,128)(2,1)S(1)}, u32[]{:S(2)}, u32[]{:S(2)}) collective-permute-start(bf16[512,128]{1,0:T(8,128)(2,1)S(1)} %get-tuple-element.87), channel_id=1, source_target_pairs={{0,64},{1,17},{2,66},{3,19},{4,68},{5,21},{6,70},{7,23},{8,72},{9,... | collective-permute-start | bytes 393224 | tf_op jit(solution)/shard_map/ppermute | solution.py:30
  (116 shorter events, 48.6 us)
Async XLA Ops:
  14.0 23.6 %collective-permute-start = (bf16[512,1024]{1,0:T(8,128)(2,1)}, bf16[512,1024]{1,0:T(8,128)(2,1)S(1)}, u32[]{:S(2)}, u32[]{:S(2)}) collective-permute-start(bf16[512,1024]{1,0:T(8,128)(2,1)} %get-tuple-element.44.refs_0_), channel_id=1, source_target_pairs={{0,2},{1,3},{2,4},{3,5},{4,6},{5,7},{6,0},{7,1},{8,10},{9,11},{10,... | collective-permute-start | bytes 3145736 | tf_op jit(solution)/shard_map/ppermute | solution.py:43
  15.2 23.7 %collective-permute-start.2 = (bf16[512,1024]{1,0:T(8,128)(2,1)}, bf16[512,1024]{1,0:T(8,128)(2,1)S(1)}, u32[]{:S(2)}, u32[]{:S(2)}) collective-permute-start(bf16[512,1024]{1,0:T(8,128)(2,1)} %get-tuple-element.44.refs_0_), channel_id=1, source_target_pairs={{0,6},{1,7},{2,0},{3,1},{4,2},{5,3},{6,4},{7,5},{8,14},{9,15},{10,... | collective-permute-start | bytes 3145736 | tf_op jit(solution)/shard_map/ppermute | solution.py:43
  20.2 19.6 %collective-permute-start.7 = (bf16[2048,256]{1,0:T(8,128)(2,1)S(1)}, bf16[2048,256]{1,0:T(8,128)(2,1)S(1)}, u32[]{:S(2)}, u32[]{:S(2)}) collective-permute-start(bf16[2048,256]{1,0:T(8,128)(2,1)S(1)} %pad_maximum_fusion.refs_0_), channel_id=1, source_target_pairs={{0,8},{1,33},{2,10},{3,35},{4,12},{5,37},{6,14},{7,39},{8,16},{9,4... | collective-permute-start | bytes 3145736 | tf_op jit(solution)/shard_map/ppermute | solution.py:30
  21.9 26.9 %collective-permute-start.8 = (bf16[2048,256]{1,0:T(8,128)(2,1)S(1)}, bf16[2048,256]{1,0:T(8,128)(2,1)S(1)}, u32[]{:S(2)}, u32[]{:S(2)}) collective-permute-start(bf16[2048,256]{1,0:T(8,128)(2,1)S(1)} %pad_maximum_fusion.refs_0_), channel_id=1, source_target_pairs={{0,16},{1,65},{2,18},{3,67},{4,20},{5,69},{6,22},{7,71},{8,24},{9,... | collective-permute-start | bytes 3145736 | tf_op jit(solution)/shard_map/ppermute | solution.py:30
  24.8 24.0 %collective-permute-start.9 = (bf16[2048,256]{1,0:T(8,128)(2,1)S(1)}, bf16[2048,256]{1,0:T(8,128)(2,1)S(1)}, u32[]{:S(2)}, u32[]{:S(2)}) collective-permute-start(bf16[2048,256]{1,0:T(8,128)(2,1)S(1)} %pad_maximum_fusion.refs_0_), channel_id=1, source_target_pairs={{0,24},{1,97},{2,26},{3,99},{4,28},{5,101},{6,30},{7,103},{8,0},{9... | collective-permute-start | bytes 3145736 | tf_op jit(solution)/shard_map/ppermute | solution.py:30
  37.6 12.4 %collective-permute-start.1 = (bf16[256,1024]{1,0:T(8,128)(2,1)S(1)}, bf16[256,1024]{1,0:T(8,128)(2,1)S(1)}, u32[]{:S(2)}, u32[]{:S(2)}) collective-permute-start(bf16[256,1024]{1,0:T(8,128)(2,1)S(1)} %slice.94), channel_id=1, source_target_pairs={{0,2},{1,3},{2,4},{3,5},{4,6},{5,7},{6,0},{7,1},{8,10},{9,11},{10,... | collective-permute-start | bytes 1572872 | tf_op jit(solution)/shard_map/ppermute | solution.py:43
  38.9 11.1 %collective-permute-start.3 = (bf16[256,1024]{1,0:T(8,128)(2,1)S(1)}, bf16[256,1024]{1,0:T(8,128)(2,1)S(1)}, u32[]{:S(2)}, u32[]{:S(2)}) collective-permute-start(bf16[256,1024]{1,0:T(8,128)(2,1)S(1)} %slice.95), channel_id=1, source_target_pairs={{0,6},{1,7},{2,0},{3,1},{4,2},{5,3},{6,4},{7,5},{8,14},{9,15},{10,... | collective-permute-start | bytes 1572872 | tf_op jit(solution)/shard_map/ppermute | solution.py:43
  39.9 14.1 %collective-permute-start.12 = (bf16[512,1024]{1,0:T(8,128)(2,1)S(1)}, bf16[512,1024]{1,0:T(8,128)(2,1)S(1)}, u32[]{:S(2)}, u32[]{:S(2)}) collective-permute-start(bf16[512,1024]{1,0:T(8,128)(2,1)S(1)} %copy-done), channel_id=1, source_target_pairs={{0,1},{1,0},{2,3},{3,2},{4,5},{5,4},{6,7},{7,6},{8,9},{9,8},{10,11... | collective-permute-start | bytes 3145736 | tf_op jit(solution)/shard_map/ppermute | solution.py:47
  50.1 23.0 %collective-permute-start.11 = (bf16[512,1024]{1,0:T(8,128)(2,1)S(1)}, bf16[512,1024]{1,0:T(8,128)(2,1)S(1)}, u32[]{:S(2)}, u32[]{:S(2)}) collective-permute-start(bf16[512,1024]{1,0:T(8,128)(2,1)S(1)} %copy-done.1), channel_id=1, source_target_pairs={{0,2},{1,3},{2,4},{3,5},{4,6},{5,7},{6,0},{7,1},{8,10},{9,11},{10,... | collective-permute-start | bytes 3145736 | tf_op jit(solution)/shard_map/ppermute | solution.py:43
  52.9 21.1 %collective-permute-start.17 = (bf16[512,1024]{1,0:T(8,128)(2,1)S(1)}, bf16[512,1024]{1,0:T(8,128)(2,1)S(1)}, u32[]{:S(2)}, u32[]{:S(2)}) collective-permute-start(bf16[512,1024]{1,0:T(8,128)(2,1)S(1)} %copy-done.1), channel_id=1, source_target_pairs={{0,6},{1,7},{2,0},{3,1},{4,2},{5,3},{6,4},{7,5},{8,14},{9,15},{10,... | collective-permute-start | bytes 3145736 | tf_op jit(solution)/shard_map/ppermute | solution.py:43
  59.1 14.9 %collective-permute-start.16 = (bf16[512,256]{1,0:T(8,128)(2,1)S(1)}, bf16[512,256]{1,0:T(8,128)(2,1)S(1)}, u32[]{:S(2)}, u32[]{:S(2)}) collective-permute-start(bf16[512,256]{1,0:T(8,128)(2,1)S(1)} %shard_map.132.kv_ref), channel_id=1, source_target_pairs={{0,64},{8,72},{16,80},{24,88},{32,96},{40,104},{48,112},{56,120},{... | collective-permute-start | bytes 786440 | tf_op jit(solution)/shard_map/ppermute | solution.py:17
  65.3 22.1 %collective-permute-start.10 = (bf16[512,1024]{1,0:T(8,128)(2,1)S(1)}, bf16[512,1024]{1,0:T(8,128)(2,1)S(1)}, u32[]{:S(2)}, u32[]{:S(2)}) collective-permute-start(bf16[512,1024]{1,0:T(8,128)(2,1)S(1)} %copy-done.1), channel_id=1, source_target_pairs={{0,1},{1,0},{2,3},{3,2},{4,5},{5,4},{6,7},{7,6},{8,9},{9,8},{10,11... | collective-permute-start | bytes 3145736 | tf_op jit(solution)/shard_map/ppermute | solution.py:47
  74.0 11.5 %collective-permute-start.20 = (bf16[256,1024]{1,0:T(8,128)(2,1)S(1)}, bf16[256,1024]{1,0:T(8,128)(2,1)S(1)}, u32[]{:S(2)}, u32[]{:S(2)}) collective-permute-start(bf16[256,1024]{1,0:T(8,128)(2,1)S(1)} %slice.84), channel_id=1, source_target_pairs={{0,2},{1,3},{2,4},{3,5},{4,6},{5,7},{6,0},{7,1},{8,10},{9,11},{10,... | collective-permute-start | bytes 1572872 | tf_op jit(solution)/shard_map/ppermute | solution.py:43
  75.8 11.5 %collective-permute-start.21 = (bf16[256,1024]{1,0:T(8,128)(2,1)S(1)}, bf16[256,1024]{1,0:T(8,128)(2,1)S(1)}, u32[]{:S(2)}, u32[]{:S(2)}) collective-permute-start(bf16[256,1024]{1,0:T(8,128)(2,1)S(1)} %slice.85), channel_id=1, source_target_pairs={{0,6},{1,7},{2,0},{3,1},{4,2},{5,3},{6,4},{7,5},{8,14},{9,15},{10,... | collective-permute-start | bytes 1572872 | tf_op jit(solution)/shard_map/ppermute | solution.py:43
  76.7 11.7 %collective-permute-start.18 = (bf16[512,1024]{1,0:T(8,128)(2,1)S(1)}, bf16[512,1024]{1,0:T(8,128)(2,1)S(1)}, u32[]{:S(2)}, u32[]{:S(2)}) collective-permute-start(bf16[512,1024]{1,0:T(8,128)(2,1)S(1)} %collective-permute-done.11.refs_2_), channel_id=1, source_target_pairs={{0,1},{1,0},{2,3},{3,2},{4,5},{5,4},{6,7},{7,6},{8,9},{9,8},{10,11... | collective-permute-start | bytes 3145736 | tf_op jit(solution)/shard_map/ppermute | solution.py:47
  77.3 27.0 %collective-permute-start.19 = (bf16[512,1024]{1,0:T(8,128)(2,1)S(1)}, bf16[512,1024]{1,0:T(8,128)(2,1)S(1)}, u32[]{:S(2)}, u32[]{:S(2)}) collective-permute-start(bf16[512,1024]{1,0:T(8,128)(2,1)S(1)} %collective-permute-done.17.refs_6_), channel_id=1, source_target_pairs={{0,1},{1,0},{2,3},{3,2},{4,5},{5,4},{6,7},{7,6},{8,9},{9,8},{10,11... | collective-permute-start | bytes 3145736 | tf_op jit(solution)/shard_map/ppermute | solution.py:47
  87.4 24.2 %collective-permute-start.22 = (bf16[512,1024]{1,0:T(8,128)(2,1)S(1)}, bf16[512,1024]{1,0:T(8,128)(2,1)S(1)}, u32[]{:S(2)}, u32[]{:S(2)}) collective-permute-start(bf16[512,1024]{1,0:T(8,128)(2,1)S(1)} %constant_dynamic-update-slice_fusion.2.refs_4_), channel_id=1, source_target_pairs={{0,1},{1,0},{2,3},{3,2},{4,5},{5,4},{6,7},{7,6},{8,9},{9,8},{10,11... | collective-permute-start | bytes 3145736 | tf_op jit(solution)/shard_map/ppermute | solution.py:47
  93.8 17.0 %collective-permute-start.23 = (bf16[512,256]{1,0:T(8,128)(2,1)S(1)}, bf16[512,256]{1,0:T(8,128)(2,1)S(1)}, u32[]{:S(2)}, u32[]{:S(2)}) collective-permute-start(bf16[512,256]{1,0:T(8,128)(2,1)S(1)} %get-tuple-element.61.grad_ref), channel_id=1, source_target_pairs={{0,64},{8,72},{16,80},{24,88},{32,96},{40,104},{48,112},{56,120},{... | collective-permute-start | bytes 786440 | tf_op jit(solution)/shard_map/ppermute | solution.py:17
  136.8 11.4 %collective-permute-start.34 = (bf16[2048,128]{1,0:T(8,128)(2,1)S(1)}, bf16[2048,128]{1,0:T(8,128)(2,1)S(1)}, u32[]{:S(2)}, u32[]{:S(2)}) collective-permute-start(bf16[2048,128]{1,0:T(8,128)(2,1)S(1)} %get-tuple-element.79), channel_id=1, source_target_pairs={{0,24},{1,97},{2,26},{3,99},{4,28},{5,101},{6,30},{7,103},{8,0},{9... | collective-permute-start | bytes 1572872 | tf_op jit(solution)/shard_map/ppermute | solution.py:30
  140.2 17.1 %collective-permute-start.28 = (bf16[2048,128]{1,0:T(8,128)(2,1)S(1)}, bf16[2048,128]{1,0:T(8,128)(2,1)S(1)}, u32[]{:S(2)}, u32[]{:S(2)}) collective-permute-start(bf16[2048,128]{1,0:T(8,128)(2,1)S(1)} %get-tuple-element.71), channel_id=1, source_target_pairs={{0,8},{1,33},{2,10},{3,35},{4,12},{5,37},{6,14},{7,39},{8,16},{9,4... | collective-permute-start | bytes 1572872 | tf_op jit(solution)/shard_map/ppermute | solution.py:30
  140.3 17.7 %collective-permute-start.29 = (bf16[2048,128]{1,0:T(8,128)(2,1)S(1)}, bf16[2048,128]{1,0:T(8,128)(2,1)S(1)}, u32[]{:S(2)}, u32[]{:S(2)}) collective-permute-start(bf16[2048,128]{1,0:T(8,128)(2,1)S(1)} %get-tuple-element.72), channel_id=1, source_target_pairs={{0,24},{1,97},{2,26},{3,99},{4,28},{5,101},{6,30},{7,103},{8,0},{9... | collective-permute-start | bytes 1572872 | tf_op jit(solution)/shard_map/ppermute | solution.py:30
  148.5 13.9 %collective-permute-start.35 = (bf16[512,128]{1,0:T(8,128)(2,1)S(1)}, bf16[512,128]{1,0:T(8,128)(2,1)S(1)}, u32[]{:S(2)}, u32[]{:S(2)}) collective-permute-start(bf16[512,128]{1,0:T(8,128)(2,1)S(1)} %get-tuple-element.84), channel_id=1, source_target_pairs={{0,64},{1,17},{2,66},{3,19},{4,68},{5,21},{6,70},{7,23},{8,72},{9,... | collective-permute-start | bytes 393224 | tf_op jit(solution)/shard_map/ppermute | solution.py:30
  151.8 13.0 %collective-permute-start.36 = (bf16[512,128]{1,0:T(8,128)(2,1)S(1)}, bf16[512,128]{1,0:T(8,128)(2,1)S(1)}, u32[]{:S(2)}, u32[]{:S(2)}) collective-permute-start(bf16[512,128]{1,0:T(8,128)(2,1)S(1)} %get-tuple-element.86), channel_id=1, source_target_pairs={{0,32},{1,9},{2,34},{3,11},{4,36},{5,13},{6,38},{7,15},{8,40},{9,1... | collective-permute-start | bytes 393224 | tf_op jit(solution)/shard_map/ppermute | solution.py:30
  152.6 12.3 %collective-permute-start.37 = (bf16[512,128]{1,0:T(8,128)(2,1)S(1)}, bf16[512,128]{1,0:T(8,128)(2,1)S(1)}, u32[]{:S(2)}, u32[]{:S(2)}) collective-permute-start(bf16[512,128]{1,0:T(8,128)(2,1)S(1)} %get-tuple-element.85), channel_id=1, source_target_pairs={{0,96},{1,25},{2,98},{3,27},{4,100},{5,29},{6,102},{7,31},{8,104},... | collective-permute-start | bytes 393224 | tf_op jit(solution)/shard_map/ppermute | solution.py:30
  (24 other events, 225.7 us)

commit v4 on v3

--- a/solution.py
+++ b/solution.py
@@ -47,13 +47,24 @@
     return lax.ppermute(x, "tensor", [(i, i ^ 1) for i in range(2 * RING)])
 
 
+def axis_groups(z_core):
+    groups = []
+    for i in range(2 * RING):
+        for fixed in range(RING):
+            along = [(k, fixed) if i % 2 == z_core else (fixed, k) for k in range(RING)]
+            groups.append([(z * RING + y) * 2 * RING + i for z, y in along])
+    return groups
+
+
+def exchanged(blocks, z_core):
+    return lax.all_to_all(
+        blocks, ("dp", "tensor"), 0, 0, tiled=True, axis_index_groups=axis_groups(z_core)
+    )
+
+
 def gathered(block, move):
     far, after, before = (move(block, step) for step in (2, 1, 3))
     return [block, after, far, before]
-
-
-def scattered(parts, move):
-    return [move(parts[step], step) for step in (2, 1, 3)]
 
 
 def summed(blocks):
@@ -159,7 +170,7 @@
 
 
 def assemble_kernel(chip, *refs):
-    pieces, out_ref, sems = refs[:RING], refs[RING], refs[RING + 1]
+    pieces, out_ref, sems = refs[: RING + 1], refs[RING + 1], refs[RING + 2]
     rows, both = pieces[0].shape
     count = rows // RING
     z, y, x, core = (chip[CHIP + i] for i in range(4))
@@ -171,7 +182,10 @@
             o = (x - from_z + RING) % RING
             start = ((o * 2 + ((from_y >> 1) ^ core)) * 2 + from_y % 2) * count
             target = out_ref.at[pl.ds(pl.multiple_of(start, count), count)]
-            source = pieces[b].at[pl.ds(a * count, count)]
+            if b == 2:
+                source = pieces[3 + a // 2].at[pl.ds(a % 2 * count, count)]
+            else:
+                source = pieces[min(b, 2)].at[pl.ds(a * count, count)]
             copies.append(pltpu.make_async_copy(source, target, sems.at[b, a]))
     for copy in copies:
         copy.start()
@@ -183,7 +197,7 @@
     rows, both = pieces[0].shape
     return pl.pallas_call(
         assemble_kernel,
-        in_specs=[SMEM] + [ANY] * RING,
+        in_specs=[SMEM] + [ANY] * (RING + 1),
         out_specs=VMEM,
         out_shape=jax.ShapeDtypeStruct((RING * rows, both), pieces[0].dtype),
         scratch_shapes=[pltpu.SemaphoreType.DMA((RING, RING))],
@@ -262,50 +276,29 @@
 
 
 def product_kernel(chip, *refs):
-    sources, (grads_ref, part_ref), refs = refs[: 2 * RING], refs[2 * RING : 2 * RING + 2], refs[2 * RING + 2 :]
-    outs, (held, sems) = refs[: 2 * RING + 2], refs[2 * RING + 2 :]
-    sems_of = [sems.at[i] for i in range(len(outs))]
+    sources, (grads_ref, part_ref, out_ref) = refs[:-3], refs[-3:]
     depth = sources[0].shape[1]
     count = depth // 2
-    z, y, x, core = (chip[CHIP + i] for i in range(4))
+    x, core = chip[CHIP + 2], chip[CHIP + 3]
     for k, source in enumerate(sources):
         total = matmul(source[...], grads_ref[...], ((0,), (0,)))
-        total = (total + part_ref[k * depth : (k + 1) * depth]).astype(held.dtype)
-        by_z = (x - k // 2 - z + 2 * RING) % RING
+        total = (total + part_ref[k * depth : (k + 1) * depth]).astype(out_ref.dtype)
+        to_z = (x - k // 2 + RING) % RING
         for h in range(2):
-            by_y = (2 * (k % 2 ^ core) + h - y + RING) % RING
-            outer_by = jnp.where(core == 0, by_y, by_z)
-            inner_by = jnp.where(core == 0, by_z, by_y)
-            start = pl.multiple_of(inner_by * count, count)
-            held[outer_by, pl.ds(start, count)] = total[h * count : (h + 1) * count]
-    half, head_dim = held.shape[1] // 2, held.shape[2] // 2
-    parts = []
-    for i in range(2):
-        columns = pl.ds(i * head_dim, head_dim)
-        parts += [held.at[2, pl.ds(0, half), columns], held.at[2, pl.ds(half, half), columns]]
-        parts += [held.at[k, :, columns] for k in (1, 3, 0)]
-    copies = [pltpu.make_async_copy(part, out, sem) for part, out, sem in zip(parts, outs, sems_of)]
-    for copy in copies:
-        copy.start()
-    for copy in copies:
-        copy.wait()
+            to_y = 2 * (k % 2 ^ core) + h
+            block = jnp.where(core == 0, to_y * RING + to_z, to_z * RING + to_y)
+            start = pl.multiple_of(block * count, count)
+            out_ref[pl.ds(start, count)] = total[h * count : (h + 1) * count]
 
 
 def product(chip, feats, grads, part):
     rows, depth = feats[0].shape
     both = grads.shape[1]
-    shape = (RING * depth // 2, both)
-    whole = jax.ShapeDtypeStruct((shape[0], both // 2), jnp.bfloat16)
-    half = jax.ShapeDtypeStruct((shape[0] // 2, both // 2), jnp.bfloat16)
     return pl.pallas_call(
         product_kernel,
         in_specs=[SMEM] + [VMEM] * (len(feats) + 2),
-        out_specs=[ANY] * (2 * RING + 2),
-        out_shape=[half, half, whole, whole, whole] * 2,
-        scratch_shapes=[
-            pltpu.VMEM((RING, *shape), jnp.bfloat16),
-            pltpu.SemaphoreType.DMA((2 * RING + 2,)),
-        ],
+        out_specs=VMEM,
+        out_shape=jax.ShapeDtypeStruct((len(feats) * depth, both), jnp.bfloat16),
         compiler_params=PARAMS,
         cost_estimate=pl.CostEstimate(
             flops=2 * len(feats) * rows * depth * both,
@@ -313,31 +306,6 @@
             transcendentals=0,
         ),
     )(chip, *feats, grads, part)
-
-
-def passed_kernel(after_ref, before_ref, upper_ref, lower_ref, to_after_ref, to_before_ref):
-    half = upper_ref.shape[0]
-
-    def added(block, piece):
-        return (block.astype(jnp.float32) + piece.astype(jnp.float32)).astype(jnp.bfloat16)
-
-    to_after_ref[:half] = added(after_ref[:half], upper_ref[...])
-    to_after_ref[half:] = after_ref[half:]
-    to_before_ref[:half] = before_ref[:half]
-    to_before_ref[half:] = added(before_ref[half:], lower_ref[...])
-
-
-def passed(after, before, upper, lower):
-    return pl.pallas_call(
-        passed_kernel,
-        in_specs=[VMEM] * 4,
-        out_specs=[VMEM] * 2,
-        out_shape=[jax.ShapeDtypeStruct(after.shape, after.dtype)] * 2,
-        compiler_params=PARAMS,
-        cost_estimate=pl.CostEstimate(
-            flops=after.size, bytes_accessed=10 * after.size, transcendentals=0
-        ),
-    )(after, before, upper, lower)
 
 
 def attend_kernel(heads, base, index, ratio_ref, q_ref, cot_ref, kv_ref, away_ref, gain_ref, *refs):
@@ -465,17 +433,19 @@
     ratio = jnp.tanh(gate)
     numbers, far_own, near_own = route(tiles, image_slot, image)
 
-    def opposite(after, before):
+    def opposite(after, before, move):
         half = after.shape[0] // 2
-        return along_x(after[:half], 1), along_x(before[half:], 3)
-
+        return [move(after[:half], 1), move(before[half:], 3)]
+
+    shard = lay(numbers, key_weight_matrix, value_weight_matrix)
     far_x = [along_x(far_own, 1), along_x(far_own, 3)]
-    shard = lay(numbers, key_weight_matrix, value_weight_matrix)
-    pieces = gathered(jnp.concatenate(gathered(shard, inner), axis=0), outer)
-    far_halves = opposite(*far_x)
+    shard = jnp.concatenate(gathered(shard, inner), axis=0)
+    shard, *far_x = lax.optimization_barrier((shard, *far_x))
+    far_halves = opposite(*far_x, along_x)
+    pieces = [outer(shard, 1), outer(shard, 3)]
     near_own, *far_halves = lax.optimization_barrier((near_own, *far_halves))
     near_x = [along_x(near_own, 1), along_x(near_own, 3)]
-    weights = assemble(numbers, pieces)
+    weights = assemble(numbers, [shard, *pieces, *opposite(*pieces, outer)])
     weights, *far_blocks = lax.optimization_barrier((weights, *far_x, *far_halves))
 
     def other_cores(*blocks):
@@ -500,15 +470,13 @@
     far_total = project(far_feats)
     far_key_value = finish(far_total, key_gain)
     away = along_z(far_key_value, RING // 2)
-    _, *near_late = lax.optimization_barrier((away, *near_x))
-    near_halves = opposite(*near_late)
+    _, *near_late = lax.optimization_barrier((far_key_value, *near_x))
+    near_halves = opposite(*near_late, along_x)
     near_others = other_cores(*near_late)
-    away, _ = lax.optimization_barrier((away, near_others[0]))
     *earlier, far_grad = attend(FAR, *shared, far_key_value, away, query_gain, ())
     back = along_z(far_grad, RING // 2)
-    far_rows = turn(FAR, numbers, far_total, far_grad, back, key_gain)
-    part = first_part(far_feats, far_rows)
-
+
+    _, *near_halves = lax.optimization_barrier((far_grad, *near_halves))
     blocks = [*near_x, jnp.concatenate(near_halves, axis=0)]
     near_others.append(other_core(blocks[2]))
     near_feats = paired(near_own, other_core(near_own), *blocks, *near_others)
@@ -518,25 +486,17 @@
         NEAR, *shared, near_key_value, near_key_value, query_gain, earlier
     )
     near_rows = turn(NEAR, numbers, near_total, near_grad, near_grad, key_gain)
+    back, near_rows = lax.optimization_barrier((back, near_rows))
+    far_rows = turn(FAR, numbers, far_total, far_grad, back, key_gain)
+    part = first_part(far_feats, far_rows)
 
     blocks = product(numbers, near_feats, near_rows, part)
-    chains = [blocks[: RING + 1], blocks[RING + 1 :]]
-    chains = [(chain, outer(chain[0], 1), outer(chain[1], 3)) for chain in chains]
-    halves = lax.optimization_barrier(tuple(half for chain in chains for half in chain[1:]))
-    chains = [
-        (chain[0], *passed(chain[0][2], chain[0][3], *halves[2 * i : 2 * i + 2]))
-        for i, chain in enumerate(chains)
-    ]
-    totals = [
-        summed([chain[4], outer(after, 1), outer(before, 3)]) for chain, after, before in chains
-    ]
-    shares = []
-    for total in totals:
-        count = total.shape[0] // RING
-        parts = [total[d * count : (d + 1) * count] for d in range(RING)]
-        sent = [None] + [part.astype(jnp.bfloat16) for part in parts[1:]]
-        shares.append(summed([parts[0], *scattered(sent, inner)]))
-    return (context, d_query, *shares)
+    for z_core in (1, 0):
+        blocks = exchanged(blocks, z_core)
+        blocks = summed(jnp.split(blocks, RING, axis=0))
+        share, blocks = blocks, blocks.astype(jnp.bfloat16)
+    head_dim = query_gain.shape[0]
+    return (context, d_query, share[:, :head_dim], share[:, head_dim:])
 
 
 def solution(mesh):

time: 170 us -> 165 us (0.971)
  blocking collectives: 0 us -> 43.6 us
  starting transfers between devices: 65.7 us -> 29.2 us
  waiting for transfers between devices: 63.7 us -> 52.7 us
    all_to_all x0 -> x2, blocking collectives: none -> 43.6 us  [exchanged(): lax.all_to_all(blocks, ('dp', 'tensor'), 0, 0, tiled=True, axis_index_gro...]
    ppermute x20 -> x7, starting transfers between devices: 38.8 us -> 12 us  [by_core(): return lax.ppermute(x, ('dp', 'tensor'), pairs)]
    ppermute x2, starting transfers between devices: 16.2 us -> 7.31 us  [along_z(): return lax.ppermute(x, 'dp', pairs)]
    ppermute x8, waiting for transfers between devices: 28.7 us -> 22.5 us  [along_x(): return lax.ppermute(x, 'tensor', pairs)]
    ppermute x20 -> x7, waiting for transfers between devices: 27.2 us -> 23.9 us  [by_core(): return lax.ppermute(x, ('dp', 'tensor'), pairs)]
  transfers between devices with their start and end apart: 38 -> 25, of which waited for: 18 -> 10; matrix products, arithmetic and copies ran while one was open for 5% -> 5% of each run, Pallas kernels for 5% -> 8%
where the time goes in v4:
time: 165 us; the launch traced here: 163 us
  waiting for transfers between devices  52.7 us (32%)
  blocking collectives  43.6 us (26%)
  starting transfers between devices  29.2 us (18%)
  Pallas kernels  24 us (15%)
  matrix products  7.22 us (4%)
  local copies, waits for them, and re-layouts  3.68 us (2%)
  between operations  1.76 us (1%)
    all_to_all x2, blocking collectives, exchanged(): lax.all_to_all(blocks, ('dp', 'tensor'), 0, 0, tiled=True, axis_index_gro...  43.6 us
    ppermute x7, waiting for transfers between devices, by_core(): return lax.ppermute(x, ('dp', 'tensor'), pairs)  23.9 us
    ppermute x8, waiting for transfers between devices, along_x(): return lax.ppermute(x, 'tensor', pairs)  22.5 us
    ppermute x7, starting transfers between devices, by_core(): return lax.ppermute(x, ('dp', 'tensor'), pairs)  12 us
    pallas_call x2, Pallas kernels, attend(): pl.pallas_call(functools.partial(attend_kernel, heads, base), grid_spec=p...  10.6 us
    ppermute x8, starting transfers between devices, along_x(): return lax.ppermute(x, 'tensor', pairs)  8.45 us
    ppermute x2, starting transfers between devices, along_z(): return lax.ppermute(x, 'dp', pairs)  7.31 us
    dot_general x16, matrix products, matmul(): lax.dot_general(a, b, (contract, ((), ())), preferred_element_type=jnp.fl...  7.22 us
  transfers between devices with their start and end apart: 25, of which 10 were waited for; matrix products, arithmetic and copies ran while one was open for 5% of the time, Pallas kernels for 8%

profile of v4, /device:TPU:4, one launch (start us, length us, event | category | flops | bytes accessed | tf_op | source)
XLA Modules:
  0.0 162.8 jit_solution(1414112010255734779)
XLA Ops:
  0.6 3.6 %shard_map.129 = (s32[10]{0:T(128)}, bf16[512,1024]{1,0:T(8,128)(2,1)}, bf16[512,1024]{1,0:T(8,128)(2,1)}) custom-call(s32[32]{0:T(128)} %tiles.1, s32[32]{0:T(128)} %slots.1, bf16[2,512,1024]{2,1,0:T(8,128)(2,1)} %image_ref.1), custom_call_target="tpu_custom_call" | custom-call | bytes 4194304 | tf_op jit(solution)/shard_map/pallas_call | solution.py:135
  9.5 4.1 %collective-permute-start.2 = (bf16[512,256]{1,0:T(8,128)(2,1)S(1)}, bf16[512,256]{1,0:T(8,128)(2,1)S(1)}, u32[]{:S(2)}, u32[]{:S(2)}) collective-permute-start(bf16[512,256]{1,0:T(8,128)(2,1)S(1)} %shard_map.130), channel_id=1, source_target_pairs={{0,96},{1,25},{2,98},{3,27},{4,100},{5,29},{6,102},{7,31},{8,104},... | collective-permute-start | bytes 786440 | tf_op jit(solution)/shard_map/ppermute | solution.py:30
  14.8 5.4 %collective-permute-done.2 = bf16[512,256]{1,0:T(8,128)(2,1)S(1)} collective-permute-done((bf16[512,256]{1,0:T(8,128)(2,1)S(1)}, bf16[512,256]{1,0:T(8,128)(2,1)S(1)}, u32[]{:S(2)}, u32[]{:S(2)}) %collective-permute-start.2) | collective-permute-done | bytes 262176 | tf_op jit(solution)/shard_map/ppermute | solution.py:30
  21.6 2.4 %collective-permute-done = bf16[512,256]{1,0:T(8,128)(2,1)S(1)} collective-permute-done((bf16[512,256]{1,0:T(8,128)(2,1)S(1)}, bf16[512,256]{1,0:T(8,128)(2,1)S(1)}, u32[]{:S(2)}, u32[]{:S(2)}) %collective-permute-start) | collective-permute-done | bytes 262176 | tf_op jit(solution)/shard_map/ppermute | solution.py:30
  24.0 5.4 %collective-permute-done.3.refs_2_ = bf16[512,1024]{1,0:T(8,128)(2,1)S(1)} collective-permute-done((bf16[512,1024]{1,0:T(8,128)(2,1)}, bf16[512,1024]{1,0:T(8,128)(2,1)S(1)}, u32[]{:S(2)}, u32[]{:S(2)}) %collective-permute-start.3) | collective-permute-done | bytes 1048608 | tf_op jit(solution)/shard_map/ppermute | solution.py:43
  30.4 1.6 collective-permute-start.7
  32.0 1.7 %collective-permute-start.8 = (bf16[2048,256]{1,0:T(8,128)(2,1)S(1)}, bf16[2048,256]{1,0:T(8,128)(2,1)S(1)}, u32[]{:S(2)}, u32[]{:S(2)}) collective-permute-start(bf16[2048,256]{1,0:T(8,128)(2,1)S(1)} %pad_maximum_fusion.refs_0_), channel_id=1, source_target_pairs={{0,24},{1,97},{2,26},{3,99},{4,28},{5,101},{6,30},{7,103},{8,0},{9... | collective-permute-start | bytes 3145736 | tf_op jit(solution)/shard_map/ppermute | solution.py:30
  33.7 1.6 %collective-permute-start.5 = (bf16[256,1024]{1,0:T(8,128)(2,1)S(1)}, bf16[256,1024]{1,0:T(8,128)(2,1)S(1)}, u32[]{:S(2)}, u32[]{:S(2)}) collective-permute-start(bf16[256,1024]{1,0:T(8,128)(2,1)S(1)} %slice.64), channel_id=1, source_target_pairs={{0,2},{1,3},{2,4},{3,5},{4,6},{5,7},{6,0},{7,1},{8,10},{9,11},{10,... | collective-permute-start | bytes 1572872 | tf_op jit(solution)/shard_map/ppermute | solution.py:43
  35.9 10.5 %collective-permute-done.7.refs_1_ = bf16[2048,256]{1,0:T(8,128)(2,1)S(1)} collective-permute-done((bf16[2048,256]{1,0:T(8,128)(2,1)S(1)}, bf16[2048,256]{1,0:T(8,128)(2,1)S(1)}, u32[]{:S(2)}, u32[]{:S(2)}) %collective-permute-start.7) | collective-permute-done | bytes 1048608 | tf_op jit(solution)/shard_map/ppermute | solution.py:30
  46.9 2.9 %collective-permute-start.10 = (bf16[1024,256]{1,0:T(8,128)(2,1)S(1)}, bf16[1024,256]{1,0:T(8,128)(2,1)S(1)}, u32[]{:S(2)}, u32[]{:S(2)}) collective-permute-start(bf16[1024,256]{1,0:T(8,128)(2,1)S(1)} %slice.81), channel_id=1, source_target_pairs={{0,24},{1,97},{2,26},{3,99},{4,28},{5,101},{6,30},{7,103},{8,0},{9... | collective-permute-start | bytes 1572872 | tf_op jit(solution)/shard_map/ppermute | solution.py:30
  50.6 1.6 %collective-permute-start.12 = (bf16[512,1024]{1,0:T(8,128)(2,1)S(1)}, bf16[512,1024]{1,0:T(8,128)(2,1)S(1)}, u32[]{:S(2)}, u32[]{:S(2)}) collective-permute-start(bf16[512,1024]{1,0:T(8,128)(2,1)S(1)} %copy-done), channel_id=1, source_target_pairs={{0,2},{1,3},{2,4},{3,5},{4,6},{5,7},{6,0},{7,1},{8,10},{9,11},{10,... | collective-permute-start | bytes 3145736 | tf_op jit(solution)/shard_map/ppermute | solution.py:43
  52.7 4.2 %collective-permute-done.9.refs_3_ = bf16[1024,256]{1,0:T(8,128)(2,1)S(1)} collective-permute-done((bf16[1024,256]{1,0:T(8,128)(2,1)S(1)}, bf16[1024,256]{1,0:T(8,128)(2,1)S(1)}, u32[]{:S(2)}, u32[]{:S(2)}) %collective-permute-start.9) | collective-permute-done | bytes 524320 | tf_op jit(solution)/shard_map/ppermute | solution.py:30
  56.9 1.3 shard_map.131
  61.3 16.2 %collective-permute-done.17.refs_6_ = bf16[512,1024]{1,0:T(8,128)(2,1)S(1)} collective-permute-done((bf16[512,1024]{1,0:T(8,128)(2,1)S(1)}, bf16[512,1024]{1,0:T(8,128)(2,1)S(1)}, u32[]{:S(2)}, u32[]{:S(2)}) %collective-permute-start.17) | collective-permute-done | bytes 1048608 | tf_op jit(solution)/shard_map/ppermute | solution.py:43
  80.2 1.7 %collective-permute-start.21 = (bf16[256,1024]{1,0:T(8,128)(2,1)S(1)}, bf16[256,1024]{1,0:T(8,128)(2,1)S(1)}, u32[]{:S(2)}, u32[]{:S(2)}) collective-permute-start(bf16[256,1024]{1,0:T(8,128)(2,1)S(1)} %slice.76), channel_id=1, source_target_pairs={{0,2},{1,3},{2,4},{3,5},{4,6},{5,7},{6,0},{7,1},{8,10},{9,11},{10,... | collective-permute-start | bytes 1572872 | tf_op jit(solution)/shard_map/ppermute | solution.py:43
  82.8 4.1 %collective-permute-start.20 = (bf16[512,256]{1,0:T(8,128)(2,1)S(1)}, bf16[512,256]{1,0:T(8,128)(2,1)S(1)}, u32[]{:S(2)}, u32[]{:S(2)}) collective-permute-start(bf16[512,256]{1,0:T(8,128)(2,1)S(1)} %shard_map.132.kv_ref), channel_id=1, source_target_pairs={{0,64},{8,72},{16,80},{24,88},{32,96},{40,104},{48,112},{56,120},{... | collective-permute-start | bytes 786440 | tf_op jit(solution)/shard_map/ppermute | solution.py:17
  87.4 5.5 %collective-permute-done.20.away_ref = bf16[512,256]{1,0:T(8,128)(2,1)S(1)} collective-permute-done((bf16[512,256]{1,0:T(8,128)(2,1)S(1)}, bf16[512,256]{1,0:T(8,128)(2,1)S(1)}, u32[]{:S(2)}, u32[]{:S(2)}) %collective-permute-start.20) | collective-permute-done | bytes 262176 | tf_op jit(solution)/shard_map/ppermute | solution.py:17
  92.8 5.3 %shard_map.133 = (bf16[2,128,1024]{2,1,0:T(8,128)(2,1)}, bf16[2,128,1024]{2,1,0:T(8,128)(2,1)}, bf16[512,256]{1,0:T(8,128)(2,1)S(1)}) custom-call(s32[10]{0:T(128)S(1)} %copy-done.5, f32[1]{0:T(128)S(6)} %tanh.3.ratio_ref, bf16[2,128,1024]{2,1,0:T(8,128)(2,1)S(1)} %copy-done.7, bf16[2,128,1024]{2,1,0:T(8,128)(2,1)S(1)} %copy-done.8, ...), custom_call_target="tpu_custom_call" | custom-call | flops 939524096 | bytes 1441792 | tf_op jit(solution)/shard_map/pallas_call | solution.py:386
  98.1 3.2 %collective-permute-start.24 = (bf16[512,256]{1,0:T(8,128)(2,1)S(1)}, bf16[512,256]{1,0:T(8,128)(2,1)S(1)}, u32[]{:S(2)}, u32[]{:S(2)}) collective-permute-start(bf16[512,256]{1,0:T(8,128)(2,1)S(1)} %get-tuple-element.46.grad_ref), channel_id=1, source_target_pairs={{0,64},{8,72},{16,80},{24,88},{32,96},{40,104},{48,112},{56,120},{... | collective-permute-start | bytes 786440 | tf_op jit(solution)/shard_map/ppermute | solution.py:17
  104.8 5.3 %shard_map.135 = (bf16[2,128,1024]{2,1,0:T(8,128)(2,1)}, bf16[2,128,1024]{2,1,0:T(8,128)(2,1)}, bf16[512,256]{1,0:T(8,128)(2,1)S(1)}) custom-call(s32[10]{0:T(128)S(1)} %copy-done.5, f32[1]{0:T(128)S(6)} %tanh.3.ratio_ref, bf16[2,128,1024]{2,1,0:T(8,128)(2,1)S(1)} %copy-done.7, ...), custom_call_target="tpu_custom_call", output_to_operand_aliasing={{0}: (7, {}), {1}: (8, {})} | custom-call | flops 939524096 | bytes 1441792 | tf_op jit(solution)/shard_map/pallas_call | solution.py:386
  111.7 2.6 %shard_map.138.refs_9_ = f32[8192,256]{1,0:T(8,128)S(1)} custom-call(bf16[512,1024]{1,0:T(8,128)(2,1)S(1)} %copy-done.1, bf16[512,1024]{1,0:T(8,128)(2,1)S(1)} %collective-permute-done.13.refs_1_, bf16[512,1024]{1,0:T(8,128)(2,1)S(1)} %collective-permute-done.3.refs_2_, bf16[512,1024]{1,0:T(8,128)(2,1)S(1)} %collective-permute-done.14.refs_3_, ...), custom_call_target="tpu_custom_call" | custom-call | flops 2147483648 | bytes 8388608 | tf_op jit(solution)/shard_map/pallas_call | solution.py:264
  114.2 3.5 %shard_map.139 = bf16[8192,256]{1,0:T(8,128)(2,1)S(1)} custom-call(s32[10]{0:T(128)S(1)} %copy-done.5, bf16[512,1024]{1,0:T(8,128)(2,1)S(1)} %copy-done, bf16[512,1024]{1,0:T(8,128)(2,1)S(1)} %collective-permute-done.11.refs_1_, bf16[512,1024]{1,0:T(8,128)(2,1)S(1)} %collective-permute-done.12.refs_2_, ...), custom_call_target="tpu_custom_call" | custom-call | flops 2147483648 | bytes 8388608 | tf_op jit(solution)/shard_map/pallas_call | solution.py:297
  117.7 30.3 %all_to_all.15 = bf16[4,2048,256]{2,1,0:T(8,128)(2,1)S(1)} all-to-all(bf16[4,2048,256]{2,1,0:T(8,128)(2,1)S(1)} %bitcast.22), channel_id=1, replica_groups={{0,8,16,24},{32,40,48,56},{64,72,80,88},{96,104,112,120},{1,33,65,97},{..., dimensions={0} | all-to-all | bytes 8388608 | tf_op jit(solution)/shard_map/all_to_all | solution.py:60
  148.6 13.3 %all_to_all.16 = bf16[4,512,256]{2,1,0:T(8,128)(2,1)S(1)} all-to-all(bf16[4,512,256]{2,1,0:T(8,128)(2,1)S(1)} %bitcast.29), channel_id=1, replica_groups={{0,32,64,96},{8,40,72,104},{16,48,80,112},{24,56,88,120},{1,9,17,25},{3..., dimensions={0} | all-to-all | bytes 2097152 | tf_op jit(solution)/shard_map/all_to_all | solution.py:60
  (89 shorter events, 23.7 us)
Async XLA Ops:
  4.3 25.2 %collective-permute-start.3 = (bf16[512,1024]{1,0:T(8,128)(2,1)}, bf16[512,1024]{1,0:T(8,128)(2,1)S(1)}, u32[]{:S(2)}, u32[]{:S(2)}) collective-permute-start(bf16[512,1024]{1,0:T(8,128)(2,1)} %get-tuple-element.32.refs_0_), channel_id=1, source_target_pairs={{0,2},{1,3},{2,4},{3,5},{4,6},{5,7},{6,0},{7,1},{8,10},{9,11},{10,... | collective-permute-start | bytes 3145736 | tf_op jit(solution)/shard_map/ppermute | solution.py:43
  5.6 24.8 %collective-permute-start.4 = (bf16[512,1024]{1,0:T(8,128)(2,1)}, bf16[512,1024]{1,0:T(8,128)(2,1)S(1)}, u32[]{:S(2)}, u32[]{:S(2)}) collective-permute-start(bf16[512,1024]{1,0:T(8,128)(2,1)} %get-tuple-element.32.refs_0_), channel_id=1, source_target_pairs={{0,6},{1,7},{2,0},{3,1},{4,2},{5,3},{6,4},{7,5},{8,14},{9,15},{10,... | collective-permute-start | bytes 3145736 | tf_op jit(solution)/shard_map/ppermute | solution.py:43
  9.5 10.8 %collective-permute-start.2 = (bf16[512,256]{1,0:T(8,128)(2,1)S(1)}, bf16[512,256]{1,0:T(8,128)(2,1)S(1)}, u32[]{:S(2)}, u32[]{:S(2)}) collective-permute-start(bf16[512,256]{1,0:T(8,128)(2,1)S(1)} %shard_map.130), channel_id=1, source_target_pairs={{0,96},{1,25},{2,98},{3,27},{4,100},{5,29},{6,102},{7,31},{8,104},... | collective-permute-start | bytes 786440 | tf_op jit(solution)/shard_map/ppermute | solution.py:30
  13.6 8.0 %collective-permute-start.1 = (bf16[512,256]{1,0:T(8,128)(2,1)S(1)}, bf16[512,256]{1,0:T(8,128)(2,1)S(1)}, u32[]{:S(2)}, u32[]{:S(2)}) collective-permute-start(bf16[512,256]{1,0:T(8,128)(2,1)S(1)} %shard_map.130), channel_id=1, source_target_pairs={{0,64},{1,17},{2,66},{3,19},{4,68},{5,21},{6,70},{7,23},{8,72},{9,... | collective-permute-start | bytes 786440 | tf_op jit(solution)/shard_map/ppermute | solution.py:30
  13.6 10.4 %collective-permute-start = (bf16[512,256]{1,0:T(8,128)(2,1)S(1)}, bf16[512,256]{1,0:T(8,128)(2,1)S(1)}, u32[]{:S(2)}, u32[]{:S(2)}) collective-permute-start(bf16[512,256]{1,0:T(8,128)(2,1)S(1)} %shard_map.130), channel_id=1, source_target_pairs={{0,32},{1,9},{2,34},{3,11},{4,36},{5,13},{6,38},{7,15},{8,40},{9,1... | collective-permute-start | bytes 786440 | tf_op jit(solution)/shard_map/ppermute | solution.py:30
  30.4 16.0 %collective-permute-start.7 = (bf16[2048,256]{1,0:T(8,128)(2,1)S(1)}, bf16[2048,256]{1,0:T(8,128)(2,1)S(1)}, u32[]{:S(2)}, u32[]{:S(2)}) collective-permute-start(bf16[2048,256]{1,0:T(8,128)(2,1)S(1)} %pad_maximum_fusion.refs_0_), channel_id=1, source_target_pairs={{0,8},{1,33},{2,10},{3,35},{4,12},{5,37},{6,14},{7,39},{8,16},{9,4... | collective-permute-start | bytes 3145736 | tf_op jit(solution)/shard_map/ppermute | solution.py:30
  32.0 14.9 %collective-permute-start.8 = (bf16[2048,256]{1,0:T(8,128)(2,1)S(1)}, bf16[2048,256]{1,0:T(8,128)(2,1)S(1)}, u32[]{:S(2)}, u32[]{:S(2)}) collective-permute-start(bf16[2048,256]{1,0:T(8,128)(2,1)S(1)} %pad_maximum_fusion.refs_0_), channel_id=1, source_target_pairs={{0,24},{1,97},{2,26},{3,99},{4,28},{5,101},{6,30},{7,103},{8,0},{9... | collective-permute-start | bytes 3145736 | tf_op jit(solution)/shard_map/ppermute | solution.py:30
  33.7 16.9 %collective-permute-start.5 = (bf16[256,1024]{1,0:T(8,128)(2,1)S(1)}, bf16[256,1024]{1,0:T(8,128)(2,1)S(1)}, u32[]{:S(2)}, u32[]{:S(2)}) collective-permute-start(bf16[256,1024]{1,0:T(8,128)(2,1)S(1)} %slice.64), channel_id=1, source_target_pairs={{0,2},{1,3},{2,4},{3,5},{4,6},{5,7},{6,0},{7,1},{8,10},{9,11},{10,... | collective-permute-start | bytes 1572872 | tf_op jit(solution)/shard_map/ppermute | solution.py:43
  35.3 15.2 %collective-permute-start.6 = (bf16[256,1024]{1,0:T(8,128)(2,1)S(1)}, bf16[256,1024]{1,0:T(8,128)(2,1)S(1)}, u32[]{:S(2)}, u32[]{:S(2)}) collective-permute-start(bf16[256,1024]{1,0:T(8,128)(2,1)S(1)} %slice.65), channel_id=1, source_target_pairs={{0,6},{1,7},{2,0},{3,1},{4,2},{5,3},{6,4},{7,5},{8,14},{9,15},{10,... | collective-permute-start | bytes 1572872 | tf_op jit(solution)/shard_map/ppermute | solution.py:43
  46.4 10.5 %collective-permute-start.9 = (bf16[1024,256]{1,0:T(8,128)(2,1)S(1)}, bf16[1024,256]{1,0:T(8,128)(2,1)S(1)}, u32[]{:S(2)}, u32[]{:S(2)}) collective-permute-start(bf16[1024,256]{1,0:T(8,128)(2,1)S(1)} %slice.80), channel_id=1, source_target_pairs={{0,8},{1,33},{2,10},{3,35},{4,12},{5,37},{6,14},{7,39},{8,16},{9,4... | collective-permute-start | bytes 1572872 | tf_op jit(solution)/shard_map/ppermute | solution.py:30
  46.9 10.0 %collective-permute-start.10 = (bf16[1024,256]{1,0:T(8,128)(2,1)S(1)}, bf16[1024,256]{1,0:T(8,128)(2,1)S(1)}, u32[]{:S(2)}, u32[]{:S(2)}) collective-permute-start(bf16[1024,256]{1,0:T(8,128)(2,1)S(1)} %slice.81), channel_id=1, source_target_pairs={{0,24},{1,97},{2,26},{3,99},{4,28},{5,101},{6,30},{7,103},{8,0},{9... | collective-permute-start | bytes 1572872 | tf_op jit(solution)/shard_map/ppermute | solution.py:30
  49.9 9.5 %collective-permute-start.13 = (bf16[512,1024]{1,0:T(8,128)(2,1)S(1)}, bf16[512,1024]{1,0:T(8,128)(2,1)S(1)}, u32[]{:S(2)}, u32[]{:S(2)}) collective-permute-start(bf16[512,1024]{1,0:T(8,128)(2,1)S(1)} %copy-done.1), channel_id=1, source_target_pairs={{0,1},{1,0},{2,3},{3,2},{4,5},{5,4},{6,7},{7,6},{8,9},{9,8},{10,11... | collective-permute-start | bytes 3145736 | tf_op jit(solution)/shard_map/ppermute | solution.py:47
  50.6 29.0 %collective-permute-start.12 = (bf16[512,1024]{1,0:T(8,128)(2,1)S(1)}, bf16[512,1024]{1,0:T(8,128)(2,1)S(1)}, u32[]{:S(2)}, u32[]{:S(2)}) collective-permute-start(bf16[512,1024]{1,0:T(8,128)(2,1)S(1)} %copy-done), channel_id=1, source_target_pairs={{0,2},{1,3},{2,4},{3,5},{4,6},{5,7},{6,0},{7,1},{8,10},{9,11},{10,... | collective-permute-start | bytes 3145736 | tf_op jit(solution)/shard_map/ppermute | solution.py:43
  52.2 25.3 %collective-permute-start.17 = (bf16[512,1024]{1,0:T(8,128)(2,1)S(1)}, bf16[512,1024]{1,0:T(8,128)(2,1)S(1)}, u32[]{:S(2)}, u32[]{:S(2)}) collective-permute-start(bf16[512,1024]{1,0:T(8,128)(2,1)S(1)} %copy-done), channel_id=1, source_target_pairs={{0,6},{1,7},{2,0},{3,1},{4,2},{5,3},{6,4},{7,5},{8,14},{9,15},{10,... | collective-permute-start | bytes 3145736 | tf_op jit(solution)/shard_map/ppermute | solution.py:43
  58.2 19.8 %collective-permute-start.14 = (bf16[512,1024]{1,0:T(8,128)(2,1)S(1)}, bf16[512,1024]{1,0:T(8,128)(2,1)S(1)}, u32[]{:S(2)}, u32[]{:S(2)}) collective-permute-start(bf16[512,1024]{1,0:T(8,128)(2,1)S(1)} %collective-permute-done.3.refs_2_), channel_id=1, source_target_pairs={{0,1},{1,0},{2,3},{3,2},{4,5},{5,4},{6,7},{7,6},{8,9},{9,8},{10,11... | collective-permute-start | bytes 3145736 | tf_op jit(solution)/shard_map/ppermute | solution.py:47
  58.3 20.2 %collective-permute-start.15 = (bf16[512,1024]{1,0:T(8,128)(2,1)S(1)}, bf16[512,1024]{1,0:T(8,128)(2,1)S(1)}, u32[]{:S(2)}, u32[]{:S(2)}) collective-permute-start(bf16[512,1024]{1,0:T(8,128)(2,1)S(1)} %collective-permute-done.4.refs_6_), channel_id=1, source_target_pairs={{0,1},{1,0},{2,3},{3,2},{4,5},{5,4},{6,7},{7,6},{8,9},{9,8},{10,11... | collective-permute-start | bytes 3145736 | tf_op jit(solution)/shard_map/ppermute | solution.py:47
  59.3 19.6 %collective-permute-start.16 = (bf16[512,1024]{1,0:T(8,128)(2,1)S(1)}, bf16[512,1024]{1,0:T(8,128)(2,1)S(1)}, u32[]{:S(2)}, u32[]{:S(2)}) collective-permute-start(bf16[512,1024]{1,0:T(8,128)(2,1)S(1)} %constant_dynamic-update-slice_fusion.refs_4_), channel_id=1, source_target_pairs={{0,1},{1,0},{2,3},{3,2},{4,5},{5,4},{6,7},{7,6},{8,9},{9,8},{10,11... | collective-permute-start | bytes 3145736 | tf_op jit(solution)/shard_map/ppermute | solution.py:47
  77.5 9.4 %collective-permute-start.11 = (bf16[512,1024]{1,0:T(8,128)(2,1)S(1)}, bf16[512,1024]{1,0:T(8,128)(2,1)S(1)}, u32[]{:S(2)}, u32[]{:S(2)}) collective-permute-start(bf16[512,1024]{1,0:T(8,128)(2,1)S(1)} %copy-done), channel_id=1, source_target_pairs={{0,1},{1,0},{2,3},{3,2},{4,5},{5,4},{6,7},{7,6},{8,9},{9,8},{10,11... | collective-permute-start | bytes 3145736 | tf_op jit(solution)/shard_map/ppermute | solution.py:47
  79.6 22.4 %collective-permute-start.19 = (bf16[512,1024]{1,0:T(8,128)(2,1)S(1)}, bf16[512,1024]{1,0:T(8,128)(2,1)S(1)}, u32[]{:S(2)}, u32[]{:S(2)}) collective-permute-start(bf16[512,1024]{1,0:T(8,128)(2,1)S(1)} %collective-permute-done.17.refs_6_), channel_id=1, source_target_pairs={{0,1},{1,0},{2,3},{3,2},{4,5},{5,4},{6,7},{7,6},{8,9},{9,8},{10,11... | collective-permute-start | bytes 3145736 | tf_op jit(solution)/shard_map/ppermute | solution.py:47
  80.2 21.1 %collective-permute-start.21 = (bf16[256,1024]{1,0:T(8,128)(2,1)S(1)}, bf16[256,1024]{1,0:T(8,128)(2,1)S(1)}, u32[]{:S(2)}, u32[]{:S(2)}) collective-permute-start(bf16[256,1024]{1,0:T(8,128)(2,1)S(1)} %slice.76), channel_id=1, source_target_pairs={{0,2},{1,3},{2,4},{3,5},{4,6},{5,7},{6,0},{7,1},{8,10},{9,11},{10,... | collective-permute-start | bytes 1572872 | tf_op jit(solution)/shard_map/ppermute | solution.py:43
  81.9 19.5 %collective-permute-start.22 = (bf16[256,1024]{1,0:T(8,128)(2,1)S(1)}, bf16[256,1024]{1,0:T(8,128)(2,1)S(1)}, u32[]{:S(2)}, u32[]{:S(2)}) collective-permute-start(bf16[256,1024]{1,0:T(8,128)(2,1)S(1)} %slice.77), channel_id=1, source_target_pairs={{0,6},{1,7},{2,0},{3,1},{4,2},{5,3},{6,4},{7,5},{8,14},{9,15},{10,... | collective-permute-start | bytes 1572872 | tf_op jit(solution)/shard_map/ppermute | solution.py:43
  82.8 10.0 %collective-permute-start.20 = (bf16[512,256]{1,0:T(8,128)(2,1)S(1)}, bf16[512,256]{1,0:T(8,128)(2,1)S(1)}, u32[]{:S(2)}, u32[]{:S(2)}) collective-permute-start(bf16[512,256]{1,0:T(8,128)(2,1)S(1)} %shard_map.132.kv_ref), channel_id=1, source_target_pairs={{0,64},{8,72},{16,80},{24,88},{32,96},{40,104},{48,112},{56,120},{... | collective-permute-start | bytes 786440 | tf_op jit(solution)/shard_map/ppermute | solution.py:17
  86.9 15.6 %collective-permute-start.18 = (bf16[512,1024]{1,0:T(8,128)(2,1)S(1)}, bf16[512,1024]{1,0:T(8,128)(2,1)S(1)}, u32[]{:S(2)}, u32[]{:S(2)}) collective-permute-start(bf16[512,1024]{1,0:T(8,128)(2,1)S(1)} %collective-permute-done.12.refs_2_), channel_id=1, source_target_pairs={{0,1},{1,0},{2,3},{3,2},{4,5},{5,4},{6,7},{7,6},{8,9},{9,8},{10,11... | collective-permute-start | bytes 3145736 | tf_op jit(solution)/shard_map/ppermute | solution.py:47
  98.1 12.8 %collective-permute-start.24 = (bf16[512,256]{1,0:T(8,128)(2,1)S(1)}, bf16[512,256]{1,0:T(8,128)(2,1)S(1)}, u32[]{:S(2)}, u32[]{:S(2)}) collective-permute-start(bf16[512,256]{1,0:T(8,128)(2,1)S(1)} %get-tuple-element.46.grad_ref), channel_id=1, source_target_pairs={{0,64},{8,72},{16,80},{24,88},{32,96},{40,104},{48,112},{56,120},{... | collective-permute-start | bytes 786440 | tf_op jit(solution)/shard_map/ppermute | solution.py:17
  (11 other events, 186.9 us)

commit v5 on v4

--- a/solution.py
+++ b/solution.py
@@ -15,27 +15,6 @@
 def along_z(x, step):
     pairs = [(z * RING + y, (z + step) % RING * RING + y) for z in range(RING) for y in range(RING)]
     return lax.ppermute(x, "dp", pairs)
-
-
-def by_core(x, step, z_core):
-    pairs = []
-    for z in range(RING):
-        for y in range(RING):
-            for i in range(RING):
-                for c in range(2):
-                    to_z, to_y = (z + step, y) if c == z_core else (z, y + step)
-                    source = (z * RING + y) * 2 * RING + i * 2 + c
-                    target = (to_z % RING * RING + to_y % RING) * 2 * RING + i * 2 + c
-                    pairs.append((source, target))
-    return lax.ppermute(x, ("dp", "tensor"), pairs)
-
-
-def inner(x, step):
-    return by_core(x, step, 0)
-
-
-def outer(x, step):
-    return by_core(x, step, 1)
 
 
 def along_x(x, step):
@@ -60,11 +39,6 @@
     return lax.all_to_all(
         blocks, ("dp", "tensor"), 0, 0, tiled=True, axis_index_groups=axis_groups(z_core)
     )
-
-
-def gathered(block, move):
-    far, after, before = (move(block, step) for step in (2, 1, 3))
-    return [block, after, far, before]
 
 
 def summed(blocks):
@@ -143,7 +117,7 @@
     )(tiles, image_slot, image)
 
 
-def lay_kernel(numbers, key_ref, value_ref, out_ref, sems):
+def lay_kernel(key_ref, value_ref, out_ref, sems):
     head_dim = key_ref.shape[1]
     copies = []
     for i, source in enumerate((key_ref, value_ref)):
@@ -154,58 +128,19 @@
         copy.wait()
 
 
-def lay(numbers, key_weights, value_weights):
+def lay(key_weights, value_weights):
     count, head_dim = key_weights.shape
     return pl.pallas_call(
         lay_kernel,
-        in_specs=[SMEM, ANY, ANY],
+        in_specs=[ANY, ANY],
         out_specs=VMEM,
         out_shape=jax.ShapeDtypeStruct((count, 2 * head_dim), key_weights.dtype),
         scratch_shapes=[pltpu.SemaphoreType.DMA((2,))],
-        compiler_params=PARAMS,
+        compiler_params=pltpu.CompilerParams(vmem_limit_bytes=60 * 1024 * 1024),
         cost_estimate=pl.CostEstimate(
             flops=0, bytes_accessed=8 * count * head_dim, transcendentals=0
         ),
-    )(numbers, key_weights, value_weights)
-
-
-def assemble_kernel(chip, *refs):
-    pieces, out_ref, sems = refs[: RING + 1], refs[RING + 1], refs[RING + 2]
-    rows, both = pieces[0].shape
-    count = rows // RING
-    z, y, x, core = (chip[CHIP + i] for i in range(4))
-    copies = []
-    for b in range(RING):
-        for a in range(RING):
-            from_z = (z - jnp.where(core == 0, a, b) + RING) % RING
-            from_y = (y - jnp.where(core == 0, b, a) + RING) % RING
-            o = (x - from_z + RING) % RING
-            start = ((o * 2 + ((from_y >> 1) ^ core)) * 2 + from_y % 2) * count
-            target = out_ref.at[pl.ds(pl.multiple_of(start, count), count)]
-            if b == 2:
-                source = pieces[3 + a // 2].at[pl.ds(a % 2 * count, count)]
-            else:
-                source = pieces[min(b, 2)].at[pl.ds(a * count, count)]
-            copies.append(pltpu.make_async_copy(source, target, sems.at[b, a]))
-    for copy in copies:
-        copy.start()
-    for copy in copies:
-        copy.wait()
-
-
-def assemble(chip, pieces):
-    rows, both = pieces[0].shape
-    return pl.pallas_call(
-        assemble_kernel,
-        in_specs=[SMEM] + [ANY] * (RING + 1),
-        out_specs=VMEM,
-        out_shape=jax.ShapeDtypeStruct((RING * rows, both), pieces[0].dtype),
-        scratch_shapes=[pltpu.SemaphoreType.DMA((RING, RING))],
-        compiler_params=PARAMS,
-        cost_estimate=pl.CostEstimate(
-            flops=0, bytes_accessed=4 * RING * rows * both, transcendentals=0
-        ),
-    )(chip, *pieces)
+    )(key_weights, value_weights)
 
 
 def finish_kernel(total_ref, gain_ref, key_value_ref):
@@ -433,20 +368,27 @@
     ratio = jnp.tanh(gate)
     numbers, far_own, near_own = route(tiles, image_slot, image)
 
-    def opposite(after, before, move):
+    def halves_of(after, before):
         half = after.shape[0] // 2
-        return [move(after[:half], 1), move(before[half:], 3)]
-
-    shard = lay(numbers, key_weight_matrix, value_weight_matrix)
+        return after[:half], before[half:]
+
+    def opposite(halves, move):
+        return [move(halves[0], 1), move(halves[1], 3)]
+
+    shard = lay(key_weight_matrix, value_weight_matrix)
+    weights = lax.all_gather(shard, "dp", axis=0, tiled=True)
     far_x = [along_x(far_own, 1), along_x(far_own, 3)]
-    shard = jnp.concatenate(gathered(shard, inner), axis=0)
-    shard, *far_x = lax.optimization_barrier((shard, *far_x))
-    far_halves = opposite(*far_x, along_x)
-    pieces = [outer(shard, 1), outer(shard, 3)]
-    near_own, *far_halves = lax.optimization_barrier((near_own, *far_halves))
+    near_own, *halves = lax.optimization_barrier((near_own, *halves_of(*far_x)))
+    far_halves = opposite(halves, along_x)
     near_x = [along_x(near_own, 1), along_x(near_own, 3)]
-    weights = assemble(numbers, [shard, *pieces, *opposite(*pieces, outer)])
-    weights, *far_blocks = lax.optimization_barrier((weights, *far_x, *far_halves))
+    place = lax.axis_index("tensor")
+    depth = image.shape[2]
+    columns = []
+    for o in range(RING):
+        for e in range(2):
+            start = ((place // 2 - o) % RING * 2 + (place % 2 ^ e)) * depth
+            columns.append(lax.dynamic_slice_in_dim(weights, start, depth, 0))
+    columns = lax.optimization_barrier(tuple(columns))
 
     def other_cores(*blocks):
         return [other_core(block) for block in blocks]
@@ -455,24 +397,22 @@
         return [own, other, after, after_other, opposite, opposite_other, before, before_other]
 
     def project(feats):
-        depth = feats[0].shape[1]
         total = None
         for o in (0, 1, 3, 2):
             for k in (2 * o, 2 * o + 1):
-                part = matmul(feats[k], weights[k * depth : (k + 1) * depth], ((1,), (0,)))
+                part = matmul(feats[k], columns[k], ((1,), (0,)))
                 total = part if total is None else total + part
         return total
 
     shared = (numbers, ratio, query, cotangent)
-    after, before, *halves = far_blocks
-    blocks = [after, before, jnp.concatenate(halves, axis=0)]
+    blocks = [*far_x, jnp.concatenate(far_halves, axis=0)]
     far_feats = paired(far_own, other_core(far_own), *blocks, *other_cores(*blocks))
     far_total = project(far_feats)
     far_key_value = finish(far_total, key_gain)
     away = along_z(far_key_value, RING // 2)
-    _, *near_late = lax.optimization_barrier((far_key_value, *near_x))
-    near_halves = opposite(*near_late, along_x)
-    near_others = other_cores(*near_late)
+    _, near_own, *near_x = lax.optimization_barrier((far_key_value, near_own, *near_x))
+    near_halves = opposite(halves_of(*near_x), along_x)
+    near_others = other_cores(*near_x)
     *earlier, far_grad = attend(FAR, *shared, far_key_value, away, query_gain, ())
     back = along_z(far_grad, RING // 2)
 

time: 165 us -> 172 us (1.042)
  starting transfers between devices: 29.2 us -> 13.4 us
  between operations: 1.76 us -> 15.1 us
  waiting for transfers between devices: 52.7 us -> 44.6 us
  matrix products: 7.22 us -> 14.4 us
  local copies, waits for them, and re-layouts: 3.68 us -> 10.1 us
  Pallas kernels: 24 us -> 26.6 us
    ppermute x7 -> x0, waiting for transfers between devices: 23.9 us -> none  [by_core(): return lax.ppermute(x, ('dp', 'tensor'), pairs)]
    ppermute x8, waiting for transfers between devices: 22.5 us -> 37.1 us  [along_x(): return lax.ppermute(x, 'tensor', pairs)]
    ppermute x7 -> x0, starting transfers between devices: 12 us -> none  [by_core(): return lax.ppermute(x, ('dp', 'tensor'), pairs)]
    dot_general x16, matrix products: 7.22 us -> 14.4 us  [matmul(): lax.dot_general(a, b, (contract, ((), ())), preferred_element_type=jnp.fl...]
    all_gather x0 -> x1, waiting for transfers between devices: none -> 5.84 us  [per_device(): weights = lax.all_gather(shard, 'dp', axis=0, tiled=True)]
    ppermute x2, waiting for transfers between devices: 5.46 us -> 1.25 us  [along_z(): return lax.ppermute(x, 'dp', pairs)]
    ppermute x2, starting transfers between devices: 7.31 us -> 3.61 us  [along_z(): return lax.ppermute(x, 'dp', pairs)]
    slice x6 -> x4, local copies, waits for them, and re-layouts: 0.21 us -> 2.77 us  [halves_of(): return (after[:half], before[half:])]
  transfers between devices with their start and end apart: 25 -> 19, of which waited for: 10 -> 8; matrix products, arithmetic and copies ran while one was open for 5% -> 14% of each run, Pallas kernels for 8% -> 9%
where the time goes in v5:
time: 172 us; the launch traced here: 170 us
  blocking collectives  45 us (26%)
  waiting for transfers between devices  44.6 us (26%)
  Pallas kernels  26.6 us (15%)
  between operations  15.1 us (9%)
  matrix products  14.4 us (8%)
  starting transfers between devices  13.4 us (8%)
  local copies, waits for them, and re-layouts  10.1 us (6%)
    all_to_all x2, blocking collectives, exchanged(): lax.all_to_all(blocks, ('dp', 'tensor'), 0, 0, tiled=True, axis_index_gro...  45 us
    ppermute x8, waiting for transfers between devices, along_x(): return lax.ppermute(x, 'tensor', pairs)  37.1 us
    dot_general x16, matrix products, matmul(): lax.dot_general(a, b, (contract, ((), ())), preferred_element_type=jnp.fl...  14.4 us
    pallas_call x2, Pallas kernels, attend(): pl.pallas_call(functools.partial(attend_kernel, heads, base), grid_spec=p...  10.6 us
    ppermute x8, starting transfers between devices, along_x(): return lax.ppermute(x, 'tensor', pairs)  8.24 us
    all_gather x1, waiting for transfers between devices, per_device(): weights = lax.all_gather(shard, 'dp', axis=0, tiled=True)  5.84 us
    pallas_call x1, Pallas kernels, first_part(): pl.pallas_call(first_part_kernel, in_specs=[VMEM] * (len(feats) + 1), out...  4.94 us
    pallas_call x1, Pallas kernels, product(): pl.pallas_call(product_kernel, in_specs=[SMEM] + [VMEM] * (len(feats) + 2...  4.04 us
  transfers between devices with their start and end apart: 19, of which 8 were waited for; matrix products, arithmetic and copies ran while one was open for 14% of the time, Pallas kernels for 9%

profile of v5, /device:TPU:4, one launch (start us, length us, event | category | flops | bytes accessed | tf_op | source)
XLA Modules:
  0.0 170.0 jit_solution(6159734348751012366)
XLA Ops:
  7.2 1.7 shard_map.130
  8.9 3.6 %shard_map.129 = (s32[10]{0:T(128)}, bf16[512,1024]{1,0:T(8,128)(2,1)}, bf16[512,1024]{1,0:T(8,128)(2,1)}) custom-call(s32[32]{0:T(128)} %tiles.1, s32[32]{0:T(128)} %slots.1, bf16[2,512,1024]{2,1,0:T(8,128)(2,1)} %image_ref.1), custom_call_target="tpu_custom_call" | custom-call | bytes 4194304 | tf_op jit(solution)/shard_map/pallas_call | solution.py:109
  14.6 23.1 %collective-permute-done.1.refs_2_ = bf16[512,1024]{1,0:T(8,128)(2,1)S(1)} collective-permute-done((bf16[512,1024]{1,0:T(8,128)(2,1)}, bf16[512,1024]{1,0:T(8,128)(2,1)S(1)}, u32[]{:S(2)}, u32[]{:S(2)}) %collective-permute-start.1) | collective-permute-done | bytes 1048608 | tf_op jit(solution)/shard_map/ppermute | solution.py:22
  39.4 1.6 collective-permute-start.5
  42.2 1.6 collective-permute-start.8
  44.3 10.3 %collective-permute-done.5 = bf16[256,1024]{1,0:T(8,128)(2,1)} collective-permute-done((bf16[256,1024]{1,0:T(8,128)(2,1)}, bf16[256,1024]{1,0:T(8,128)(2,1)}, u32[]{:S(2)}, u32[]{:S(2)}) %collective-permute-start.5) | collective-permute-done | bytes 524320 | tf_op jit(solution)/shard_map/ppermute | solution.py:22
  54.6 1.9 %constant_dynamic-update-slice_fusion.1 = bf16[512,1024]{1,0:T(8,128)(2,1)} fusion(bf16[256,1024]{1,0:T(8,128)(2,1)} %collective-permute-done.5), kind=kLoop, calls=%fused_computation.17 | loop fusion | bytes 1048576
  56.5 1.9 %constant_dynamic-update-slice_fusion.refs_4_ = bf16[512,1024]{1,0:T(8,128)(2,1)} fusion(bf16[512,1024]{1,0:T(8,128)(2,1)} %constant_dynamic-update-slice_fusion.1, bf16[256,1024]{1,0:T(8,128)(2,1)} %collective-permute-done.6), kind=kLoop, calls=%fused_computation.16 | loop fusion | bytes 1048576 | tf_op jit(solution)/shard_map/concatenate | solution.py:408
  58.9 5.8 %all-gather.2.cloned.1.call-done = bf16[8192,256]{1,0:T(8,128)(2,1)} async-done(((bf16[512,256]{1,0:T(8,128)(2,1)}), bf16[8192,256]{1,0:T(8,128)(2,1)}) %all-gather.2.cloned.1.call-update) | async-done | bytes 4194320 | tf_op jit(solution)/shard_map/all_gather | solution.py:379
  64.7 2.4 %constant_dynamic-slice_fusion = (bf16[1024,256]{1,0:T(8,128)(2,1)S(1)}, bf16[1024,256]{1,0:T(8,128)(2,1)S(1)}, bf16[1024,256]{1,0:T(8,128)(2,1)S(1)}, bf16[1024...) fusion(bf16[8192,256]{1,0:T(8,128)(2,1)} %all-gather.2.cloned.1, ...), kind=kLoop, calls=%fused_computation.20 | loop fusion | bytes 8388640 | tf_op jit(solution)/shard_map/dynamic_slice | solution.py:390
  67.2 1.7 fusion.9
  68.9 1.7 convolution_add_fusion.5
  70.6 1.7 fusion.11
  72.8 1.7 fusion.12
  74.9 1.7 fusion
  77.4 3.0 %collective-permute-start.13 = (bf16[512,256]{1,0:T(8,128)(2,1)S(1)}, bf16[512,256]{1,0:T(8,128)(2,1)S(1)}, u32[]{:S(2)}, u32[]{:S(2)}) collective-permute-start(bf16[512,256]{1,0:T(8,128)(2,1)S(1)} %shard_map.131.kv_ref), channel_id=1, source_target_pairs={{0,64},{8,72},{16,80},{24,88},{32,96},{40,104},{48,112},{56,120},{... | collective-permute-start | bytes 786440 | tf_op jit(solution)/shard_map/ppermute | solution.py:17
  84.3 1.7 fusion.16
  87.7 5.3 %shard_map.132 = (bf16[2,128,1024]{2,1,0:T(8,128)(2,1)}, bf16[2,128,1024]{2,1,0:T(8,128)(2,1)}, bf16[512,256]{1,0:T(8,128)(2,1)S(1)}) custom-call(s32[10]{0:T(128)S(1)} %copy-done.2, f32[1]{0:T(128)S(6)} %tanh.3.ratio_ref, bf16[2,128,1024]{2,1,0:T(8,128)(2,1)S(1)} %copy-done.3, bf16[2,128,1024]{2,1,0:T(8,128)(2,1)S(1)} %copy-done.4, ...), custom_call_target="tpu_custom_call" | custom-call | flops 939524096 | bytes 1441792 | tf_op jit(solution)/shard_map/pallas_call | solution.py:321
  93.0 3.3 %collective-permute-done.14 = bf16[256,1024]{1,0:T(8,128)(2,1)S(1)} collective-permute-done((bf16[256,1024]{1,0:T(8,128)(2,1)S(1)}, bf16[256,1024]{1,0:T(8,128)(2,1)S(1)}, u32[]{:S(2)}, u32[]{:S(2)}) %collective-permute-start.14) | collective-permute-done | bytes 524320 | tf_op jit(solution)/shard_map/ppermute | solution.py:22
  100.8 5.3 %shard_map.134 = (bf16[2,128,1024]{2,1,0:T(8,128)(2,1)}, bf16[2,128,1024]{2,1,0:T(8,128)(2,1)}, bf16[512,256]{1,0:T(8,128)(2,1)S(1)}) custom-call(s32[10]{0:T(128)S(1)} %copy-done.2, f32[1]{0:T(128)S(6)} %tanh.3.ratio_ref, bf16[2,128,1024]{2,1,0:T(8,128)(2,1)S(1)} %copy-done.3, ...), custom_call_target="tpu_custom_call", output_to_operand_aliasing={{0}: (7, {}), {1}: (8, {})} | custom-call | flops 939524096 | bytes 1441792 | tf_op jit(solution)/shard_map/pallas_call | solution.py:321
  107.6 4.9 %shard_map.137.refs_9_ = f32[8192,256]{1,0:T(8,128)S(1)} custom-call(bf16[512,1024]{1,0:T(8,128)(2,1)} %get-tuple-element.32.refs_0_, bf16[512,1024]{1,0:T(8,128)(2,1)} %collective-permute-done.refs_1_, bf16[512,1024]{1,0:T(8,128)(2,1)S(1)} %collective-permute-done.1.refs_2_, bf16[512,1024]{1,0:T(8,128)(2,1)} %collective-permute-done.2.refs_3_, ...), custom_call_target="tpu_custom_call" | custom-call | flops 2147483648 | bytes 8388608 | tf_op jit(solution)/shard_map/pallas_call | solution.py:199
  112.6 4.0 %shard_map.138 = bf16[8192,256]{1,0:T(8,128)(2,1)S(1)} custom-call(s32[10]{0:T(128)S(1)} %copy-done.2, bf16[512,1024]{1,0:T(8,128)(2,1)S(1)} %copy-done, bf16[512,1024]{1,0:T(8,128)(2,1)S(1)} %collective-permute-done.10.refs_1_, bf16[512,1024]{1,0:T(8,128)(2,1)S(1)} %collective-permute-done.8.refs_2_, bf16[512,1024]{1,0:T(8,128)(2,1)S(1)} %collective-permute-done.11.refs_3_, ...), custom_call_target="tpu_custom_call" | custom-call | flops 2147483648 | bytes 8388608 | tf_op jit(solution)/shard_map/pallas_call | solution.py:232
  116.6 31.5 %all_to_all.15 = bf16[4,2048,256]{2,1,0:T(8,128)(2,1)S(1)} all-to-all(bf16[4,2048,256]{2,1,0:T(8,128)(2,1)S(1)} %bitcast.38), channel_id=1, replica_groups={{0,8,16,24},{32,40,48,56},{64,72,80,88},{96,104,112,120},{1,33,65,97},{..., dimensions={0} | all-to-all | bytes 8388608 | tf_op jit(solution)/shard_map/all_to_all | solution.py:39
  148.7 13.5 %all_to_all.16 = bf16[4,512,256]{2,1,0:T(8,128)(2,1)S(1)} all-to-all(bf16[4,512,256]{2,1,0:T(8,128)(2,1)S(1)} %bitcast.45), channel_id=1, replica_groups={{0,32,64,96},{8,40,72,104},{16,48,80,112},{24,56,88,120},{1,9,17,25},{3..., dimensions={0} | all-to-all | bytes 2097152 | tf_op jit(solution)/shard_map/all_to_all | solution.py:39
  (67 shorter events, 20.0 us)
Async XLA Ops:
  7.2 57.6 %all-gather.2.cloned.1.call-start = ((), (), s32[]{:S(2)}) async-start(), calls=%async_computation.2 | async-start | bytes 4456448 | tf_op jit(solution)/shard_map/all_gather | solution.py:379
  12.5 25.2 %collective-permute-start.1 = (bf16[512,1024]{1,0:T(8,128)(2,1)}, bf16[512,1024]{1,0:T(8,128)(2,1)S(1)}, u32[]{:S(2)}, u32[]{:S(2)}) collective-permute-start(bf16[512,1024]{1,0:T(8,128)(2,1)} %get-tuple-element.32.refs_0_), channel_id=1, source_target_pairs={{0,2},{1,3},{2,4},{3,5},{4,6},{5,7},{6,0},{7,1},{8,10},{9,11},{10,... | collective-permute-start | bytes 3145736 | tf_op jit(solution)/shard_map/ppermute | solution.py:22
  13.8 24.8 %collective-permute-start.3 = (bf16[512,1024]{1,0:T(8,128)(2,1)}, bf16[512,1024]{1,0:T(8,128)(2,1)S(1)}, u32[]{:S(2)}, u32[]{:S(2)}) collective-permute-start(bf16[512,1024]{1,0:T(8,128)(2,1)} %get-tuple-element.32.refs_0_), channel_id=1, source_target_pairs={{0,6},{1,7},{2,0},{3,1},{4,2},{5,3},{6,4},{7,5},{8,14},{9,15},{10,... | collective-permute-start | bytes 3145736 | tf_op jit(solution)/shard_map/ppermute | solution.py:22
  39.4 15.2 %collective-permute-start.5 = (bf16[256,1024]{1,0:T(8,128)(2,1)}, bf16[256,1024]{1,0:T(8,128)(2,1)}, u32[]{:S(2)}, u32[]{:S(2)}) collective-permute-start(bf16[256,1024]{1,0:T(8,128)(2,1)} %slice.32), channel_id=1, source_target_pairs={{0,2},{1,3},{2,4},{3,5},{4,6},{5,7},{6,0},{7,1},{8,10},{9,11},{10,... | collective-permute-start | bytes 1572872 | tf_op jit(solution)/shard_map/ppermute | solution.py:22
  41.0 15.5 %collective-permute-start.6 = (bf16[256,1024]{1,0:T(8,128)(2,1)}, bf16[256,1024]{1,0:T(8,128)(2,1)}, u32[]{:S(2)}, u32[]{:S(2)}) collective-permute-start(bf16[256,1024]{1,0:T(8,128)(2,1)} %slice.33), channel_id=1, source_target_pairs={{0,6},{1,7},{2,0},{3,1},{4,2},{5,3},{6,4},{7,5},{8,14},{9,15},{10,... | collective-permute-start | bytes 1572872 | tf_op jit(solution)/shard_map/ppermute | solution.py:22
  41.5 27.4 %collective-permute-start = (bf16[512,1024]{1,0:T(8,128)(2,1)}, bf16[512,1024]{1,0:T(8,128)(2,1)}, u32[]{:S(2)}, u32[]{:S(2)}) collective-permute-start(bf16[512,1024]{1,0:T(8,128)(2,1)} %get-tuple-element.32.refs_0_), channel_id=1, source_target_pairs={{0,1},{1,0},{2,3},{3,2},{4,5},{5,4},{6,7},{7,6},{8,9},{9,8},{10,11... | collective-permute-start | bytes 3145736 | tf_op jit(solution)/shard_map/ppermute | solution.py:26
  42.2 38.2 %collective-permute-start.8 = (bf16[512,1024]{1,0:T(8,128)(2,1)}, bf16[512,1024]{1,0:T(8,128)(2,1)S(1)}, u32[]{:S(2)}, u32[]{:S(2)}) collective-permute-start(bf16[512,1024]{1,0:T(8,128)(2,1)} %get-tuple-element.45.refs_0_), channel_id=1, source_target_pairs={{0,2},{1,3},{2,4},{3,5},{4,6},{5,7},{6,0},{7,1},{8,10},{9,11},{10,... | collective-permute-start | bytes 3145736 | tf_op jit(solution)/shard_map/ppermute | solution.py:22
  43.8 36.6 %collective-permute-start.9 = (bf16[512,1024]{1,0:T(8,128)(2,1)}, bf16[512,1024]{1,0:T(8,128)(2,1)}, u32[]{:S(2)}, u32[]{:S(2)}) collective-permute-start(bf16[512,1024]{1,0:T(8,128)(2,1)} %get-tuple-element.45.refs_0_), channel_id=1, source_target_pairs={{0,6},{1,7},{2,0},{3,1},{4,2},{5,3},{6,4},{7,5},{8,14},{9,15},{10,... | collective-permute-start | bytes 3145736 | tf_op jit(solution)/shard_map/ppermute | solution.py:22
  54.6 20.3 %collective-permute-start.2 = (bf16[512,1024]{1,0:T(8,128)(2,1)S(1)}, bf16[512,1024]{1,0:T(8,128)(2,1)}, u32[]{:S(2)}, u32[]{:S(2)}) collective-permute-start(bf16[512,1024]{1,0:T(8,128)(2,1)S(1)} %collective-permute-done.1.refs_2_), channel_id=1, source_target_pairs={{0,1},{1,0},{2,3},{3,2},{4,5},{5,4},{6,7},{7,6},{8,9},{9,8},{10,11... | collective-permute-start | bytes 3145736 | tf_op jit(solution)/shard_map/ppermute | solution.py:26
  58.4 14.4 %collective-permute-start.7 = (bf16[512,1024]{1,0:T(8,128)(2,1)}, bf16[512,1024]{1,0:T(8,128)(2,1)}, u32[]{:S(2)}, u32[]{:S(2)}) collective-permute-start(bf16[512,1024]{1,0:T(8,128)(2,1)} %constant_dynamic-update-slice_fusion.refs_4_), channel_id=1, source_target_pairs={{0,1},{1,0},{2,3},{3,2},{4,5},{5,4},{6,7},{7,6},{8,9},{9,8},{10,11... | collective-permute-start | bytes 3145736 | tf_op jit(solution)/shard_map/ppermute | solution.py:26
  68.9 7.7 %collective-permute-start.4 = (bf16[512,1024]{1,0:T(8,128)(2,1)S(1)}, bf16[512,1024]{1,0:T(8,128)(2,1)S(1)}, u32[]{:S(2)}, u32[]{:S(2)}) collective-permute-start(bf16[512,1024]{1,0:T(8,128)(2,1)S(1)} %collective-permute-done.3.refs_6_), channel_id=1, source_target_pairs={{0,1},{1,0},{2,3},{3,2},{4,5},{5,4},{6,7},{7,6},{8,9},{9,8},{10,11... | collective-permute-start | bytes 3145736 | tf_op jit(solution)/shard_map/ppermute | solution.py:26
  77.4 10.3 %collective-permute-start.13 = (bf16[512,256]{1,0:T(8,128)(2,1)S(1)}, bf16[512,256]{1,0:T(8,128)(2,1)S(1)}, u32[]{:S(2)}, u32[]{:S(2)}) collective-permute-start(bf16[512,256]{1,0:T(8,128)(2,1)S(1)} %shard_map.131.kv_ref), channel_id=1, source_target_pairs={{0,64},{8,72},{16,80},{24,88},{32,96},{40,104},{48,112},{56,120},{... | collective-permute-start | bytes 786440 | tf_op jit(solution)/shard_map/ppermute | solution.py:17
  81.5 16.5 %collective-permute-start.12 = (bf16[512,1024]{1,0:T(8,128)(2,1)}, bf16[512,1024]{1,0:T(8,128)(2,1)S(1)}, u32[]{:S(2)}, u32[]{:S(2)}) collective-permute-start(bf16[512,1024]{1,0:T(8,128)(2,1)} %collective-permute-done.9.refs_6_), channel_id=1, source_target_pairs={{0,1},{1,0},{2,3},{3,2},{4,5},{5,4},{6,7},{7,6},{8,9},{9,8},{10,11... | collective-permute-start | bytes 3145736 | tf_op jit(solution)/shard_map/ppermute | solution.py:26
  81.8 5.8 %copy-start = (bf16[512,1024]{1,0:T(8,128)(2,1)S(1)}, bf16[512,1024]{1,0:T(8,128)(2,1)}, u32[]{:S(2)}) copy-start(bf16[512,1024]{1,0:T(8,128)(2,1)} %get-tuple-element.45.refs_0_) | copy-start | bytes 3145732
  81.9 5.8 %copy-start.2 = (s32[10]{0:T(128)S(1)}, s32[10]{0:T(128)}, u32[]{:S(2)}) copy-start(s32[10]{0:T(128)} %get-tuple-element.31.index.numbers.chip) | copy-start | bytes 124
  81.9 5.8 %copy-start.3 = (bf16[2,128,1024]{2,1,0:T(8,128)(2,1)S(1)}, bf16[2,128,1024]{2,1,0:T(8,128)(2,1)}, u32[]{:S(2)}) copy-start(bf16[2,128,1024]{2,1,0:T(8,128)(2,1)} %q_ref.3) | copy-start | bytes 1572868
  81.9 5.8 %copy-start.4 = (bf16[2,128,1024]{2,1,0:T(8,128)(2,1)S(1)}, bf16[2,128,1024]{2,1,0:T(8,128)(2,1)}, u32[]{:S(2)}) copy-start(bf16[2,128,1024]{2,1,0:T(8,128)(2,1)} %cot_ref.3) | copy-start | bytes 1572868
  81.9 5.8 %copy-start.5 = (f32[128]{0:T(128)S(1)}, f32[128]{0:T(128)}, u32[]{:S(2)}) copy-start(f32[128]{0:T(128)} %param.16) | copy-start | bytes 1540
  81.9 16.6 %collective-permute-start.11 = (bf16[512,1024]{1,0:T(8,128)(2,1)S(1)}, bf16[512,1024]{1,0:T(8,128)(2,1)S(1)}, u32[]{:S(2)}, u32[]{:S(2)}) collective-permute-start(bf16[512,1024]{1,0:T(8,128)(2,1)S(1)} %collective-permute-done.8.refs_2_), channel_id=1, source_target_pairs={{0,1},{1,0},{2,3},{3,2},{4,5},{5,4},{6,7},{7,6},{8,9},{9,8},{10,11... | collective-permute-start | bytes 3145736 | tf_op jit(solution)/shard_map/ppermute | solution.py:26
  82.3 14.0 %collective-permute-start.14 = (bf16[256,1024]{1,0:T(8,128)(2,1)S(1)}, bf16[256,1024]{1,0:T(8,128)(2,1)S(1)}, u32[]{:S(2)}, u32[]{:S(2)}) collective-permute-start(bf16[256,1024]{1,0:T(8,128)(2,1)S(1)} %slice.28), channel_id=1, source_target_pairs={{0,2},{1,3},{2,4},{3,5},{4,6},{5,7},{6,0},{7,1},{8,10},{9,11},{10,... | collective-permute-start | bytes 1572872 | tf_op jit(solution)/shard_map/ppermute | solution.py:22
  83.4 13.8 %collective-permute-start.15 = (bf16[256,1024]{1,0:T(8,128)(2,1)S(1)}, bf16[256,1024]{1,0:T(8,128)(2,1)S(1)}, u32[]{:S(2)}, u32[]{:S(2)}) collective-permute-start(bf16[256,1024]{1,0:T(8,128)(2,1)S(1)} %slice.29), channel_id=1, source_target_pairs={{0,6},{1,7},{2,0},{3,1},{4,2},{5,3},{6,4},{7,5},{8,14},{9,15},{10,... | collective-permute-start | bytes 1572872 | tf_op jit(solution)/shard_map/ppermute | solution.py:22
  87.7 11.2 %collective-permute-start.10 = (bf16[512,1024]{1,0:T(8,128)(2,1)S(1)}, bf16[512,1024]{1,0:T(8,128)(2,1)S(1)}, u32[]{:S(2)}, u32[]{:S(2)}) collective-permute-start(bf16[512,1024]{1,0:T(8,128)(2,1)S(1)} %copy-done), channel_id=1, source_target_pairs={{0,1},{1,0},{2,3},{3,2},{4,5},{5,4},{6,7},{7,6},{8,9},{9,8},{10,11... | collective-permute-start | bytes 3145736 | tf_op jit(solution)/shard_map/ppermute | solution.py:26
  96.3 10.5 %collective-permute-start.17 = (bf16[512,256]{1,0:T(8,128)(2,1)S(1)}, bf16[512,256]{1,0:T(8,128)(2,1)S(1)}, u32[]{:S(2)}, u32[]{:S(2)}) collective-permute-start(bf16[512,256]{1,0:T(8,128)(2,1)S(1)} %get-tuple-element.48.grad_ref), channel_id=1, source_target_pairs={{0,64},{8,72},{16,80},{24,88},{32,96},{40,104},{48,112},{56,120},{... | collective-permute-start | bytes 786440 | tf_op jit(solution)/shard_map/ppermute | solution.py:17
  97.3 2.9 %collective-permute-start.16 = (bf16[512,1024]{1,0:T(8,128)(2,1)S(1)}, bf16[512,1024]{1,0:T(8,128)(2,1)S(1)}, u32[]{:S(2)}, u32[]{:S(2)}) collective-permute-start(bf16[512,1024]{1,0:T(8,128)(2,1)S(1)} %constant_dynamic-update-slice_fusion.2.refs_4_), channel_id=1, source_target_pairs={{0,1},{1,0},{2,3},{3,2},{4,5},{5,4},{6,7},{7,6},{8,9},{9,8},{10,11... | collective-permute-start | bytes 3145736 | tf_op jit(solution)/shard_map/ppermute | solution.py:26
  (1 other events, 0.7 us)
Sparse Core Ops, SparseCore 0:
  10.7 53.9 all-gather.1

commit v6 on v4

--- a/solution.py
+++ b/solution.py
@@ -47,24 +47,13 @@
     return lax.ppermute(x, "tensor", [(i, i ^ 1) for i in range(2 * RING)])
 
 
-def axis_groups(z_core):
-    groups = []
-    for i in range(2 * RING):
-        for fixed in range(RING):
-            along = [(k, fixed) if i % 2 == z_core else (fixed, k) for k in range(RING)]
-            groups.append([(z * RING + y) * 2 * RING + i for z, y in along])
-    return groups
-
-
-def exchanged(blocks, z_core):
-    return lax.all_to_all(
-        blocks, ("dp", "tensor"), 0, 0, tiled=True, axis_index_groups=axis_groups(z_core)
-    )
-
-
 def gathered(block, move):
     far, after, before = (move(block, step) for step in (2, 1, 3))
     return [block, after, far, before]
+
+
+def scattered(parts, move):
+    return [move(parts[step], step) for step in (2, 1, 3)]
 
 
 def summed(blocks):
@@ -276,29 +265,41 @@
 
 
 def product_kernel(chip, *refs):
-    sources, (grads_ref, part_ref, out_ref) = refs[:-3], refs[-3:]
+    sources, (grads_ref, part_ref), refs = refs[: 2 * RING], refs[2 * RING : 2 * RING + 2], refs[2 * RING + 2 :]
+    outs, (held, sems) = refs[:RING], refs[RING:]
     depth = sources[0].shape[1]
     count = depth // 2
-    x, core = chip[CHIP + 2], chip[CHIP + 3]
+    z, y, x, core = (chip[CHIP + i] for i in range(4))
     for k, source in enumerate(sources):
         total = matmul(source[...], grads_ref[...], ((0,), (0,)))
-        total = (total + part_ref[k * depth : (k + 1) * depth]).astype(out_ref.dtype)
-        to_z = (x - k // 2 + RING) % RING
+        total = (total + part_ref[k * depth : (k + 1) * depth]).astype(held.dtype)
+        by_z = (x - k // 2 - z + 2 * RING) % RING
         for h in range(2):
-            to_y = 2 * (k % 2 ^ core) + h
-            block = jnp.where(core == 0, to_y * RING + to_z, to_z * RING + to_y)
-            start = pl.multiple_of(block * count, count)
-            out_ref[pl.ds(start, count)] = total[h * count : (h + 1) * count]
+            by_y = (2 * (k % 2 ^ core) + h - y + RING) % RING
+            outer_by = jnp.where(core == 0, by_y, by_z)
+            inner_by = jnp.where(core == 0, by_z, by_y)
+            start = pl.multiple_of(inner_by * count, count)
+            held[outer_by, pl.ds(start, count)] = total[h * count : (h + 1) * count]
+    copies = [pltpu.make_async_copy(held.at[k], outs[k], sems.at[k]) for k in range(RING)]
+    for copy in copies:
+        copy.start()
+    for copy in copies:
+        copy.wait()
 
 
 def product(chip, feats, grads, part):
     rows, depth = feats[0].shape
     both = grads.shape[1]
+    shape = (RING * depth // 2, both)
     return pl.pallas_call(
         product_kernel,
         in_specs=[SMEM] + [VMEM] * (len(feats) + 2),
-        out_specs=VMEM,
-        out_shape=jax.ShapeDtypeStruct((len(feats) * depth, both), jnp.bfloat16),
+        out_specs=[ANY] * RING,
+        out_shape=[jax.ShapeDtypeStruct(shape, jnp.bfloat16)] * RING,
+        scratch_shapes=[
+            pltpu.VMEM((RING, *shape), jnp.bfloat16),
+            pltpu.SemaphoreType.DMA((RING,)),
+        ],
         compiler_params=PARAMS,
         cost_estimate=pl.CostEstimate(
             flops=2 * len(feats) * rows * depth * both,
@@ -433,20 +434,35 @@
     ratio = jnp.tanh(gate)
     numbers, far_own, near_own = route(tiles, image_slot, image)
 
+    half = image.shape[1] // 2
+
     def opposite(after, before, move):
-        half = after.shape[0] // 2
-        return [move(after[:half], 1), move(before[half:], 3)]
+        middle = after.shape[0] // 2
+        return [move(after[:middle], 1), move(before[middle:], 3)]
 
     shard = lay(numbers, key_weight_matrix, value_weight_matrix)
     far_x = [along_x(far_own, 1), along_x(far_own, 3)]
     shard = jnp.concatenate(gathered(shard, inner), axis=0)
-    shard, *far_x = lax.optimization_barrier((shard, *far_x))
-    far_halves = opposite(*far_x, along_x)
+    ahead = [
+        jnp.concatenate([near_own[:half], near_own], axis=0),
+        jnp.concatenate([near_own[half:], near_own], axis=0),
+    ]
+    shard, *ahead = lax.optimization_barrier((shard, *ahead))
+    far_other, near_other = other_core(far_own), other_core(near_own)
+    shard, far_other, near_other, *far_x = lax.optimization_barrier(
+        (shard, far_other, near_other, *far_x)
+    )
+    ahead = [
+        lax.dynamic_update_slice_in_dim(ahead[0], far_x[0][:half], 0, 0),
+        lax.dynamic_update_slice_in_dim(ahead[1], far_x[1][half:], 0, 0),
+    ]
+    ahead = [along_x(ahead[0], 1), along_x(ahead[1], 3)]
     pieces = [outer(shard, 1), outer(shard, 3)]
-    near_own, *far_halves = lax.optimization_barrier((near_own, *far_halves))
-    near_x = [along_x(near_own, 1), along_x(near_own, 3)]
     weights = assemble(numbers, [shard, *pieces, *opposite(*pieces, outer)])
-    weights, *far_blocks = lax.optimization_barrier((weights, *far_x, *far_halves))
+    weights, *far_x = lax.optimization_barrier((weights, *far_x))
+    far_halves = [block[:half] for block in ahead]
+    near_x = [block[half:] for block in ahead]
+    near_halves = opposite(*near_x, along_x)
 
     def other_cores(*blocks):
         return [other_core(block) for block in blocks]
@@ -464,22 +480,18 @@
         return total
 
     shared = (numbers, ratio, query, cotangent)
-    after, before, *halves = far_blocks
-    blocks = [after, before, jnp.concatenate(halves, axis=0)]
-    far_feats = paired(far_own, other_core(far_own), *blocks, *other_cores(*blocks))
+    blocks = [*far_x, jnp.concatenate(far_halves, axis=0)]
+    far_feats = paired(far_own, far_other, *blocks, *other_cores(*blocks))
     far_total = project(far_feats)
     far_key_value = finish(far_total, key_gain)
     away = along_z(far_key_value, RING // 2)
-    _, *near_late = lax.optimization_barrier((far_key_value, *near_x))
-    near_halves = opposite(*near_late, along_x)
-    near_others = other_cores(*near_late)
+    _, *blocks = lax.optimization_barrier((far_key_value, *near_x, *near_halves))
+    near_x, near_halves = blocks[:2], blocks[2:]
     *earlier, far_grad = attend(FAR, *shared, far_key_value, away, query_gain, ())
     back = along_z(far_grad, RING // 2)
 
-    _, *near_halves = lax.optimization_barrier((far_grad, *near_halves))
     blocks = [*near_x, jnp.concatenate(near_halves, axis=0)]
-    near_others.append(other_core(blocks[2]))
-    near_feats = paired(near_own, other_core(near_own), *blocks, *near_others)
+    near_feats = paired(near_own, near_other, *blocks, *other_cores(*blocks))
     near_total = project(near_feats)
     near_key_value = finish(near_total, key_gain)
     context, d_query, near_grad = attend(
@@ -491,10 +503,11 @@
     part = first_part(far_feats, far_rows)
 
     blocks = product(numbers, near_feats, near_rows, part)
-    for z_core in (1, 0):
-        blocks = exchanged(blocks, z_core)
-        blocks = summed(jnp.split(blocks, RING, axis=0))
-        share, blocks = blocks, blocks.astype(jnp.bfloat16)
+    total = summed([blocks[0], *scattered(blocks, outer)])
+    count = total.shape[0] // RING
+    parts = [total[d * count : (d + 1) * count] for d in range(RING)]
+    sent = [None] + [part.astype(jnp.bfloat16) for part in parts[1:]]
+    share = summed([parts[0], *scattered(sent, inner)])
     head_dim = query_gain.shape[0]
     return (context, d_query, share[:, :head_dim], share[:, head_dim:])
 

time: 165 us -> 171 us (1.036)
  blocking collectives: 43.6 us -> 0 us
  waiting for transfers between devices: 52.7 us -> 94 us
  starting transfers between devices: 29.2 us -> 36.9 us
    all_to_all x2 -> x0, blocking collectives: 43.6 us -> none  [exchanged(): lax.all_to_all(blocks, ('dp', 'tensor'), 0, 0, tiled=True, axis_index_gro...]
    ppermute x7 -> x13, waiting for transfers between devices: 23.9 us -> 56.7 us  [by_core(): return lax.ppermute(x, ('dp', 'tensor'), pairs)]
    ppermute x7 -> x13, starting transfers between devices: 12 us -> 22 us  [by_core(): return lax.ppermute(x, ('dp', 'tensor'), pairs)]
    ppermute x8 -> x6, waiting for transfers between devices: 22.5 us -> 31.6 us  [along_x(): return lax.ppermute(x, 'tensor', pairs)]
    ppermute x8 -> x6, starting transfers between devices: 8.45 us -> 6.81 us  [along_x(): return lax.ppermute(x, 'tensor', pairs)]
  transfers between devices with their start and end apart: 25 -> 29, of which waited for: 10 -> 16; matrix products, arithmetic and copies ran while one was open for 5% -> 6% of each run, Pallas kernels for 8% -> 8%
where the time goes in v6:
time: 171 us; the launch traced here: 169 us
  waiting for transfers between devices  94 us (55%)
  starting transfers between devices  36.9 us (22%)
  Pallas kernels  24.4 us (14%)
  matrix products  7.22 us (4%)
  local copies, waits for them, and re-layouts  3.59 us (2%)
  between operations  1.84 us (1%)
    ppermute x13, waiting for transfers between devices, by_core(): return lax.ppermute(x, ('dp', 'tensor'), pairs)  56.7 us
    ppermute x6, waiting for transfers between devices, along_x(): return lax.ppermute(x, 'tensor', pairs)  31.6 us
    ppermute x13, starting transfers between devices, by_core(): return lax.ppermute(x, ('dp', 'tensor'), pairs)  22 us
    pallas_call x2, Pallas kernels, attend(): pl.pallas_call(functools.partial(attend_kernel, heads, base), grid_spec=p...  10.6 us
    dot_general x16, matrix products, matmul(): lax.dot_general(a, b, (contract, ((), ())), preferred_element_type=jnp.fl...  7.22 us
    ppermute x6, starting transfers between devices, along_x(): return lax.ppermute(x, 'tensor', pairs)  6.81 us
    ppermute x2, starting transfers between devices, along_z(): return lax.ppermute(x, 'dp', pairs)  6.2 us
    ppermute x2, waiting for transfers between devices, along_z(): return lax.ppermute(x, 'dp', pairs)  5.62 us
  transfers between devices with their start and end apart: 29, of which 16 were waited for; matrix products, arithmetic and copies ran while one was open for 6% of the time, Pallas kernels for 8%

profile of v6, /device:TPU:4, one launch (start us, length us, event | category | flops | bytes accessed | tf_op | source)
XLA Modules:
  0.0 168.9 jit_solution(2194265616744629005)
XLA Ops:
  0.7 3.7 %shard_map.129 = (s32[10]{0:T(128)}, bf16[512,1024]{1,0:T(8,128)(2,1)}, bf16[512,1024]{1,0:T(8,128)(2,1)}) custom-call(s32[32]{0:T(128)} %tiles.1, s32[32]{0:T(128)} %slots.1, bf16[2,512,1024]{2,1,0:T(8,128)(2,1)} %image_ref.1), custom_call_target="tpu_custom_call" | custom-call | bytes 4194304 | tf_op jit(solution)/shard_map/pallas_call | solution.py:124
  5.8 4.1 %collective-permute-start.2 = (bf16[512,256]{1,0:T(8,128)(2,1)S(1)}, bf16[512,256]{1,0:T(8,128)(2,1)S(1)}, u32[]{:S(2)}, u32[]{:S(2)}) collective-permute-start(bf16[512,256]{1,0:T(8,128)(2,1)S(1)} %shard_map.130), channel_id=1, source_target_pairs={{0,96},{1,25},{2,98},{3,27},{4,100},{5,29},{6,102},{7,31},{8,104},... | collective-permute-start | bytes 786440 | tf_op jit(solution)/shard_map/ppermute | solution.py:30
  13.8 2.3 %collective-permute-start.1 = (bf16[512,256]{1,0:T(8,128)(2,1)S(1)}, bf16[512,256]{1,0:T(8,128)(2,1)S(1)}, u32[]{:S(2)}, u32[]{:S(2)}) collective-permute-start(bf16[512,256]{1,0:T(8,128)(2,1)S(1)} %shard_map.130), channel_id=1, source_target_pairs={{0,64},{1,17},{2,66},{3,19},{4,68},{5,21},{6,70},{7,23},{8,72},{9,... | collective-permute-start | bytes 786440 | tf_op jit(solution)/shard_map/ppermute | solution.py:30
  16.1 5.6 %collective-permute-done.1 = bf16[512,256]{1,0:T(8,128)(2,1)S(1)} collective-permute-done((bf16[512,256]{1,0:T(8,128)(2,1)S(1)}, bf16[512,256]{1,0:T(8,128)(2,1)S(1)}, u32[]{:S(2)}, u32[]{:S(2)}) %collective-permute-start.1) | collective-permute-done | bytes 262176 | tf_op jit(solution)/shard_map/ppermute | solution.py:30
  24.2 5.5 %collective-permute-done = bf16[512,256]{1,0:T(8,128)(2,1)S(1)} collective-permute-done((bf16[512,256]{1,0:T(8,128)(2,1)S(1)}, bf16[512,256]{1,0:T(8,128)(2,1)S(1)}, u32[]{:S(2)}, u32[]{:S(2)}) %collective-permute-start) | collective-permute-done | bytes 262176 | tf_op jit(solution)/shard_map/ppermute | solution.py:30
  29.8 5.9 %collective-permute-done.5.refs_2_ = bf16[512,1024]{1,0:T(8,128)(2,1)S(1)} collective-permute-done((bf16[512,1024]{1,0:T(8,128)(2,1)}, bf16[512,1024]{1,0:T(8,128)(2,1)S(1)}, u32[]{:S(2)}, u32[]{:S(2)}) %collective-permute-start.5) | collective-permute-done | bytes 1048608 | tf_op jit(solution)/shard_map/ppermute | solution.py:43
  42.8 12.1 %collective-permute-done.7.refs_1_ = bf16[2048,256]{1,0:T(8,128)(2,1)S(1)} collective-permute-done((bf16[2048,256]{1,0:T(8,128)(2,1)S(1)}, bf16[2048,256]{1,0:T(8,128)(2,1)S(1)}, u32[]{:S(2)}, u32[]{:S(2)}) %collective-permute-start.7) | collective-permute-done | bytes 1048608 | tf_op jit(solution)/shard_map/ppermute | solution.py:30
  55.3 2.9 %collective-permute-start.10 = (bf16[1024,256]{1,0:T(8,128)(2,1)S(1)}, bf16[1024,256]{1,0:T(8,128)(2,1)S(1)}, u32[]{:S(2)}, u32[]{:S(2)}) collective-permute-start(bf16[1024,256]{1,0:T(8,128)(2,1)S(1)} %slice.118), channel_id=1, source_target_pairs={{0,24},{1,97},{2,26},{3,99},{4,28},{5,101},{6,30},{7,103},{8,0},{9... | collective-permute-start | bytes 1572872 | tf_op jit(solution)/shard_map/ppermute | solution.py:30
  58.3 13.5 %collective-permute-done.14 = bf16[768,1024]{1,0:T(8,128)(2,1)S(1)} collective-permute-done((bf16[768,1024]{1,0:T(8,128)(2,1)S(1)}, bf16[768,1024]{1,0:T(8,128)(2,1)S(1)}, u32[]{:S(2)}, u32[]{:S(2)}) %collective-permute-start.14) | collective-permute-done | bytes 1572896 | tf_op jit(solution)/shard_map/ppermute | solution.py:43
  75.2 2.6 %collective-permute-start.16 = (bf16[256,1024]{1,0:T(8,128)(2,1)S(1)}, bf16[256,1024]{1,0:T(8,128)(2,1)S(1)}, u32[]{:S(2)}, u32[]{:S(2)}) collective-permute-start(bf16[256,1024]{1,0:T(8,128)(2,1)S(1)} %get-tuple-element.68), channel_id=1, source_target_pairs={{0,2},{1,3},{2,4},{3,5},{4,6},{5,7},{6,0},{7,1},{8,10},{9,11},{10,... | collective-permute-start | bytes 1572872 | tf_op jit(solution)/shard_map/ppermute | solution.py:43
  82.0 7.5 %collective-permute-done.16 = bf16[256,1024]{1,0:T(8,128)(2,1)S(1)} collective-permute-done((bf16[256,1024]{1,0:T(8,128)(2,1)S(1)}, bf16[256,1024]{1,0:T(8,128)(2,1)S(1)}, u32[]{:S(2)}, u32[]{:S(2)}) %collective-permute-start.16) | collective-permute-done | bytes 524320 | tf_op jit(solution)/shard_map/ppermute | solution.py:43
  89.4 3.3 %collective-permute-done.17 = bf16[256,1024]{1,0:T(8,128)(2,1)S(1)} collective-permute-done((bf16[256,1024]{1,0:T(8,128)(2,1)S(1)}, bf16[256,1024]{1,0:T(8,128)(2,1)S(1)}, u32[]{:S(2)}, u32[]{:S(2)}) %collective-permute-start.17) | collective-permute-done | bytes 524320 | tf_op jit(solution)/shard_map/ppermute | solution.py:43
  93.2 3.2 %collective-permute-start.21 = (bf16[512,256]{1,0:T(8,128)(2,1)S(1)}, bf16[512,256]{1,0:T(8,128)(2,1)S(1)}, u32[]{:S(2)}, u32[]{:S(2)}) collective-permute-start(bf16[512,256]{1,0:T(8,128)(2,1)S(1)} %shard_map.132.kv_ref), channel_id=1, source_target_pairs={{0,64},{8,72},{16,80},{24,88},{32,96},{40,104},{48,112},{56,120},{... | collective-permute-start | bytes 786440 | tf_op jit(solution)/shard_map/ppermute | solution.py:17
  98.1 5.6 %collective-permute-done.21.away_ref = bf16[512,256]{1,0:T(8,128)(2,1)S(1)} collective-permute-done((bf16[512,256]{1,0:T(8,128)(2,1)S(1)}, bf16[512,256]{1,0:T(8,128)(2,1)S(1)}, u32[]{:S(2)}, u32[]{:S(2)}) %collective-permute-start.21) | collective-permute-done | bytes 262176 | tf_op jit(solution)/shard_map/ppermute | solution.py:17
  103.7 5.3 %shard_map.134 = (bf16[2,128,1024]{2,1,0:T(8,128)(2,1)}, bf16[2,128,1024]{2,1,0:T(8,128)(2,1)}, bf16[512,256]{1,0:T(8,128)(2,1)S(1)}) custom-call(s32[10]{0:T(128)S(1)} %copy-done.5, f32[1]{0:T(128)S(6)} %tanh.3.ratio_ref, bf16[2,128,1024]{2,1,0:T(8,128)(2,1)S(1)} %copy-done.7, bf16[2,128,1024]{2,1,0:T(8,128)(2,1)S(1)} %copy-done.8, ...), custom_call_target="tpu_custom_call" | custom-call | flops 939524096 | bytes 1441792 | tf_op jit(solution)/shard_map/pallas_call | solution.py:387
  109.0 3.0 %collective-permute-start.22 = (bf16[512,256]{1,0:T(8,128)(2,1)S(1)}, bf16[512,256]{1,0:T(8,128)(2,1)S(1)}, u32[]{:S(2)}, u32[]{:S(2)}) collective-permute-start(bf16[512,256]{1,0:T(8,128)(2,1)S(1)} %get-tuple-element.56.grad_ref), channel_id=1, source_target_pairs={{0,64},{8,72},{16,80},{24,88},{32,96},{40,104},{48,112},{56,120},{... | collective-permute-start | bytes 786440 | tf_op jit(solution)/shard_map/ppermute | solution.py:17
  114.0 5.3 %shard_map.135 = (bf16[2,128,1024]{2,1,0:T(8,128)(2,1)}, bf16[2,128,1024]{2,1,0:T(8,128)(2,1)}, bf16[512,256]{1,0:T(8,128)(2,1)S(1)}) custom-call(s32[10]{0:T(128)S(1)} %copy-done.5, f32[1]{0:T(128)S(6)} %tanh.3.ratio_ref, bf16[2,128,1024]{2,1,0:T(8,128)(2,1)S(1)} %copy-done.7, ...), custom_call_target="tpu_custom_call", output_to_operand_aliasing={{0}: (7, {}), {1}: (8, {})} | custom-call | flops 939524096 | bytes 1441792 | tf_op jit(solution)/shard_map/pallas_call | solution.py:387
  120.8 2.6 %shard_map.138.refs_9_ = f32[8192,256]{1,0:T(8,128)S(1)} custom-call(bf16[512,1024]{1,0:T(8,128)(2,1)S(1)} %copy-done.1, bf16[512,1024]{1,0:T(8,128)(2,1)S(1)} %collective-permute-done.3.refs_1_, bf16[512,1024]{1,0:T(8,128)(2,1)S(1)} %collective-permute-done.5.refs_2_, bf16[512,1024]{1,0:T(8,128)(2,1)S(1)} %collective-permute-done.11.refs_3_, ...), custom_call_target="tpu_custom_call" | custom-call | flops 2147483648 | bytes 8388608 | tf_op jit(solution)/shard_map/pallas_call | solution.py:253
  123.4 3.8 %shard_map.139 = (bf16[2048,256]{1,0:T(8,128)(2,1)S(1)}, bf16[2048,256]{1,0:T(8,128)(2,1)S(1)}, bf16[2048,256]{1,0:T(8,128)(2,1)S(1)}, bf16[2048,256]{1,0:T(8,128)(2,1)S(1)}) custom-call(s32[10]{0:T(128)S(1)} %copy-done.5, bf16[512,1024]{1,0:T(8,128)(2,1)S(1)} %copy-done, bf16[512,1024]{1,0:T(8,128)(2,1)S(1)} %collective-permute-done.4.refs_1_, ...), custom_call_target="tpu_custom_call" | custom-call | flops 2147483648 | bytes 8388608 | tf_op jit(solution)/shard_map/pallas_call | solution.py:294
  130.9 11.2 %collective-permute-done.25 = bf16[2048,256]{1,0:T(8,128)(2,1)S(1)} collective-permute-done((bf16[2048,256]{1,0:T(8,128)(2,1)S(1)}, bf16[2048,256]{1,0:T(8,128)(2,1)S(1)}, u32[]{:S(2)}, u32[]{:S(2)}) %collective-permute-start.25) | collective-permute-done | bytes 1048608 | tf_op jit(solution)/shard_map/ppermute | solution.py:30
  142.1 13.8 %collective-permute-done.24 = bf16[2048,256]{1,0:T(8,128)(2,1)S(1)} collective-permute-done((bf16[2048,256]{1,0:T(8,128)(2,1)S(1)}, bf16[2048,256]{1,0:T(8,128)(2,1)S(1)}, u32[]{:S(2)}, u32[]{:S(2)}) %collective-permute-start.24) | collective-permute-done | bytes 1048608 | tf_op jit(solution)/shard_map/ppermute | solution.py:30
  158.6 2.2 %collective-permute-start.26 = (bf16[512,256]{1,0:T(8,128)(2,1)S(1)}, bf16[512,256]{1,0:T(8,128)(2,1)S(1)}, u32[]{:S(2)}, u32[]{:S(2)}) collective-permute-start(bf16[512,256]{1,0:T(8,128)(2,1)S(1)} %get-tuple-element.70), channel_id=1, source_target_pairs={{0,64},{1,17},{2,66},{3,19},{4,68},{5,21},{6,70},{7,23},{8,72},{9,... | collective-permute-start | bytes 786440 | tf_op jit(solution)/shard_map/ppermute | solution.py:30
  160.8 2.1 %collective-permute-done.28 = bf16[512,256]{1,0:T(8,128)(2,1)S(1)} collective-permute-done((bf16[512,256]{1,0:T(8,128)(2,1)S(1)}, bf16[512,256]{1,0:T(8,128)(2,1)S(1)}, u32[]{:S(2)}, u32[]{:S(2)}) %collective-permute-start.28) | collective-permute-done | bytes 262176 | tf_op jit(solution)/shard_map/ppermute | solution.py:30
  164.6 3.4 %collective-permute-done.26 = bf16[512,256]{1,0:T(8,128)(2,1)S(1)} collective-permute-done((bf16[512,256]{1,0:T(8,128)(2,1)S(1)}, bf16[512,256]{1,0:T(8,128)(2,1)S(1)}, u32[]{:S(2)}, u32[]{:S(2)}) %collective-permute-start.26) | collective-permute-done | bytes 262176 | tf_op jit(solution)/shard_map/ppermute | solution.py:30
  (99 shorter events, 36.5 us)
Async XLA Ops:
  5.8 8.0 %collective-permute-start.2 = (bf16[512,256]{1,0:T(8,128)(2,1)S(1)}, bf16[512,256]{1,0:T(8,128)(2,1)S(1)}, u32[]{:S(2)}, u32[]{:S(2)}) collective-permute-start(bf16[512,256]{1,0:T(8,128)(2,1)S(1)} %shard_map.130), channel_id=1, source_target_pairs={{0,96},{1,25},{2,98},{3,27},{4,100},{5,29},{6,102},{7,31},{8,104},... | collective-permute-start | bytes 786440 | tf_op jit(solution)/shard_map/ppermute | solution.py:30
  9.9 19.9 %collective-permute-start.3 = (bf16[512,1024]{1,0:T(8,128)(2,1)}, bf16[512,1024]{1,0:T(8,128)(2,1)S(1)}, u32[]{:S(2)}, u32[]{:S(2)}) collective-permute-start(bf16[512,1024]{1,0:T(8,128)(2,1)} %get-tuple-element.37.refs_0_), channel_id=1, source_target_pairs={{0,1},{1,0},{2,3},{3,2},{4,5},{5,4},{6,7},{7,6},{8,9},{9,8},{10,11... | collective-permute-start | bytes 3145736 | tf_op jit(solution)/shard_map/ppermute | solution.py:47
  9.9 19.9 %collective-permute-start.4 = (bf16[512,1024]{1,0:T(8,128)(2,1)}, bf16[512,1024]{1,0:T(8,128)(2,1)S(1)}, u32[]{:S(2)}, u32[]{:S(2)}) collective-permute-start(bf16[512,1024]{1,0:T(8,128)(2,1)} %get-tuple-element.35.refs_0_), channel_id=1, source_target_pairs={{0,1},{1,0},{2,3},{3,2},{4,5},{5,4},{6,7},{7,6},{8,9},{9,8},{10,11... | collective-permute-start | bytes 3145736 | tf_op jit(solution)/shard_map/ppermute | solution.py:47
  10.4 25.3 %collective-permute-start.5 = (bf16[512,1024]{1,0:T(8,128)(2,1)}, bf16[512,1024]{1,0:T(8,128)(2,1)S(1)}, u32[]{:S(2)}, u32[]{:S(2)}) collective-permute-start(bf16[512,1024]{1,0:T(8,128)(2,1)} %get-tuple-element.37.refs_0_), channel_id=1, source_target_pairs={{0,2},{1,3},{2,4},{3,5},{4,6},{5,7},{6,0},{7,1},{8,10},{9,11},{10,... | collective-permute-start | bytes 3145736 | tf_op jit(solution)/shard_map/ppermute | solution.py:43
  11.6 25.0 %collective-permute-start.6 = (bf16[512,1024]{1,0:T(8,128)(2,1)}, bf16[512,1024]{1,0:T(8,128)(2,1)S(1)}, u32[]{:S(2)}, u32[]{:S(2)}) collective-permute-start(bf16[512,1024]{1,0:T(8,128)(2,1)} %get-tuple-element.37.refs_0_), channel_id=1, source_target_pairs={{0,6},{1,7},{2,0},{3,1},{4,2},{5,3},{6,4},{7,5},{8,14},{9,15},{10,... | collective-permute-start | bytes 3145736 | tf_op jit(solution)/shard_map/ppermute | solution.py:43
  21.6 8.0 %collective-permute-start = (bf16[512,256]{1,0:T(8,128)(2,1)S(1)}, bf16[512,256]{1,0:T(8,128)(2,1)S(1)}, u32[]{:S(2)}, u32[]{:S(2)}) collective-permute-start(bf16[512,256]{1,0:T(8,128)(2,1)S(1)} %shard_map.130), channel_id=1, source_target_pairs={{0,32},{1,9},{2,34},{3,11},{4,36},{5,13},{6,38},{7,15},{8,40},{9,1... | collective-permute-start | bytes 786440 | tf_op jit(solution)/shard_map/ppermute | solution.py:30
  36.6 35.2 %collective-permute-start.14 = (bf16[768,1024]{1,0:T(8,128)(2,1)S(1)}, bf16[768,1024]{1,0:T(8,128)(2,1)S(1)}, u32[]{:S(2)}, u32[]{:S(2)}) collective-permute-start(bf16[768,1024]{1,0:T(8,128)(2,1)S(1)} %slice_dynamic-update-slice_fusion), channel_id=1, source_target_pairs={{0,6},{1,7},{2,0},{3,1},{4,2},{5,3},{6,4},{7,5},{8,14},{9,15},{10,... | collective-permute-start | bytes 4718600 | tf_op jit(solution)/shard_map/ppermute | solution.py:43
  37.6 34.9 %collective-permute-start.13 = (bf16[768,1024]{1,0:T(8,128)(2,1)S(1)}, bf16[768,1024]{1,0:T(8,128)(2,1)S(1)}, u32[]{:S(2)}, u32[]{:S(2)}) collective-permute-start(bf16[768,1024]{1,0:T(8,128)(2,1)S(1)} %slice_dynamic-update-slice_fusion.1), channel_id=1, source_target_pairs={{0,2},{1,3},{2,4},{3,5},{4,6},{5,7},{6,0},{7,1},{8,10},{9,11},{10,... | collective-permute-start | bytes 4718600 | tf_op jit(solution)/shard_map/ppermute | solution.py:43
  38.8 16.0 %collective-permute-start.7 = (bf16[2048,256]{1,0:T(8,128)(2,1)S(1)}, bf16[2048,256]{1,0:T(8,128)(2,1)S(1)}, u32[]{:S(2)}, u32[]{:S(2)}) collective-permute-start(bf16[2048,256]{1,0:T(8,128)(2,1)S(1)} %pad_maximum_fusion.2.refs_0_), channel_id=1, source_target_pairs={{0,8},{1,33},{2,10},{3,35},{4,12},{5,37},{6,14},{7,39},{8,16},{9,4... | collective-permute-start | bytes 3145736 | tf_op jit(solution)/shard_map/ppermute | solution.py:30
  40.4 14.9 %collective-permute-start.8 = (bf16[2048,256]{1,0:T(8,128)(2,1)S(1)}, bf16[2048,256]{1,0:T(8,128)(2,1)S(1)}, u32[]{:S(2)}, u32[]{:S(2)}) collective-permute-start(bf16[2048,256]{1,0:T(8,128)(2,1)S(1)} %pad_maximum_fusion.2.refs_0_), channel_id=1, source_target_pairs={{0,24},{1,97},{2,26},{3,99},{4,28},{5,101},{6,30},{7,103},{8,0},{9... | collective-permute-start | bytes 3145736 | tf_op jit(solution)/shard_map/ppermute | solution.py:30
  54.9 17.9 %collective-permute-start.9 = (bf16[1024,256]{1,0:T(8,128)(2,1)S(1)}, bf16[1024,256]{1,0:T(8,128)(2,1)S(1)}, u32[]{:S(2)}, u32[]{:S(2)}) collective-permute-start(bf16[1024,256]{1,0:T(8,128)(2,1)S(1)} %slice.117), channel_id=1, source_target_pairs={{0,8},{1,33},{2,10},{3,35},{4,12},{5,37},{6,14},{7,39},{8,16},{9,4... | collective-permute-start | bytes 1572872 | tf_op jit(solution)/shard_map/ppermute | solution.py:30
  55.3 17.4 %collective-permute-start.10 = (bf16[1024,256]{1,0:T(8,128)(2,1)S(1)}, bf16[1024,256]{1,0:T(8,128)(2,1)S(1)}, u32[]{:S(2)}, u32[]{:S(2)}) collective-permute-start(bf16[1024,256]{1,0:T(8,128)(2,1)S(1)} %slice.118), channel_id=1, source_target_pairs={{0,24},{1,97},{2,26},{3,99},{4,28},{5,101},{6,30},{7,103},{8,0},{9... | collective-permute-start | bytes 1572872 | tf_op jit(solution)/shard_map/ppermute | solution.py:30
  72.6 8.1 %collective-permute-start.15 = (bf16[512,1024]{1,0:T(8,128)(2,1)S(1)}, bf16[512,1024]{1,0:T(8,128)(2,1)S(1)}, u32[]{:S(2)}, u32[]{:S(2)}) collective-permute-start(bf16[512,1024]{1,0:T(8,128)(2,1)S(1)} %pad_maximum_fusion.3.refs_4_), channel_id=1, source_target_pairs={{0,1},{1,0},{2,3},{3,2},{4,5},{5,4},{6,7},{7,6},{8,9},{9,8},{10,11... | collective-permute-start | bytes 3145736 | tf_op jit(solution)/shard_map/ppermute | solution.py:47
  75.2 14.3 %collective-permute-start.16 = (bf16[256,1024]{1,0:T(8,128)(2,1)S(1)}, bf16[256,1024]{1,0:T(8,128)(2,1)S(1)}, u32[]{:S(2)}, u32[]{:S(2)}) collective-permute-start(bf16[256,1024]{1,0:T(8,128)(2,1)S(1)} %get-tuple-element.68), channel_id=1, source_target_pairs={{0,2},{1,3},{2,4},{3,5},{4,6},{5,7},{6,0},{7,1},{8,10},{9,11},{10,... | collective-permute-start | bytes 1572872 | tf_op jit(solution)/shard_map/ppermute | solution.py:43
  77.8 14.9 %collective-permute-start.17 = (bf16[256,1024]{1,0:T(8,128)(2,1)S(1)}, bf16[256,1024]{1,0:T(8,128)(2,1)S(1)}, u32[]{:S(2)}, u32[]{:S(2)}) collective-permute-start(bf16[256,1024]{1,0:T(8,128)(2,1)S(1)} %get-tuple-element.66), channel_id=1, source_target_pairs={{0,6},{1,7},{2,0},{3,1},{4,2},{5,3},{6,4},{7,5},{8,14},{9,15},{10,... | collective-permute-start | bytes 1572872 | tf_op jit(solution)/shard_map/ppermute | solution.py:43
  92.7 19.3 %collective-permute-start.19 = (bf16[512,1024]{1,0:T(8,128)(2,1)S(1)}, bf16[512,1024]{1,0:T(8,128)(2,1)S(1)}, u32[]{:S(2)}, u32[]{:S(2)}) collective-permute-start(bf16[512,1024]{1,0:T(8,128)(2,1)S(1)} %slice.122.refs_6_), channel_id=1, source_target_pairs={{0,1},{1,0},{2,3},{3,2},{4,5},{5,4},{6,7},{7,6},{8,9},{9,8},{10,11... | collective-permute-start | bytes 3145736 | tf_op jit(solution)/shard_map/ppermute | solution.py:47
  93.2 10.5 %collective-permute-start.21 = (bf16[512,256]{1,0:T(8,128)(2,1)S(1)}, bf16[512,256]{1,0:T(8,128)(2,1)S(1)}, u32[]{:S(2)}, u32[]{:S(2)}) collective-permute-start(bf16[512,256]{1,0:T(8,128)(2,1)S(1)} %shard_map.132.kv_ref), channel_id=1, source_target_pairs={{0,64},{8,72},{16,80},{24,88},{32,96},{40,104},{48,112},{56,120},{... | collective-permute-start | bytes 786440 | tf_op jit(solution)/shard_map/ppermute | solution.py:17
  96.4 16.0 %collective-permute-start.18 = (bf16[512,1024]{1,0:T(8,128)(2,1)S(1)}, bf16[512,1024]{1,0:T(8,128)(2,1)S(1)}, u32[]{:S(2)}, u32[]{:S(2)}) collective-permute-start(bf16[512,1024]{1,0:T(8,128)(2,1)S(1)} %slice.121.refs_2_), channel_id=1, source_target_pairs={{0,1},{1,0},{2,3},{3,2},{4,5},{5,4},{6,7},{7,6},{8,9},{9,8},{10,11... | collective-permute-start | bytes 3145736 | tf_op jit(solution)/shard_map/ppermute | solution.py:47
  96.8 16.6 %collective-permute-start.20 = (bf16[512,1024]{1,0:T(8,128)(2,1)S(1)}, bf16[512,1024]{1,0:T(8,128)(2,1)S(1)}, u32[]{:S(2)}, u32[]{:S(2)}) collective-permute-start(bf16[512,1024]{1,0:T(8,128)(2,1)S(1)} %constant_dynamic-update-slice_fusion.refs_4_), channel_id=1, source_target_pairs={{0,1},{1,0},{2,3},{3,2},{4,5},{5,4},{6,7},{7,6},{8,9},{9,8},{10,11... | collective-permute-start | bytes 3145736 | tf_op jit(solution)/shard_map/ppermute | solution.py:47
  109.0 11.0 %collective-permute-start.22 = (bf16[512,256]{1,0:T(8,128)(2,1)S(1)}, bf16[512,256]{1,0:T(8,128)(2,1)S(1)}, u32[]{:S(2)}, u32[]{:S(2)}) collective-permute-start(bf16[512,256]{1,0:T(8,128)(2,1)S(1)} %get-tuple-element.56.grad_ref), channel_id=1, source_target_pairs={{0,64},{8,72},{16,80},{24,88},{32,96},{40,104},{48,112},{56,120},{... | collective-permute-start | bytes 786440 | tf_op jit(solution)/shard_map/ppermute | solution.py:17
  127.2 14.9 %collective-permute-start.25 = (bf16[2048,256]{1,0:T(8,128)(2,1)S(1)}, bf16[2048,256]{1,0:T(8,128)(2,1)S(1)}, u32[]{:S(2)}, u32[]{:S(2)}) collective-permute-start(bf16[2048,256]{1,0:T(8,128)(2,1)S(1)} %get-tuple-element.63), channel_id=1, source_target_pairs={{0,24},{1,97},{2,26},{3,99},{4,28},{5,101},{6,30},{7,103},{8,0},{9... | collective-permute-start | bytes 3145736 | tf_op jit(solution)/shard_map/ppermute | solution.py:30
  128.7 27.2 %collective-permute-start.24 = (bf16[2048,256]{1,0:T(8,128)(2,1)S(1)}, bf16[2048,256]{1,0:T(8,128)(2,1)S(1)}, u32[]{:S(2)}, u32[]{:S(2)}) collective-permute-start(bf16[2048,256]{1,0:T(8,128)(2,1)S(1)} %get-tuple-element.62), channel_id=1, source_target_pairs={{0,8},{1,33},{2,10},{3,35},{4,12},{5,37},{6,14},{7,39},{8,16},{9,4... | collective-permute-start | bytes 3145736 | tf_op jit(solution)/shard_map/ppermute | solution.py:30
  129.3 26.6 %collective-permute-start.23 = (bf16[2048,256]{1,0:T(8,128)(2,1)S(1)}, bf16[2048,256]{1,0:T(8,128)(2,1)S(1)}, u32[]{:S(2)}, u32[]{:S(2)}) collective-permute-start(bf16[2048,256]{1,0:T(8,128)(2,1)S(1)} %get-tuple-element.61), channel_id=1, source_target_pairs={{0,16},{1,65},{2,18},{3,67},{4,20},{5,69},{6,22},{7,71},{8,24},{9,... | collective-permute-start | bytes 3145736 | tf_op jit(solution)/shard_map/ppermute | solution.py:30
  158.6 9.4 %collective-permute-start.26 = (bf16[512,256]{1,0:T(8,128)(2,1)S(1)}, bf16[512,256]{1,0:T(8,128)(2,1)S(1)}, u32[]{:S(2)}, u32[]{:S(2)}) collective-permute-start(bf16[512,256]{1,0:T(8,128)(2,1)S(1)} %get-tuple-element.70), channel_id=1, source_target_pairs={{0,64},{1,17},{2,66},{3,19},{4,68},{5,21},{6,70},{7,23},{8,72},{9,... | collective-permute-start | bytes 786440 | tf_op jit(solution)/shard_map/ppermute | solution.py:30
  (15 other events, 85.3 us)

commit v7 on v6

--- a/solution.py
+++ b/solution.py
@@ -434,35 +434,21 @@
     ratio = jnp.tanh(gate)
     numbers, far_own, near_own = route(tiles, image_slot, image)
 
-    half = image.shape[1] // 2
-
     def opposite(after, before, move):
-        middle = after.shape[0] // 2
-        return [move(after[:middle], 1), move(before[middle:], 3)]
+        half = after.shape[0] // 2
+        return [move(after[:half], 1), move(before[half:], 3)]
 
     shard = lay(numbers, key_weight_matrix, value_weight_matrix)
     far_x = [along_x(far_own, 1), along_x(far_own, 3)]
     shard = jnp.concatenate(gathered(shard, inner), axis=0)
-    ahead = [
-        jnp.concatenate([near_own[:half], near_own], axis=0),
-        jnp.concatenate([near_own[half:], near_own], axis=0),
-    ]
-    shard, *ahead = lax.optimization_barrier((shard, *ahead))
-    far_other, near_other = other_core(far_own), other_core(near_own)
-    shard, far_other, near_other, *far_x = lax.optimization_barrier(
-        (shard, far_other, near_other, *far_x)
-    )
-    ahead = [
-        lax.dynamic_update_slice_in_dim(ahead[0], far_x[0][:half], 0, 0),
-        lax.dynamic_update_slice_in_dim(ahead[1], far_x[1][half:], 0, 0),
-    ]
-    ahead = [along_x(ahead[0], 1), along_x(ahead[1], 3)]
+    shard, *far_x = lax.optimization_barrier((shard, *far_x))
+    far_halves = opposite(*far_x, along_x)
     pieces = [outer(shard, 1), outer(shard, 3)]
+    near_own, *blocks = lax.optimization_barrier((near_own, *far_halves, *pieces))
+    far_halves, pieces = blocks[:2], blocks[2:]
+    near_x = [along_x(near_own, 1), along_x(near_own, 3)]
     weights = assemble(numbers, [shard, *pieces, *opposite(*pieces, outer)])
-    weights, *far_x = lax.optimization_barrier((weights, *far_x))
-    far_halves = [block[:half] for block in ahead]
-    near_x = [block[half:] for block in ahead]
-    near_halves = opposite(*near_x, along_x)
+    weights, *far_blocks = lax.optimization_barrier((weights, *far_x, *far_halves))
 
     def other_cores(*blocks):
         return [other_core(block) for block in blocks]
@@ -480,18 +466,22 @@
         return total
 
     shared = (numbers, ratio, query, cotangent)
-    blocks = [*far_x, jnp.concatenate(far_halves, axis=0)]
-    far_feats = paired(far_own, far_other, *blocks, *other_cores(*blocks))
+    after, before, *halves = far_blocks
+    blocks = [after, before, jnp.concatenate(halves, axis=0)]
+    far_feats = paired(far_own, other_core(far_own), *blocks, *other_cores(*blocks))
     far_total = project(far_feats)
     far_key_value = finish(far_total, key_gain)
     away = along_z(far_key_value, RING // 2)
-    _, *blocks = lax.optimization_barrier((far_key_value, *near_x, *near_halves))
-    near_x, near_halves = blocks[:2], blocks[2:]
+    _, near_own, *near_x = lax.optimization_barrier((far_key_value, near_own, *near_x))
+    near_halves = opposite(*near_x, along_x)
+    near_others = other_cores(*near_x)
     *earlier, far_grad = attend(FAR, *shared, far_key_value, away, query_gain, ())
     back = along_z(far_grad, RING // 2)
 
+    _, *near_halves = lax.optimization_barrier((far_grad, *near_halves))
     blocks = [*near_x, jnp.concatenate(near_halves, axis=0)]
-    near_feats = paired(near_own, near_other, *blocks, *other_cores(*blocks))
+    near_others.append(other_core(blocks[2]))
+    near_feats = paired(near_own, other_core(near_own), *blocks, *near_others)
     near_total = project(near_feats)
     near_key_value = finish(near_total, key_gain)
     context, d_query, near_grad = attend(

time: 171 us -> 156 us (0.912)
  waiting for transfers between devices: 94 us -> 83.8 us
  starting transfers between devices: 36.9 us -> 34 us
    ppermute x13, waiting for transfers between devices: 56.7 us -> 47.4 us  [by_core(): return lax.ppermute(x, ('dp', 'tensor'), pairs)]
    ppermute x2, waiting for transfers between devices: 5.62 us -> 0.01 us  [along_z(): return lax.ppermute(x, 'dp', pairs)]
    ppermute x6 -> x8, waiting for transfers between devices: 31.6 us -> 34.4 us  [along_x(): return lax.ppermute(x, 'tensor', pairs)]
    ppermute x13, starting transfers between devices: 22 us -> 19.3 us  [by_core(): return lax.ppermute(x, ('dp', 'tensor'), pairs)]
    ppermute x8, waiting for transfers between devices: 0.02 us -> 1.97 us  [other_core(): return lax.ppermute(x, 'tensor', [(i, i ^ 1) for i in range(2 * RING)])]
    ppermute x6 -> x8, starting transfers between devices: 6.81 us -> 8.38 us  [along_x(): return lax.ppermute(x, 'tensor', pairs)]
  transfers between devices with their start and end apart: 29 -> 31, of which waited for: 16 -> 19; matrix products, arithmetic and copies ran while one was open for 6% -> 5% of each run, Pallas kernels for 8% -> 9%
where the time goes in v7:
time: 156 us
  waiting for transfers between devices  83.8 us (54%)
  starting transfers between devices  34 us (22%)
  Pallas kernels  24.3 us (16%)
  matrix products  7.22 us (5%)
  local copies, waits for them, and re-layouts  3.73 us (2%)
  between operations  1.79 us (1%)
    ppermute x13, waiting for transfers between devices, by_core(): return lax.ppermute(x, ('dp', 'tensor'), pairs)  47.4 us
    ppermute x8, waiting for transfers between devices, along_x(): return lax.ppermute(x, 'tensor', pairs)  34.4 us
    ppermute x13, starting transfers between devices, by_core(): return lax.ppermute(x, ('dp', 'tensor'), pairs)  19.3 us
    pallas_call x2, Pallas kernels, attend(): pl.pallas_call(functools.partial(attend_kernel, heads, base), grid_spec=p...  10.6 us
    ppermute x8, starting transfers between devices, along_x(): return lax.ppermute(x, 'tensor', pairs)  8.38 us
    dot_general x16, matrix products, matmul(): lax.dot_general(a, b, (contract, ((), ())), preferred_element_type=jnp.fl...  7.22 us
    ppermute x2, starting transfers between devices, along_z(): return lax.ppermute(x, 'dp', pairs)  4.73 us
    pallas_call x1, Pallas kernels, product(): pl.pallas_call(product_kernel, in_specs=[SMEM] + [VMEM] * (len(feats) + 2...  3.81 us
  transfers between devices with their start and end apart: 31, of which 19 were waited for; matrix products, arithmetic and copies ran while one was open for 5% of the time, Pallas kernels for 9%

profile of v7, /device:TPU:4, one launch (start us, length us, event | category | flops | bytes accessed | tf_op | source)
XLA Modules:
  0.0 155.5 jit_solution(16451809895778289619)
XLA Ops:
  0.6 3.6 %shard_map.129 = (s32[10]{0:T(128)}, bf16[512,1024]{1,0:T(8,128)(2,1)}, bf16[512,1024]{1,0:T(8,128)(2,1)}) custom-call(s32[32]{0:T(128)} %tiles.1, s32[32]{0:T(128)} %slots.1, bf16[2,512,1024]{2,1,0:T(8,128)(2,1)} %image_ref.1), custom_call_target="tpu_custom_call" | custom-call | bytes 4194304 | tf_op jit(solution)/shard_map/pallas_call | solution.py:124
  9.4 4.1 %collective-permute-start.2 = (bf16[512,256]{1,0:T(8,128)(2,1)S(1)}, bf16[512,256]{1,0:T(8,128)(2,1)S(1)}, u32[]{:S(2)}, u32[]{:S(2)}) collective-permute-start(bf16[512,256]{1,0:T(8,128)(2,1)S(1)} %shard_map.130), channel_id=1, source_target_pairs={{0,96},{1,25},{2,98},{3,27},{4,100},{5,29},{6,102},{7,31},{8,104},... | collective-permute-start | bytes 786440 | tf_op jit(solution)/shard_map/ppermute | solution.py:30
  14.8 5.4 %collective-permute-done.2 = bf16[512,256]{1,0:T(8,128)(2,1)S(1)} collective-permute-done((bf16[512,256]{1,0:T(8,128)(2,1)S(1)}, bf16[512,256]{1,0:T(8,128)(2,1)S(1)}, u32[]{:S(2)}, u32[]{:S(2)}) %collective-permute-start.2) | collective-permute-done | bytes 262176 | tf_op jit(solution)/shard_map/ppermute | solution.py:30
  21.5 2.4 %collective-permute-done = bf16[512,256]{1,0:T(8,128)(2,1)S(1)} collective-permute-done((bf16[512,256]{1,0:T(8,128)(2,1)S(1)}, bf16[512,256]{1,0:T(8,128)(2,1)S(1)}, u32[]{:S(2)}, u32[]{:S(2)}) %collective-permute-start) | collective-permute-done | bytes 262176 | tf_op jit(solution)/shard_map/ppermute | solution.py:30
  24.0 5.4 %collective-permute-done.3.refs_2_ = bf16[512,1024]{1,0:T(8,128)(2,1)S(1)} collective-permute-done((bf16[512,1024]{1,0:T(8,128)(2,1)}, bf16[512,1024]{1,0:T(8,128)(2,1)S(1)}, u32[]{:S(2)}, u32[]{:S(2)}) %collective-permute-start.3) | collective-permute-done | bytes 1048608 | tf_op jit(solution)/shard_map/ppermute | solution.py:43
  31.9 1.7 %collective-permute-start.8 = (bf16[2048,256]{1,0:T(8,128)(2,1)S(1)}, bf16[2048,256]{1,0:T(8,128)(2,1)S(1)}, u32[]{:S(2)}, u32[]{:S(2)}) collective-permute-start(bf16[2048,256]{1,0:T(8,128)(2,1)S(1)} %pad_maximum_fusion.refs_0_), channel_id=1, source_target_pairs={{0,24},{1,97},{2,26},{3,99},{4,28},{5,101},{6,30},{7,103},{8,0},{9... | collective-permute-start | bytes 3145736 | tf_op jit(solution)/shard_map/ppermute | solution.py:30
  35.8 10.9 %collective-permute-done.5 = bf16[256,1024]{1,0:T(8,128)(2,1)S(1)} collective-permute-done((bf16[256,1024]{1,0:T(8,128)(2,1)S(1)}, bf16[256,1024]{1,0:T(8,128)(2,1)S(1)}, u32[]{:S(2)}, u32[]{:S(2)}) %collective-permute-start.5) | collective-permute-done | bytes 524320 | tf_op jit(solution)/shard_map/ppermute | solution.py:43
  49.9 1.7 %collective-permute-start.10 = (bf16[1024,256]{1,0:T(8,128)(2,1)S(1)}, bf16[1024,256]{1,0:T(8,128)(2,1)S(1)}, u32[]{:S(2)}, u32[]{:S(2)}) collective-permute-start(bf16[1024,256]{1,0:T(8,128)(2,1)S(1)} %slice.74), channel_id=1, source_target_pairs={{0,24},{1,97},{2,26},{3,99},{4,28},{5,101},{6,30},{7,103},{8,0},{9... | collective-permute-start | bytes 1572872 | tf_op jit(solution)/shard_map/ppermute | solution.py:30
  52.4 1.9 %collective-permute-start.15 = (bf16[512,1024]{1,0:T(8,128)(2,1)S(1)}, bf16[512,1024]{1,0:T(8,128)(2,1)S(1)}, u32[]{:S(2)}, u32[]{:S(2)}) collective-permute-start(bf16[512,1024]{1,0:T(8,128)(2,1)S(1)} %copy-done), channel_id=1, source_target_pairs={{0,2},{1,3},{2,4},{3,5},{4,6},{5,7},{6,0},{7,1},{8,10},{9,11},{10,... | collective-permute-start | bytes 3145736 | tf_op jit(solution)/shard_map/ppermute | solution.py:43
  54.5 4.2 %collective-permute-done.9.refs_3_ = bf16[1024,256]{1,0:T(8,128)(2,1)S(1)} collective-permute-done((bf16[1024,256]{1,0:T(8,128)(2,1)S(1)}, bf16[1024,256]{1,0:T(8,128)(2,1)S(1)}, u32[]{:S(2)}, u32[]{:S(2)}) %collective-permute-start.9) | collective-permute-done | bytes 524320 | tf_op jit(solution)/shard_map/ppermute | solution.py:30
  66.9 2.5 %collective-permute-start.20 = (bf16[512,256]{1,0:T(8,128)(2,1)S(1)}, bf16[512,256]{1,0:T(8,128)(2,1)S(1)}, u32[]{:S(2)}, u32[]{:S(2)}) collective-permute-start(bf16[512,256]{1,0:T(8,128)(2,1)S(1)} %shard_map.132.kv_ref), channel_id=1, source_target_pairs={{0,64},{8,72},{16,80},{24,88},{32,96},{40,104},{48,112},{56,120},{... | collective-permute-start | bytes 786440 | tf_op jit(solution)/shard_map/ppermute | solution.py:17
  69.3 8.7 %collective-permute-done.15.refs_2_ = bf16[512,1024]{1,0:T(8,128)(2,1)S(1)} collective-permute-done((bf16[512,1024]{1,0:T(8,128)(2,1)S(1)}, bf16[512,1024]{1,0:T(8,128)(2,1)S(1)}, u32[]{:S(2)}, u32[]{:S(2)}) %collective-permute-start.15) | collective-permute-done | bytes 1048608 | tf_op jit(solution)/shard_map/ppermute | solution.py:43
  83.4 5.3 %shard_map.133 = (bf16[2,128,1024]{2,1,0:T(8,128)(2,1)}, bf16[2,128,1024]{2,1,0:T(8,128)(2,1)}, bf16[512,256]{1,0:T(8,128)(2,1)S(1)}) custom-call(s32[10]{0:T(128)S(1)} %copy-done.5, f32[1]{0:T(128)S(6)} %tanh.3.ratio_ref, bf16[2,128,1024]{2,1,0:T(8,128)(2,1)S(1)} %copy-done.7, bf16[2,128,1024]{2,1,0:T(8,128)(2,1)S(1)} %copy-done.8, ...), custom_call_target="tpu_custom_call" | custom-call | flops 939524096 | bytes 1441792 | tf_op jit(solution)/shard_map/pallas_call | solution.py:387
  88.7 5.5 %collective-permute-done.21 = bf16[256,1024]{1,0:T(8,128)(2,1)S(1)} collective-permute-done((bf16[256,1024]{1,0:T(8,128)(2,1)S(1)}, bf16[256,1024]{1,0:T(8,128)(2,1)S(1)}, u32[]{:S(2)}, u32[]{:S(2)}) %collective-permute-start.21) | collective-permute-done | bytes 524320 | tf_op jit(solution)/shard_map/ppermute | solution.py:43
  94.2 2.3 %collective-permute-start.24 = (bf16[512,256]{1,0:T(8,128)(2,1)S(1)}, bf16[512,256]{1,0:T(8,128)(2,1)S(1)}, u32[]{:S(2)}, u32[]{:S(2)}) collective-permute-start(bf16[512,256]{1,0:T(8,128)(2,1)S(1)} %get-tuple-element.56.grad_ref), channel_id=1, source_target_pairs={{0,64},{8,72},{16,80},{24,88},{32,96},{40,104},{48,112},{56,120},{... | collective-permute-start | bytes 786440 | tf_op jit(solution)/shard_map/ppermute | solution.py:17
  99.9 5.3 %shard_map.135 = (bf16[2,128,1024]{2,1,0:T(8,128)(2,1)}, bf16[2,128,1024]{2,1,0:T(8,128)(2,1)}, bf16[512,256]{1,0:T(8,128)(2,1)S(1)}) custom-call(s32[10]{0:T(128)S(1)} %copy-done.5, f32[1]{0:T(128)S(6)} %tanh.3.ratio_ref, bf16[2,128,1024]{2,1,0:T(8,128)(2,1)S(1)} %copy-done.7, ...), custom_call_target="tpu_custom_call", output_to_operand_aliasing={{0}: (7, {}), {1}: (8, {})} | custom-call | flops 939524096 | bytes 1441792 | tf_op jit(solution)/shard_map/pallas_call | solution.py:387
  106.7 2.6 %shard_map.138.refs_9_ = f32[8192,256]{1,0:T(8,128)S(1)} custom-call(bf16[512,1024]{1,0:T(8,128)(2,1)S(1)} %copy-done.1, bf16[512,1024]{1,0:T(8,128)(2,1)S(1)} %collective-permute-done.11.refs_1_, bf16[512,1024]{1,0:T(8,128)(2,1)S(1)} %collective-permute-done.3.refs_2_, bf16[512,1024]{1,0:T(8,128)(2,1)S(1)} %collective-permute-done.12.refs_3_, ...), custom_call_target="tpu_custom_call" | custom-call | flops 2147483648 | bytes 8388608 | tf_op jit(solution)/shard_map/pallas_call | solution.py:253
  109.3 3.8 %shard_map.139 = (bf16[2048,256]{1,0:T(8,128)(2,1)S(1)}, bf16[2048,256]{1,0:T(8,128)(2,1)S(1)}, bf16[2048,256]{1,0:T(8,128)(2,1)S(1)}, bf16[2048,256]{1,0:T(8,128)(2,1)S(1)}) custom-call(s32[10]{0:T(128)S(1)} %copy-done.5, bf16[512,1024]{1,0:T(8,128)(2,1)S(1)} %copy-done, bf16[512,1024]{1,0:T(8,128)(2,1)S(1)} %collective-permute-done.17.refs_1_, ...), custom_call_target="tpu_custom_call" | custom-call | flops 2147483648 | bytes 8388608 | tf_op jit(solution)/shard_map/pallas_call | solution.py:294
  113.1 1.7 %collective-permute-start.27 = (bf16[2048,256]{1,0:T(8,128)(2,1)S(1)}, bf16[2048,256]{1,0:T(8,128)(2,1)S(1)}, u32[]{:S(2)}, u32[]{:S(2)}) collective-permute-start(bf16[2048,256]{1,0:T(8,128)(2,1)S(1)} %get-tuple-element.69), channel_id=1, source_target_pairs={{0,24},{1,97},{2,26},{3,99},{4,28},{5,101},{6,30},{7,103},{8,0},{9... | collective-permute-start | bytes 3145736 | tf_op jit(solution)/shard_map/ppermute | solution.py:30
  115.2 1.7 %collective-permute-start.25 = (bf16[2048,256]{1,0:T(8,128)(2,1)S(1)}, bf16[2048,256]{1,0:T(8,128)(2,1)S(1)}, u32[]{:S(2)}, u32[]{:S(2)}) collective-permute-start(bf16[2048,256]{1,0:T(8,128)(2,1)S(1)} %get-tuple-element.67), channel_id=1, source_target_pairs={{0,16},{1,65},{2,18},{3,67},{4,20},{5,69},{6,22},{7,71},{8,24},{9,... | collective-permute-start | bytes 3145736 | tf_op jit(solution)/shard_map/ppermute | solution.py:30
  116.9 11.1 %collective-permute-done.27 = bf16[2048,256]{1,0:T(8,128)(2,1)S(1)} collective-permute-done((bf16[2048,256]{1,0:T(8,128)(2,1)S(1)}, bf16[2048,256]{1,0:T(8,128)(2,1)S(1)}, u32[]{:S(2)}, u32[]{:S(2)}) %collective-permute-start.27) | collective-permute-done | bytes 1048608 | tf_op jit(solution)/shard_map/ppermute | solution.py:30
  128.0 14.1 %collective-permute-done.26 = bf16[2048,256]{1,0:T(8,128)(2,1)S(1)} collective-permute-done((bf16[2048,256]{1,0:T(8,128)(2,1)S(1)}, bf16[2048,256]{1,0:T(8,128)(2,1)S(1)}, u32[]{:S(2)}, u32[]{:S(2)}) %collective-permute-start.26) | collective-permute-done | bytes 1048608 | tf_op jit(solution)/shard_map/ppermute | solution.py:30
  146.2 2.9 %collective-permute-done.30 = bf16[512,256]{1,0:T(8,128)(2,1)S(1)} collective-permute-done((bf16[512,256]{1,0:T(8,128)(2,1)S(1)}, bf16[512,256]{1,0:T(8,128)(2,1)S(1)}, u32[]{:S(2)}, u32[]{:S(2)}) %collective-permute-start.30) | collective-permute-done | bytes 262176 | tf_op jit(solution)/shard_map/ppermute | solution.py:30
  149.1 5.5 %collective-permute-done.29 = bf16[512,256]{1,0:T(8,128)(2,1)S(1)} collective-permute-done((bf16[512,256]{1,0:T(8,128)(2,1)S(1)}, bf16[512,256]{1,0:T(8,128)(2,1)S(1)}, u32[]{:S(2)}, u32[]{:S(2)}) %collective-permute-start.29) | collective-permute-done | bytes 262176 | tf_op jit(solution)/shard_map/ppermute | solution.py:30
  (100 shorter events, 39.5 us)
Async XLA Ops:
  4.3 25.2 %collective-permute-start.3 = (bf16[512,1024]{1,0:T(8,128)(2,1)}, bf16[512,1024]{1,0:T(8,128)(2,1)S(1)}, u32[]{:S(2)}, u32[]{:S(2)}) collective-permute-start(bf16[512,1024]{1,0:T(8,128)(2,1)} %get-tuple-element.38.refs_0_), channel_id=1, source_target_pairs={{0,2},{1,3},{2,4},{3,5},{4,6},{5,7},{6,0},{7,1},{8,10},{9,11},{10,... | collective-permute-start | bytes 3145736 | tf_op jit(solution)/shard_map/ppermute | solution.py:43
  5.5 24.8 %collective-permute-start.4 = (bf16[512,1024]{1,0:T(8,128)(2,1)}, bf16[512,1024]{1,0:T(8,128)(2,1)S(1)}, u32[]{:S(2)}, u32[]{:S(2)}) collective-permute-start(bf16[512,1024]{1,0:T(8,128)(2,1)} %get-tuple-element.38.refs_0_), channel_id=1, source_target_pairs={{0,6},{1,7},{2,0},{3,1},{4,2},{5,3},{6,4},{7,5},{8,14},{9,15},{10,... | collective-permute-start | bytes 3145736 | tf_op jit(solution)/shard_map/ppermute | solution.py:43
  9.4 10.8 %collective-permute-start.2 = (bf16[512,256]{1,0:T(8,128)(2,1)S(1)}, bf16[512,256]{1,0:T(8,128)(2,1)S(1)}, u32[]{:S(2)}, u32[]{:S(2)}) collective-permute-start(bf16[512,256]{1,0:T(8,128)(2,1)S(1)} %shard_map.130), channel_id=1, source_target_pairs={{0,96},{1,25},{2,98},{3,27},{4,100},{5,29},{6,102},{7,31},{8,104},... | collective-permute-start | bytes 786440 | tf_op jit(solution)/shard_map/ppermute | solution.py:30
  13.5 10.4 %collective-permute-start = (bf16[512,256]{1,0:T(8,128)(2,1)S(1)}, bf16[512,256]{1,0:T(8,128)(2,1)S(1)}, u32[]{:S(2)}, u32[]{:S(2)}) collective-permute-start(bf16[512,256]{1,0:T(8,128)(2,1)S(1)} %shard_map.130), channel_id=1, source_target_pairs={{0,32},{1,9},{2,34},{3,11},{4,36},{5,13},{6,38},{7,15},{8,40},{9,1... | collective-permute-start | bytes 786440 | tf_op jit(solution)/shard_map/ppermute | solution.py:30
  30.4 17.9 %collective-permute-start.7 = (bf16[2048,256]{1,0:T(8,128)(2,1)S(1)}, bf16[2048,256]{1,0:T(8,128)(2,1)S(1)}, u32[]{:S(2)}, u32[]{:S(2)}) collective-permute-start(bf16[2048,256]{1,0:T(8,128)(2,1)S(1)} %pad_maximum_fusion.refs_0_), channel_id=1, source_target_pairs={{0,8},{1,33},{2,10},{3,35},{4,12},{5,37},{6,14},{7,39},{8,16},{9,4... | collective-permute-start | bytes 3145736 | tf_op jit(solution)/shard_map/ppermute | solution.py:30
  31.9 16.3 %collective-permute-start.8 = (bf16[2048,256]{1,0:T(8,128)(2,1)S(1)}, bf16[2048,256]{1,0:T(8,128)(2,1)S(1)}, u32[]{:S(2)}, u32[]{:S(2)}) collective-permute-start(bf16[2048,256]{1,0:T(8,128)(2,1)S(1)} %pad_maximum_fusion.refs_0_), channel_id=1, source_target_pairs={{0,24},{1,97},{2,26},{3,99},{4,28},{5,101},{6,30},{7,103},{8,0},{9... | collective-permute-start | bytes 3145736 | tf_op jit(solution)/shard_map/ppermute | solution.py:30
  33.6 13.1 %collective-permute-start.5 = (bf16[256,1024]{1,0:T(8,128)(2,1)S(1)}, bf16[256,1024]{1,0:T(8,128)(2,1)S(1)}, u32[]{:S(2)}, u32[]{:S(2)}) collective-permute-start(bf16[256,1024]{1,0:T(8,128)(2,1)S(1)} %slice.71), channel_id=1, source_target_pairs={{0,2},{1,3},{2,4},{3,5},{4,6},{5,7},{6,0},{7,1},{8,10},{9,11},{10,... | collective-permute-start | bytes 1572872 | tf_op jit(solution)/shard_map/ppermute | solution.py:43
  35.3 12.9 %collective-permute-start.6 = (bf16[256,1024]{1,0:T(8,128)(2,1)S(1)}, bf16[256,1024]{1,0:T(8,128)(2,1)S(1)}, u32[]{:S(2)}, u32[]{:S(2)}) collective-permute-start(bf16[256,1024]{1,0:T(8,128)(2,1)S(1)} %slice.72), channel_id=1, source_target_pairs={{0,6},{1,7},{2,0},{3,1},{4,2},{5,3},{6,4},{7,5},{8,14},{9,15},{10,... | collective-permute-start | bytes 1572872 | tf_op jit(solution)/shard_map/ppermute | solution.py:43
  48.3 10.5 %collective-permute-start.9 = (bf16[1024,256]{1,0:T(8,128)(2,1)S(1)}, bf16[1024,256]{1,0:T(8,128)(2,1)S(1)}, u32[]{:S(2)}, u32[]{:S(2)}) collective-permute-start(bf16[1024,256]{1,0:T(8,128)(2,1)S(1)} %slice.73), channel_id=1, source_target_pairs={{0,8},{1,33},{2,10},{3,35},{4,12},{5,37},{6,14},{7,39},{8,16},{9,4... | collective-permute-start | bytes 1572872 | tf_op jit(solution)/shard_map/ppermute | solution.py:30
  51.7 9.9 %collective-permute-start.11 = (bf16[512,1024]{1,0:T(8,128)(2,1)S(1)}, bf16[512,1024]{1,0:T(8,128)(2,1)S(1)}, u32[]{:S(2)}, u32[]{:S(2)}) collective-permute-start(bf16[512,1024]{1,0:T(8,128)(2,1)S(1)} %copy-done.1), channel_id=1, source_target_pairs={{0,1},{1,0},{2,3},{3,2},{4,5},{5,4},{6,7},{7,6},{8,9},{9,8},{10,11... | collective-permute-start | bytes 3145736 | tf_op jit(solution)/shard_map/ppermute | solution.py:47
  52.4 25.6 %collective-permute-start.15 = (bf16[512,1024]{1,0:T(8,128)(2,1)S(1)}, bf16[512,1024]{1,0:T(8,128)(2,1)S(1)}, u32[]{:S(2)}, u32[]{:S(2)}) collective-permute-start(bf16[512,1024]{1,0:T(8,128)(2,1)S(1)} %copy-done), channel_id=1, source_target_pairs={{0,2},{1,3},{2,4},{3,5},{4,6},{5,7},{6,0},{7,1},{8,10},{9,11},{10,... | collective-permute-start | bytes 3145736 | tf_op jit(solution)/shard_map/ppermute | solution.py:43
  54.3 25.3 %collective-permute-start.16 = (bf16[512,1024]{1,0:T(8,128)(2,1)S(1)}, bf16[512,1024]{1,0:T(8,128)(2,1)S(1)}, u32[]{:S(2)}, u32[]{:S(2)}) collective-permute-start(bf16[512,1024]{1,0:T(8,128)(2,1)S(1)} %copy-done), channel_id=1, source_target_pairs={{0,6},{1,7},{2,0},{3,1},{4,2},{5,3},{6,4},{7,5},{8,14},{9,15},{10,... | collective-permute-start | bytes 3145736 | tf_op jit(solution)/shard_map/ppermute | solution.py:43
  66.9 16.4 %collective-permute-start.20 = (bf16[512,256]{1,0:T(8,128)(2,1)S(1)}, bf16[512,256]{1,0:T(8,128)(2,1)S(1)}, u32[]{:S(2)}, u32[]{:S(2)}) collective-permute-start(bf16[512,256]{1,0:T(8,128)(2,1)S(1)} %shard_map.132.kv_ref), channel_id=1, source_target_pairs={{0,64},{8,72},{16,80},{24,88},{32,96},{40,104},{48,112},{56,120},{... | collective-permute-start | bytes 786440 | tf_op jit(solution)/shard_map/ppermute | solution.py:17
  79.6 17.5 %collective-permute-start.19 = (bf16[512,1024]{1,0:T(8,128)(2,1)S(1)}, bf16[512,1024]{1,0:T(8,128)(2,1)S(1)}, u32[]{:S(2)}, u32[]{:S(2)}) collective-permute-start(bf16[512,1024]{1,0:T(8,128)(2,1)S(1)} %collective-permute-done.16.refs_6_), channel_id=1, source_target_pairs={{0,1},{1,0},{2,3},{3,2},{4,5},{5,4},{6,7},{7,6},{8,9},{9,8},{10,11... | collective-permute-start | bytes 3145736 | tf_op jit(solution)/shard_map/ppermute | solution.py:47
  79.7 17.9 %collective-permute-start.18 = (bf16[512,1024]{1,0:T(8,128)(2,1)S(1)}, bf16[512,1024]{1,0:T(8,128)(2,1)S(1)}, u32[]{:S(2)}, u32[]{:S(2)}) collective-permute-start(bf16[512,1024]{1,0:T(8,128)(2,1)S(1)} %collective-permute-done.15.refs_2_), channel_id=1, source_target_pairs={{0,1},{1,0},{2,3},{3,2},{4,5},{5,4},{6,7},{7,6},{8,9},{9,8},{10,11... | collective-permute-start | bytes 3145736 | tf_op jit(solution)/shard_map/ppermute | solution.py:47
  80.3 13.9 %collective-permute-start.21 = (bf16[256,1024]{1,0:T(8,128)(2,1)S(1)}, bf16[256,1024]{1,0:T(8,128)(2,1)S(1)}, u32[]{:S(2)}, u32[]{:S(2)}) collective-permute-start(bf16[256,1024]{1,0:T(8,128)(2,1)S(1)} %slice.83), channel_id=1, source_target_pairs={{0,2},{1,3},{2,4},{3,5},{4,6},{5,7},{6,0},{7,1},{8,10},{9,11},{10,... | collective-permute-start | bytes 1572872 | tf_op jit(solution)/shard_map/ppermute | solution.py:43
  81.9 14.6 %collective-permute-start.22 = (bf16[256,1024]{1,0:T(8,128)(2,1)S(1)}, bf16[256,1024]{1,0:T(8,128)(2,1)S(1)}, u32[]{:S(2)}, u32[]{:S(2)}) collective-permute-start(bf16[256,1024]{1,0:T(8,128)(2,1)S(1)} %slice.84), channel_id=1, source_target_pairs={{0,6},{1,7},{2,0},{3,1},{4,2},{5,3},{6,4},{7,5},{8,14},{9,15},{10,... | collective-permute-start | bytes 1572872 | tf_op jit(solution)/shard_map/ppermute | solution.py:43
  83.3 14.8 %collective-permute-start.17 = (bf16[512,1024]{1,0:T(8,128)(2,1)S(1)}, bf16[512,1024]{1,0:T(8,128)(2,1)S(1)}, u32[]{:S(2)}, u32[]{:S(2)}) collective-permute-start(bf16[512,1024]{1,0:T(8,128)(2,1)S(1)} %copy-done), channel_id=1, source_target_pairs={{0,1},{1,0},{2,3},{3,2},{4,5},{5,4},{6,7},{7,6},{8,9},{9,8},{10,11... | collective-permute-start | bytes 3145736 | tf_op jit(solution)/shard_map/ppermute | solution.py:47
  94.2 11.8 %collective-permute-start.24 = (bf16[512,256]{1,0:T(8,128)(2,1)S(1)}, bf16[512,256]{1,0:T(8,128)(2,1)S(1)}, u32[]{:S(2)}, u32[]{:S(2)}) collective-permute-start(bf16[512,256]{1,0:T(8,128)(2,1)S(1)} %get-tuple-element.56.grad_ref), channel_id=1, source_target_pairs={{0,64},{8,72},{16,80},{24,88},{32,96},{40,104},{48,112},{56,120},{... | collective-permute-start | bytes 786440 | tf_op jit(solution)/shard_map/ppermute | solution.py:17
  113.1 14.9 %collective-permute-start.27 = (bf16[2048,256]{1,0:T(8,128)(2,1)S(1)}, bf16[2048,256]{1,0:T(8,128)(2,1)S(1)}, u32[]{:S(2)}, u32[]{:S(2)}) collective-permute-start(bf16[2048,256]{1,0:T(8,128)(2,1)S(1)} %get-tuple-element.69), channel_id=1, source_target_pairs={{0,24},{1,97},{2,26},{3,99},{4,28},{5,101},{6,30},{7,103},{8,0},{9... | collective-permute-start | bytes 3145736 | tf_op jit(solution)/shard_map/ppermute | solution.py:30
  114.8 27.2 %collective-permute-start.26 = (bf16[2048,256]{1,0:T(8,128)(2,1)S(1)}, bf16[2048,256]{1,0:T(8,128)(2,1)S(1)}, u32[]{:S(2)}, u32[]{:S(2)}) collective-permute-start(bf16[2048,256]{1,0:T(8,128)(2,1)S(1)} %get-tuple-element.68), channel_id=1, source_target_pairs={{0,8},{1,33},{2,10},{3,35},{4,12},{5,37},{6,14},{7,39},{8,16},{9,4... | collective-permute-start | bytes 3145736 | tf_op jit(solution)/shard_map/ppermute | solution.py:30
  115.2 26.9 %collective-permute-start.25 = (bf16[2048,256]{1,0:T(8,128)(2,1)S(1)}, bf16[2048,256]{1,0:T(8,128)(2,1)S(1)}, u32[]{:S(2)}, u32[]{:S(2)}) collective-permute-start(bf16[2048,256]{1,0:T(8,128)(2,1)S(1)} %get-tuple-element.67), channel_id=1, source_target_pairs={{0,16},{1,65},{2,18},{3,67},{4,20},{5,69},{6,22},{7,71},{8,24},{9,... | collective-permute-start | bytes 3145736 | tf_op jit(solution)/shard_map/ppermute | solution.py:30
  144.2 10.4 %collective-permute-start.29 = (bf16[512,256]{1,0:T(8,128)(2,1)S(1)}, bf16[512,256]{1,0:T(8,128)(2,1)S(1)}, u32[]{:S(2)}, u32[]{:S(2)}) collective-permute-start(bf16[512,256]{1,0:T(8,128)(2,1)S(1)} %get-tuple-element.74), channel_id=1, source_target_pairs={{0,32},{1,9},{2,34},{3,11},{4,36},{5,13},{6,38},{7,15},{8,40},{9,1... | collective-permute-start | bytes 786440 | tf_op jit(solution)/shard_map/ppermute | solution.py:30
  144.8 9.8 %collective-permute-start.28 = (bf16[512,256]{1,0:T(8,128)(2,1)S(1)}, bf16[512,256]{1,0:T(8,128)(2,1)S(1)}, u32[]{:S(2)}, u32[]{:S(2)}) collective-permute-start(bf16[512,256]{1,0:T(8,128)(2,1)S(1)} %get-tuple-element.72), channel_id=1, source_target_pairs={{0,64},{1,17},{2,66},{3,19},{4,68},{5,21},{6,70},{7,23},{8,72},{9,... | collective-permute-start | bytes 786440 | tf_op jit(solution)/shard_map/ppermute | solution.py:30
  (17 other events, 239.8 us)

commit v8 on v7

--- a/solution.py
+++ b/solution.py
@@ -159,7 +159,7 @@
 
 
 def assemble_kernel(chip, *refs):
-    pieces, out_ref, sems = refs[: RING + 1], refs[RING + 1], refs[RING + 2]
+    pieces, out_ref, sems = refs[:RING], refs[RING], refs[RING + 1]
     rows, both = pieces[0].shape
     count = rows // RING
     z, y, x, core = (chip[CHIP + i] for i in range(4))
@@ -171,10 +171,7 @@
             o = (x - from_z + RING) % RING
             start = ((o * 2 + ((from_y >> 1) ^ core)) * 2 + from_y % 2) * count
             target = out_ref.at[pl.ds(pl.multiple_of(start, count), count)]
-            if b == 2:
-                source = pieces[3 + a // 2].at[pl.ds(a % 2 * count, count)]
-            else:
-                source = pieces[min(b, 2)].at[pl.ds(a * count, count)]
+            source = pieces[b].at[pl.ds(a * count, count)]
             copies.append(pltpu.make_async_copy(source, target, sems.at[b, a]))
     for copy in copies:
         copy.start()
@@ -186,7 +183,7 @@
     rows, both = pieces[0].shape
     return pl.pallas_call(
         assemble_kernel,
-        in_specs=[SMEM] + [ANY] * (RING + 1),
+        in_specs=[SMEM] + [ANY] * RING,
         out_specs=VMEM,
         out_shape=jax.ShapeDtypeStruct((RING * rows, both), pieces[0].dtype),
         scratch_shapes=[pltpu.SemaphoreType.DMA((RING, RING))],
@@ -443,11 +440,10 @@
     shard = jnp.concatenate(gathered(shard, inner), axis=0)
     shard, *far_x = lax.optimization_barrier((shard, *far_x))
     far_halves = opposite(*far_x, along_x)
-    pieces = [outer(shard, 1), outer(shard, 3)]
-    near_own, *blocks = lax.optimization_barrier((near_own, *far_halves, *pieces))
-    far_halves, pieces = blocks[:2], blocks[2:]
+    pieces = gathered(shard, outer)
+    near_own, far_own, *far_halves = lax.optimization_barrier((near_own, far_own, *far_halves))
     near_x = [along_x(near_own, 1), along_x(near_own, 3)]
-    weights = assemble(numbers, [shard, *pieces, *opposite(*pieces, outer)])
+    weights = assemble(numbers, pieces)
     weights, *far_blocks = lax.optimization_barrier((weights, *far_x, *far_halves))
 
     def other_cores(*blocks):
@@ -478,7 +474,7 @@
     *earlier, far_grad = attend(FAR, *shared, far_key_value, away, query_gain, ())
     back = along_z(far_grad, RING // 2)
 
-    _, *near_halves = lax.optimization_barrier((far_grad, *near_halves))
+    back, *near_halves = lax.optimization_barrier((back, *near_halves))
     blocks = [*near_x, jnp.concatenate(near_halves, axis=0)]
     near_others.append(other_core(blocks[2]))
     near_feats = paired(near_own, other_core(near_own), *blocks, *near_others)
@@ -488,7 +484,6 @@
         NEAR, *shared, near_key_value, near_key_value, query_gain, earlier
     )
     near_rows = turn(NEAR, numbers, near_total, near_grad, near_grad, key_gain)
-    back, near_rows = lax.optimization_barrier((back, near_rows))
     far_rows = turn(FAR, numbers, far_total, far_grad, back, key_gain)
     part = first_part(far_feats, far_rows)
 

time: 156 us -> 153 us (0.981)
  waiting for transfers between devices: 83.8 us -> 72.3 us
  starting transfers between devices: 34 us -> 41.3 us
    ppermute x8, waiting for transfers between devices: 34.4 us -> 27.2 us  [along_x(): return lax.ppermute(x, 'tensor', pairs)]
    ppermute x13 -> x12, waiting for transfers between devices: 47.4 us -> 41.1 us  [by_core(): return lax.ppermute(x, ('dp', 'tensor'), pairs)]
    ppermute x13 -> x12, starting transfers between devices: 19.3 us -> 24.8 us  [by_core(): return lax.ppermute(x, ('dp', 'tensor'), pairs)]
    ppermute x2, waiting for transfers between devices: 0.01 us -> 2.4 us  [along_z(): return lax.ppermute(x, 'dp', pairs)]
    ppermute x2, starting transfers between devices: 4.73 us -> 7.04 us  [along_z(): return lax.ppermute(x, 'dp', pairs)]
  transfers between devices with their start and end apart: 31 -> 30, of which waited for: 19 -> 19; matrix products, arithmetic and copies ran while one was open for 5% -> 5% of each run, Pallas kernels for 9% -> 5%
where the time goes in v8:
time: 153 us; the launch traced here: 151 us
  waiting for transfers between devices  72.3 us (47%)
  starting transfers between devices  41.3 us (27%)
  Pallas kernels  24.3 us (16%)
  matrix products  7.25 us (5%)
  local copies, waits for them, and re-layouts  3.66 us (2%)
  between operations  1.77 us (1%)
    ppermute x12, waiting for transfers between devices, by_core(): return lax.ppermute(x, ('dp', 'tensor'), pairs)  41.1 us
    ppermute x8, waiting for transfers between devices, along_x(): return lax.ppermute(x, 'tensor', pairs)  27.2 us
    ppermute x12, starting transfers between devices, by_core(): return lax.ppermute(x, ('dp', 'tensor'), pairs)  24.8 us
    pallas_call x2, Pallas kernels, attend(): pl.pallas_call(functools.partial(attend_kernel, heads, base), grid_spec=p...  10.6 us
    ppermute x8, starting transfers between devices, along_x(): return lax.ppermute(x, 'tensor', pairs)  8.45 us
    dot_general x16, matrix products, matmul(): lax.dot_general(a, b, (contract, ((), ())), preferred_element_type=jnp.fl...  7.25 us
    ppermute x2, starting transfers between devices, along_z(): return lax.ppermute(x, 'dp', pairs)  7.04 us
    pallas_call x1, Pallas kernels, product(): pl.pallas_call(product_kernel, in_specs=[SMEM] + [VMEM] * (len(feats) + 2...  3.81 us
  transfers between devices with their start and end apart: 30, of which 19 were waited for; matrix products, arithmetic and copies ran while one was open for 5% of the time, Pallas kernels for 5%

profile of v8, /device:TPU:4, one launch (start us, length us, event | category | flops | bytes accessed | tf_op | source)
XLA Modules:
  0.0 151.3 jit_solution(7280488166215495868)
XLA Ops:
  0.6 3.6 %shard_map.129 = (s32[10]{0:T(128)}, bf16[512,1024]{1,0:T(8,128)(2,1)}, bf16[512,1024]{1,0:T(8,128)(2,1)}) custom-call(s32[32]{0:T(128)} %tiles.1, s32[32]{0:T(128)} %slots.1, bf16[2,512,1024]{2,1,0:T(8,128)(2,1)} %image_ref.1), custom_call_target="tpu_custom_call" | custom-call | bytes 4194304 | tf_op jit(solution)/shard_map/pallas_call | solution.py:124
  9.4 2.0 %collective-permute-start = (bf16[512,256]{1,0:T(8,128)(2,1)S(1)}, bf16[512,256]{1,0:T(8,128)(2,1)S(1)}, u32[]{:S(2)}, u32[]{:S(2)}) collective-permute-start(bf16[512,256]{1,0:T(8,128)(2,1)S(1)} %shard_map.130), channel_id=1, source_target_pairs={{0,32},{1,9},{2,34},{3,11},{4,36},{5,13},{6,38},{7,15},{8,40},{9,1... | collective-permute-start | bytes 786440 | tf_op jit(solution)/shard_map/ppermute | solution.py:30
  11.4 3.6 %collective-permute-start.1 = (bf16[512,256]{1,0:T(8,128)(2,1)S(1)}, bf16[512,256]{1,0:T(8,128)(2,1)S(1)}, u32[]{:S(2)}, u32[]{:S(2)}) collective-permute-start(bf16[512,256]{1,0:T(8,128)(2,1)S(1)} %shard_map.130), channel_id=1, source_target_pairs={{0,64},{1,17},{2,66},{3,19},{4,68},{5,21},{6,70},{7,23},{8,72},{9,... | collective-permute-start | bytes 786440 | tf_op jit(solution)/shard_map/ppermute | solution.py:30
  17.9 4.3 %collective-permute-done.1 = bf16[512,256]{1,0:T(8,128)(2,1)S(1)} collective-permute-done((bf16[512,256]{1,0:T(8,128)(2,1)S(1)}, bf16[512,256]{1,0:T(8,128)(2,1)S(1)}, u32[]{:S(2)}, u32[]{:S(2)}) %collective-permute-start.1) | collective-permute-done | bytes 262176 | tf_op jit(solution)/shard_map/ppermute | solution.py:30
  22.2 7.2 %collective-permute-done.3.refs_2_ = bf16[512,1024]{1,0:T(8,128)(2,1)S(1)} collective-permute-done((bf16[512,1024]{1,0:T(8,128)(2,1)}, bf16[512,1024]{1,0:T(8,128)(2,1)S(1)}, u32[]{:S(2)}, u32[]{:S(2)}) %collective-permute-start.3) | collective-permute-done | bytes 1048608 | tf_op jit(solution)/shard_map/ppermute | solution.py:43
  31.9 2.9 %collective-permute-start.8 = (bf16[2048,256]{1,0:T(8,128)(2,1)S(1)}, bf16[2048,256]{1,0:T(8,128)(2,1)S(1)}, u32[]{:S(2)}, u32[]{:S(2)}) collective-permute-start(bf16[2048,256]{1,0:T(8,128)(2,1)S(1)} %pad_maximum_fusion.refs_0_), channel_id=1, source_target_pairs={{0,16},{1,65},{2,18},{3,67},{4,20},{5,69},{6,22},{7,71},{8,24},{9,... | collective-permute-start | bytes 3145736 | tf_op jit(solution)/shard_map/ppermute | solution.py:30
  39.1 9.5 %collective-permute-done.5 = bf16[256,1024]{1,0:T(8,128)(2,1)S(1)} collective-permute-done((bf16[256,1024]{1,0:T(8,128)(2,1)S(1)}, bf16[256,1024]{1,0:T(8,128)(2,1)S(1)}, u32[]{:S(2)}, u32[]{:S(2)}) %collective-permute-start.5) | collective-permute-done | bytes 524320 | tf_op jit(solution)/shard_map/ppermute | solution.py:43
  52.2 6.7 %collective-permute-done.8.refs_2_ = bf16[2048,256]{1,0:T(8,128)(2,1)S(1)} collective-permute-done((bf16[2048,256]{1,0:T(8,128)(2,1)S(1)}, bf16[2048,256]{1,0:T(8,128)(2,1)S(1)}, u32[]{:S(2)}, u32[]{:S(2)}) %collective-permute-start.8) | collective-permute-done | bytes 1048608 | tf_op jit(solution)/shard_map/ppermute | solution.py:30
  66.5 4.0 %collective-permute-start.19 = (bf16[512,256]{1,0:T(8,128)(2,1)S(1)}, bf16[512,256]{1,0:T(8,128)(2,1)S(1)}, u32[]{:S(2)}, u32[]{:S(2)}) collective-permute-start(bf16[512,256]{1,0:T(8,128)(2,1)S(1)} %shard_map.132.kv_ref), channel_id=1, source_target_pairs={{0,64},{8,72},{16,80},{24,88},{32,96},{40,104},{48,112},{56,120},{... | collective-permute-start | bytes 786440 | tf_op jit(solution)/shard_map/ppermute | solution.py:17
  70.5 2.0 %collective-permute-done.14.refs_2_ = bf16[512,1024]{1,0:T(8,128)(2,1)S(1)} collective-permute-done((bf16[512,1024]{1,0:T(8,128)(2,1)S(1)}, bf16[512,1024]{1,0:T(8,128)(2,1)S(1)}, u32[]{:S(2)}, u32[]{:S(2)}) %collective-permute-start.14) | collective-permute-done | bytes 1048608 | tf_op jit(solution)/shard_map/ppermute | solution.py:43
  77.2 5.3 %shard_map.133 = (bf16[2,128,1024]{2,1,0:T(8,128)(2,1)}, bf16[2,128,1024]{2,1,0:T(8,128)(2,1)}, bf16[512,256]{1,0:T(8,128)(2,1)S(1)}) custom-call(s32[10]{0:T(128)S(1)} %copy-done.5, f32[1]{0:T(128)S(6)} %tanh.3.ratio_ref, bf16[2,128,1024]{2,1,0:T(8,128)(2,1)S(1)} %copy-done.7, bf16[2,128,1024]{2,1,0:T(8,128)(2,1)S(1)} %copy-done.8, ...), custom_call_target="tpu_custom_call" | custom-call | flops 939524096 | bytes 1441792 | tf_op jit(solution)/shard_map/pallas_call | solution.py:384
  82.5 3.1 %collective-permute-start.20 = (bf16[512,256]{1,0:T(8,128)(2,1)S(1)}, bf16[512,256]{1,0:T(8,128)(2,1)S(1)}, u32[]{:S(2)}, u32[]{:S(2)}) collective-permute-start(bf16[512,256]{1,0:T(8,128)(2,1)S(1)} %get-tuple-element.53.grad_ref), channel_id=1, source_target_pairs={{0,64},{8,72},{16,80},{24,88},{32,96},{40,104},{48,112},{56,120},{... | collective-permute-start | bytes 786440 | tf_op jit(solution)/shard_map/ppermute | solution.py:17
  86.1 2.7 %collective-permute-done.21 = bf16[256,1024]{1,0:T(8,128)(2,1)S(1)} collective-permute-done((bf16[256,1024]{1,0:T(8,128)(2,1)S(1)}, bf16[256,1024]{1,0:T(8,128)(2,1)S(1)}, u32[]{:S(2)}, u32[]{:S(2)}) %collective-permute-start.21) | collective-permute-done | bytes 524320 | tf_op jit(solution)/shard_map/ppermute | solution.py:43
  90.3 2.4 %collective-permute-done.20.other_ref = bf16[512,256]{1,0:T(8,128)(2,1)S(1)} collective-permute-done((bf16[512,256]{1,0:T(8,128)(2,1)S(1)}, bf16[512,256]{1,0:T(8,128)(2,1)S(1)}, u32[]{:S(2)}, u32[]{:S(2)}) %collective-permute-start.20) | collective-permute-done | bytes 262176 | tf_op jit(solution)/shard_map/ppermute | solution.py:17
  96.5 2.6 %shard_map.138.refs_9_ = f32[8192,256]{1,0:T(8,128)S(1)} custom-call(bf16[512,1024]{1,0:T(8,128)(2,1)S(1)} %copy-done.1, bf16[512,1024]{1,0:T(8,128)(2,1)S(1)} %collective-permute-done.10.refs_1_, bf16[512,1024]{1,0:T(8,128)(2,1)S(1)} %collective-permute-done.3.refs_2_, bf16[512,1024]{1,0:T(8,128)(2,1)S(1)} %collective-permute-done.11.refs_3_, ...), custom_call_target="tpu_custom_call" | custom-call | flops 2147483648 | bytes 8388608 | tf_op jit(solution)/shard_map/pallas_call | solution.py:250
  99.3 5.3 %shard_map.135 = (bf16[2,128,1024]{2,1,0:T(8,128)(2,1)}, bf16[2,128,1024]{2,1,0:T(8,128)(2,1)}, bf16[512,256]{1,0:T(8,128)(2,1)S(1)}) custom-call(s32[10]{0:T(128)S(1)} %copy-done.5, f32[1]{0:T(128)S(6)} %tanh.3.ratio_ref, bf16[2,128,1024]{2,1,0:T(8,128)(2,1)S(1)} %copy-done.7, ...), custom_call_target="tpu_custom_call", output_to_operand_aliasing={{0}: (7, {}), {1}: (8, {})} | custom-call | flops 939524096 | bytes 1441792 | tf_op jit(solution)/shard_map/pallas_call | solution.py:384
  105.3 3.8 %shard_map.139 = (bf16[2048,256]{1,0:T(8,128)(2,1)S(1)}, bf16[2048,256]{1,0:T(8,128)(2,1)S(1)}, bf16[2048,256]{1,0:T(8,128)(2,1)S(1)}, bf16[2048,256]{1,0:T(8,128)(2,1)S(1)}) custom-call(s32[10]{0:T(128)S(1)} %copy-done.5, bf16[512,1024]{1,0:T(8,128)(2,1)S(1)} %copy-done, bf16[512,1024]{1,0:T(8,128)(2,1)S(1)} %collective-permute-done.16.refs_1_, ...), custom_call_target="tpu_custom_call" | custom-call | flops 2147483648 | bytes 8388608 | tf_op jit(solution)/shard_map/pallas_call | solution.py:291
  109.1 5.2 %collective-permute-start.24 = (bf16[2048,256]{1,0:T(8,128)(2,1)S(1)}, bf16[2048,256]{1,0:T(8,128)(2,1)S(1)}, u32[]{:S(2)}, u32[]{:S(2)}) collective-permute-start(bf16[2048,256]{1,0:T(8,128)(2,1)S(1)} %get-tuple-element.63), channel_id=1, source_target_pairs={{0,16},{1,65},{2,18},{3,67},{4,20},{5,69},{6,22},{7,71},{8,24},{9,... | collective-permute-start | bytes 3145736 | tf_op jit(solution)/shard_map/ppermute | solution.py:30
  115.0 2.6 %collective-permute-start.26 = (bf16[2048,256]{1,0:T(8,128)(2,1)S(1)}, bf16[2048,256]{1,0:T(8,128)(2,1)S(1)}, u32[]{:S(2)}, u32[]{:S(2)}) collective-permute-start(bf16[2048,256]{1,0:T(8,128)(2,1)S(1)} %get-tuple-element.65), channel_id=1, source_target_pairs={{0,24},{1,97},{2,26},{3,99},{4,28},{5,101},{6,30},{7,103},{8,0},{9... | collective-permute-start | bytes 3145736 | tf_op jit(solution)/shard_map/ppermute | solution.py:30
  117.5 9.6 %collective-permute-done.24 = bf16[2048,256]{1,0:T(8,128)(2,1)S(1)} collective-permute-done((bf16[2048,256]{1,0:T(8,128)(2,1)S(1)}, bf16[2048,256]{1,0:T(8,128)(2,1)S(1)}, u32[]{:S(2)}, u32[]{:S(2)}) %collective-permute-start.24) | collective-permute-done | bytes 1048608 | tf_op jit(solution)/shard_map/ppermute | solution.py:30
  127.2 11.1 %collective-permute-done.25 = bf16[2048,256]{1,0:T(8,128)(2,1)S(1)} collective-permute-done((bf16[2048,256]{1,0:T(8,128)(2,1)S(1)}, bf16[2048,256]{1,0:T(8,128)(2,1)S(1)}, u32[]{:S(2)}, u32[]{:S(2)}) %collective-permute-start.25) | collective-permute-done | bytes 1048608 | tf_op jit(solution)/shard_map/ppermute | solution.py:30
  141.2 2.4 %collective-permute-start.29 = (bf16[512,256]{1,0:T(8,128)(2,1)S(1)}, bf16[512,256]{1,0:T(8,128)(2,1)S(1)}, u32[]{:S(2)}, u32[]{:S(2)}) collective-permute-start(bf16[512,256]{1,0:T(8,128)(2,1)S(1)} %get-tuple-element.69), channel_id=1, source_target_pairs={{0,96},{1,25},{2,98},{3,27},{4,100},{5,29},{6,102},{7,31},{8,104},... | collective-permute-start | bytes 786440 | tf_op jit(solution)/shard_map/ppermute | solution.py:30
  143.6 4.0 %collective-permute-done.27 = bf16[512,256]{1,0:T(8,128)(2,1)S(1)} collective-permute-done((bf16[512,256]{1,0:T(8,128)(2,1)S(1)}, bf16[512,256]{1,0:T(8,128)(2,1)S(1)}, u32[]{:S(2)}, u32[]{:S(2)}) %collective-permute-start.27) | collective-permute-done | bytes 262176 | tf_op jit(solution)/shard_map/ppermute | solution.py:30
  147.7 2.7 %collective-permute-done.28 = bf16[512,256]{1,0:T(8,128)(2,1)S(1)} collective-permute-done((bf16[512,256]{1,0:T(8,128)(2,1)S(1)}, bf16[512,256]{1,0:T(8,128)(2,1)S(1)}, u32[]{:S(2)}, u32[]{:S(2)}) %collective-permute-start.28) | collective-permute-done | bytes 262176 | tf_op jit(solution)/shard_map/ppermute | solution.py:30
  (96 shorter events, 41.1 us)
Async XLA Ops:
  4.3 25.2 %collective-permute-start.3 = (bf16[512,1024]{1,0:T(8,128)(2,1)}, bf16[512,1024]{1,0:T(8,128)(2,1)S(1)}, u32[]{:S(2)}, u32[]{:S(2)}) collective-permute-start(bf16[512,1024]{1,0:T(8,128)(2,1)} %get-tuple-element.40.refs_0_), channel_id=1, source_target_pairs={{0,2},{1,3},{2,4},{3,5},{4,6},{5,7},{6,0},{7,1},{8,10},{9,11},{10,... | collective-permute-start | bytes 3145736 | tf_op jit(solution)/shard_map/ppermute | solution.py:43
  5.5 24.8 %collective-permute-start.4 = (bf16[512,1024]{1,0:T(8,128)(2,1)}, bf16[512,1024]{1,0:T(8,128)(2,1)S(1)}, u32[]{:S(2)}, u32[]{:S(2)}) collective-permute-start(bf16[512,1024]{1,0:T(8,128)(2,1)} %get-tuple-element.40.refs_0_), channel_id=1, source_target_pairs={{0,6},{1,7},{2,0},{3,1},{4,2},{5,3},{6,4},{7,5},{8,14},{9,15},{10,... | collective-permute-start | bytes 3145736 | tf_op jit(solution)/shard_map/ppermute | solution.py:43
  9.4 8.5 %collective-permute-start = (bf16[512,256]{1,0:T(8,128)(2,1)S(1)}, bf16[512,256]{1,0:T(8,128)(2,1)S(1)}, u32[]{:S(2)}, u32[]{:S(2)}) collective-permute-start(bf16[512,256]{1,0:T(8,128)(2,1)S(1)} %shard_map.130), channel_id=1, source_target_pairs={{0,32},{1,9},{2,34},{3,11},{4,36},{5,13},{6,38},{7,15},{8,40},{9,1... | collective-permute-start | bytes 786440 | tf_op jit(solution)/shard_map/ppermute | solution.py:30
  11.4 10.7 %collective-permute-start.1 = (bf16[512,256]{1,0:T(8,128)(2,1)S(1)}, bf16[512,256]{1,0:T(8,128)(2,1)S(1)}, u32[]{:S(2)}, u32[]{:S(2)}) collective-permute-start(bf16[512,256]{1,0:T(8,128)(2,1)S(1)} %shard_map.130), channel_id=1, source_target_pairs={{0,64},{1,17},{2,66},{3,19},{4,68},{5,21},{6,70},{7,23},{8,72},{9,... | collective-permute-start | bytes 786440 | tf_op jit(solution)/shard_map/ppermute | solution.py:30
  30.4 21.8 %collective-permute-start.7 = (bf16[2048,256]{1,0:T(8,128)(2,1)S(1)}, bf16[2048,256]{1,0:T(8,128)(2,1)S(1)}, u32[]{:S(2)}, u32[]{:S(2)}) collective-permute-start(bf16[2048,256]{1,0:T(8,128)(2,1)S(1)} %pad_maximum_fusion.refs_0_), channel_id=1, source_target_pairs={{0,8},{1,33},{2,10},{3,35},{4,12},{5,37},{6,14},{7,39},{8,16},{9,4... | collective-permute-start | bytes 3145736 | tf_op jit(solution)/shard_map/ppermute | solution.py:30
  31.9 26.9 %collective-permute-start.8 = (bf16[2048,256]{1,0:T(8,128)(2,1)S(1)}, bf16[2048,256]{1,0:T(8,128)(2,1)S(1)}, u32[]{:S(2)}, u32[]{:S(2)}) collective-permute-start(bf16[2048,256]{1,0:T(8,128)(2,1)S(1)} %pad_maximum_fusion.refs_0_), channel_id=1, source_target_pairs={{0,16},{1,65},{2,18},{3,67},{4,20},{5,69},{6,22},{7,71},{8,24},{9,... | collective-permute-start | bytes 3145736 | tf_op jit(solution)/shard_map/ppermute | solution.py:30
  34.8 24.0 %collective-permute-start.9 = (bf16[2048,256]{1,0:T(8,128)(2,1)S(1)}, bf16[2048,256]{1,0:T(8,128)(2,1)S(1)}, u32[]{:S(2)}, u32[]{:S(2)}) collective-permute-start(bf16[2048,256]{1,0:T(8,128)(2,1)S(1)} %pad_maximum_fusion.refs_0_), channel_id=1, source_target_pairs={{0,24},{1,97},{2,26},{3,99},{4,28},{5,101},{6,30},{7,103},{8,0},{9... | collective-permute-start | bytes 3145736 | tf_op jit(solution)/shard_map/ppermute | solution.py:30
  36.2 12.4 %collective-permute-start.5 = (bf16[256,1024]{1,0:T(8,128)(2,1)S(1)}, bf16[256,1024]{1,0:T(8,128)(2,1)S(1)}, u32[]{:S(2)}, u32[]{:S(2)}) collective-permute-start(bf16[256,1024]{1,0:T(8,128)(2,1)S(1)} %slice.65), channel_id=1, source_target_pairs={{0,2},{1,3},{2,4},{3,5},{4,6},{5,7},{6,0},{7,1},{8,10},{9,11},{10,... | collective-permute-start | bytes 1572872 | tf_op jit(solution)/shard_map/ppermute | solution.py:43
  38.0 12.1 %collective-permute-start.6 = (bf16[256,1024]{1,0:T(8,128)(2,1)S(1)}, bf16[256,1024]{1,0:T(8,128)(2,1)S(1)}, u32[]{:S(2)}, u32[]{:S(2)}) collective-permute-start(bf16[256,1024]{1,0:T(8,128)(2,1)S(1)} %slice.66), channel_id=1, source_target_pairs={{0,6},{1,7},{2,0},{3,1},{4,2},{5,3},{6,4},{7,5},{8,14},{9,15},{10,... | collective-permute-start | bytes 1572872 | tf_op jit(solution)/shard_map/ppermute | solution.py:43
  50.1 22.3 %collective-permute-start.14 = (bf16[512,1024]{1,0:T(8,128)(2,1)S(1)}, bf16[512,1024]{1,0:T(8,128)(2,1)S(1)}, u32[]{:S(2)}, u32[]{:S(2)}) collective-permute-start(bf16[512,1024]{1,0:T(8,128)(2,1)S(1)} %copy-done), channel_id=1, source_target_pairs={{0,2},{1,3},{2,4},{3,5},{4,6},{5,7},{6,0},{7,1},{8,10},{9,11},{10,... | collective-permute-start | bytes 3145736 | tf_op jit(solution)/shard_map/ppermute | solution.py:43
  51.9 22.4 %collective-permute-start.15 = (bf16[512,1024]{1,0:T(8,128)(2,1)S(1)}, bf16[512,1024]{1,0:T(8,128)(2,1)S(1)}, u32[]{:S(2)}, u32[]{:S(2)}) collective-permute-start(bf16[512,1024]{1,0:T(8,128)(2,1)S(1)} %copy-done), channel_id=1, source_target_pairs={{0,6},{1,7},{2,0},{3,1},{4,2},{5,3},{6,4},{7,5},{8,14},{9,15},{10,... | collective-permute-start | bytes 3145736 | tf_op jit(solution)/shard_map/ppermute | solution.py:43
  52.2 10.0 %collective-permute-start.10 = (bf16[512,1024]{1,0:T(8,128)(2,1)S(1)}, bf16[512,1024]{1,0:T(8,128)(2,1)S(1)}, u32[]{:S(2)}, u32[]{:S(2)}) collective-permute-start(bf16[512,1024]{1,0:T(8,128)(2,1)S(1)} %copy-done.1), channel_id=1, source_target_pairs={{0,1},{1,0},{2,3},{3,2},{4,5},{5,4},{6,7},{7,6},{8,9},{9,8},{10,11... | collective-permute-start | bytes 3145736 | tf_op jit(solution)/shard_map/ppermute | solution.py:47
  66.5 10.7 %collective-permute-start.19 = (bf16[512,256]{1,0:T(8,128)(2,1)S(1)}, bf16[512,256]{1,0:T(8,128)(2,1)S(1)}, u32[]{:S(2)}, u32[]{:S(2)}) collective-permute-start(bf16[512,256]{1,0:T(8,128)(2,1)S(1)} %shard_map.132.kv_ref), channel_id=1, source_target_pairs={{0,64},{8,72},{16,80},{24,88},{32,96},{40,104},{48,112},{56,120},{... | collective-permute-start | bytes 786440 | tf_op jit(solution)/shard_map/ppermute | solution.py:17
  74.4 20.2 %collective-permute-start.17 = (bf16[512,1024]{1,0:T(8,128)(2,1)S(1)}, bf16[512,1024]{1,0:T(8,128)(2,1)S(1)}, u32[]{:S(2)}, u32[]{:S(2)}) collective-permute-start(bf16[512,1024]{1,0:T(8,128)(2,1)S(1)} %collective-permute-done.14.refs_2_), channel_id=1, source_target_pairs={{0,1},{1,0},{2,3},{3,2},{4,5},{5,4},{6,7},{7,6},{8,9},{9,8},{10,11... | collective-permute-start | bytes 3145736 | tf_op jit(solution)/shard_map/ppermute | solution.py:47
  74.5 14.3 %collective-permute-start.21 = (bf16[256,1024]{1,0:T(8,128)(2,1)S(1)}, bf16[256,1024]{1,0:T(8,128)(2,1)S(1)}, u32[]{:S(2)}, u32[]{:S(2)}) collective-permute-start(bf16[256,1024]{1,0:T(8,128)(2,1)S(1)} %slice.75), channel_id=1, source_target_pairs={{0,2},{1,3},{2,4},{3,5},{4,6},{5,7},{6,0},{7,1},{8,10},{9,11},{10,... | collective-permute-start | bytes 1572872 | tf_op jit(solution)/shard_map/ppermute | solution.py:43
  76.2 14.1 %collective-permute-start.22 = (bf16[256,1024]{1,0:T(8,128)(2,1)S(1)}, bf16[256,1024]{1,0:T(8,128)(2,1)S(1)}, u32[]{:S(2)}, u32[]{:S(2)}) collective-permute-start(bf16[256,1024]{1,0:T(8,128)(2,1)S(1)} %slice.76), channel_id=1, source_target_pairs={{0,6},{1,7},{2,0},{3,1},{4,2},{5,3},{6,4},{7,5},{8,14},{9,15},{10,... | collective-permute-start | bytes 1572872 | tf_op jit(solution)/shard_map/ppermute | solution.py:43
  76.7 17.5 %collective-permute-start.16 = (bf16[512,1024]{1,0:T(8,128)(2,1)S(1)}, bf16[512,1024]{1,0:T(8,128)(2,1)S(1)}, u32[]{:S(2)}, u32[]{:S(2)}) collective-permute-start(bf16[512,1024]{1,0:T(8,128)(2,1)S(1)} %copy-done), channel_id=1, source_target_pairs={{0,1},{1,0},{2,3},{3,2},{4,5},{5,4},{6,7},{7,6},{8,9},{9,8},{10,11... | collective-permute-start | bytes 3145736 | tf_op jit(solution)/shard_map/ppermute | solution.py:47
  82.5 10.2 %collective-permute-start.20 = (bf16[512,256]{1,0:T(8,128)(2,1)S(1)}, bf16[512,256]{1,0:T(8,128)(2,1)S(1)}, u32[]{:S(2)}, u32[]{:S(2)}) collective-permute-start(bf16[512,256]{1,0:T(8,128)(2,1)S(1)} %get-tuple-element.53.grad_ref), channel_id=1, source_target_pairs={{0,64},{8,72},{16,80},{24,88},{32,96},{40,104},{48,112},{56,120},{... | collective-permute-start | bytes 786440 | tf_op jit(solution)/shard_map/ppermute | solution.py:17
  109.1 18.1 %collective-permute-start.24 = (bf16[2048,256]{1,0:T(8,128)(2,1)S(1)}, bf16[2048,256]{1,0:T(8,128)(2,1)S(1)}, u32[]{:S(2)}, u32[]{:S(2)}) collective-permute-start(bf16[2048,256]{1,0:T(8,128)(2,1)S(1)} %get-tuple-element.63), channel_id=1, source_target_pairs={{0,16},{1,65},{2,18},{3,67},{4,20},{5,69},{6,22},{7,71},{8,24},{9,... | collective-permute-start | bytes 3145736 | tf_op jit(solution)/shard_map/ppermute | solution.py:30
  114.3 24.0 %collective-permute-start.25 = (bf16[2048,256]{1,0:T(8,128)(2,1)S(1)}, bf16[2048,256]{1,0:T(8,128)(2,1)S(1)}, u32[]{:S(2)}, u32[]{:S(2)}) collective-permute-start(bf16[2048,256]{1,0:T(8,128)(2,1)S(1)} %get-tuple-element.64), channel_id=1, source_target_pairs={{0,8},{1,33},{2,10},{3,35},{4,12},{5,37},{6,14},{7,39},{8,16},{9,4... | collective-permute-start | bytes 3145736 | tf_op jit(solution)/shard_map/ppermute | solution.py:30
  115.0 24.1 %collective-permute-start.26 = (bf16[2048,256]{1,0:T(8,128)(2,1)S(1)}, bf16[2048,256]{1,0:T(8,128)(2,1)S(1)}, u32[]{:S(2)}, u32[]{:S(2)}) collective-permute-start(bf16[2048,256]{1,0:T(8,128)(2,1)S(1)} %get-tuple-element.65), channel_id=1, source_target_pairs={{0,24},{1,97},{2,26},{3,99},{4,28},{5,101},{6,30},{7,103},{8,0},{9... | collective-permute-start | bytes 3145736 | tf_op jit(solution)/shard_map/ppermute | solution.py:30
  139.6 8.1 %collective-permute-start.27 = (bf16[512,256]{1,0:T(8,128)(2,1)S(1)}, bf16[512,256]{1,0:T(8,128)(2,1)S(1)}, u32[]{:S(2)}, u32[]{:S(2)}) collective-permute-start(bf16[512,256]{1,0:T(8,128)(2,1)S(1)} %get-tuple-element.68), channel_id=1, source_target_pairs={{0,64},{1,17},{2,66},{3,19},{4,68},{5,21},{6,70},{7,23},{8,72},{9,... | collective-permute-start | bytes 786440 | tf_op jit(solution)/shard_map/ppermute | solution.py:30
  140.0 10.4 %collective-permute-start.28 = (bf16[512,256]{1,0:T(8,128)(2,1)S(1)}, bf16[512,256]{1,0:T(8,128)(2,1)S(1)}, u32[]{:S(2)}, u32[]{:S(2)}) collective-permute-start(bf16[512,256]{1,0:T(8,128)(2,1)S(1)} %get-tuple-element.70), channel_id=1, source_target_pairs={{0,32},{1,9},{2,34},{3,11},{4,36},{5,13},{6,38},{7,15},{8,40},{9,1... | collective-permute-start | bytes 786440 | tf_op jit(solution)/shard_map/ppermute | solution.py:30
  141.2 9.1 %collective-permute-start.29 = (bf16[512,256]{1,0:T(8,128)(2,1)S(1)}, bf16[512,256]{1,0:T(8,128)(2,1)S(1)}, u32[]{:S(2)}, u32[]{:S(2)}) collective-permute-start(bf16[512,256]{1,0:T(8,128)(2,1)S(1)} %get-tuple-element.69), channel_id=1, source_target_pairs={{0,96},{1,25},{2,98},{3,27},{4,100},{5,29},{6,102},{7,31},{8,104},... | collective-permute-start | bytes 786440 | tf_op jit(solution)/shard_map/ppermute | solution.py:30
  (16 other events, 214.2 us)

commit v9 on v8

--- a/solution.py
+++ b/solution.py
@@ -237,39 +237,18 @@
     )(numbers, total, grad, other, gain[None, :])
 
 
-def first_part_kernel(*refs):
-    sources, (grads_ref, out_ref) = refs[:-2], refs[-2:]
-    depth = sources[0].shape[1]
-    for k, source in enumerate(sources):
-        out_ref[k * depth : (k + 1) * depth] = matmul(source[...], grads_ref[...], ((0,), (0,)))
-
-
-def first_part(feats, grads):
-    rows, depth = feats[0].shape
-    both = grads.shape[1]
-    return pl.pallas_call(
-        first_part_kernel,
-        in_specs=[VMEM] * (len(feats) + 1),
-        out_specs=VMEM,
-        out_shape=jax.ShapeDtypeStruct((len(feats) * depth, both), jnp.float32),
-        compiler_params=PARAMS,
-        cost_estimate=pl.CostEstimate(
-            flops=2 * len(feats) * rows * depth * both,
-            bytes_accessed=2 * len(feats) * rows * depth,
-            transcendentals=0,
-        ),
-    )(*feats, grads)
-
-
 def product_kernel(chip, *refs):
-    sources, (grads_ref, part_ref), refs = refs[: 2 * RING], refs[2 * RING : 2 * RING + 2], refs[2 * RING + 2 :]
+    count = 2 * RING
+    first, second, (first_ref, second_ref) = refs[:count], refs[count : 2 * count], refs[2 * count : 2 * count + 2]
+    refs = refs[2 * count + 2 :]
     outs, (held, sems) = refs[:RING], refs[RING:]
-    depth = sources[0].shape[1]
+    depth = first[0].shape[1]
     count = depth // 2
     z, y, x, core = (chip[CHIP + i] for i in range(4))
-    for k, source in enumerate(sources):
-        total = matmul(source[...], grads_ref[...], ((0,), (0,)))
-        total = (total + part_ref[k * depth : (k + 1) * depth]).astype(held.dtype)
+    for k in range(len(first)):
+        total = matmul(first[k][...], first_ref[...], ((0,), (0,)))
+        total = total + matmul(second[k][...], second_ref[...], ((0,), (0,)))
+        total = total.astype(held.dtype)
         by_z = (x - k // 2 - z + 2 * RING) % RING
         for h in range(2):
             by_y = (2 * (k % 2 ^ core) + h - y + RING) % RING
@@ -284,13 +263,13 @@
         copy.wait()
 
 
-def product(chip, feats, grads, part):
+def product(chip, feats, others, grads, other_grads):
     rows, depth = feats[0].shape
     both = grads.shape[1]
     shape = (RING * depth // 2, both)
     return pl.pallas_call(
         product_kernel,
-        in_specs=[SMEM] + [VMEM] * (len(feats) + 2),
+        in_specs=[SMEM] + [VMEM] * (2 * len(feats) + 2),
         out_specs=[ANY] * RING,
         out_shape=[jax.ShapeDtypeStruct(shape, jnp.bfloat16)] * RING,
         scratch_shapes=[
@@ -299,11 +278,11 @@
         ],
         compiler_params=PARAMS,
         cost_estimate=pl.CostEstimate(
-            flops=2 * len(feats) * rows * depth * both,
-            bytes_accessed=2 * len(feats) * rows * depth,
+            flops=4 * len(feats) * rows * depth * both,
+            bytes_accessed=4 * len(feats) * rows * depth,
             transcendentals=0,
         ),
-    )(chip, *feats, grads, part)
+    )(chip, *feats, *others, grads, other_grads)
 
 
 def attend_kernel(heads, base, index, ratio_ref, q_ref, cot_ref, kv_ref, away_ref, gain_ref, *refs):
@@ -361,7 +340,7 @@
         d_kv_ref[:, head_dim:] = d_value_sum[...].astype(d_kv_ref.dtype)
 
 
-def attend(base, index, ratio, query, cot, key_value, away, gain, earlier, heads=2):
+def attend(base, index, ratio, query, cot, key_value, away, gain, earlier, heads=8):
     rows, both = key_value.shape
     head_dim = both // 2
     text = query.shape[1]
@@ -474,7 +453,7 @@
     *earlier, far_grad = attend(FAR, *shared, far_key_value, away, query_gain, ())
     back = along_z(far_grad, RING // 2)
 
-    back, *near_halves = lax.optimization_barrier((back, *near_halves))
+    _, *near_halves = lax.optimization_barrier((far_grad, *near_halves))
     blocks = [*near_x, jnp.concatenate(near_halves, axis=0)]
     near_others.append(other_core(blocks[2]))
     near_feats = paired(near_own, other_core(near_own), *blocks, *near_others)
@@ -484,10 +463,10 @@
         NEAR, *shared, near_key_value, near_key_value, query_gain, earlier
     )
     near_rows = turn(NEAR, numbers, near_total, near_grad, near_grad, key_gain)
+    back, near_rows = lax.optimization_barrier((back, near_rows))
     far_rows = turn(FAR, numbers, far_total, far_grad, back, key_gain)
-    part = first_part(far_feats, far_rows)
-
-    blocks = product(numbers, near_feats, near_rows, part)
+
+    blocks = product(numbers, far_feats, near_feats, far_rows, near_rows)
     total = summed([blocks[0], *scattered(blocks, outer)])
     count = total.shape[0] // RING
     parts = [total[d * count : (d + 1) * count] for d in range(RING)]

time: 153 us -> 153 us (level)
  waiting for transfers between devices: 72.3 us -> 81.3 us
  starting transfers between devices: 41.3 us -> 36.7 us
  Pallas kernels: 24.3 us -> 20 us
    ppermute x12, waiting for transfers between devices: 41.1 us -> 49.6 us  [by_core(): return lax.ppermute(x, ('dp', 'tensor'), pairs)]
    pallas_call x2, Pallas kernels: 10.6 us -> 6.8 us  [attend(): pl.pallas_call(functools.partial(attend_kernel, heads, base), grid_spec=p...]
    ppermute x2, starting transfers between devices: 7.04 us -> 3.95 us  [along_z(): return lax.ppermute(x, 'dp', pairs)]
    ppermute x8, waiting for transfers between devices: 27.2 us -> 29.8 us  [along_x(): return lax.ppermute(x, 'tensor', pairs)]
    ppermute x2, waiting for transfers between devices: 2.4 us -> 0.01 us  [along_z(): return lax.ppermute(x, 'dp', pairs)]
    ppermute x12, starting transfers between devices: 24.8 us -> 22.7 us  [by_core(): return lax.ppermute(x, ('dp', 'tensor'), pairs)]
    pallas_call x2 -> x1, Pallas kernels: 6.37 us -> 5.92 us  [product(): pl.pallas_call(product_kernel, in_specs=[SMEM] + [VMEM] * (2 * len(feats)...]
  transfers between devices with their start and end apart: 30 -> 30, of which waited for: 19 -> 19; matrix products, arithmetic and copies ran while one was open for 5% -> 5% of each run, Pallas kernels for 5% -> 6%
where the time goes in v9:
time: 153 us; the launch traced here: 152 us
  waiting for transfers between devices  81.3 us (53%)
  starting transfers between devices  36.7 us (24%)
  Pallas kernels  20 us (13%)
  matrix products  7.29 us (5%)
  local copies, waits for them, and re-layouts  3.66 us (2%)
  between operations  1.78 us (1%)
    ppermute x12, waiting for transfers between devices, by_core(): return lax.ppermute(x, ('dp', 'tensor'), pairs)  49.6 us
    ppermute x8, waiting for transfers between devices, along_x(): return lax.ppermute(x, 'tensor', pairs)  29.8 us
    ppermute x12, starting transfers between devices, by_core(): return lax.ppermute(x, ('dp', 'tensor'), pairs)  22.7 us
    ppermute x8, starting transfers between devices, along_x(): return lax.ppermute(x, 'tensor', pairs)  8.31 us
    dot_general x16, matrix products, matmul(): lax.dot_general(a, b, (contract, ((), ())), preferred_element_type=jnp.fl...  7.29 us
    pallas_call x2, Pallas kernels, attend(): pl.pallas_call(functools.partial(attend_kernel, heads, base), grid_spec=p...  6.8 us
    pallas_call x1, Pallas kernels, product(): pl.pallas_call(product_kernel, in_specs=[SMEM] + [VMEM] * (2 * len(feats)...  5.92 us
    ppermute x2, starting transfers between devices, along_z(): return lax.ppermute(x, 'dp', pairs)  3.95 us
  transfers between devices with their start and end apart: 30, of which 19 were waited for; matrix products, arithmetic and copies ran while one was open for 5% of the time, Pallas kernels for 6%

profile of v9, /device:TPU:4, one launch (start us, length us, event | category | flops | bytes accessed | tf_op | source)
XLA Modules:
  0.0 151.6 jit_solution(10207079917016769936)
XLA Ops:
  0.6 3.6 %shard_map.129 = (s32[10]{0:T(128)}, bf16[512,1024]{1,0:T(8,128)(2,1)}, bf16[512,1024]{1,0:T(8,128)(2,1)}) custom-call(s32[32]{0:T(128)} %tiles.1, s32[32]{0:T(128)} %slots.1, bf16[2,512,1024]{2,1,0:T(8,128)(2,1)} %image_ref.1), custom_call_target="tpu_custom_call" | custom-call | bytes 4194304 | tf_op jit(solution)/shard_map/pallas_call | solution.py:124
  9.4 4.1 %collective-permute-start.2 = (bf16[512,256]{1,0:T(8,128)(2,1)S(1)}, bf16[512,256]{1,0:T(8,128)(2,1)S(1)}, u32[]{:S(2)}, u32[]{:S(2)}) collective-permute-start(bf16[512,256]{1,0:T(8,128)(2,1)S(1)} %shard_map.130), channel_id=1, source_target_pairs={{0,96},{1,25},{2,98},{3,27},{4,100},{5,29},{6,102},{7,31},{8,104},... | collective-permute-start | bytes 786440 | tf_op jit(solution)/shard_map/ppermute | solution.py:30
  14.8 5.4 %collective-permute-done.2 = bf16[512,256]{1,0:T(8,128)(2,1)S(1)} collective-permute-done((bf16[512,256]{1,0:T(8,128)(2,1)S(1)}, bf16[512,256]{1,0:T(8,128)(2,1)S(1)}, u32[]{:S(2)}, u32[]{:S(2)}) %collective-permute-start.2) | collective-permute-done | bytes 262176 | tf_op jit(solution)/shard_map/ppermute | solution.py:30
  21.5 2.4 %collective-permute-done = bf16[512,256]{1,0:T(8,128)(2,1)S(1)} collective-permute-done((bf16[512,256]{1,0:T(8,128)(2,1)S(1)}, bf16[512,256]{1,0:T(8,128)(2,1)S(1)}, u32[]{:S(2)}, u32[]{:S(2)}) %collective-permute-start) | collective-permute-done | bytes 262176 | tf_op jit(solution)/shard_map/ppermute | solution.py:30
  24.0 5.4 %collective-permute-done.3.refs_2_ = bf16[512,1024]{1,0:T(8,128)(2,1)S(1)} collective-permute-done((bf16[512,1024]{1,0:T(8,128)(2,1)}, bf16[512,1024]{1,0:T(8,128)(2,1)S(1)}, u32[]{:S(2)}, u32[]{:S(2)}) %collective-permute-start.3) | collective-permute-done | bytes 1048608 | tf_op jit(solution)/shard_map/ppermute | solution.py:43
  31.9 2.9 %collective-permute-start.8 = (bf16[2048,256]{1,0:T(8,128)(2,1)S(1)}, bf16[2048,256]{1,0:T(8,128)(2,1)S(1)}, u32[]{:S(2)}, u32[]{:S(2)}) collective-permute-start(bf16[2048,256]{1,0:T(8,128)(2,1)S(1)} %pad_maximum_fusion.refs_0_), channel_id=1, source_target_pairs={{0,16},{1,65},{2,18},{3,67},{4,20},{5,69},{6,22},{7,71},{8,24},{9,... | collective-permute-start | bytes 3145736 | tf_op jit(solution)/shard_map/ppermute | solution.py:30
  36.2 1.8 %collective-permute-start.5 = (bf16[256,1024]{1,0:T(8,128)(2,1)S(1)}, bf16[256,1024]{1,0:T(8,128)(2,1)S(1)}, u32[]{:S(2)}, u32[]{:S(2)}) collective-permute-start(bf16[256,1024]{1,0:T(8,128)(2,1)S(1)} %slice.65), channel_id=1, source_target_pairs={{0,2},{1,3},{2,4},{3,5},{4,6},{5,7},{6,0},{7,1},{8,10},{9,11},{10,... | collective-permute-start | bytes 1572872 | tf_op jit(solution)/shard_map/ppermute | solution.py:43
  39.1 9.5 %collective-permute-done.5 = bf16[256,1024]{1,0:T(8,128)(2,1)S(1)} collective-permute-done((bf16[256,1024]{1,0:T(8,128)(2,1)S(1)}, bf16[256,1024]{1,0:T(8,128)(2,1)S(1)}, u32[]{:S(2)}, u32[]{:S(2)}) %collective-permute-start.5) | collective-permute-done | bytes 524320 | tf_op jit(solution)/shard_map/ppermute | solution.py:43
  50.1 1.8 %collective-permute-start.14 = (bf16[512,1024]{1,0:T(8,128)(2,1)S(1)}, bf16[512,1024]{1,0:T(8,128)(2,1)S(1)}, u32[]{:S(2)}, u32[]{:S(2)}) collective-permute-start(bf16[512,1024]{1,0:T(8,128)(2,1)S(1)} %copy-done.1), channel_id=1, source_target_pairs={{0,2},{1,3},{2,4},{3,5},{4,6},{5,7},{6,0},{7,1},{8,10},{9,11},{10,... | collective-permute-start | bytes 3145736 | tf_op jit(solution)/shard_map/ppermute | solution.py:43
  52.2 6.7 %collective-permute-done.8.refs_2_ = bf16[2048,256]{1,0:T(8,128)(2,1)S(1)} collective-permute-done((bf16[2048,256]{1,0:T(8,128)(2,1)S(1)}, bf16[2048,256]{1,0:T(8,128)(2,1)S(1)}, u32[]{:S(2)}, u32[]{:S(2)}) %collective-permute-start.8) | collective-permute-done | bytes 1048608 | tf_op jit(solution)/shard_map/ppermute | solution.py:30
  66.6 4.0 %collective-permute-start.19 = (bf16[512,256]{1,0:T(8,128)(2,1)S(1)}, bf16[512,256]{1,0:T(8,128)(2,1)S(1)}, u32[]{:S(2)}, u32[]{:S(2)}) collective-permute-start(bf16[512,256]{1,0:T(8,128)(2,1)S(1)} %shard_map.132.kv_ref), channel_id=1, source_target_pairs={{0,64},{8,72},{16,80},{24,88},{32,96},{40,104},{48,112},{56,120},{... | collective-permute-start | bytes 786440 | tf_op jit(solution)/shard_map/ppermute | solution.py:17
  70.5 2.0 %collective-permute-done.14.refs_10_ = bf16[512,1024]{1,0:T(8,128)(2,1)S(1)} collective-permute-done((bf16[512,1024]{1,0:T(8,128)(2,1)S(1)}, bf16[512,1024]{1,0:T(8,128)(2,1)S(1)}, u32[]{:S(2)}, u32[]{:S(2)}) %collective-permute-start.14) | collective-permute-done | bytes 1048608 | tf_op jit(solution)/shard_map/ppermute | solution.py:43
  72.5 1.9 %collective-permute-done.15.refs_14_ = bf16[512,1024]{1,0:T(8,128)(2,1)S(1)} collective-permute-done((bf16[512,1024]{1,0:T(8,128)(2,1)S(1)}, bf16[512,1024]{1,0:T(8,128)(2,1)S(1)}, u32[]{:S(2)}, u32[]{:S(2)}) %collective-permute-start.15) | collective-permute-done | bytes 1048608 | tf_op jit(solution)/shard_map/ppermute | solution.py:43
  78.3 3.4 %shard_map.133 = (bf16[2,128,1024]{2,1,0:T(8,128)(2,1)}, bf16[2,128,1024]{2,1,0:T(8,128)(2,1)}, bf16[512,256]{1,0:T(8,128)(2,1)S(1)}) custom-call(s32[10]{0:T(128)S(1)} %copy-done.5, f32[1]{0:T(128)S(6)} %tanh.3.ratio_ref, bf16[2,128,1024]{2,1,0:T(8,128)(2,1)S(1)} %copy-done.7, bf16[2,128,1024]{2,1,0:T(8,128)(2,1)S(1)} %copy-done.8, ...), custom_call_target="tpu_custom_call" | custom-call | flops 939524096 | bytes 1441792 | tf_op jit(solution)/shard_map/pallas_call | solution.py:363
  81.7 7.3 %collective-permute-done.20 = bf16[256,1024]{1,0:T(8,128)(2,1)S(1)} collective-permute-done((bf16[256,1024]{1,0:T(8,128)(2,1)S(1)}, bf16[256,1024]{1,0:T(8,128)(2,1)S(1)}, u32[]{:S(2)}, u32[]{:S(2)}) %collective-permute-start.20) | collective-permute-done | bytes 524320 | tf_op jit(solution)/shard_map/ppermute | solution.py:43
  93.8 3.4 %shard_map.135 = (bf16[2,128,1024]{2,1,0:T(8,128)(2,1)}, bf16[2,128,1024]{2,1,0:T(8,128)(2,1)}, bf16[512,256]{1,0:T(8,128)(2,1)S(1)}) custom-call(s32[10]{0:T(128)S(1)} %copy-done.5, f32[1]{0:T(128)S(6)} %tanh.3.ratio_ref, bf16[2,128,1024]{2,1,0:T(8,128)(2,1)S(1)} %copy-done.7, ...), custom_call_target="tpu_custom_call", output_to_operand_aliasing={{0}: (7, {}), {1}: (8, {})} | custom-call | flops 939524096 | bytes 1441792 | tf_op jit(solution)/shard_map/pallas_call | solution.py:363
  98.8 5.9 %shard_map.138 = (bf16[2048,256]{1,0:T(8,128)(2,1)S(1)}, bf16[2048,256]{1,0:T(8,128)(2,1)S(1)}, bf16[2048,256]{1,0:T(8,128)(2,1)S(1)}, bf16[2048,256]{1,0:T(8,128)(2,1)S(1)}) custom-call(s32[10]{0:T(128)S(1)} %copy-done.5, bf16[512,1024]{1,0:T(8,128)(2,1)S(1)} %copy-done, bf16[512,1024]{1,0:T(8,128)(2,1)S(1)} %collective-permute-done.10.refs_1_, ...), custom_call_target="tpu_custom_call" | custom-call | flops 4294967296 | bytes 16777216 | tf_op jit(solution)/shard_map/pallas_call | solution.py:270
  104.7 5.0 %collective-permute-start.26 = (bf16[2048,256]{1,0:T(8,128)(2,1)S(1)}, bf16[2048,256]{1,0:T(8,128)(2,1)S(1)}, u32[]{:S(2)}, u32[]{:S(2)}) collective-permute-start(bf16[2048,256]{1,0:T(8,128)(2,1)S(1)} %get-tuple-element.67), channel_id=1, source_target_pairs={{0,24},{1,97},{2,26},{3,99},{4,28},{5,101},{6,30},{7,103},{8,0},{9... | collective-permute-start | bytes 3145736 | tf_op jit(solution)/shard_map/ppermute | solution.py:30
  109.7 2.2 %collective-permute-start.24 = (bf16[2048,256]{1,0:T(8,128)(2,1)S(1)}, bf16[2048,256]{1,0:T(8,128)(2,1)S(1)}, u32[]{:S(2)}, u32[]{:S(2)}) collective-permute-start(bf16[2048,256]{1,0:T(8,128)(2,1)S(1)} %get-tuple-element.65), channel_id=1, source_target_pairs={{0,16},{1,65},{2,18},{3,67},{4,20},{5,69},{6,22},{7,71},{8,24},{9,... | collective-permute-start | bytes 3145736 | tf_op jit(solution)/shard_map/ppermute | solution.py:30
  111.9 21.3 %collective-permute-done.26 = bf16[2048,256]{1,0:T(8,128)(2,1)S(1)} collective-permute-done((bf16[2048,256]{1,0:T(8,128)(2,1)S(1)}, bf16[2048,256]{1,0:T(8,128)(2,1)S(1)}, u32[]{:S(2)}, u32[]{:S(2)}) %collective-permute-start.26) | collective-permute-done | bytes 1048608 | tf_op jit(solution)/shard_map/ppermute | solution.py:30
  133.2 3.7 %collective-permute-done.25 = bf16[2048,256]{1,0:T(8,128)(2,1)S(1)} collective-permute-done((bf16[2048,256]{1,0:T(8,128)(2,1)S(1)}, bf16[2048,256]{1,0:T(8,128)(2,1)S(1)}, u32[]{:S(2)}, u32[]{:S(2)}) %collective-permute-start.25) | collective-permute-done | bytes 1048608 | tf_op jit(solution)/shard_map/ppermute | solution.py:30
  137.6 2.6 %collective-permute-start.29 = (bf16[512,256]{1,0:T(8,128)(2,1)S(1)}, bf16[512,256]{1,0:T(8,128)(2,1)S(1)}, u32[]{:S(2)}, u32[]{:S(2)}) collective-permute-start(bf16[512,256]{1,0:T(8,128)(2,1)S(1)} %get-tuple-element.71), channel_id=1, source_target_pairs={{0,96},{1,25},{2,98},{3,27},{4,100},{5,29},{6,102},{7,31},{8,104},... | collective-permute-start | bytes 786440 | tf_op jit(solution)/shard_map/ppermute | solution.py:30
  141.9 2.2 %collective-permute-done.29 = bf16[512,256]{1,0:T(8,128)(2,1)S(1)} collective-permute-done((bf16[512,256]{1,0:T(8,128)(2,1)S(1)}, bf16[512,256]{1,0:T(8,128)(2,1)S(1)}, u32[]{:S(2)}, u32[]{:S(2)}) %collective-permute-start.29) | collective-permute-done | bytes 262176 | tf_op jit(solution)/shard_map/ppermute | solution.py:30
  144.1 6.5 %collective-permute-done.28 = bf16[512,256]{1,0:T(8,128)(2,1)S(1)} collective-permute-done((bf16[512,256]{1,0:T(8,128)(2,1)S(1)}, bf16[512,256]{1,0:T(8,128)(2,1)S(1)}, u32[]{:S(2)}, u32[]{:S(2)}) %collective-permute-start.28) | collective-permute-done | bytes 262176 | tf_op jit(solution)/shard_map/ppermute | solution.py:30
  (95 shorter events, 34.8 us)
Async XLA Ops:
  4.3 25.2 %collective-permute-start.3 = (bf16[512,1024]{1,0:T(8,128)(2,1)}, bf16[512,1024]{1,0:T(8,128)(2,1)S(1)}, u32[]{:S(2)}, u32[]{:S(2)}) collective-permute-start(bf16[512,1024]{1,0:T(8,128)(2,1)} %get-tuple-element.41.refs_0_), channel_id=1, source_target_pairs={{0,2},{1,3},{2,4},{3,5},{4,6},{5,7},{6,0},{7,1},{8,10},{9,11},{10,... | collective-permute-start | bytes 3145736 | tf_op jit(solution)/shard_map/ppermute | solution.py:43
  5.5 24.8 %collective-permute-start.4 = (bf16[512,1024]{1,0:T(8,128)(2,1)}, bf16[512,1024]{1,0:T(8,128)(2,1)S(1)}, u32[]{:S(2)}, u32[]{:S(2)}) collective-permute-start(bf16[512,1024]{1,0:T(8,128)(2,1)} %get-tuple-element.41.refs_0_), channel_id=1, source_target_pairs={{0,6},{1,7},{2,0},{3,1},{4,2},{5,3},{6,4},{7,5},{8,14},{9,15},{10,... | collective-permute-start | bytes 3145736 | tf_op jit(solution)/shard_map/ppermute | solution.py:43
  9.4 10.8 %collective-permute-start.2 = (bf16[512,256]{1,0:T(8,128)(2,1)S(1)}, bf16[512,256]{1,0:T(8,128)(2,1)S(1)}, u32[]{:S(2)}, u32[]{:S(2)}) collective-permute-start(bf16[512,256]{1,0:T(8,128)(2,1)S(1)} %shard_map.130), channel_id=1, source_target_pairs={{0,96},{1,25},{2,98},{3,27},{4,100},{5,29},{6,102},{7,31},{8,104},... | collective-permute-start | bytes 786440 | tf_op jit(solution)/shard_map/ppermute | solution.py:30
  13.6 10.4 %collective-permute-start = (bf16[512,256]{1,0:T(8,128)(2,1)S(1)}, bf16[512,256]{1,0:T(8,128)(2,1)S(1)}, u32[]{:S(2)}, u32[]{:S(2)}) collective-permute-start(bf16[512,256]{1,0:T(8,128)(2,1)S(1)} %shard_map.130), channel_id=1, source_target_pairs={{0,32},{1,9},{2,34},{3,11},{4,36},{5,13},{6,38},{7,15},{8,40},{9,1... | collective-permute-start | bytes 786440 | tf_op jit(solution)/shard_map/ppermute | solution.py:30
  30.4 21.8 %collective-permute-start.7 = (bf16[2048,256]{1,0:T(8,128)(2,1)S(1)}, bf16[2048,256]{1,0:T(8,128)(2,1)S(1)}, u32[]{:S(2)}, u32[]{:S(2)}) collective-permute-start(bf16[2048,256]{1,0:T(8,128)(2,1)S(1)} %pad_maximum_fusion.refs_0_), channel_id=1, source_target_pairs={{0,8},{1,33},{2,10},{3,35},{4,12},{5,37},{6,14},{7,39},{8,16},{9,4... | collective-permute-start | bytes 3145736 | tf_op jit(solution)/shard_map/ppermute | solution.py:30
  31.9 26.9 %collective-permute-start.8 = (bf16[2048,256]{1,0:T(8,128)(2,1)S(1)}, bf16[2048,256]{1,0:T(8,128)(2,1)S(1)}, u32[]{:S(2)}, u32[]{:S(2)}) collective-permute-start(bf16[2048,256]{1,0:T(8,128)(2,1)S(1)} %pad_maximum_fusion.refs_0_), channel_id=1, source_target_pairs={{0,16},{1,65},{2,18},{3,67},{4,20},{5,69},{6,22},{7,71},{8,24},{9,... | collective-permute-start | bytes 3145736 | tf_op jit(solution)/shard_map/ppermute | solution.py:30
  34.8 24.0 %collective-permute-start.9 = (bf16[2048,256]{1,0:T(8,128)(2,1)S(1)}, bf16[2048,256]{1,0:T(8,128)(2,1)S(1)}, u32[]{:S(2)}, u32[]{:S(2)}) collective-permute-start(bf16[2048,256]{1,0:T(8,128)(2,1)S(1)} %pad_maximum_fusion.refs_0_), channel_id=1, source_target_pairs={{0,24},{1,97},{2,26},{3,99},{4,28},{5,101},{6,30},{7,103},{8,0},{9... | collective-permute-start | bytes 3145736 | tf_op jit(solution)/shard_map/ppermute | solution.py:30
  36.2 12.4 %collective-permute-start.5 = (bf16[256,1024]{1,0:T(8,128)(2,1)S(1)}, bf16[256,1024]{1,0:T(8,128)(2,1)S(1)}, u32[]{:S(2)}, u32[]{:S(2)}) collective-permute-start(bf16[256,1024]{1,0:T(8,128)(2,1)S(1)} %slice.65), channel_id=1, source_target_pairs={{0,2},{1,3},{2,4},{3,5},{4,6},{5,7},{6,0},{7,1},{8,10},{9,11},{10,... | collective-permute-start | bytes 1572872 | tf_op jit(solution)/shard_map/ppermute | solution.py:43
  38.0 12.1 %collective-permute-start.6 = (bf16[256,1024]{1,0:T(8,128)(2,1)S(1)}, bf16[256,1024]{1,0:T(8,128)(2,1)S(1)}, u32[]{:S(2)}, u32[]{:S(2)}) collective-permute-start(bf16[256,1024]{1,0:T(8,128)(2,1)S(1)} %slice.66), channel_id=1, source_target_pairs={{0,6},{1,7},{2,0},{3,1},{4,2},{5,3},{6,4},{7,5},{8,14},{9,15},{10,... | collective-permute-start | bytes 1572872 | tf_op jit(solution)/shard_map/ppermute | solution.py:43
  50.1 22.3 %collective-permute-start.14 = (bf16[512,1024]{1,0:T(8,128)(2,1)S(1)}, bf16[512,1024]{1,0:T(8,128)(2,1)S(1)}, u32[]{:S(2)}, u32[]{:S(2)}) collective-permute-start(bf16[512,1024]{1,0:T(8,128)(2,1)S(1)} %copy-done.1), channel_id=1, source_target_pairs={{0,2},{1,3},{2,4},{3,5},{4,6},{5,7},{6,0},{7,1},{8,10},{9,11},{10,... | collective-permute-start | bytes 3145736 | tf_op jit(solution)/shard_map/ppermute | solution.py:43
  51.9 22.4 %collective-permute-start.15 = (bf16[512,1024]{1,0:T(8,128)(2,1)S(1)}, bf16[512,1024]{1,0:T(8,128)(2,1)S(1)}, u32[]{:S(2)}, u32[]{:S(2)}) collective-permute-start(bf16[512,1024]{1,0:T(8,128)(2,1)S(1)} %copy-done.1), channel_id=1, source_target_pairs={{0,6},{1,7},{2,0},{3,1},{4,2},{5,3},{6,4},{7,5},{8,14},{9,15},{10,... | collective-permute-start | bytes 3145736 | tf_op jit(solution)/shard_map/ppermute | solution.py:43
  52.2 10.0 %collective-permute-start.10 = (bf16[512,1024]{1,0:T(8,128)(2,1)S(1)}, bf16[512,1024]{1,0:T(8,128)(2,1)S(1)}, u32[]{:S(2)}, u32[]{:S(2)}) collective-permute-start(bf16[512,1024]{1,0:T(8,128)(2,1)S(1)} %copy-done), channel_id=1, source_target_pairs={{0,1},{1,0},{2,3},{3,2},{4,5},{5,4},{6,7},{7,6},{8,9},{9,8},{10,11... | collective-permute-start | bytes 3145736 | tf_op jit(solution)/shard_map/ppermute | solution.py:47
  66.6 11.5 %collective-permute-start.19 = (bf16[512,256]{1,0:T(8,128)(2,1)S(1)}, bf16[512,256]{1,0:T(8,128)(2,1)S(1)}, u32[]{:S(2)}, u32[]{:S(2)}) collective-permute-start(bf16[512,256]{1,0:T(8,128)(2,1)S(1)} %shard_map.132.kv_ref), channel_id=1, source_target_pairs={{0,64},{8,72},{16,80},{24,88},{32,96},{40,104},{48,112},{56,120},{... | collective-permute-start | bytes 786440 | tf_op jit(solution)/shard_map/ppermute | solution.py:17
  74.4 16.6 %collective-permute-start.18 = (bf16[512,1024]{1,0:T(8,128)(2,1)S(1)}, bf16[512,1024]{1,0:T(8,128)(2,1)S(1)}, u32[]{:S(2)}, u32[]{:S(2)}) collective-permute-start(bf16[512,1024]{1,0:T(8,128)(2,1)S(1)} %collective-permute-done.15.refs_14_), channel_id=1, source_target_pairs={{0,1},{1,0},{2,3},{3,2},{4,5},{5,4},{6,7},{7,6},{8,9},{9,8},{10,11... | collective-permute-start | bytes 3145736 | tf_op jit(solution)/shard_map/ppermute | solution.py:47
  74.5 17.0 %collective-permute-start.17 = (bf16[512,1024]{1,0:T(8,128)(2,1)S(1)}, bf16[512,1024]{1,0:T(8,128)(2,1)S(1)}, u32[]{:S(2)}, u32[]{:S(2)}) collective-permute-start(bf16[512,1024]{1,0:T(8,128)(2,1)S(1)} %collective-permute-done.14.refs_10_), channel_id=1, source_target_pairs={{0,1},{1,0},{2,3},{3,2},{4,5},{5,4},{6,7},{7,6},{8,9},{9,8},{10,11... | collective-permute-start | bytes 3145736 | tf_op jit(solution)/shard_map/ppermute | solution.py:47
  75.1 13.9 %collective-permute-start.20 = (bf16[256,1024]{1,0:T(8,128)(2,1)S(1)}, bf16[256,1024]{1,0:T(8,128)(2,1)S(1)}, u32[]{:S(2)}, u32[]{:S(2)}) collective-permute-start(bf16[256,1024]{1,0:T(8,128)(2,1)S(1)} %slice.75), channel_id=1, source_target_pairs={{0,2},{1,3},{2,4},{3,5},{4,6},{5,7},{6,0},{7,1},{8,10},{9,11},{10,... | collective-permute-start | bytes 1572872 | tf_op jit(solution)/shard_map/ppermute | solution.py:43
  76.7 13.6 %collective-permute-start.21 = (bf16[256,1024]{1,0:T(8,128)(2,1)S(1)}, bf16[256,1024]{1,0:T(8,128)(2,1)S(1)}, u32[]{:S(2)}, u32[]{:S(2)}) collective-permute-start(bf16[256,1024]{1,0:T(8,128)(2,1)S(1)} %slice.76), channel_id=1, source_target_pairs={{0,6},{1,7},{2,0},{3,1},{4,2},{5,3},{6,4},{7,5},{8,14},{9,15},{10,... | collective-permute-start | bytes 1572872 | tf_op jit(solution)/shard_map/ppermute | solution.py:43
  78.0 13.9 %collective-permute-start.16 = (bf16[512,1024]{1,0:T(8,128)(2,1)S(1)}, bf16[512,1024]{1,0:T(8,128)(2,1)S(1)}, u32[]{:S(2)}, u32[]{:S(2)}) collective-permute-start(bf16[512,1024]{1,0:T(8,128)(2,1)S(1)} %copy-done.1), channel_id=1, source_target_pairs={{0,1},{1,0},{2,3},{3,2},{4,5},{5,4},{6,7},{7,6},{8,9},{9,8},{10,11... | collective-permute-start | bytes 3145736 | tf_op jit(solution)/shard_map/ppermute | solution.py:47
  89.0 9.0 %collective-permute-start.23 = (bf16[512,256]{1,0:T(8,128)(2,1)S(1)}, bf16[512,256]{1,0:T(8,128)(2,1)S(1)}, u32[]{:S(2)}, u32[]{:S(2)}) collective-permute-start(bf16[512,256]{1,0:T(8,128)(2,1)S(1)} %get-tuple-element.54.grad_ref), channel_id=1, source_target_pairs={{0,64},{8,72},{16,80},{24,88},{32,96},{40,104},{48,112},{56,120},{... | collective-permute-start | bytes 786440 | tf_op jit(solution)/shard_map/ppermute | solution.py:17
  104.7 28.5 %collective-permute-start.26 = (bf16[2048,256]{1,0:T(8,128)(2,1)S(1)}, bf16[2048,256]{1,0:T(8,128)(2,1)S(1)}, u32[]{:S(2)}, u32[]{:S(2)}) collective-permute-start(bf16[2048,256]{1,0:T(8,128)(2,1)S(1)} %get-tuple-element.67), channel_id=1, source_target_pairs={{0,24},{1,97},{2,26},{3,99},{4,28},{5,101},{6,30},{7,103},{8,0},{9... | collective-permute-start | bytes 3145736 | tf_op jit(solution)/shard_map/ppermute | solution.py:30
  109.7 27.2 %collective-permute-start.25 = (bf16[2048,256]{1,0:T(8,128)(2,1)S(1)}, bf16[2048,256]{1,0:T(8,128)(2,1)S(1)}, u32[]{:S(2)}, u32[]{:S(2)}) collective-permute-start(bf16[2048,256]{1,0:T(8,128)(2,1)S(1)} %get-tuple-element.66), channel_id=1, source_target_pairs={{0,8},{1,33},{2,10},{3,35},{4,12},{5,37},{6,14},{7,39},{8,16},{9,4... | collective-permute-start | bytes 3145736 | tf_op jit(solution)/shard_map/ppermute | solution.py:30
  109.7 27.2 %collective-permute-start.24 = (bf16[2048,256]{1,0:T(8,128)(2,1)S(1)}, bf16[2048,256]{1,0:T(8,128)(2,1)S(1)}, u32[]{:S(2)}, u32[]{:S(2)}) collective-permute-start(bf16[2048,256]{1,0:T(8,128)(2,1)S(1)} %get-tuple-element.65), channel_id=1, source_target_pairs={{0,16},{1,65},{2,18},{3,67},{4,20},{5,69},{6,22},{7,71},{8,24},{9,... | collective-permute-start | bytes 3145736 | tf_op jit(solution)/shard_map/ppermute | solution.py:30
  140.2 10.4 %collective-permute-start.28 = (bf16[512,256]{1,0:T(8,128)(2,1)S(1)}, bf16[512,256]{1,0:T(8,128)(2,1)S(1)}, u32[]{:S(2)}, u32[]{:S(2)}) collective-permute-start(bf16[512,256]{1,0:T(8,128)(2,1)S(1)} %get-tuple-element.72), channel_id=1, source_target_pairs={{0,32},{1,9},{2,34},{3,11},{4,36},{5,13},{6,38},{7,15},{8,40},{9,1... | collective-permute-start | bytes 786440 | tf_op jit(solution)/shard_map/ppermute | solution.py:30
  140.2 10.4 %collective-permute-start.27 = (bf16[512,256]{1,0:T(8,128)(2,1)S(1)}, bf16[512,256]{1,0:T(8,128)(2,1)S(1)}, u32[]{:S(2)}, u32[]{:S(2)}) collective-permute-start(bf16[512,256]{1,0:T(8,128)(2,1)S(1)} %get-tuple-element.70), channel_id=1, source_target_pairs={{0,64},{1,17},{2,66},{3,19},{4,68},{5,21},{6,70},{7,23},{8,72},{9,... | collective-permute-start | bytes 786440 | tf_op jit(solution)/shard_map/ppermute | solution.py:30
  (16 other events, 213.5 us)

commit v10 on v9

--- a/solution.py
+++ b/solution.py
@@ -53,7 +53,7 @@
 
 
 def scattered(parts, move):
-    return [move(parts[step], step) for step in (2, 1, 3)]
+    return [move(parts[step], step) for step in (3, 1, 2)]
 
 
 def summed(blocks):
@@ -87,10 +87,10 @@
 PARAMS = pltpu.CompilerParams(vmem_limit_bytes=16 * 1024 * 1024)
 
 
-NEAR, FAR, CHIP = 0, 3, 6
-
-
-def route_kernel(tiles, slots, image_ref, numbers, far_ref, near_ref, sems):
+NEAR, FAR, CHIP, NEAR_SLOT = 0, 3, 6, 10
+
+
+def route_kernel(tiles, slots, image_ref, numbers, far_ref, sem):
     rank, place = lax.axis_index("dp"), lax.axis_index("tensor")
     first = 2 * rank
     homes = (slots[first], slots[first + 1])
@@ -99,10 +99,8 @@
     ]
     swaps = jnp.logical_or(away[0], away[1])
     far_slot = jnp.where(away[1], 1, 0)
-    copies = []
-    for i, (slot, target) in enumerate(((far_slot, far_ref), (1 - far_slot, near_ref))):
-        copies.append(pltpu.make_async_copy(image_ref.at[slot], target, sems.at[i]))
-        copies[i].start()
+    copy = pltpu.make_async_copy(image_ref.at[far_slot], far_ref, sem)
+    copy.start()
     of_slot = jnp.where(homes[1] == first + far_slot, 1, 0)
     far_own = jnp.where(swaps, jnp.where(homes[1] >> 1 != rank, 1, 0), of_slot)
     numbers[NEAR] = 1 - far_own
@@ -115,8 +113,8 @@
     numbers[CHIP + 1] = rank % RING
     numbers[CHIP + 2] = place // 2
     numbers[CHIP + 3] = place % 2
-    for copy in copies:
-        copy.wait()
+    numbers[NEAR_SLOT] = 1 - far_slot
+    copy.wait()
 
 
 def route(tiles, image_slot, image):
@@ -124,38 +122,42 @@
     return pl.pallas_call(
         route_kernel,
         in_specs=[SMEM, SMEM, HBM],
-        out_specs=[SMEM, VMEM, VMEM],
-        out_shape=[jax.ShapeDtypeStruct((CHIP + 4,), jnp.int32), rows, rows],
-        scratch_shapes=[pltpu.SemaphoreType.DMA((2,))],
+        out_specs=[SMEM, VMEM],
+        out_shape=[jax.ShapeDtypeStruct((NEAR_SLOT + 1,), jnp.int32), rows],
+        scratch_shapes=[pltpu.SemaphoreType.DMA],
         compiler_params=pltpu.CompilerParams(vmem_limit_bytes=60 * 1024 * 1024),
         cost_estimate=pl.CostEstimate(flops=0, bytes_accessed=4 * image.size, transcendentals=0),
     )(tiles, image_slot, image)
 
 
-def lay_kernel(numbers, key_ref, value_ref, out_ref, sems):
+def lay_kernel(numbers, image_ref, key_ref, value_ref, near_ref, out_ref, sems):
     head_dim = key_ref.shape[1]
-    copies = []
+    copies = [pltpu.make_async_copy(image_ref.at[numbers[NEAR_SLOT]], near_ref, sems.at[2])]
+    copies[0].start()
     for i, source in enumerate((key_ref, value_ref)):
         target = out_ref.at[:, pl.ds(i * head_dim, head_dim)]
         copies.append(pltpu.make_async_copy(source, target, sems.at[i]))
-        copies[i].start()
+        copies[1 + i].start()
     for copy in copies:
         copy.wait()
 
 
-def lay(numbers, key_weights, value_weights):
+def lay(numbers, image, key_weights, value_weights):
     count, head_dim = key_weights.shape
     return pl.pallas_call(
         lay_kernel,
-        in_specs=[SMEM, ANY, ANY],
-        out_specs=VMEM,
-        out_shape=jax.ShapeDtypeStruct((count, 2 * head_dim), key_weights.dtype),
-        scratch_shapes=[pltpu.SemaphoreType.DMA((2,))],
+        in_specs=[SMEM, HBM, HBM, HBM],
+        out_specs=[VMEM, VMEM],
+        out_shape=[
+            jax.ShapeDtypeStruct(image.shape[1:], image.dtype),
+            jax.ShapeDtypeStruct((count, 2 * head_dim), key_weights.dtype),
+        ],
+        scratch_shapes=[pltpu.SemaphoreType.DMA((3,))],
         compiler_params=PARAMS,
         cost_estimate=pl.CostEstimate(
             flops=0, bytes_accessed=8 * count * head_dim, transcendentals=0
         ),
-    )(numbers, key_weights, value_weights)
+    )(numbers, image, key_weights, value_weights)
 
 
 def assemble_kernel(chip, *refs):
@@ -408,13 +410,13 @@
     cotangent,
 ):
     ratio = jnp.tanh(gate)
-    numbers, far_own, near_own = route(tiles, image_slot, image)
+    numbers, far_own = route(tiles, image_slot, image)
 
     def opposite(after, before, move):
         half = after.shape[0] // 2
         return [move(after[:half], 1), move(before[half:], 3)]
 
-    shard = lay(numbers, key_weight_matrix, value_weight_matrix)
+    near_own, shard = lay(numbers, image, key_weight_matrix, value_weight_matrix)
     far_x = [along_x(far_own, 1), along_x(far_own, 3)]
     shard = jnp.concatenate(gathered(shard, inner), axis=0)
     shard, *far_x = lax.optimization_barrier((shard, *far_x))
@@ -453,7 +455,7 @@
     *earlier, far_grad = attend(FAR, *shared, far_key_value, away, query_gain, ())
     back = along_z(far_grad, RING // 2)
 
-    _, *near_halves = lax.optimization_barrier((far_grad, *near_halves))
+    back, *near_halves = lax.optimization_barrier((back, *near_halves))
     blocks = [*near_x, jnp.concatenate(near_halves, axis=0)]
     near_others.append(other_core(blocks[2]))
     near_feats = paired(near_own, other_core(near_own), *blocks, *near_others)
@@ -463,7 +465,6 @@
         NEAR, *shared, near_key_value, near_key_value, query_gain, earlier
     )
     near_rows = turn(NEAR, numbers, near_total, near_grad, near_grad, key_gain)
-    back, near_rows = lax.optimization_barrier((back, near_rows))
     far_rows = turn(FAR, numbers, far_total, far_grad, back, key_gain)
 
     blocks = product(numbers, far_feats, near_feats, far_rows, near_rows)

time: 153 us -> 148 us (0.967)
  waiting for transfers between devices: 81.3 us -> 71.6 us
  starting transfers between devices: 36.7 us -> 40.1 us
  local copies, waits for them, and re-layouts: 3.66 us -> 5.25 us
    ppermute x12, waiting for transfers between devices: 49.6 us -> 44 us  [by_core(): return lax.ppermute(x, ('dp', 'tensor'), pairs)]
    ppermute x8, waiting for transfers between devices: 29.8 us -> 25.7 us  [along_x(): return lax.ppermute(x, 'tensor', pairs)]
    ppermute x2, starting transfers between devices: 3.95 us -> 6.69 us  [along_z(): return lax.ppermute(x, 'dp', pairs)]
    unnamed x22, local copies, waits for them, and re-layouts: 2.57 us -> 4.16 us
  transfers between devices with their start and end apart: 30 -> 30, of which waited for: 19 -> 20; matrix products, arithmetic and copies ran while one was open for 5% -> 5% of each run, Pallas kernels for 6% -> 4%
where the time goes in v10:
time: 148 us; the launch traced here: 146 us
  waiting for transfers between devices  71.6 us (48%)
  starting transfers between devices  40.1 us (27%)
  Pallas kernels  19.5 us (13%)
  matrix products  7.29 us (5%)
  local copies, waits for them, and re-layouts  5.25 us (4%)
  between operations  1.75 us (1%)
    ppermute x12, waiting for transfers between devices, by_core(): return lax.ppermute(x, ('dp', 'tensor'), pairs)  44 us
    ppermute x8, waiting for transfers between devices, along_x(): return lax.ppermute(x, 'tensor', pairs)  25.7 us
    ppermute x12, starting transfers between devices, by_core(): return lax.ppermute(x, ('dp', 'tensor'), pairs)  23.6 us
    ppermute x8, starting transfers between devices, along_x(): return lax.ppermute(x, 'tensor', pairs)  8.31 us
    dot_general x16, matrix products, matmul(): lax.dot_general(a, b, (contract, ((), ())), preferred_element_type=jnp.fl...  7.29 us
    pallas_call x2, Pallas kernels, attend(): pl.pallas_call(functools.partial(attend_kernel, heads, base), grid_spec=p...  6.81 us
    ppermute x2, starting transfers between devices, along_z(): return lax.ppermute(x, 'dp', pairs)  6.69 us
    pallas_call x1, Pallas kernels, product(): pl.pallas_call(product_kernel, in_specs=[SMEM] + [VMEM] * (2 * len(feats)...  5.94 us
  transfers between devices with their start and end apart: 30, of which 20 were waited for; matrix products, arithmetic and copies ran while one was open for 5% of the time, Pallas kernels for 4%

profile of v10, /device:TPU:4, one launch (start us, length us, event | category | flops | bytes accessed | tf_op | source)
XLA Modules:
  0.0 146.3 jit_solution(16338551681579662762)
XLA Ops:
  0.6 2.9 %shard_map.129 = (s32[11]{0:T(128)}, bf16[512,1024]{1,0:T(8,128)(2,1)}) custom-call(s32[32]{0:T(128)} %tiles.1, s32[32]{0:T(128)} %slots.1, bf16[2,512,1024]{2,1,0:T(8,128)(2,1)} %image_ref.3), custom_call_target="tpu_custom_call" | custom-call | bytes 4194304 | tf_op jit(solution)/shard_map/pallas_call | solution.py:122
  10.4 4.1 %collective-permute-start.2 = (bf16[512,256]{1,0:T(8,128)(2,1)S(1)}, bf16[512,256]{1,0:T(8,128)(2,1)S(1)}, u32[]{:S(2)}, u32[]{:S(2)}) collective-permute-start(bf16[512,256]{1,0:T(8,128)(2,1)S(1)} %get-tuple-element.39), channel_id=1, source_target_pairs={{0,96},{1,25},{2,98},{3,27},{4,100},{5,29},{6,102},{7,31},{8,104},... | collective-permute-start | bytes 786440 | tf_op jit(solution)/shard_map/ppermute | solution.py:30
  15.8 5.4 %collective-permute-done.2 = bf16[512,256]{1,0:T(8,128)(2,1)S(1)} collective-permute-done((bf16[512,256]{1,0:T(8,128)(2,1)S(1)}, bf16[512,256]{1,0:T(8,128)(2,1)S(1)}, u32[]{:S(2)}, u32[]{:S(2)}) %collective-permute-start.2) | collective-permute-done | bytes 262176 | tf_op jit(solution)/shard_map/ppermute | solution.py:30
  22.5 2.4 %collective-permute-done = bf16[512,256]{1,0:T(8,128)(2,1)S(1)} collective-permute-done((bf16[512,256]{1,0:T(8,128)(2,1)S(1)}, bf16[512,256]{1,0:T(8,128)(2,1)S(1)}, u32[]{:S(2)}, u32[]{:S(2)}) %collective-permute-start) | collective-permute-done | bytes 262176 | tf_op jit(solution)/shard_map/ppermute | solution.py:30
  25.0 3.8 %collective-permute-done.3.refs_2_ = bf16[512,1024]{1,0:T(8,128)(2,1)S(1)} collective-permute-done((bf16[512,1024]{1,0:T(8,128)(2,1)}, bf16[512,1024]{1,0:T(8,128)(2,1)S(1)}, u32[]{:S(2)}, u32[]{:S(2)}) %collective-permute-start.3) | collective-permute-done | bytes 1048608 | tf_op jit(solution)/shard_map/ppermute | solution.py:43
  31.3 2.9 %collective-permute-start.8 = (bf16[2048,256]{1,0:T(8,128)(2,1)S(1)}, bf16[2048,256]{1,0:T(8,128)(2,1)S(1)}, u32[]{:S(2)}, u32[]{:S(2)}) collective-permute-start(bf16[2048,256]{1,0:T(8,128)(2,1)S(1)} %pad_maximum_fusion.refs_0_), channel_id=1, source_target_pairs={{0,16},{1,65},{2,18},{3,67},{4,20},{5,69},{6,22},{7,71},{8,24},{9,... | collective-permute-start | bytes 3145736 | tf_op jit(solution)/shard_map/ppermute | solution.py:30
  38.4 9.5 %collective-permute-done.5 = bf16[256,1024]{1,0:T(8,128)(2,1)S(1)} collective-permute-done((bf16[256,1024]{1,0:T(8,128)(2,1)S(1)}, bf16[256,1024]{1,0:T(8,128)(2,1)S(1)}, u32[]{:S(2)}, u32[]{:S(2)}) %collective-permute-start.5) | collective-permute-done | bytes 524320 | tf_op jit(solution)/shard_map/ppermute | solution.py:43
  49.5 1.8 %collective-permute-start.14 = (bf16[512,1024]{1,0:T(8,128)(2,1)S(1)}, bf16[512,1024]{1,0:T(8,128)(2,1)S(1)}, u32[]{:S(2)}, u32[]{:S(2)}) collective-permute-start(bf16[512,1024]{1,0:T(8,128)(2,1)S(1)} %get-tuple-element.52.refs_8_), channel_id=1, source_target_pairs={{0,2},{1,3},{2,4},{3,5},{4,6},{5,7},{6,0},{7,1},{8,10},{9,11},{10,... | collective-permute-start | bytes 3145736 | tf_op jit(solution)/shard_map/ppermute | solution.py:43
  51.5 6.7 %collective-permute-done.8.refs_2_ = bf16[2048,256]{1,0:T(8,128)(2,1)S(1)} collective-permute-done((bf16[2048,256]{1,0:T(8,128)(2,1)S(1)}, bf16[2048,256]{1,0:T(8,128)(2,1)S(1)}, u32[]{:S(2)}, u32[]{:S(2)}) %collective-permute-start.8) | collective-permute-done | bytes 1048608 | tf_op jit(solution)/shard_map/ppermute | solution.py:30
  65.8 4.0 %collective-permute-start.19 = (bf16[512,256]{1,0:T(8,128)(2,1)S(1)}, bf16[512,256]{1,0:T(8,128)(2,1)S(1)}, u32[]{:S(2)}, u32[]{:S(2)}) collective-permute-start(bf16[512,256]{1,0:T(8,128)(2,1)S(1)} %shard_map.132.kv_ref), channel_id=1, source_target_pairs={{0,64},{8,72},{16,80},{24,88},{32,96},{40,104},{48,112},{56,120},{... | collective-permute-start | bytes 786440 | tf_op jit(solution)/shard_map/ppermute | solution.py:17
  69.8 2.0 %collective-permute-done.14.refs_10_ = bf16[512,1024]{1,0:T(8,128)(2,1)S(1)} collective-permute-done((bf16[512,1024]{1,0:T(8,128)(2,1)S(1)}, bf16[512,1024]{1,0:T(8,128)(2,1)S(1)}, u32[]{:S(2)}, u32[]{:S(2)}) %collective-permute-start.14) | collective-permute-done | bytes 1048608 | tf_op jit(solution)/shard_map/ppermute | solution.py:43
  71.8 1.9 %collective-permute-done.15.refs_14_ = bf16[512,1024]{1,0:T(8,128)(2,1)S(1)} collective-permute-done((bf16[512,1024]{1,0:T(8,128)(2,1)S(1)}, bf16[512,1024]{1,0:T(8,128)(2,1)S(1)}, u32[]{:S(2)}, u32[]{:S(2)}) %collective-permute-start.15) | collective-permute-done | bytes 1048608 | tf_op jit(solution)/shard_map/ppermute | solution.py:43
  76.9 3.4 %shard_map.133 = (bf16[2,128,1024]{2,1,0:T(8,128)(2,1)}, bf16[2,128,1024]{2,1,0:T(8,128)(2,1)}, bf16[512,256]{1,0:T(8,128)(2,1)S(1)}) custom-call(s32[11]{0:T(128)S(1)} %copy-done.5, f32[1]{0:T(128)S(6)} %tanh.3.ratio_ref, bf16[2,128,1024]{2,1,0:T(8,128)(2,1)S(1)} %copy-done.7, bf16[2,128,1024]{2,1,0:T(8,128)(2,1)S(1)} %copy-done.8, ...), custom_call_target="tpu_custom_call" | custom-call | flops 939524096 | bytes 1441792 | tf_op jit(solution)/shard_map/pallas_call | solution.py:365
  80.3 2.7 %collective-permute-start.20 = (bf16[512,256]{1,0:T(8,128)(2,1)S(1)}, bf16[512,256]{1,0:T(8,128)(2,1)S(1)}, u32[]{:S(2)}, u32[]{:S(2)}) collective-permute-start(bf16[512,256]{1,0:T(8,128)(2,1)S(1)} %get-tuple-element.55.grad_ref), channel_id=1, source_target_pairs={{0,64},{8,72},{16,80},{24,88},{32,96},{40,104},{48,112},{56,120},{... | collective-permute-start | bytes 786440 | tf_op jit(solution)/shard_map/ppermute | solution.py:17
  83.5 4.8 %collective-permute-done.21 = bf16[256,1024]{1,0:T(8,128)(2,1)S(1)} collective-permute-done((bf16[256,1024]{1,0:T(8,128)(2,1)S(1)}, bf16[256,1024]{1,0:T(8,128)(2,1)S(1)}, u32[]{:S(2)}, u32[]{:S(2)}) %collective-permute-start.21) | collective-permute-done | bytes 524320 | tf_op jit(solution)/shard_map/ppermute | solution.py:43
  93.9 3.4 %shard_map.135 = (bf16[2,128,1024]{2,1,0:T(8,128)(2,1)}, bf16[2,128,1024]{2,1,0:T(8,128)(2,1)}, bf16[512,256]{1,0:T(8,128)(2,1)S(1)}) custom-call(s32[11]{0:T(128)S(1)} %copy-done.5, f32[1]{0:T(128)S(6)} %tanh.3.ratio_ref, bf16[2,128,1024]{2,1,0:T(8,128)(2,1)S(1)} %copy-done.7, ...), custom_call_target="tpu_custom_call", output_to_operand_aliasing={{0}: (7, {}), {1}: (8, {})} | custom-call | flops 939524096 | bytes 1441792 | tf_op jit(solution)/shard_map/pallas_call | solution.py:365
  98.1 5.9 %shard_map.138 = (bf16[2048,256]{1,0:T(8,128)(2,1)S(1)}, bf16[2048,256]{1,0:T(8,128)(2,1)S(1)}, bf16[2048,256]{1,0:T(8,128)(2,1)S(1)}, bf16[2048,256]{1,0:T(8,128)(2,1)S(1)}) custom-call(s32[11]{0:T(128)S(1)} %copy-done.5, bf16[512,1024]{1,0:T(8,128)(2,1)S(1)} %copy-done.1, bf16[512,1024]{1,0:T(8,128)(2,1)S(1)} %collective-permute-done.10.refs_1_, ...), custom_call_target="tpu_custom_call" | custom-call | flops 4294967296 | bytes 16777216 | tf_op jit(solution)/shard_map/pallas_call | solution.py:272
  104.0 5.2 %collective-permute-start.26 = (bf16[2048,256]{1,0:T(8,128)(2,1)S(1)}, bf16[2048,256]{1,0:T(8,128)(2,1)S(1)}, u32[]{:S(2)}, u32[]{:S(2)}) collective-permute-start(bf16[2048,256]{1,0:T(8,128)(2,1)S(1)} %get-tuple-element.67), channel_id=1, source_target_pairs={{0,16},{1,65},{2,18},{3,67},{4,20},{5,69},{6,22},{7,71},{8,24},{9,... | collective-permute-start | bytes 3145736 | tf_op jit(solution)/shard_map/ppermute | solution.py:30
  109.9 2.6 %collective-permute-start.24 = (bf16[2048,256]{1,0:T(8,128)(2,1)S(1)}, bf16[2048,256]{1,0:T(8,128)(2,1)S(1)}, u32[]{:S(2)}, u32[]{:S(2)}) collective-permute-start(bf16[2048,256]{1,0:T(8,128)(2,1)S(1)} %get-tuple-element.65), channel_id=1, source_target_pairs={{0,24},{1,97},{2,26},{3,99},{4,28},{5,101},{6,30},{7,103},{8,0},{9... | collective-permute-start | bytes 3145736 | tf_op jit(solution)/shard_map/ppermute | solution.py:30
  112.4 9.6 %collective-permute-done.26 = bf16[2048,256]{1,0:T(8,128)(2,1)S(1)} collective-permute-done((bf16[2048,256]{1,0:T(8,128)(2,1)S(1)}, bf16[2048,256]{1,0:T(8,128)(2,1)S(1)}, u32[]{:S(2)}, u32[]{:S(2)}) %collective-permute-start.26) | collective-permute-done | bytes 1048608 | tf_op jit(solution)/shard_map/ppermute | solution.py:30
  122.1 11.1 %collective-permute-done.25 = bf16[2048,256]{1,0:T(8,128)(2,1)S(1)} collective-permute-done((bf16[2048,256]{1,0:T(8,128)(2,1)S(1)}, bf16[2048,256]{1,0:T(8,128)(2,1)S(1)}, u32[]{:S(2)}, u32[]{:S(2)}) %collective-permute-start.25) | collective-permute-done | bytes 1048608 | tf_op jit(solution)/shard_map/ppermute | solution.py:30
  136.1 2.5 %collective-permute-start.27 = (bf16[512,256]{1,0:T(8,128)(2,1)S(1)}, bf16[512,256]{1,0:T(8,128)(2,1)S(1)}, u32[]{:S(2)}, u32[]{:S(2)}) collective-permute-start(bf16[512,256]{1,0:T(8,128)(2,1)S(1)} %get-tuple-element.70), channel_id=1, source_target_pairs={{0,96},{1,25},{2,98},{3,27},{4,100},{5,29},{6,102},{7,31},{8,104},... | collective-permute-start | bytes 786440 | tf_op jit(solution)/shard_map/ppermute | solution.py:30
  138.6 4.0 %collective-permute-done.29 = bf16[512,256]{1,0:T(8,128)(2,1)S(1)} collective-permute-done((bf16[512,256]{1,0:T(8,128)(2,1)S(1)}, bf16[512,256]{1,0:T(8,128)(2,1)S(1)}, u32[]{:S(2)}, u32[]{:S(2)}) %collective-permute-start.29) | collective-permute-done | bytes 262176 | tf_op jit(solution)/shard_map/ppermute | solution.py:30
  142.7 2.7 %collective-permute-done.28 = bf16[512,256]{1,0:T(8,128)(2,1)S(1)} collective-permute-done((bf16[512,256]{1,0:T(8,128)(2,1)S(1)}, bf16[512,256]{1,0:T(8,128)(2,1)S(1)}, u32[]{:S(2)}, u32[]{:S(2)}) %collective-permute-start.28) | collective-permute-done | bytes 262176 | tf_op jit(solution)/shard_map/ppermute | solution.py:30
  (95 shorter events, 39.2 us)
Async XLA Ops:
  3.6 25.2 %collective-permute-start.3 = (bf16[512,1024]{1,0:T(8,128)(2,1)}, bf16[512,1024]{1,0:T(8,128)(2,1)S(1)}, u32[]{:S(2)}, u32[]{:S(2)}) collective-permute-start(bf16[512,1024]{1,0:T(8,128)(2,1)} %get-tuple-element.42.refs_0_), channel_id=1, source_target_pairs={{0,2},{1,3},{2,4},{3,5},{4,6},{5,7},{6,0},{7,1},{8,10},{9,11},{10,... | collective-permute-start | bytes 3145736 | tf_op jit(solution)/shard_map/ppermute | solution.py:43
  4.9 24.8 %collective-permute-start.4 = (bf16[512,1024]{1,0:T(8,128)(2,1)}, bf16[512,1024]{1,0:T(8,128)(2,1)S(1)}, u32[]{:S(2)}, u32[]{:S(2)}) collective-permute-start(bf16[512,1024]{1,0:T(8,128)(2,1)} %get-tuple-element.42.refs_0_), channel_id=1, source_target_pairs={{0,6},{1,7},{2,0},{3,1},{4,2},{5,3},{6,4},{7,5},{8,14},{9,15},{10,... | collective-permute-start | bytes 3145736 | tf_op jit(solution)/shard_map/ppermute | solution.py:43
  10.4 10.8 %collective-permute-start.2 = (bf16[512,256]{1,0:T(8,128)(2,1)S(1)}, bf16[512,256]{1,0:T(8,128)(2,1)S(1)}, u32[]{:S(2)}, u32[]{:S(2)}) collective-permute-start(bf16[512,256]{1,0:T(8,128)(2,1)S(1)} %get-tuple-element.39), channel_id=1, source_target_pairs={{0,96},{1,25},{2,98},{3,27},{4,100},{5,29},{6,102},{7,31},{8,104},... | collective-permute-start | bytes 786440 | tf_op jit(solution)/shard_map/ppermute | solution.py:30
  14.6 10.4 %collective-permute-start = (bf16[512,256]{1,0:T(8,128)(2,1)S(1)}, bf16[512,256]{1,0:T(8,128)(2,1)S(1)}, u32[]{:S(2)}, u32[]{:S(2)}) collective-permute-start(bf16[512,256]{1,0:T(8,128)(2,1)S(1)} %get-tuple-element.39), channel_id=1, source_target_pairs={{0,32},{1,9},{2,34},{3,11},{4,36},{5,13},{6,38},{7,15},{8,40},{9,1... | collective-permute-start | bytes 786440 | tf_op jit(solution)/shard_map/ppermute | solution.py:30
  29.7 21.8 %collective-permute-start.7 = (bf16[2048,256]{1,0:T(8,128)(2,1)S(1)}, bf16[2048,256]{1,0:T(8,128)(2,1)S(1)}, u32[]{:S(2)}, u32[]{:S(2)}) collective-permute-start(bf16[2048,256]{1,0:T(8,128)(2,1)S(1)} %pad_maximum_fusion.refs_0_), channel_id=1, source_target_pairs={{0,8},{1,33},{2,10},{3,35},{4,12},{5,37},{6,14},{7,39},{8,16},{9,4... | collective-permute-start | bytes 3145736 | tf_op jit(solution)/shard_map/ppermute | solution.py:30
  31.3 26.9 %collective-permute-start.8 = (bf16[2048,256]{1,0:T(8,128)(2,1)S(1)}, bf16[2048,256]{1,0:T(8,128)(2,1)S(1)}, u32[]{:S(2)}, u32[]{:S(2)}) collective-permute-start(bf16[2048,256]{1,0:T(8,128)(2,1)S(1)} %pad_maximum_fusion.refs_0_), channel_id=1, source_target_pairs={{0,16},{1,65},{2,18},{3,67},{4,20},{5,69},{6,22},{7,71},{8,24},{9,... | collective-permute-start | bytes 3145736 | tf_op jit(solution)/shard_map/ppermute | solution.py:30
  34.2 24.0 %collective-permute-start.9 = (bf16[2048,256]{1,0:T(8,128)(2,1)S(1)}, bf16[2048,256]{1,0:T(8,128)(2,1)S(1)}, u32[]{:S(2)}, u32[]{:S(2)}) collective-permute-start(bf16[2048,256]{1,0:T(8,128)(2,1)S(1)} %pad_maximum_fusion.refs_0_), channel_id=1, source_target_pairs={{0,24},{1,97},{2,26},{3,99},{4,28},{5,101},{6,30},{7,103},{8,0},{9... | collective-permute-start | bytes 3145736 | tf_op jit(solution)/shard_map/ppermute | solution.py:30
  35.5 12.4 %collective-permute-start.5 = (bf16[256,1024]{1,0:T(8,128)(2,1)S(1)}, bf16[256,1024]{1,0:T(8,128)(2,1)S(1)}, u32[]{:S(2)}, u32[]{:S(2)}) collective-permute-start(bf16[256,1024]{1,0:T(8,128)(2,1)S(1)} %slice.65), channel_id=1, source_target_pairs={{0,2},{1,3},{2,4},{3,5},{4,6},{5,7},{6,0},{7,1},{8,10},{9,11},{10,... | collective-permute-start | bytes 1572872 | tf_op jit(solution)/shard_map/ppermute | solution.py:43
  37.3 12.1 %collective-permute-start.6 = (bf16[256,1024]{1,0:T(8,128)(2,1)S(1)}, bf16[256,1024]{1,0:T(8,128)(2,1)S(1)}, u32[]{:S(2)}, u32[]{:S(2)}) collective-permute-start(bf16[256,1024]{1,0:T(8,128)(2,1)S(1)} %slice.66), channel_id=1, source_target_pairs={{0,6},{1,7},{2,0},{3,1},{4,2},{5,3},{6,4},{7,5},{8,14},{9,15},{10,... | collective-permute-start | bytes 1572872 | tf_op jit(solution)/shard_map/ppermute | solution.py:43
  49.5 22.3 %collective-permute-start.14 = (bf16[512,1024]{1,0:T(8,128)(2,1)S(1)}, bf16[512,1024]{1,0:T(8,128)(2,1)S(1)}, u32[]{:S(2)}, u32[]{:S(2)}) collective-permute-start(bf16[512,1024]{1,0:T(8,128)(2,1)S(1)} %get-tuple-element.52.refs_8_), channel_id=1, source_target_pairs={{0,2},{1,3},{2,4},{3,5},{4,6},{5,7},{6,0},{7,1},{8,10},{9,11},{10,... | collective-permute-start | bytes 3145736 | tf_op jit(solution)/shard_map/ppermute | solution.py:43
  51.3 22.4 %collective-permute-start.15 = (bf16[512,1024]{1,0:T(8,128)(2,1)S(1)}, bf16[512,1024]{1,0:T(8,128)(2,1)S(1)}, u32[]{:S(2)}, u32[]{:S(2)}) collective-permute-start(bf16[512,1024]{1,0:T(8,128)(2,1)S(1)} %get-tuple-element.52.refs_8_), channel_id=1, source_target_pairs={{0,6},{1,7},{2,0},{3,1},{4,2},{5,3},{6,4},{7,5},{8,14},{9,15},{10,... | collective-permute-start | bytes 3145736 | tf_op jit(solution)/shard_map/ppermute | solution.py:43
  51.5 10.0 %collective-permute-start.10 = (bf16[512,1024]{1,0:T(8,128)(2,1)S(1)}, bf16[512,1024]{1,0:T(8,128)(2,1)S(1)}, u32[]{:S(2)}, u32[]{:S(2)}) collective-permute-start(bf16[512,1024]{1,0:T(8,128)(2,1)S(1)} %copy-done.1), channel_id=1, source_target_pairs={{0,1},{1,0},{2,3},{3,2},{4,5},{5,4},{6,7},{7,6},{8,9},{9,8},{10,11... | collective-permute-start | bytes 3145736 | tf_op jit(solution)/shard_map/ppermute | solution.py:47
  65.8 11.1 %collective-permute-start.19 = (bf16[512,256]{1,0:T(8,128)(2,1)S(1)}, bf16[512,256]{1,0:T(8,128)(2,1)S(1)}, u32[]{:S(2)}, u32[]{:S(2)}) collective-permute-start(bf16[512,256]{1,0:T(8,128)(2,1)S(1)} %shard_map.132.kv_ref), channel_id=1, source_target_pairs={{0,64},{8,72},{16,80},{24,88},{32,96},{40,104},{48,112},{56,120},{... | collective-permute-start | bytes 786440 | tf_op jit(solution)/shard_map/ppermute | solution.py:17
  73.7 16.6 %collective-permute-start.18 = (bf16[512,1024]{1,0:T(8,128)(2,1)S(1)}, bf16[512,1024]{1,0:T(8,128)(2,1)S(1)}, u32[]{:S(2)}, u32[]{:S(2)}) collective-permute-start(bf16[512,1024]{1,0:T(8,128)(2,1)S(1)} %collective-permute-done.15.refs_14_), channel_id=1, source_target_pairs={{0,1},{1,0},{2,3},{3,2},{4,5},{5,4},{6,7},{7,6},{8,9},{9,8},{10,11... | collective-permute-start | bytes 3145736 | tf_op jit(solution)/shard_map/ppermute | solution.py:47
  73.8 17.0 %collective-permute-start.17 = (bf16[512,1024]{1,0:T(8,128)(2,1)S(1)}, bf16[512,1024]{1,0:T(8,128)(2,1)S(1)}, u32[]{:S(2)}, u32[]{:S(2)}) collective-permute-start(bf16[512,1024]{1,0:T(8,128)(2,1)S(1)} %collective-permute-done.14.refs_10_), channel_id=1, source_target_pairs={{0,1},{1,0},{2,3},{3,2},{4,5},{5,4},{6,7},{7,6},{8,9},{9,8},{10,11... | collective-permute-start | bytes 3145736 | tf_op jit(solution)/shard_map/ppermute | solution.py:47
  74.4 13.9 %collective-permute-start.21 = (bf16[256,1024]{1,0:T(8,128)(2,1)S(1)}, bf16[256,1024]{1,0:T(8,128)(2,1)S(1)}, u32[]{:S(2)}, u32[]{:S(2)}) collective-permute-start(bf16[256,1024]{1,0:T(8,128)(2,1)S(1)} %slice.75), channel_id=1, source_target_pairs={{0,2},{1,3},{2,4},{3,5},{4,6},{5,7},{6,0},{7,1},{8,10},{9,11},{10,... | collective-permute-start | bytes 1572872 | tf_op jit(solution)/shard_map/ppermute | solution.py:43
  76.1 13.6 %collective-permute-start.22 = (bf16[256,1024]{1,0:T(8,128)(2,1)S(1)}, bf16[256,1024]{1,0:T(8,128)(2,1)S(1)}, u32[]{:S(2)}, u32[]{:S(2)}) collective-permute-start(bf16[256,1024]{1,0:T(8,128)(2,1)S(1)} %slice.76), channel_id=1, source_target_pairs={{0,6},{1,7},{2,0},{3,1},{4,2},{5,3},{6,4},{7,5},{8,14},{9,15},{10,... | collective-permute-start | bytes 1572872 | tf_op jit(solution)/shard_map/ppermute | solution.py:43
  80.3 9.4 %collective-permute-start.20 = (bf16[512,256]{1,0:T(8,128)(2,1)S(1)}, bf16[512,256]{1,0:T(8,128)(2,1)S(1)}, u32[]{:S(2)}, u32[]{:S(2)}) collective-permute-start(bf16[512,256]{1,0:T(8,128)(2,1)S(1)} %get-tuple-element.55.grad_ref), channel_id=1, source_target_pairs={{0,64},{8,72},{16,80},{24,88},{32,96},{40,104},{48,112},{56,120},{... | collective-permute-start | bytes 786440 | tf_op jit(solution)/shard_map/ppermute | solution.py:17
  104.0 18.1 %collective-permute-start.26 = (bf16[2048,256]{1,0:T(8,128)(2,1)S(1)}, bf16[2048,256]{1,0:T(8,128)(2,1)S(1)}, u32[]{:S(2)}, u32[]{:S(2)}) collective-permute-start(bf16[2048,256]{1,0:T(8,128)(2,1)S(1)} %get-tuple-element.67), channel_id=1, source_target_pairs={{0,16},{1,65},{2,18},{3,67},{4,20},{5,69},{6,22},{7,71},{8,24},{9,... | collective-permute-start | bytes 3145736 | tf_op jit(solution)/shard_map/ppermute | solution.py:30
  109.2 24.0 %collective-permute-start.25 = (bf16[2048,256]{1,0:T(8,128)(2,1)S(1)}, bf16[2048,256]{1,0:T(8,128)(2,1)S(1)}, u32[]{:S(2)}, u32[]{:S(2)}) collective-permute-start(bf16[2048,256]{1,0:T(8,128)(2,1)S(1)} %get-tuple-element.66), channel_id=1, source_target_pairs={{0,8},{1,33},{2,10},{3,35},{4,12},{5,37},{6,14},{7,39},{8,16},{9,4... | collective-permute-start | bytes 3145736 | tf_op jit(solution)/shard_map/ppermute | solution.py:30
  109.9 24.1 %collective-permute-start.24 = (bf16[2048,256]{1,0:T(8,128)(2,1)S(1)}, bf16[2048,256]{1,0:T(8,128)(2,1)S(1)}, u32[]{:S(2)}, u32[]{:S(2)}) collective-permute-start(bf16[2048,256]{1,0:T(8,128)(2,1)S(1)} %get-tuple-element.65), channel_id=1, source_target_pairs={{0,24},{1,97},{2,26},{3,99},{4,28},{5,101},{6,30},{7,103},{8,0},{9... | collective-permute-start | bytes 3145736 | tf_op jit(solution)/shard_map/ppermute | solution.py:30
  134.6 8.1 %collective-permute-start.29 = (bf16[512,256]{1,0:T(8,128)(2,1)S(1)}, bf16[512,256]{1,0:T(8,128)(2,1)S(1)}, u32[]{:S(2)}, u32[]{:S(2)}) collective-permute-start(bf16[512,256]{1,0:T(8,128)(2,1)S(1)} %get-tuple-element.71), channel_id=1, source_target_pairs={{0,64},{1,17},{2,66},{3,19},{4,68},{5,21},{6,70},{7,23},{8,72},{9,... | collective-permute-start | bytes 786440 | tf_op jit(solution)/shard_map/ppermute | solution.py:30
  134.9 10.5 %collective-permute-start.28 = (bf16[512,256]{1,0:T(8,128)(2,1)S(1)}, bf16[512,256]{1,0:T(8,128)(2,1)S(1)}, u32[]{:S(2)}, u32[]{:S(2)}) collective-permute-start(bf16[512,256]{1,0:T(8,128)(2,1)S(1)} %get-tuple-element.72), channel_id=1, source_target_pairs={{0,32},{1,9},{2,34},{3,11},{4,36},{5,13},{6,38},{7,15},{8,40},{9,1... | collective-permute-start | bytes 786440 | tf_op jit(solution)/shard_map/ppermute | solution.py:30
  136.1 9.3 %collective-permute-start.27 = (bf16[512,256]{1,0:T(8,128)(2,1)S(1)}, bf16[512,256]{1,0:T(8,128)(2,1)S(1)}, u32[]{:S(2)}, u32[]{:S(2)}) collective-permute-start(bf16[512,256]{1,0:T(8,128)(2,1)S(1)} %get-tuple-element.70), channel_id=1, source_target_pairs={{0,96},{1,25},{2,98},{3,27},{4,100},{5,29},{6,102},{7,31},{8,104},... | collective-permute-start | bytes 786440 | tf_op jit(solution)/shard_map/ppermute | solution.py:30
  (16 other events, 166.3 us)

commit v11 on v10

--- a/solution.py
+++ b/solution.py
@@ -217,39 +217,27 @@
     )(total, gain[None, :])
 
 
-def turn_kernel(base, numbers, total_ref, grad_ref, other_ref, gain_ref, out_ref):
-    head_dim = gain_ref.shape[1]
-    grad = jnp.where(numbers[base + 2] != 0, other_ref[...], grad_ref[...])
-    raw = total_ref[:, :head_dim]
-    d_raw = norm_back(raw, rms_factor(raw), gain_ref[...], grad[:, :head_dim].astype(jnp.float32))
-    out_ref[:, :head_dim] = d_raw.astype(jnp.bfloat16)
-    out_ref[:, head_dim:] = grad[:, head_dim:]
-
-
-def turn(base, numbers, total, grad, other, gain):
-    return pl.pallas_call(
-        functools.partial(turn_kernel, base),
-        in_specs=[SMEM] + [VMEM] * 4,
-        out_specs=VMEM,
-        out_shape=jax.ShapeDtypeStruct(grad.shape, jnp.bfloat16),
-        compiler_params=PARAMS,
-        cost_estimate=pl.CostEstimate(
-            flops=6 * grad.size, bytes_accessed=8 * grad.size, transcendentals=grad.shape[0]
-        ),
-    )(numbers, total, grad, other, gain[None, :])
+def turned(total, grad, gain):
+    head_dim = gain.shape[1]
+    raw = total[:, :head_dim]
+    d_raw = norm_back(raw, rms_factor(raw), gain, grad[:, :head_dim].astype(jnp.float32))
+    return jnp.concatenate([d_raw.astype(jnp.bfloat16), grad[:, head_dim:]], axis=1)
 
 
 def product_kernel(chip, *refs):
     count = 2 * RING
-    first, second, (first_ref, second_ref) = refs[:count], refs[count : 2 * count], refs[2 * count : 2 * count + 2]
-    refs = refs[2 * count + 2 :]
+    first, second, refs = refs[:count], refs[count : 2 * count], refs[2 * count :]
+    first_total, first_grad, first_back, second_total, second_grad, gain_ref, *refs = refs
+    first_grads = jnp.where(chip[FAR + 2] != 0, first_back[...], first_grad[...])
+    first_grads = turned(first_total[...], first_grads, gain_ref[...])
+    second_grads = turned(second_total[...], second_grad[...], gain_ref[...])
     outs, (held, sems) = refs[:RING], refs[RING:]
     depth = first[0].shape[1]
     count = depth // 2
     z, y, x, core = (chip[CHIP + i] for i in range(4))
     for k in range(len(first)):
-        total = matmul(first[k][...], first_ref[...], ((0,), (0,)))
-        total = total + matmul(second[k][...], second_ref[...], ((0,), (0,)))
+        total = matmul(first[k][...], first_grads, ((0,), (0,)))
+        total = total + matmul(second[k][...], second_grads, ((0,), (0,)))
         total = total.astype(held.dtype)
         by_z = (x - k // 2 - z + 2 * RING) % RING
         for h in range(2):
@@ -265,13 +253,13 @@
         copy.wait()
 
 
-def product(chip, feats, others, grads, other_grads):
+def product(chip, feats, others, first, second, gain):
     rows, depth = feats[0].shape
-    both = grads.shape[1]
+    both = first[0].shape[1]
     shape = (RING * depth // 2, both)
     return pl.pallas_call(
         product_kernel,
-        in_specs=[SMEM] + [VMEM] * (2 * len(feats) + 2),
+        in_specs=[SMEM] + [VMEM] * (2 * len(feats) + 6),
         out_specs=[ANY] * RING,
         out_shape=[jax.ShapeDtypeStruct(shape, jnp.bfloat16)] * RING,
         scratch_shapes=[
@@ -284,7 +272,7 @@
             bytes_accessed=4 * len(feats) * rows * depth,
             transcendentals=0,
         ),
-    )(chip, *feats, *others, grads, other_grads)
+    )(chip, *feats, *others, *first, *second, gain[None, :])
 
 
 def attend_kernel(heads, base, index, ratio_ref, q_ref, cot_ref, kv_ref, away_ref, gain_ref, *refs):
@@ -451,6 +439,7 @@
     away = along_z(far_key_value, RING // 2)
     _, near_own, *near_x = lax.optimization_barrier((far_key_value, near_own, *near_x))
     near_halves = opposite(*near_x, along_x)
+    away, *near_x = lax.optimization_barrier((away, *near_x))
     near_others = other_cores(*near_x)
     *earlier, far_grad = attend(FAR, *shared, far_key_value, away, query_gain, ())
     back = along_z(far_grad, RING // 2)
@@ -464,10 +453,9 @@
     context, d_query, near_grad = attend(
         NEAR, *shared, near_key_value, near_key_value, query_gain, earlier
     )
-    near_rows = turn(NEAR, numbers, near_total, near_grad, near_grad, key_gain)
-    far_rows = turn(FAR, numbers, far_total, far_grad, back, key_gain)
-
-    blocks = product(numbers, far_feats, near_feats, far_rows, near_rows)
+
+    far, near = (far_total, far_grad, back), (near_total, near_grad)
+    blocks = product(numbers, far_feats, near_feats, far, near, key_gain)
     total = summed([blocks[0], *scattered(blocks, outer)])
     count = total.shape[0] // RING
     parts = [total[d * count : (d + 1) * count] for d in range(RING)]

time: 148 us -> 147 us (level)
    ppermute x8, waiting for transfers between devices: 25.7 us -> 21.1 us  [along_x(): return lax.ppermute(x, 'tensor', pairs)]
    ppermute x2, waiting for transfers between devices: 0.01 us -> 4.23 us  [along_z(): return lax.ppermute(x, 'dp', pairs)]
    pallas_call x2 -> x0, Pallas kernels: 1.51 us -> none  [turn(): pl.pallas_call(functools.partial(turn_kernel, base), in_specs=[SMEM] + [V...]
  transfers between devices with their start and end apart: 30 -> 30, of which waited for: 20 -> 22; matrix products, arithmetic and copies ran while one was open for 5% -> 5% of each run, Pallas kernels for 4% -> 4%
where the time goes in v11:
time: 147 us; the launch traced here: 145 us
  waiting for transfers between devices  71.3 us (49%)
  starting transfers between devices  40.4 us (27%)
  Pallas kernels  18.2 us (12%)
  matrix products  7.3 us (5%)
  local copies, waits for them, and re-layouts  5.25 us (4%)
  between operations  1.7 us (1%)
    ppermute x12, waiting for transfers between devices, by_core(): return lax.ppermute(x, ('dp', 'tensor'), pairs)  44.1 us
    ppermute x12, starting transfers between devices, by_core(): return lax.ppermute(x, ('dp', 'tensor'), pairs)  23.6 us
    ppermute x8, waiting for transfers between devices, along_x(): return lax.ppermute(x, 'tensor', pairs)  21.1 us
    ppermute x8, starting transfers between devices, along_x(): return lax.ppermute(x, 'tensor', pairs)  8.45 us
    dot_general x16, matrix products, matmul(): lax.dot_general(a, b, (contract, ((), ())), preferred_element_type=jnp.fl...  7.3 us
    ppermute x2, starting transfers between devices, along_z(): return lax.ppermute(x, 'dp', pairs)  7.2 us
    pallas_call x2, Pallas kernels, attend(): pl.pallas_call(functools.partial(attend_kernel, heads, base), grid_spec=p...  6.81 us
    pallas_call x1, Pallas kernels, product(): pl.pallas_call(product_kernel, in_specs=[SMEM] + [VMEM] * (2 * len(feats)...  6.19 us
  transfers between devices with their start and end apart: 30, of which 22 were waited for; matrix products, arithmetic and copies ran while one was open for 5% of the time, Pallas kernels for 4%

profile of v11, /device:TPU:4, one launch (start us, length us, event | category | flops | bytes accessed | tf_op | source)
XLA Modules:
  0.0 144.9 jit_solution(4474240775101302976)
XLA Ops:
  0.6 2.9 %shard_map.129 = (s32[11]{0:T(128)}, bf16[512,1024]{1,0:T(8,128)(2,1)}) custom-call(s32[32]{0:T(128)} %tiles.1, s32[32]{0:T(128)} %slots.1, bf16[2,512,1024]{2,1,0:T(8,128)(2,1)} %image_ref.3), custom_call_target="tpu_custom_call" | custom-call | bytes 4194304 | tf_op jit(solution)/shard_map/pallas_call | solution.py:122
  10.4 4.1 %collective-permute-start.2 = (bf16[512,256]{1,0:T(8,128)(2,1)S(1)}, bf16[512,256]{1,0:T(8,128)(2,1)S(1)}, u32[]{:S(2)}, u32[]{:S(2)}) collective-permute-start(bf16[512,256]{1,0:T(8,128)(2,1)S(1)} %get-tuple-element.42), channel_id=1, source_target_pairs={{0,96},{1,25},{2,98},{3,27},{4,100},{5,29},{6,102},{7,31},{8,104},... | collective-permute-start | bytes 786440 | tf_op jit(solution)/shard_map/ppermute | solution.py:30
  15.8 5.4 %collective-permute-done.2 = bf16[512,256]{1,0:T(8,128)(2,1)S(1)} collective-permute-done((bf16[512,256]{1,0:T(8,128)(2,1)S(1)}, bf16[512,256]{1,0:T(8,128)(2,1)S(1)}, u32[]{:S(2)}, u32[]{:S(2)}) %collective-permute-start.2) | collective-permute-done | bytes 262176 | tf_op jit(solution)/shard_map/ppermute | solution.py:30
  22.5 2.4 %collective-permute-done = bf16[512,256]{1,0:T(8,128)(2,1)S(1)} collective-permute-done((bf16[512,256]{1,0:T(8,128)(2,1)S(1)}, bf16[512,256]{1,0:T(8,128)(2,1)S(1)}, u32[]{:S(2)}, u32[]{:S(2)}) %collective-permute-start) | collective-permute-done | bytes 262176 | tf_op jit(solution)/shard_map/ppermute | solution.py:30
  25.0 3.8 %collective-permute-done.3.refs_2_ = bf16[512,1024]{1,0:T(8,128)(2,1)S(1)} collective-permute-done((bf16[512,1024]{1,0:T(8,128)(2,1)}, bf16[512,1024]{1,0:T(8,128)(2,1)S(1)}, u32[]{:S(2)}, u32[]{:S(2)}) %collective-permute-start.3) | collective-permute-done | bytes 1048608 | tf_op jit(solution)/shard_map/ppermute | solution.py:43
  31.3 2.9 %collective-permute-start.8 = (bf16[2048,256]{1,0:T(8,128)(2,1)S(1)}, bf16[2048,256]{1,0:T(8,128)(2,1)S(1)}, u32[]{:S(2)}, u32[]{:S(2)}) collective-permute-start(bf16[2048,256]{1,0:T(8,128)(2,1)S(1)} %pad_maximum_fusion.refs_0_), channel_id=1, source_target_pairs={{0,16},{1,65},{2,18},{3,67},{4,20},{5,69},{6,22},{7,71},{8,24},{9,... | collective-permute-start | bytes 3145736 | tf_op jit(solution)/shard_map/ppermute | solution.py:30
  35.5 1.8 %collective-permute-start.5 = (bf16[256,1024]{1,0:T(8,128)(2,1)S(1)}, bf16[256,1024]{1,0:T(8,128)(2,1)S(1)}, u32[]{:S(2)}, u32[]{:S(2)}) collective-permute-start(bf16[256,1024]{1,0:T(8,128)(2,1)S(1)} %slice.65), channel_id=1, source_target_pairs={{0,2},{1,3},{2,4},{3,5},{4,6},{5,7},{6,0},{7,1},{8,10},{9,11},{10,... | collective-permute-start | bytes 1572872 | tf_op jit(solution)/shard_map/ppermute | solution.py:43
  37.8 10.2 %collective-permute-done.5 = bf16[256,1024]{1,0:T(8,128)(2,1)S(1)} collective-permute-done((bf16[256,1024]{1,0:T(8,128)(2,1)S(1)}, bf16[256,1024]{1,0:T(8,128)(2,1)S(1)}, u32[]{:S(2)}, u32[]{:S(2)}) %collective-permute-start.5) | collective-permute-done | bytes 524320 | tf_op jit(solution)/shard_map/ppermute | solution.py:43
  49.5 1.8 %collective-permute-start.14 = (bf16[512,1024]{1,0:T(8,128)(2,1)S(1)}, bf16[512,1024]{1,0:T(8,128)(2,1)S(1)}, u32[]{:S(2)}, u32[]{:S(2)}) collective-permute-start(bf16[512,1024]{1,0:T(8,128)(2,1)S(1)} %get-tuple-element.55.refs_8_), channel_id=1, source_target_pairs={{0,2},{1,3},{2,4},{3,5},{4,6},{5,7},{6,0},{7,1},{8,10},{9,11},{10,... | collective-permute-start | bytes 3145736 | tf_op jit(solution)/shard_map/ppermute | solution.py:43
  51.5 6.7 %collective-permute-done.8.refs_2_ = bf16[2048,256]{1,0:T(8,128)(2,1)S(1)} collective-permute-done((bf16[2048,256]{1,0:T(8,128)(2,1)S(1)}, bf16[2048,256]{1,0:T(8,128)(2,1)S(1)}, u32[]{:S(2)}, u32[]{:S(2)}) %collective-permute-start.8) | collective-permute-done | bytes 1048608 | tf_op jit(solution)/shard_map/ppermute | solution.py:30
  65.8 4.0 %collective-permute-start.17 = (bf16[512,256]{1,0:T(8,128)(2,1)S(1)}, bf16[512,256]{1,0:T(8,128)(2,1)S(1)}, u32[]{:S(2)}, u32[]{:S(2)}) collective-permute-start(bf16[512,256]{1,0:T(8,128)(2,1)S(1)} %shard_map.132.kv_ref), channel_id=1, source_target_pairs={{0,64},{8,72},{16,80},{24,88},{32,96},{40,104},{48,112},{56,120},{... | collective-permute-start | bytes 786440 | tf_op jit(solution)/shard_map/ppermute | solution.py:17
  71.8 1.9 %collective-permute-done.15.refs_14_ = bf16[512,1024]{1,0:T(8,128)(2,1)S(1)} collective-permute-done((bf16[512,1024]{1,0:T(8,128)(2,1)S(1)}, bf16[512,1024]{1,0:T(8,128)(2,1)S(1)}, u32[]{:S(2)}, u32[]{:S(2)}) %collective-permute-start.15) | collective-permute-done | bytes 1048608 | tf_op jit(solution)/shard_map/ppermute | solution.py:43
  76.4 3.4 %shard_map.133 = (bf16[2,128,1024]{2,1,0:T(8,128)(2,1)}, bf16[2,128,1024]{2,1,0:T(8,128)(2,1)}, bf16[512,256]{1,0:T(8,128)(2,1)S(1)}) custom-call(s32[11]{0:T(128)S(1)} %copy-done.5, f32[1]{0:T(128)S(6)} %tanh.3.ratio_ref, bf16[2,128,1024]{2,1,0:T(8,128)(2,1)S(1)} %copy-done.7, bf16[2,128,1024]{2,1,0:T(8,128)(2,1)S(1)} %copy-done.8, ...), custom_call_target="tpu_custom_call" | custom-call | flops 939524096 | bytes 1441792 | tf_op jit(solution)/shard_map/pallas_call | solution.py:353
  79.8 3.2 %collective-permute-start.20 = (bf16[512,256]{1,0:T(8,128)(2,1)S(1)}, bf16[512,256]{1,0:T(8,128)(2,1)S(1)}, u32[]{:S(2)}, u32[]{:S(2)}) collective-permute-start(bf16[512,256]{1,0:T(8,128)(2,1)S(1)} %get-tuple-element.61.refs_17_), channel_id=1, source_target_pairs={{0,64},{8,72},{16,80},{24,88},{32,96},{40,104},{48,112},{56,120},{... | collective-permute-start | bytes 786440 | tf_op jit(solution)/shard_map/ppermute | solution.py:17
  85.8 3.7 %collective-permute-done.20.refs_18_ = bf16[512,256]{1,0:T(8,128)(2,1)S(1)} collective-permute-done((bf16[512,256]{1,0:T(8,128)(2,1)S(1)}, bf16[512,256]{1,0:T(8,128)(2,1)S(1)}, u32[]{:S(2)}, u32[]{:S(2)}) %collective-permute-start.20) | collective-permute-done | bytes 262176 | tf_op jit(solution)/shard_map/ppermute | solution.py:17
  93.0 3.4 %shard_map.135 = (bf16[2,128,1024]{2,1,0:T(8,128)(2,1)}, bf16[2,128,1024]{2,1,0:T(8,128)(2,1)}, bf16[512,256]{1,0:T(8,128)(2,1)S(1)}) custom-call(s32[11]{0:T(128)S(1)} %copy-done.5, f32[1]{0:T(128)S(6)} %tanh.3.ratio_ref, bf16[2,128,1024]{2,1,0:T(8,128)(2,1)S(1)} %copy-done.7, ...), custom_call_target="tpu_custom_call", output_to_operand_aliasing={{0}: (7, {}), {1}: (8, {})} | custom-call | flops 939524096 | bytes 1441792 | tf_op jit(solution)/shard_map/pallas_call | solution.py:353
  96.4 6.2 %shard_map.136 = (bf16[2048,256]{1,0:T(8,128)(2,1)S(1)}, bf16[2048,256]{1,0:T(8,128)(2,1)S(1)}, bf16[2048,256]{1,0:T(8,128)(2,1)S(1)}, bf16[2048,256]{1,0:T(8,128)(2,1)S(1)}) custom-call(s32[11]{0:T(128)S(1)} %copy-done.5, bf16[512,1024]{1,0:T(8,128)(2,1)S(1)} %copy-done.1, bf16[512,1024]{1,0:T(8,128)(2,1)S(1)} %collective-permute-done.10.refs_1_, ...), custom_call_target="tpu_custom_call" | custom-call | flops 4294967296 | bytes 16777216 | tf_op jit(solution)/shard_map/pallas_call | solution.py:260
  102.6 5.2 %collective-permute-start.26 = (bf16[2048,256]{1,0:T(8,128)(2,1)S(1)}, bf16[2048,256]{1,0:T(8,128)(2,1)S(1)}, u32[]{:S(2)}, u32[]{:S(2)}) collective-permute-start(bf16[2048,256]{1,0:T(8,128)(2,1)S(1)} %get-tuple-element.73), channel_id=1, source_target_pairs={{0,16},{1,65},{2,18},{3,67},{4,20},{5,69},{6,22},{7,71},{8,24},{9,... | collective-permute-start | bytes 3145736 | tf_op jit(solution)/shard_map/ppermute | solution.py:30
  108.5 2.6 %collective-permute-start.24 = (bf16[2048,256]{1,0:T(8,128)(2,1)S(1)}, bf16[2048,256]{1,0:T(8,128)(2,1)S(1)}, u32[]{:S(2)}, u32[]{:S(2)}) collective-permute-start(bf16[2048,256]{1,0:T(8,128)(2,1)S(1)} %get-tuple-element.71), channel_id=1, source_target_pairs={{0,24},{1,97},{2,26},{3,99},{4,28},{5,101},{6,30},{7,103},{8,0},{9... | collective-permute-start | bytes 3145736 | tf_op jit(solution)/shard_map/ppermute | solution.py:30
  111.0 9.6 %collective-permute-done.26 = bf16[2048,256]{1,0:T(8,128)(2,1)S(1)} collective-permute-done((bf16[2048,256]{1,0:T(8,128)(2,1)S(1)}, bf16[2048,256]{1,0:T(8,128)(2,1)S(1)}, u32[]{:S(2)}, u32[]{:S(2)}) %collective-permute-start.26) | collective-permute-done | bytes 1048608 | tf_op jit(solution)/shard_map/ppermute | solution.py:30
  120.7 11.1 %collective-permute-done.25 = bf16[2048,256]{1,0:T(8,128)(2,1)S(1)} collective-permute-done((bf16[2048,256]{1,0:T(8,128)(2,1)S(1)}, bf16[2048,256]{1,0:T(8,128)(2,1)S(1)}, u32[]{:S(2)}, u32[]{:S(2)}) %collective-permute-start.25) | collective-permute-done | bytes 1048608 | tf_op jit(solution)/shard_map/ppermute | solution.py:30
  134.8 2.4 %collective-permute-start.27 = (bf16[512,256]{1,0:T(8,128)(2,1)S(1)}, bf16[512,256]{1,0:T(8,128)(2,1)S(1)}, u32[]{:S(2)}, u32[]{:S(2)}) collective-permute-start(bf16[512,256]{1,0:T(8,128)(2,1)S(1)} %get-tuple-element.76), channel_id=1, source_target_pairs={{0,96},{1,25},{2,98},{3,27},{4,100},{5,29},{6,102},{7,31},{8,104},... | collective-permute-start | bytes 786440 | tf_op jit(solution)/shard_map/ppermute | solution.py:30
  137.2 4.1 %collective-permute-done.29 = bf16[512,256]{1,0:T(8,128)(2,1)S(1)} collective-permute-done((bf16[512,256]{1,0:T(8,128)(2,1)S(1)}, bf16[512,256]{1,0:T(8,128)(2,1)S(1)}, u32[]{:S(2)}, u32[]{:S(2)}) %collective-permute-start.29) | collective-permute-done | bytes 262176 | tf_op jit(solution)/shard_map/ppermute | solution.py:30
  141.3 2.7 %collective-permute-done.28 = bf16[512,256]{1,0:T(8,128)(2,1)S(1)} collective-permute-done((bf16[512,256]{1,0:T(8,128)(2,1)S(1)}, bf16[512,256]{1,0:T(8,128)(2,1)S(1)}, u32[]{:S(2)}, u32[]{:S(2)}) %collective-permute-start.28) | collective-permute-done | bytes 262176 | tf_op jit(solution)/shard_map/ppermute | solution.py:30
  (93 shorter events, 37.8 us)
Async XLA Ops:
  3.6 25.2 %collective-permute-start.3 = (bf16[512,1024]{1,0:T(8,128)(2,1)}, bf16[512,1024]{1,0:T(8,128)(2,1)S(1)}, u32[]{:S(2)}, u32[]{:S(2)}) collective-permute-start(bf16[512,1024]{1,0:T(8,128)(2,1)} %get-tuple-element.45.refs_0_), channel_id=1, source_target_pairs={{0,2},{1,3},{2,4},{3,5},{4,6},{5,7},{6,0},{7,1},{8,10},{9,11},{10,... | collective-permute-start | bytes 3145736 | tf_op jit(solution)/shard_map/ppermute | solution.py:43
  4.9 24.8 %collective-permute-start.4 = (bf16[512,1024]{1,0:T(8,128)(2,1)}, bf16[512,1024]{1,0:T(8,128)(2,1)S(1)}, u32[]{:S(2)}, u32[]{:S(2)}) collective-permute-start(bf16[512,1024]{1,0:T(8,128)(2,1)} %get-tuple-element.45.refs_0_), channel_id=1, source_target_pairs={{0,6},{1,7},{2,0},{3,1},{4,2},{5,3},{6,4},{7,5},{8,14},{9,15},{10,... | collective-permute-start | bytes 3145736 | tf_op jit(solution)/shard_map/ppermute | solution.py:43
  10.4 10.8 %collective-permute-start.2 = (bf16[512,256]{1,0:T(8,128)(2,1)S(1)}, bf16[512,256]{1,0:T(8,128)(2,1)S(1)}, u32[]{:S(2)}, u32[]{:S(2)}) collective-permute-start(bf16[512,256]{1,0:T(8,128)(2,1)S(1)} %get-tuple-element.42), channel_id=1, source_target_pairs={{0,96},{1,25},{2,98},{3,27},{4,100},{5,29},{6,102},{7,31},{8,104},... | collective-permute-start | bytes 786440 | tf_op jit(solution)/shard_map/ppermute | solution.py:30
  14.5 8.0 %collective-permute-start.1 = (bf16[512,256]{1,0:T(8,128)(2,1)S(1)}, bf16[512,256]{1,0:T(8,128)(2,1)S(1)}, u32[]{:S(2)}, u32[]{:S(2)}) collective-permute-start(bf16[512,256]{1,0:T(8,128)(2,1)S(1)} %get-tuple-element.42), channel_id=1, source_target_pairs={{0,64},{1,17},{2,66},{3,19},{4,68},{5,21},{6,70},{7,23},{8,72},{9,... | collective-permute-start | bytes 786440 | tf_op jit(solution)/shard_map/ppermute | solution.py:30
  14.6 10.4 %collective-permute-start = (bf16[512,256]{1,0:T(8,128)(2,1)S(1)}, bf16[512,256]{1,0:T(8,128)(2,1)S(1)}, u32[]{:S(2)}, u32[]{:S(2)}) collective-permute-start(bf16[512,256]{1,0:T(8,128)(2,1)S(1)} %get-tuple-element.42), channel_id=1, source_target_pairs={{0,32},{1,9},{2,34},{3,11},{4,36},{5,13},{6,38},{7,15},{8,40},{9,1... | collective-permute-start | bytes 786440 | tf_op jit(solution)/shard_map/ppermute | solution.py:30
  29.7 21.8 %collective-permute-start.7 = (bf16[2048,256]{1,0:T(8,128)(2,1)S(1)}, bf16[2048,256]{1,0:T(8,128)(2,1)S(1)}, u32[]{:S(2)}, u32[]{:S(2)}) collective-permute-start(bf16[2048,256]{1,0:T(8,128)(2,1)S(1)} %pad_maximum_fusion.refs_0_), channel_id=1, source_target_pairs={{0,8},{1,33},{2,10},{3,35},{4,12},{5,37},{6,14},{7,39},{8,16},{9,4... | collective-permute-start | bytes 3145736 | tf_op jit(solution)/shard_map/ppermute | solution.py:30
  31.3 26.9 %collective-permute-start.8 = (bf16[2048,256]{1,0:T(8,128)(2,1)S(1)}, bf16[2048,256]{1,0:T(8,128)(2,1)S(1)}, u32[]{:S(2)}, u32[]{:S(2)}) collective-permute-start(bf16[2048,256]{1,0:T(8,128)(2,1)S(1)} %pad_maximum_fusion.refs_0_), channel_id=1, source_target_pairs={{0,16},{1,65},{2,18},{3,67},{4,20},{5,69},{6,22},{7,71},{8,24},{9,... | collective-permute-start | bytes 3145736 | tf_op jit(solution)/shard_map/ppermute | solution.py:30
  34.2 24.0 %collective-permute-start.9 = (bf16[2048,256]{1,0:T(8,128)(2,1)S(1)}, bf16[2048,256]{1,0:T(8,128)(2,1)S(1)}, u32[]{:S(2)}, u32[]{:S(2)}) collective-permute-start(bf16[2048,256]{1,0:T(8,128)(2,1)S(1)} %pad_maximum_fusion.refs_0_), channel_id=1, source_target_pairs={{0,24},{1,97},{2,26},{3,99},{4,28},{5,101},{6,30},{7,103},{8,0},{9... | collective-permute-start | bytes 3145736 | tf_op jit(solution)/shard_map/ppermute | solution.py:30
  35.5 12.4 %collective-permute-start.5 = (bf16[256,1024]{1,0:T(8,128)(2,1)S(1)}, bf16[256,1024]{1,0:T(8,128)(2,1)S(1)}, u32[]{:S(2)}, u32[]{:S(2)}) collective-permute-start(bf16[256,1024]{1,0:T(8,128)(2,1)S(1)} %slice.65), channel_id=1, source_target_pairs={{0,2},{1,3},{2,4},{3,5},{4,6},{5,7},{6,0},{7,1},{8,10},{9,11},{10,... | collective-permute-start | bytes 1572872 | tf_op jit(solution)/shard_map/ppermute | solution.py:43
  37.3 12.1 %collective-permute-start.6 = (bf16[256,1024]{1,0:T(8,128)(2,1)S(1)}, bf16[256,1024]{1,0:T(8,128)(2,1)S(1)}, u32[]{:S(2)}, u32[]{:S(2)}) collective-permute-start(bf16[256,1024]{1,0:T(8,128)(2,1)S(1)} %slice.66), channel_id=1, source_target_pairs={{0,6},{1,7},{2,0},{3,1},{4,2},{5,3},{6,4},{7,5},{8,14},{9,15},{10,... | collective-permute-start | bytes 1572872 | tf_op jit(solution)/shard_map/ppermute | solution.py:43
  49.5 22.3 %collective-permute-start.14 = (bf16[512,1024]{1,0:T(8,128)(2,1)S(1)}, bf16[512,1024]{1,0:T(8,128)(2,1)S(1)}, u32[]{:S(2)}, u32[]{:S(2)}) collective-permute-start(bf16[512,1024]{1,0:T(8,128)(2,1)S(1)} %get-tuple-element.55.refs_8_), channel_id=1, source_target_pairs={{0,2},{1,3},{2,4},{3,5},{4,6},{5,7},{6,0},{7,1},{8,10},{9,11},{10,... | collective-permute-start | bytes 3145736 | tf_op jit(solution)/shard_map/ppermute | solution.py:43
  51.3 22.4 %collective-permute-start.15 = (bf16[512,1024]{1,0:T(8,128)(2,1)S(1)}, bf16[512,1024]{1,0:T(8,128)(2,1)S(1)}, u32[]{:S(2)}, u32[]{:S(2)}) collective-permute-start(bf16[512,1024]{1,0:T(8,128)(2,1)S(1)} %get-tuple-element.55.refs_8_), channel_id=1, source_target_pairs={{0,6},{1,7},{2,0},{3,1},{4,2},{5,3},{6,4},{7,5},{8,14},{9,15},{10,... | collective-permute-start | bytes 3145736 | tf_op jit(solution)/shard_map/ppermute | solution.py:43
  51.5 10.0 %collective-permute-start.10 = (bf16[512,1024]{1,0:T(8,128)(2,1)S(1)}, bf16[512,1024]{1,0:T(8,128)(2,1)S(1)}, u32[]{:S(2)}, u32[]{:S(2)}) collective-permute-start(bf16[512,1024]{1,0:T(8,128)(2,1)S(1)} %copy-done.1), channel_id=1, source_target_pairs={{0,1},{1,0},{2,3},{3,2},{4,5},{5,4},{6,7},{7,6},{8,9},{9,8},{10,11... | collective-permute-start | bytes 3145736 | tf_op jit(solution)/shard_map/ppermute | solution.py:47
  65.8 10.6 %collective-permute-start.17 = (bf16[512,256]{1,0:T(8,128)(2,1)S(1)}, bf16[512,256]{1,0:T(8,128)(2,1)S(1)}, u32[]{:S(2)}, u32[]{:S(2)}) collective-permute-start(bf16[512,256]{1,0:T(8,128)(2,1)S(1)} %shard_map.132.kv_ref), channel_id=1, source_target_pairs={{0,64},{8,72},{16,80},{24,88},{32,96},{40,104},{48,112},{56,120},{... | collective-permute-start | bytes 786440 | tf_op jit(solution)/shard_map/ppermute | solution.py:17
  73.7 10.6 %collective-permute-start.21 = (bf16[256,1024]{1,0:T(8,128)(2,1)S(1)}, bf16[256,1024]{1,0:T(8,128)(2,1)S(1)}, u32[]{:S(2)}, u32[]{:S(2)}) collective-permute-start(bf16[256,1024]{1,0:T(8,128)(2,1)S(1)} %slice.75), channel_id=1, source_target_pairs={{0,2},{1,3},{2,4},{3,5},{4,6},{5,7},{6,0},{7,1},{8,10},{9,11},{10,... | collective-permute-start | bytes 1572872 | tf_op jit(solution)/shard_map/ppermute | solution.py:43
  75.5 10.4 %collective-permute-start.22 = (bf16[256,1024]{1,0:T(8,128)(2,1)S(1)}, bf16[256,1024]{1,0:T(8,128)(2,1)S(1)}, u32[]{:S(2)}, u32[]{:S(2)}) collective-permute-start(bf16[256,1024]{1,0:T(8,128)(2,1)S(1)} %slice.76), channel_id=1, source_target_pairs={{0,6},{1,7},{2,0},{3,1},{4,2},{5,3},{6,4},{7,5},{8,14},{9,15},{10,... | collective-permute-start | bytes 1572872 | tf_op jit(solution)/shard_map/ppermute | solution.py:43
  75.9 14.3 %collective-permute-start.16 = (bf16[512,1024]{1,0:T(8,128)(2,1)S(1)}, bf16[512,1024]{1,0:T(8,128)(2,1)S(1)}, u32[]{:S(2)}, u32[]{:S(2)}) collective-permute-start(bf16[512,1024]{1,0:T(8,128)(2,1)S(1)} %get-tuple-element.55.refs_8_), channel_id=1, source_target_pairs={{0,1},{1,0},{2,3},{3,2},{4,5},{5,4},{6,7},{7,6},{8,9},{9,8},{10,11... | collective-permute-start | bytes 3145736 | tf_op jit(solution)/shard_map/ppermute | solution.py:47
  79.8 9.7 %collective-permute-start.20 = (bf16[512,256]{1,0:T(8,128)(2,1)S(1)}, bf16[512,256]{1,0:T(8,128)(2,1)S(1)}, u32[]{:S(2)}, u32[]{:S(2)}) collective-permute-start(bf16[512,256]{1,0:T(8,128)(2,1)S(1)} %get-tuple-element.61.refs_17_), channel_id=1, source_target_pairs={{0,64},{8,72},{16,80},{24,88},{32,96},{40,104},{48,112},{56,120},{... | collective-permute-start | bytes 786440 | tf_op jit(solution)/shard_map/ppermute | solution.py:17
  102.6 18.1 %collective-permute-start.26 = (bf16[2048,256]{1,0:T(8,128)(2,1)S(1)}, bf16[2048,256]{1,0:T(8,128)(2,1)S(1)}, u32[]{:S(2)}, u32[]{:S(2)}) collective-permute-start(bf16[2048,256]{1,0:T(8,128)(2,1)S(1)} %get-tuple-element.73), channel_id=1, source_target_pairs={{0,16},{1,65},{2,18},{3,67},{4,20},{5,69},{6,22},{7,71},{8,24},{9,... | collective-permute-start | bytes 3145736 | tf_op jit(solution)/shard_map/ppermute | solution.py:30
  107.8 24.0 %collective-permute-start.25 = (bf16[2048,256]{1,0:T(8,128)(2,1)S(1)}, bf16[2048,256]{1,0:T(8,128)(2,1)S(1)}, u32[]{:S(2)}, u32[]{:S(2)}) collective-permute-start(bf16[2048,256]{1,0:T(8,128)(2,1)S(1)} %get-tuple-element.72), channel_id=1, source_target_pairs={{0,8},{1,33},{2,10},{3,35},{4,12},{5,37},{6,14},{7,39},{8,16},{9,4... | collective-permute-start | bytes 3145736 | tf_op jit(solution)/shard_map/ppermute | solution.py:30
  108.5 24.1 %collective-permute-start.24 = (bf16[2048,256]{1,0:T(8,128)(2,1)S(1)}, bf16[2048,256]{1,0:T(8,128)(2,1)S(1)}, u32[]{:S(2)}, u32[]{:S(2)}) collective-permute-start(bf16[2048,256]{1,0:T(8,128)(2,1)S(1)} %get-tuple-element.71), channel_id=1, source_target_pairs={{0,24},{1,97},{2,26},{3,99},{4,28},{5,101},{6,30},{7,103},{8,0},{9... | collective-permute-start | bytes 3145736 | tf_op jit(solution)/shard_map/ppermute | solution.py:30
  133.2 8.1 %collective-permute-start.29 = (bf16[512,256]{1,0:T(8,128)(2,1)S(1)}, bf16[512,256]{1,0:T(8,128)(2,1)S(1)}, u32[]{:S(2)}, u32[]{:S(2)}) collective-permute-start(bf16[512,256]{1,0:T(8,128)(2,1)S(1)} %get-tuple-element.77), channel_id=1, source_target_pairs={{0,64},{1,17},{2,66},{3,19},{4,68},{5,21},{6,70},{7,23},{8,72},{9,... | collective-permute-start | bytes 786440 | tf_op jit(solution)/shard_map/ppermute | solution.py:30
  133.6 10.4 %collective-permute-start.28 = (bf16[512,256]{1,0:T(8,128)(2,1)S(1)}, bf16[512,256]{1,0:T(8,128)(2,1)S(1)}, u32[]{:S(2)}, u32[]{:S(2)}) collective-permute-start(bf16[512,256]{1,0:T(8,128)(2,1)S(1)} %get-tuple-element.78), channel_id=1, source_target_pairs={{0,32},{1,9},{2,34},{3,11},{4,36},{5,13},{6,38},{7,15},{8,40},{9,1... | collective-permute-start | bytes 786440 | tf_op jit(solution)/shard_map/ppermute | solution.py:30
  134.8 9.2 %collective-permute-start.27 = (bf16[512,256]{1,0:T(8,128)(2,1)S(1)}, bf16[512,256]{1,0:T(8,128)(2,1)S(1)}, u32[]{:S(2)}, u32[]{:S(2)}) collective-permute-start(bf16[512,256]{1,0:T(8,128)(2,1)S(1)} %get-tuple-element.76), channel_id=1, source_target_pairs={{0,96},{1,25},{2,98},{3,27},{4,100},{5,29},{6,102},{7,31},{8,104},... | collective-permute-start | bytes 786440 | tf_op jit(solution)/shard_map/ppermute | solution.py:30
  (16 other events, 171.4 us)

commit v12 on v11

--- a/solution.py
+++ b/solution.py
@@ -235,6 +235,7 @@
     depth = first[0].shape[1]
     count = depth // 2
     z, y, x, core = (chip[CHIP + i] for i in range(4))
+    waits = []
     for k in range(len(first)):
         total = matmul(first[k][...], first_grads, ((0,), (0,)))
         total = total + matmul(second[k][...], second_grads, ((0,), (0,)))
@@ -246,10 +247,14 @@
             inner_by = jnp.where(core == 0, by_z, by_y)
             start = pl.multiple_of(inner_by * count, count)
             held[outer_by, pl.ds(start, count)] = total[h * count : (h + 1) * count]
-    copies = [pltpu.make_async_copy(held.at[k], outs[k], sems.at[k]) for k in range(RING)]
-    for copy in copies:
-        copy.start()
-    for copy in copies:
+            for place, out in enumerate(outs):
+                target = out.at[pl.ds(start, count)]
+                copy = pltpu.make_async_copy(
+                    held.at[place, pl.ds(start, count)], target, sems.at[k, h]
+                )
+                pl.when(outer_by == place)(copy.start)
+            waits.append(copy)
+    for copy in waits:
         copy.wait()
 
 
@@ -264,7 +269,7 @@
         out_shape=[jax.ShapeDtypeStruct(shape, jnp.bfloat16)] * RING,
         scratch_shapes=[
             pltpu.VMEM((RING, *shape), jnp.bfloat16),
-            pltpu.SemaphoreType.DMA((RING,)),
+            pltpu.SemaphoreType.DMA((len(feats), 2)),
         ],
         compiler_params=PARAMS,
         cost_estimate=pl.CostEstimate(

time: 147 us -> 152 us (1.034)
  Pallas kernels: 18.2 us -> 23.8 us
    pallas_call x1, Pallas kernels: 6.19 us -> 11.8 us  [product(): pl.pallas_call(product_kernel, in_specs=[SMEM] + [VMEM] * (2 * len(feats)...]
where the time goes in v12:
time: 152 us; the launch traced here: 150 us
  waiting for transfers between devices  71.2 us (47%)
  starting transfers between devices  40.4 us (27%)
  Pallas kernels  23.8 us (16%)
  matrix products  7.3 us (5%)
  local copies, waits for them, and re-layouts  5.25 us (3%)
  between operations  1.7 us (1%)
    ppermute x12, waiting for transfers between devices, by_core(): return lax.ppermute(x, ('dp', 'tensor'), pairs)  44.1 us
    ppermute x12, starting transfers between devices, by_core(): return lax.ppermute(x, ('dp', 'tensor'), pairs)  23.6 us
    ppermute x8, waiting for transfers between devices, along_x(): return lax.ppermute(x, 'tensor', pairs)  21.1 us
    pallas_call x1, Pallas kernels, product(): pl.pallas_call(product_kernel, in_specs=[SMEM] + [VMEM] * (2 * len(feats)...  11.8 us
    ppermute x8, starting transfers between devices, along_x(): return lax.ppermute(x, 'tensor', pairs)  8.45 us
    dot_general x16, matrix products, matmul(): lax.dot_general(a, b, (contract, ((), ())), preferred_element_type=jnp.fl...  7.3 us
    ppermute x2, starting transfers between devices, along_z(): return lax.ppermute(x, 'dp', pairs)  7.2 us
    pallas_call x2, Pallas kernels, attend(): pl.pallas_call(functools.partial(attend_kernel, heads, base), grid_spec=p...  6.81 us
  transfers between devices with their start and end apart: 30, of which 22 were waited for; matrix products, arithmetic and copies ran while one was open for 5% of the time, Pallas kernels for 4%

profile of v12, /device:TPU:4, one launch (start us, length us, event | category | flops | bytes accessed | tf_op | source)
XLA Modules:
  0.0 150.5 jit_solution(13186032392208477054)
XLA Ops:
  0.6 2.9 %shard_map.129 = (s32[11]{0:T(128)}, bf16[512,1024]{1,0:T(8,128)(2,1)}) custom-call(s32[32]{0:T(128)} %tiles.1, s32[32]{0:T(128)} %slots.1, bf16[2,512,1024]{2,1,0:T(8,128)(2,1)} %image_ref.3), custom_call_target="tpu_custom_call" | custom-call | bytes 4194304 | tf_op jit(solution)/shard_map/pallas_call | solution.py:122
  10.4 4.1 %collective-permute-start.2 = (bf16[512,256]{1,0:T(8,128)(2,1)S(1)}, bf16[512,256]{1,0:T(8,128)(2,1)S(1)}, u32[]{:S(2)}, u32[]{:S(2)}) collective-permute-start(bf16[512,256]{1,0:T(8,128)(2,1)S(1)} %get-tuple-element.42), channel_id=1, source_target_pairs={{0,96},{1,25},{2,98},{3,27},{4,100},{5,29},{6,102},{7,31},{8,104},... | collective-permute-start | bytes 786440 | tf_op jit(solution)/shard_map/ppermute | solution.py:30
  15.8 5.4 %collective-permute-done.2 = bf16[512,256]{1,0:T(8,128)(2,1)S(1)} collective-permute-done((bf16[512,256]{1,0:T(8,128)(2,1)S(1)}, bf16[512,256]{1,0:T(8,128)(2,1)S(1)}, u32[]{:S(2)}, u32[]{:S(2)}) %collective-permute-start.2) | collective-permute-done | bytes 262176 | tf_op jit(solution)/shard_map/ppermute | solution.py:30
  22.5 2.4 %collective-permute-done = bf16[512,256]{1,0:T(8,128)(2,1)S(1)} collective-permute-done((bf16[512,256]{1,0:T(8,128)(2,1)S(1)}, bf16[512,256]{1,0:T(8,128)(2,1)S(1)}, u32[]{:S(2)}, u32[]{:S(2)}) %collective-permute-start) | collective-permute-done | bytes 262176 | tf_op jit(solution)/shard_map/ppermute | solution.py:30
  25.0 3.8 %collective-permute-done.3.refs_2_ = bf16[512,1024]{1,0:T(8,128)(2,1)S(1)} collective-permute-done((bf16[512,1024]{1,0:T(8,128)(2,1)}, bf16[512,1024]{1,0:T(8,128)(2,1)S(1)}, u32[]{:S(2)}, u32[]{:S(2)}) %collective-permute-start.3) | collective-permute-done | bytes 1048608 | tf_op jit(solution)/shard_map/ppermute | solution.py:43
  31.3 2.9 %collective-permute-start.8 = (bf16[2048,256]{1,0:T(8,128)(2,1)S(1)}, bf16[2048,256]{1,0:T(8,128)(2,1)S(1)}, u32[]{:S(2)}, u32[]{:S(2)}) collective-permute-start(bf16[2048,256]{1,0:T(8,128)(2,1)S(1)} %pad_maximum_fusion.refs_0_), channel_id=1, source_target_pairs={{0,16},{1,65},{2,18},{3,67},{4,20},{5,69},{6,22},{7,71},{8,24},{9,... | collective-permute-start | bytes 3145736 | tf_op jit(solution)/shard_map/ppermute | solution.py:30
  35.5 1.8 %collective-permute-start.5 = (bf16[256,1024]{1,0:T(8,128)(2,1)S(1)}, bf16[256,1024]{1,0:T(8,128)(2,1)S(1)}, u32[]{:S(2)}, u32[]{:S(2)}) collective-permute-start(bf16[256,1024]{1,0:T(8,128)(2,1)S(1)} %slice.65), channel_id=1, source_target_pairs={{0,2},{1,3},{2,4},{3,5},{4,6},{5,7},{6,0},{7,1},{8,10},{9,11},{10,... | collective-permute-start | bytes 1572872 | tf_op jit(solution)/shard_map/ppermute | solution.py:43
  37.8 10.2 %collective-permute-done.5 = bf16[256,1024]{1,0:T(8,128)(2,1)S(1)} collective-permute-done((bf16[256,1024]{1,0:T(8,128)(2,1)S(1)}, bf16[256,1024]{1,0:T(8,128)(2,1)S(1)}, u32[]{:S(2)}, u32[]{:S(2)}) %collective-permute-start.5) | collective-permute-done | bytes 524320 | tf_op jit(solution)/shard_map/ppermute | solution.py:43
  49.5 1.8 %collective-permute-start.14 = (bf16[512,1024]{1,0:T(8,128)(2,1)S(1)}, bf16[512,1024]{1,0:T(8,128)(2,1)S(1)}, u32[]{:S(2)}, u32[]{:S(2)}) collective-permute-start(bf16[512,1024]{1,0:T(8,128)(2,1)S(1)} %get-tuple-element.55.refs_8_), channel_id=1, source_target_pairs={{0,2},{1,3},{2,4},{3,5},{4,6},{5,7},{6,0},{7,1},{8,10},{9,11},{10,... | collective-permute-start | bytes 3145736 | tf_op jit(solution)/shard_map/ppermute | solution.py:43
  51.5 6.7 %collective-permute-done.8.refs_2_ = bf16[2048,256]{1,0:T(8,128)(2,1)S(1)} collective-permute-done((bf16[2048,256]{1,0:T(8,128)(2,1)S(1)}, bf16[2048,256]{1,0:T(8,128)(2,1)S(1)}, u32[]{:S(2)}, u32[]{:S(2)}) %collective-permute-start.8) | collective-permute-done | bytes 1048608 | tf_op jit(solution)/shard_map/ppermute | solution.py:30
  65.8 4.0 %collective-permute-start.17 = (bf16[512,256]{1,0:T(8,128)(2,1)S(1)}, bf16[512,256]{1,0:T(8,128)(2,1)S(1)}, u32[]{:S(2)}, u32[]{:S(2)}) collective-permute-start(bf16[512,256]{1,0:T(8,128)(2,1)S(1)} %shard_map.132.kv_ref), channel_id=1, source_target_pairs={{0,64},{8,72},{16,80},{24,88},{32,96},{40,104},{48,112},{56,120},{... | collective-permute-start | bytes 786440 | tf_op jit(solution)/shard_map/ppermute | solution.py:17
  71.8 1.9 %collective-permute-done.15.refs_14_ = bf16[512,1024]{1,0:T(8,128)(2,1)S(1)} collective-permute-done((bf16[512,1024]{1,0:T(8,128)(2,1)S(1)}, bf16[512,1024]{1,0:T(8,128)(2,1)S(1)}, u32[]{:S(2)}, u32[]{:S(2)}) %collective-permute-start.15) | collective-permute-done | bytes 1048608 | tf_op jit(solution)/shard_map/ppermute | solution.py:43
  76.4 3.4 %shard_map.133 = (bf16[2,128,1024]{2,1,0:T(8,128)(2,1)}, bf16[2,128,1024]{2,1,0:T(8,128)(2,1)}, bf16[512,256]{1,0:T(8,128)(2,1)S(1)}) custom-call(s32[11]{0:T(128)S(1)} %copy-done.5, f32[1]{0:T(128)S(6)} %tanh.3.ratio_ref, bf16[2,128,1024]{2,1,0:T(8,128)(2,1)S(1)} %copy-done.7, bf16[2,128,1024]{2,1,0:T(8,128)(2,1)S(1)} %copy-done.8, ...), custom_call_target="tpu_custom_call" | custom-call | flops 939524096 | bytes 1441792 | tf_op jit(solution)/shard_map/pallas_call | solution.py:358
  79.8 3.2 %collective-permute-start.20 = (bf16[512,256]{1,0:T(8,128)(2,1)S(1)}, bf16[512,256]{1,0:T(8,128)(2,1)S(1)}, u32[]{:S(2)}, u32[]{:S(2)}) collective-permute-start(bf16[512,256]{1,0:T(8,128)(2,1)S(1)} %get-tuple-element.61.refs_17_), channel_id=1, source_target_pairs={{0,64},{8,72},{16,80},{24,88},{32,96},{40,104},{48,112},{56,120},{... | collective-permute-start | bytes 786440 | tf_op jit(solution)/shard_map/ppermute | solution.py:17
  85.8 3.7 %collective-permute-done.20.refs_18_ = bf16[512,256]{1,0:T(8,128)(2,1)S(1)} collective-permute-done((bf16[512,256]{1,0:T(8,128)(2,1)S(1)}, bf16[512,256]{1,0:T(8,128)(2,1)S(1)}, u32[]{:S(2)}, u32[]{:S(2)}) %collective-permute-start.20) | collective-permute-done | bytes 262176 | tf_op jit(solution)/shard_map/ppermute | solution.py:17
  93.0 3.4 %shard_map.135 = (bf16[2,128,1024]{2,1,0:T(8,128)(2,1)}, bf16[2,128,1024]{2,1,0:T(8,128)(2,1)}, bf16[512,256]{1,0:T(8,128)(2,1)S(1)}) custom-call(s32[11]{0:T(128)S(1)} %copy-done.5, f32[1]{0:T(128)S(6)} %tanh.3.ratio_ref, bf16[2,128,1024]{2,1,0:T(8,128)(2,1)S(1)} %copy-done.7, ...), custom_call_target="tpu_custom_call", output_to_operand_aliasing={{0}: (7, {}), {1}: (8, {})} | custom-call | flops 939524096 | bytes 1441792 | tf_op jit(solution)/shard_map/pallas_call | solution.py:358
  96.4 11.8 %shard_map.136 = (bf16[2048,256]{1,0:T(8,128)(2,1)S(1)}, bf16[2048,256]{1,0:T(8,128)(2,1)S(1)}, bf16[2048,256]{1,0:T(8,128)(2,1)S(1)}, bf16[2048,256]{1,0:T(8,128)(2,1)S(1)}) custom-call(s32[11]{0:T(128)S(1)} %copy-done.5, bf16[512,1024]{1,0:T(8,128)(2,1)S(1)} %copy-done.1, bf16[512,1024]{1,0:T(8,128)(2,1)S(1)} %collective-permute-done.10.refs_1_, ...), custom_call_target="tpu_custom_call" | custom-call | flops 4294967296 | bytes 16777216 | tf_op jit(solution)/shard_map/pallas_call | solution.py:265
  108.2 5.2 %collective-permute-start.26 = (bf16[2048,256]{1,0:T(8,128)(2,1)S(1)}, bf16[2048,256]{1,0:T(8,128)(2,1)S(1)}, u32[]{:S(2)}, u32[]{:S(2)}) collective-permute-start(bf16[2048,256]{1,0:T(8,128)(2,1)S(1)} %get-tuple-element.73), channel_id=1, source_target_pairs={{0,16},{1,65},{2,18},{3,67},{4,20},{5,69},{6,22},{7,71},{8,24},{9,... | collective-permute-start | bytes 3145736 | tf_op jit(solution)/shard_map/ppermute | solution.py:30
  114.1 2.6 %collective-permute-start.24 = (bf16[2048,256]{1,0:T(8,128)(2,1)S(1)}, bf16[2048,256]{1,0:T(8,128)(2,1)S(1)}, u32[]{:S(2)}, u32[]{:S(2)}) collective-permute-start(bf16[2048,256]{1,0:T(8,128)(2,1)S(1)} %get-tuple-element.71), channel_id=1, source_target_pairs={{0,24},{1,97},{2,26},{3,99},{4,28},{5,101},{6,30},{7,103},{8,0},{9... | collective-permute-start | bytes 3145736 | tf_op jit(solution)/shard_map/ppermute | solution.py:30
  116.6 9.6 %collective-permute-done.26 = bf16[2048,256]{1,0:T(8,128)(2,1)S(1)} collective-permute-done((bf16[2048,256]{1,0:T(8,128)(2,1)S(1)}, bf16[2048,256]{1,0:T(8,128)(2,1)S(1)}, u32[]{:S(2)}, u32[]{:S(2)}) %collective-permute-start.26) | collective-permute-done | bytes 1048608 | tf_op jit(solution)/shard_map/ppermute | solution.py:30
  126.3 11.1 %collective-permute-done.25 = bf16[2048,256]{1,0:T(8,128)(2,1)S(1)} collective-permute-done((bf16[2048,256]{1,0:T(8,128)(2,1)S(1)}, bf16[2048,256]{1,0:T(8,128)(2,1)S(1)}, u32[]{:S(2)}, u32[]{:S(2)}) %collective-permute-start.25) | collective-permute-done | bytes 1048608 | tf_op jit(solution)/shard_map/ppermute | solution.py:30
  140.4 2.4 %collective-permute-start.27 = (bf16[512,256]{1,0:T(8,128)(2,1)S(1)}, bf16[512,256]{1,0:T(8,128)(2,1)S(1)}, u32[]{:S(2)}, u32[]{:S(2)}) collective-permute-start(bf16[512,256]{1,0:T(8,128)(2,1)S(1)} %get-tuple-element.76), channel_id=1, source_target_pairs={{0,96},{1,25},{2,98},{3,27},{4,100},{5,29},{6,102},{7,31},{8,104},... | collective-permute-start | bytes 786440 | tf_op jit(solution)/shard_map/ppermute | solution.py:30
  142.8 4.1 %collective-permute-done.29 = bf16[512,256]{1,0:T(8,128)(2,1)S(1)} collective-permute-done((bf16[512,256]{1,0:T(8,128)(2,1)S(1)}, bf16[512,256]{1,0:T(8,128)(2,1)S(1)}, u32[]{:S(2)}, u32[]{:S(2)}) %collective-permute-start.29) | collective-permute-done | bytes 262176 | tf_op jit(solution)/shard_map/ppermute | solution.py:30
  146.8 2.7 %collective-permute-done.28 = bf16[512,256]{1,0:T(8,128)(2,1)S(1)} collective-permute-done((bf16[512,256]{1,0:T(8,128)(2,1)S(1)}, bf16[512,256]{1,0:T(8,128)(2,1)S(1)}, u32[]{:S(2)}, u32[]{:S(2)}) %collective-permute-start.28) | collective-permute-done | bytes 262176 | tf_op jit(solution)/shard_map/ppermute | solution.py:30
  (93 shorter events, 37.8 us)
Async XLA Ops:
  3.6 25.2 %collective-permute-start.3 = (bf16[512,1024]{1,0:T(8,128)(2,1)}, bf16[512,1024]{1,0:T(8,128)(2,1)S(1)}, u32[]{:S(2)}, u32[]{:S(2)}) collective-permute-start(bf16[512,1024]{1,0:T(8,128)(2,1)} %get-tuple-element.45.refs_0_), channel_id=1, source_target_pairs={{0,2},{1,3},{2,4},{3,5},{4,6},{5,7},{6,0},{7,1},{8,10},{9,11},{10,... | collective-permute-start | bytes 3145736 | tf_op jit(solution)/shard_map/ppermute | solution.py:43
  4.9 24.8 %collective-permute-start.4 = (bf16[512,1024]{1,0:T(8,128)(2,1)}, bf16[512,1024]{1,0:T(8,128)(2,1)S(1)}, u32[]{:S(2)}, u32[]{:S(2)}) collective-permute-start(bf16[512,1024]{1,0:T(8,128)(2,1)} %get-tuple-element.45.refs_0_), channel_id=1, source_target_pairs={{0,6},{1,7},{2,0},{3,1},{4,2},{5,3},{6,4},{7,5},{8,14},{9,15},{10,... | collective-permute-start | bytes 3145736 | tf_op jit(solution)/shard_map/ppermute | solution.py:43
  10.4 10.8 %collective-permute-start.2 = (bf16[512,256]{1,0:T(8,128)(2,1)S(1)}, bf16[512,256]{1,0:T(8,128)(2,1)S(1)}, u32[]{:S(2)}, u32[]{:S(2)}) collective-permute-start(bf16[512,256]{1,0:T(8,128)(2,1)S(1)} %get-tuple-element.42), channel_id=1, source_target_pairs={{0,96},{1,25},{2,98},{3,27},{4,100},{5,29},{6,102},{7,31},{8,104},... | collective-permute-start | bytes 786440 | tf_op jit(solution)/shard_map/ppermute | solution.py:30
  14.5 8.0 %collective-permute-start.1 = (bf16[512,256]{1,0:T(8,128)(2,1)S(1)}, bf16[512,256]{1,0:T(8,128)(2,1)S(1)}, u32[]{:S(2)}, u32[]{:S(2)}) collective-permute-start(bf16[512,256]{1,0:T(8,128)(2,1)S(1)} %get-tuple-element.42), channel_id=1, source_target_pairs={{0,64},{1,17},{2,66},{3,19},{4,68},{5,21},{6,70},{7,23},{8,72},{9,... | collective-permute-start | bytes 786440 | tf_op jit(solution)/shard_map/ppermute | solution.py:30
  14.6 10.4 %collective-permute-start = (bf16[512,256]{1,0:T(8,128)(2,1)S(1)}, bf16[512,256]{1,0:T(8,128)(2,1)S(1)}, u32[]{:S(2)}, u32[]{:S(2)}) collective-permute-start(bf16[512,256]{1,0:T(8,128)(2,1)S(1)} %get-tuple-element.42), channel_id=1, source_target_pairs={{0,32},{1,9},{2,34},{3,11},{4,36},{5,13},{6,38},{7,15},{8,40},{9,1... | collective-permute-start | bytes 786440 | tf_op jit(solution)/shard_map/ppermute | solution.py:30
  29.7 21.8 %collective-permute-start.7 = (bf16[2048,256]{1,0:T(8,128)(2,1)S(1)}, bf16[2048,256]{1,0:T(8,128)(2,1)S(1)}, u32[]{:S(2)}, u32[]{:S(2)}) collective-permute-start(bf16[2048,256]{1,0:T(8,128)(2,1)S(1)} %pad_maximum_fusion.refs_0_), channel_id=1, source_target_pairs={{0,8},{1,33},{2,10},{3,35},{4,12},{5,37},{6,14},{7,39},{8,16},{9,4... | collective-permute-start | bytes 3145736 | tf_op jit(solution)/shard_map/ppermute | solution.py:30
  31.3 26.9 %collective-permute-start.8 = (bf16[2048,256]{1,0:T(8,128)(2,1)S(1)}, bf16[2048,256]{1,0:T(8,128)(2,1)S(1)}, u32[]{:S(2)}, u32[]{:S(2)}) collective-permute-start(bf16[2048,256]{1,0:T(8,128)(2,1)S(1)} %pad_maximum_fusion.refs_0_), channel_id=1, source_target_pairs={{0,16},{1,65},{2,18},{3,67},{4,20},{5,69},{6,22},{7,71},{8,24},{9,... | collective-permute-start | bytes 3145736 | tf_op jit(solution)/shard_map/ppermute | solution.py:30
  34.2 24.0 %collective-permute-start.9 = (bf16[2048,256]{1,0:T(8,128)(2,1)S(1)}, bf16[2048,256]{1,0:T(8,128)(2,1)S(1)}, u32[]{:S(2)}, u32[]{:S(2)}) collective-permute-start(bf16[2048,256]{1,0:T(8,128)(2,1)S(1)} %pad_maximum_fusion.refs_0_), channel_id=1, source_target_pairs={{0,24},{1,97},{2,26},{3,99},{4,28},{5,101},{6,30},{7,103},{8,0},{9... | collective-permute-start | bytes 3145736 | tf_op jit(solution)/shard_map/ppermute | solution.py:30
  35.5 12.4 %collective-permute-start.5 = (bf16[256,1024]{1,0:T(8,128)(2,1)S(1)}, bf16[256,1024]{1,0:T(8,128)(2,1)S(1)}, u32[]{:S(2)}, u32[]{:S(2)}) collective-permute-start(bf16[256,1024]{1,0:T(8,128)(2,1)S(1)} %slice.65), channel_id=1, source_target_pairs={{0,2},{1,3},{2,4},{3,5},{4,6},{5,7},{6,0},{7,1},{8,10},{9,11},{10,... | collective-permute-start | bytes 1572872 | tf_op jit(solution)/shard_map/ppermute | solution.py:43
  37.3 12.1 %collective-permute-start.6 = (bf16[256,1024]{1,0:T(8,128)(2,1)S(1)}, bf16[256,1024]{1,0:T(8,128)(2,1)S(1)}, u32[]{:S(2)}, u32[]{:S(2)}) collective-permute-start(bf16[256,1024]{1,0:T(8,128)(2,1)S(1)} %slice.66), channel_id=1, source_target_pairs={{0,6},{1,7},{2,0},{3,1},{4,2},{5,3},{6,4},{7,5},{8,14},{9,15},{10,... | collective-permute-start | bytes 1572872 | tf_op jit(solution)/shard_map/ppermute | solution.py:43
  49.5 22.3 %collective-permute-start.14 = (bf16[512,1024]{1,0:T(8,128)(2,1)S(1)}, bf16[512,1024]{1,0:T(8,128)(2,1)S(1)}, u32[]{:S(2)}, u32[]{:S(2)}) collective-permute-start(bf16[512,1024]{1,0:T(8,128)(2,1)S(1)} %get-tuple-element.55.refs_8_), channel_id=1, source_target_pairs={{0,2},{1,3},{2,4},{3,5},{4,6},{5,7},{6,0},{7,1},{8,10},{9,11},{10,... | collective-permute-start | bytes 3145736 | tf_op jit(solution)/shard_map/ppermute | solution.py:43
  51.3 22.4 %collective-permute-start.15 = (bf16[512,1024]{1,0:T(8,128)(2,1)S(1)}, bf16[512,1024]{1,0:T(8,128)(2,1)S(1)}, u32[]{:S(2)}, u32[]{:S(2)}) collective-permute-start(bf16[512,1024]{1,0:T(8,128)(2,1)S(1)} %get-tuple-element.55.refs_8_), channel_id=1, source_target_pairs={{0,6},{1,7},{2,0},{3,1},{4,2},{5,3},{6,4},{7,5},{8,14},{9,15},{10,... | collective-permute-start | bytes 3145736 | tf_op jit(solution)/shard_map/ppermute | solution.py:43
  51.5 10.0 %collective-permute-start.10 = (bf16[512,1024]{1,0:T(8,128)(2,1)S(1)}, bf16[512,1024]{1,0:T(8,128)(2,1)S(1)}, u32[]{:S(2)}, u32[]{:S(2)}) collective-permute-start(bf16[512,1024]{1,0:T(8,128)(2,1)S(1)} %copy-done.1), channel_id=1, source_target_pairs={{0,1},{1,0},{2,3},{3,2},{4,5},{5,4},{6,7},{7,6},{8,9},{9,8},{10,11... | collective-permute-start | bytes 3145736 | tf_op jit(solution)/shard_map/ppermute | solution.py:47
  65.8 10.6 %collective-permute-start.17 = (bf16[512,256]{1,0:T(8,128)(2,1)S(1)}, bf16[512,256]{1,0:T(8,128)(2,1)S(1)}, u32[]{:S(2)}, u32[]{:S(2)}) collective-permute-start(bf16[512,256]{1,0:T(8,128)(2,1)S(1)} %shard_map.132.kv_ref), channel_id=1, source_target_pairs={{0,64},{8,72},{16,80},{24,88},{32,96},{40,104},{48,112},{56,120},{... | collective-permute-start | bytes 786440 | tf_op jit(solution)/shard_map/ppermute | solution.py:17
  73.7 10.6 %collective-permute-start.21 = (bf16[256,1024]{1,0:T(8,128)(2,1)S(1)}, bf16[256,1024]{1,0:T(8,128)(2,1)S(1)}, u32[]{:S(2)}, u32[]{:S(2)}) collective-permute-start(bf16[256,1024]{1,0:T(8,128)(2,1)S(1)} %slice.75), channel_id=1, source_target_pairs={{0,2},{1,3},{2,4},{3,5},{4,6},{5,7},{6,0},{7,1},{8,10},{9,11},{10,... | collective-permute-start | bytes 1572872 | tf_op jit(solution)/shard_map/ppermute | solution.py:43
  75.5 10.4 %collective-permute-start.22 = (bf16[256,1024]{1,0:T(8,128)(2,1)S(1)}, bf16[256,1024]{1,0:T(8,128)(2,1)S(1)}, u32[]{:S(2)}, u32[]{:S(2)}) collective-permute-start(bf16[256,1024]{1,0:T(8,128)(2,1)S(1)} %slice.76), channel_id=1, source_target_pairs={{0,6},{1,7},{2,0},{3,1},{4,2},{5,3},{6,4},{7,5},{8,14},{9,15},{10,... | collective-permute-start | bytes 1572872 | tf_op jit(solution)/shard_map/ppermute | solution.py:43
  75.9 14.3 %collective-permute-start.16 = (bf16[512,1024]{1,0:T(8,128)(2,1)S(1)}, bf16[512,1024]{1,0:T(8,128)(2,1)S(1)}, u32[]{:S(2)}, u32[]{:S(2)}) collective-permute-start(bf16[512,1024]{1,0:T(8,128)(2,1)S(1)} %get-tuple-element.55.refs_8_), channel_id=1, source_target_pairs={{0,1},{1,0},{2,3},{3,2},{4,5},{5,4},{6,7},{7,6},{8,9},{9,8},{10,11... | collective-permute-start | bytes 3145736 | tf_op jit(solution)/shard_map/ppermute | solution.py:47
  79.8 9.7 %collective-permute-start.20 = (bf16[512,256]{1,0:T(8,128)(2,1)S(1)}, bf16[512,256]{1,0:T(8,128)(2,1)S(1)}, u32[]{:S(2)}, u32[]{:S(2)}) collective-permute-start(bf16[512,256]{1,0:T(8,128)(2,1)S(1)} %get-tuple-element.61.refs_17_), channel_id=1, source_target_pairs={{0,64},{8,72},{16,80},{24,88},{32,96},{40,104},{48,112},{56,120},{... | collective-permute-start | bytes 786440 | tf_op jit(solution)/shard_map/ppermute | solution.py:17
  108.2 18.1 %collective-permute-start.26 = (bf16[2048,256]{1,0:T(8,128)(2,1)S(1)}, bf16[2048,256]{1,0:T(8,128)(2,1)S(1)}, u32[]{:S(2)}, u32[]{:S(2)}) collective-permute-start(bf16[2048,256]{1,0:T(8,128)(2,1)S(1)} %get-tuple-element.73), channel_id=1, source_target_pairs={{0,16},{1,65},{2,18},{3,67},{4,20},{5,69},{6,22},{7,71},{8,24},{9,... | collective-permute-start | bytes 3145736 | tf_op jit(solution)/shard_map/ppermute | solution.py:30
  113.4 24.0 %collective-permute-start.25 = (bf16[2048,256]{1,0:T(8,128)(2,1)S(1)}, bf16[2048,256]{1,0:T(8,128)(2,1)S(1)}, u32[]{:S(2)}, u32[]{:S(2)}) collective-permute-start(bf16[2048,256]{1,0:T(8,128)(2,1)S(1)} %get-tuple-element.72), channel_id=1, source_target_pairs={{0,8},{1,33},{2,10},{3,35},{4,12},{5,37},{6,14},{7,39},{8,16},{9,4... | collective-permute-start | bytes 3145736 | tf_op jit(solution)/shard_map/ppermute | solution.py:30
  114.1 24.1 %collective-permute-start.24 = (bf16[2048,256]{1,0:T(8,128)(2,1)S(1)}, bf16[2048,256]{1,0:T(8,128)(2,1)S(1)}, u32[]{:S(2)}, u32[]{:S(2)}) collective-permute-start(bf16[2048,256]{1,0:T(8,128)(2,1)S(1)} %get-tuple-element.71), channel_id=1, source_target_pairs={{0,24},{1,97},{2,26},{3,99},{4,28},{5,101},{6,30},{7,103},{8,0},{9... | collective-permute-start | bytes 3145736 | tf_op jit(solution)/shard_map/ppermute | solution.py:30
  138.8 8.1 %collective-permute-start.29 = (bf16[512,256]{1,0:T(8,128)(2,1)S(1)}, bf16[512,256]{1,0:T(8,128)(2,1)S(1)}, u32[]{:S(2)}, u32[]{:S(2)}) collective-permute-start(bf16[512,256]{1,0:T(8,128)(2,1)S(1)} %get-tuple-element.77), channel_id=1, source_target_pairs={{0,64},{1,17},{2,66},{3,19},{4,68},{5,21},{6,70},{7,23},{8,72},{9,... | collective-permute-start | bytes 786440 | tf_op jit(solution)/shard_map/ppermute | solution.py:30
  139.1 10.4 %collective-permute-start.28 = (bf16[512,256]{1,0:T(8,128)(2,1)S(1)}, bf16[512,256]{1,0:T(8,128)(2,1)S(1)}, u32[]{:S(2)}, u32[]{:S(2)}) collective-permute-start(bf16[512,256]{1,0:T(8,128)(2,1)S(1)} %get-tuple-element.78), channel_id=1, source_target_pairs={{0,32},{1,9},{2,34},{3,11},{4,36},{5,13},{6,38},{7,15},{8,40},{9,1... | collective-permute-start | bytes 786440 | tf_op jit(solution)/shard_map/ppermute | solution.py:30
  140.4 9.2 %collective-permute-start.27 = (bf16[512,256]{1,0:T(8,128)(2,1)S(1)}, bf16[512,256]{1,0:T(8,128)(2,1)S(1)}, u32[]{:S(2)}, u32[]{:S(2)}) collective-permute-start(bf16[512,256]{1,0:T(8,128)(2,1)S(1)} %get-tuple-element.76), channel_id=1, source_target_pairs={{0,96},{1,25},{2,98},{3,27},{4,100},{5,29},{6,102},{7,31},{8,104},... | collective-permute-start | bytes 786440 | tf_op jit(solution)/shard_map/ppermute | solution.py:30
  (16 other events, 171.4 us)

commit v13 on v11

--- a/solution.py
+++ b/solution.py
@@ -231,26 +231,21 @@
     first_grads = jnp.where(chip[FAR + 2] != 0, first_back[...], first_grad[...])
     first_grads = turned(first_total[...], first_grads, gain_ref[...])
     second_grads = turned(second_total[...], second_grad[...], gain_ref[...])
-    outs, (held, sems) = refs[:RING], refs[RING:]
+    (out_ref,) = refs
     depth = first[0].shape[1]
     count = depth // 2
     z, y, x, core = (chip[CHIP + i] for i in range(4))
     for k in range(len(first)):
         total = matmul(first[k][...], first_grads, ((0,), (0,)))
         total = total + matmul(second[k][...], second_grads, ((0,), (0,)))
-        total = total.astype(held.dtype)
+        total = total.astype(out_ref.dtype)
         by_z = (x - k // 2 - z + 2 * RING) % RING
         for h in range(2):
             by_y = (2 * (k % 2 ^ core) + h - y + RING) % RING
             outer_by = jnp.where(core == 0, by_y, by_z)
             inner_by = jnp.where(core == 0, by_z, by_y)
-            start = pl.multiple_of(inner_by * count, count)
-            held[outer_by, pl.ds(start, count)] = total[h * count : (h + 1) * count]
-    copies = [pltpu.make_async_copy(held.at[k], outs[k], sems.at[k]) for k in range(RING)]
-    for copy in copies:
-        copy.start()
-    for copy in copies:
-        copy.wait()
+            start = pl.multiple_of((outer_by * RING + inner_by) * count, count)
+            out_ref[pl.ds(start, count)] = total[h * count : (h + 1) * count]
 
 
 def product(chip, feats, others, first, second, gain):
@@ -260,12 +255,8 @@
     return pl.pallas_call(
         product_kernel,
         in_specs=[SMEM] + [VMEM] * (2 * len(feats) + 6),
-        out_specs=[ANY] * RING,
-        out_shape=[jax.ShapeDtypeStruct(shape, jnp.bfloat16)] * RING,
-        scratch_shapes=[
-            pltpu.VMEM((RING, *shape), jnp.bfloat16),
-            pltpu.SemaphoreType.DMA((RING,)),
-        ],
+        out_specs=VMEM,
+        out_shape=jax.ShapeDtypeStruct((RING * shape[0], both), jnp.bfloat16),
         compiler_params=PARAMS,
         cost_estimate=pl.CostEstimate(
             flops=4 * len(feats) * rows * depth * both,
@@ -456,6 +447,7 @@
 
     far, near = (far_total, far_grad, back), (near_total, near_grad)
     blocks = product(numbers, far_feats, near_feats, far, near, key_gain)
+    blocks = jnp.split(blocks, RING, axis=0)
     total = summed([blocks[0], *scattered(blocks, outer)])
     count = total.shape[0] // RING
     parts = [total[d * count : (d + 1) * count] for d in range(RING)]

time: 147 us -> 146 us (level)
  no operation moved by 1% of the time
where the time goes in v13:
time: 146 us; the launch traced here: 145 us
  waiting for transfers between devices  71.3 us (49%)
  starting transfers between devices  40.4 us (28%)
  Pallas kernels  17.9 us (12%)
  matrix products  7.3 us (5%)
  local copies, waits for them, and re-layouts  5.45 us (4%)
  between operations  1.71 us (1%)
    ppermute x12, waiting for transfers between devices, by_core(): return lax.ppermute(x, ('dp', 'tensor'), pairs)  44.1 us
    ppermute x12, starting transfers between devices, by_core(): return lax.ppermute(x, ('dp', 'tensor'), pairs)  23.6 us
    ppermute x8, waiting for transfers between devices, along_x(): return lax.ppermute(x, 'tensor', pairs)  21.1 us
    ppermute x8, starting transfers between devices, along_x(): return lax.ppermute(x, 'tensor', pairs)  8.45 us
    dot_general x16, matrix products, matmul(): lax.dot_general(a, b, (contract, ((), ())), preferred_element_type=jnp.fl...  7.3 us
    ppermute x2, starting transfers between devices, along_z(): return lax.ppermute(x, 'dp', pairs)  7.2 us
    pallas_call x2, Pallas kernels, attend(): pl.pallas_call(functools.partial(attend_kernel, heads, base), grid_spec=p...  6.81 us
    pallas_call x1, Pallas kernels, product(): pl.pallas_call(product_kernel, in_specs=[SMEM] + [VMEM] * (2 * len(feats)...  5.88 us
  transfers between devices with their start and end apart: 30, of which 22 were waited for; matrix products, arithmetic and copies ran while one was open for 5% of the time, Pallas kernels for 4%

profile of v13, /device:TPU:4, one launch (start us, length us, event | category | flops | bytes accessed | tf_op | source)
XLA Modules:
  0.0 144.8 jit_solution(7620721229313114365)
XLA Ops:
  0.6 2.9 %shard_map.129 = (s32[11]{0:T(128)}, bf16[512,1024]{1,0:T(8,128)(2,1)}) custom-call(s32[32]{0:T(128)} %tiles.1, s32[32]{0:T(128)} %slots.1, bf16[2,512,1024]{2,1,0:T(8,128)(2,1)} %image_ref.3), custom_call_target="tpu_custom_call" | custom-call | bytes 4194304 | tf_op jit(solution)/shard_map/pallas_call | solution.py:122
  10.4 4.1 %collective-permute-start.2 = (bf16[512,256]{1,0:T(8,128)(2,1)S(1)}, bf16[512,256]{1,0:T(8,128)(2,1)S(1)}, u32[]{:S(2)}, u32[]{:S(2)}) collective-permute-start(bf16[512,256]{1,0:T(8,128)(2,1)S(1)} %get-tuple-element.38), channel_id=1, source_target_pairs={{0,96},{1,25},{2,98},{3,27},{4,100},{5,29},{6,102},{7,31},{8,104},... | collective-permute-start | bytes 786440 | tf_op jit(solution)/shard_map/ppermute | solution.py:30
  15.8 5.4 %collective-permute-done.2 = bf16[512,256]{1,0:T(8,128)(2,1)S(1)} collective-permute-done((bf16[512,256]{1,0:T(8,128)(2,1)S(1)}, bf16[512,256]{1,0:T(8,128)(2,1)S(1)}, u32[]{:S(2)}, u32[]{:S(2)}) %collective-permute-start.2) | collective-permute-done | bytes 262176 | tf_op jit(solution)/shard_map/ppermute | solution.py:30
  22.5 2.4 %collective-permute-done = bf16[512,256]{1,0:T(8,128)(2,1)S(1)} collective-permute-done((bf16[512,256]{1,0:T(8,128)(2,1)S(1)}, bf16[512,256]{1,0:T(8,128)(2,1)S(1)}, u32[]{:S(2)}, u32[]{:S(2)}) %collective-permute-start) | collective-permute-done | bytes 262176 | tf_op jit(solution)/shard_map/ppermute | solution.py:30
  25.0 3.8 %collective-permute-done.3.refs_2_ = bf16[512,1024]{1,0:T(8,128)(2,1)S(1)} collective-permute-done((bf16[512,1024]{1,0:T(8,128)(2,1)}, bf16[512,1024]{1,0:T(8,128)(2,1)S(1)}, u32[]{:S(2)}, u32[]{:S(2)}) %collective-permute-start.3) | collective-permute-done | bytes 1048608 | tf_op jit(solution)/shard_map/ppermute | solution.py:43
  31.3 2.9 %collective-permute-start.8 = (bf16[2048,256]{1,0:T(8,128)(2,1)S(1)}, bf16[2048,256]{1,0:T(8,128)(2,1)S(1)}, u32[]{:S(2)}, u32[]{:S(2)}) collective-permute-start(bf16[2048,256]{1,0:T(8,128)(2,1)S(1)} %pad_maximum_fusion.refs_0_), channel_id=1, source_target_pairs={{0,16},{1,65},{2,18},{3,67},{4,20},{5,69},{6,22},{7,71},{8,24},{9,... | collective-permute-start | bytes 3145736 | tf_op jit(solution)/shard_map/ppermute | solution.py:30
  35.5 1.8 %collective-permute-start.5 = (bf16[256,1024]{1,0:T(8,128)(2,1)S(1)}, bf16[256,1024]{1,0:T(8,128)(2,1)S(1)}, u32[]{:S(2)}, u32[]{:S(2)}) collective-permute-start(bf16[256,1024]{1,0:T(8,128)(2,1)S(1)} %slice.65), channel_id=1, source_target_pairs={{0,2},{1,3},{2,4},{3,5},{4,6},{5,7},{6,0},{7,1},{8,10},{9,11},{10,... | collective-permute-start | bytes 1572872 | tf_op jit(solution)/shard_map/ppermute | solution.py:43
  37.8 10.2 %collective-permute-done.5 = bf16[256,1024]{1,0:T(8,128)(2,1)S(1)} collective-permute-done((bf16[256,1024]{1,0:T(8,128)(2,1)S(1)}, bf16[256,1024]{1,0:T(8,128)(2,1)S(1)}, u32[]{:S(2)}, u32[]{:S(2)}) %collective-permute-start.5) | collective-permute-done | bytes 524320 | tf_op jit(solution)/shard_map/ppermute | solution.py:43
  49.5 1.8 %collective-permute-start.14 = (bf16[512,1024]{1,0:T(8,128)(2,1)S(1)}, bf16[512,1024]{1,0:T(8,128)(2,1)S(1)}, u32[]{:S(2)}, u32[]{:S(2)}) collective-permute-start(bf16[512,1024]{1,0:T(8,128)(2,1)S(1)} %get-tuple-element.51.refs_8_), channel_id=1, source_target_pairs={{0,2},{1,3},{2,4},{3,5},{4,6},{5,7},{6,0},{7,1},{8,10},{9,11},{10,... | collective-permute-start | bytes 3145736 | tf_op jit(solution)/shard_map/ppermute | solution.py:43
  51.5 6.7 %collective-permute-done.8.refs_2_ = bf16[2048,256]{1,0:T(8,128)(2,1)S(1)} collective-permute-done((bf16[2048,256]{1,0:T(8,128)(2,1)S(1)}, bf16[2048,256]{1,0:T(8,128)(2,1)S(1)}, u32[]{:S(2)}, u32[]{:S(2)}) %collective-permute-start.8) | collective-permute-done | bytes 1048608 | tf_op jit(solution)/shard_map/ppermute | solution.py:30
  65.8 4.0 %collective-permute-start.17 = (bf16[512,256]{1,0:T(8,128)(2,1)S(1)}, bf16[512,256]{1,0:T(8,128)(2,1)S(1)}, u32[]{:S(2)}, u32[]{:S(2)}) collective-permute-start(bf16[512,256]{1,0:T(8,128)(2,1)S(1)} %shard_map.132.kv_ref), channel_id=1, source_target_pairs={{0,64},{8,72},{16,80},{24,88},{32,96},{40,104},{48,112},{56,120},{... | collective-permute-start | bytes 786440 | tf_op jit(solution)/shard_map/ppermute | solution.py:17
  71.8 1.9 %collective-permute-done.15.refs_14_ = bf16[512,1024]{1,0:T(8,128)(2,1)S(1)} collective-permute-done((bf16[512,1024]{1,0:T(8,128)(2,1)S(1)}, bf16[512,1024]{1,0:T(8,128)(2,1)S(1)}, u32[]{:S(2)}, u32[]{:S(2)}) %collective-permute-start.15) | collective-permute-done | bytes 1048608 | tf_op jit(solution)/shard_map/ppermute | solution.py:43
  76.4 3.4 %shard_map.133 = (bf16[2,128,1024]{2,1,0:T(8,128)(2,1)}, bf16[2,128,1024]{2,1,0:T(8,128)(2,1)}, bf16[512,256]{1,0:T(8,128)(2,1)S(1)}) custom-call(s32[11]{0:T(128)S(1)} %copy-done.5, f32[1]{0:T(128)S(6)} %tanh.3.ratio_ref, bf16[2,128,1024]{2,1,0:T(8,128)(2,1)S(1)} %copy-done.7, bf16[2,128,1024]{2,1,0:T(8,128)(2,1)S(1)} %copy-done.8, ...), custom_call_target="tpu_custom_call" | custom-call | flops 939524096 | bytes 1441792 | tf_op jit(solution)/shard_map/pallas_call | solution.py:344
  79.8 3.2 %collective-permute-start.20 = (bf16[512,256]{1,0:T(8,128)(2,1)S(1)}, bf16[512,256]{1,0:T(8,128)(2,1)S(1)}, u32[]{:S(2)}, u32[]{:S(2)}) collective-permute-start(bf16[512,256]{1,0:T(8,128)(2,1)S(1)} %get-tuple-element.57.refs_17_), channel_id=1, source_target_pairs={{0,64},{8,72},{16,80},{24,88},{32,96},{40,104},{48,112},{56,120},{... | collective-permute-start | bytes 786440 | tf_op jit(solution)/shard_map/ppermute | solution.py:17
  85.8 3.7 %collective-permute-done.20.refs_18_ = bf16[512,256]{1,0:T(8,128)(2,1)S(1)} collective-permute-done((bf16[512,256]{1,0:T(8,128)(2,1)S(1)}, bf16[512,256]{1,0:T(8,128)(2,1)S(1)}, u32[]{:S(2)}, u32[]{:S(2)}) %collective-permute-start.20) | collective-permute-done | bytes 262176 | tf_op jit(solution)/shard_map/ppermute | solution.py:17
  93.0 3.4 %shard_map.135 = (bf16[2,128,1024]{2,1,0:T(8,128)(2,1)}, bf16[2,128,1024]{2,1,0:T(8,128)(2,1)}, bf16[512,256]{1,0:T(8,128)(2,1)S(1)}) custom-call(s32[11]{0:T(128)S(1)} %copy-done.5, f32[1]{0:T(128)S(6)} %tanh.3.ratio_ref, bf16[2,128,1024]{2,1,0:T(8,128)(2,1)S(1)} %copy-done.7, ...), custom_call_target="tpu_custom_call", output_to_operand_aliasing={{0}: (7, {}), {1}: (8, {})} | custom-call | flops 939524096 | bytes 1441792 | tf_op jit(solution)/shard_map/pallas_call | solution.py:344
  96.4 5.9 %shard_map.136 = bf16[8192,256]{1,0:T(8,128)(2,1)S(1)} custom-call(s32[11]{0:T(128)S(1)} %copy-done.5, bf16[512,1024]{1,0:T(8,128)(2,1)S(1)} %copy-done.1, bf16[512,1024]{1,0:T(8,128)(2,1)S(1)} %collective-permute-done.10.refs_1_, bf16[512,1024]{1,0:T(8,128)(2,1)S(1)} %collective-permute-done.3.refs_2_, ...), custom_call_target="tpu_custom_call" | custom-call | flops 4294967296 | bytes 16777216 | tf_op jit(solution)/shard_map/pallas_call | solution.py:255
  102.5 5.2 %collective-permute-start.26 = (bf16[2048,256]{1,0:T(8,128)(2,1)S(1)}, bf16[2048,256]{1,0:T(8,128)(2,1)S(1)}, u32[]{:S(2)}, u32[]{:S(2)}) collective-permute-start(bf16[2048,256]{1,0:T(8,128)(2,1)S(1)} %get-tuple-element.69), channel_id=1, source_target_pairs={{0,16},{1,65},{2,18},{3,67},{4,20},{5,69},{6,22},{7,71},{8,24},{9,... | collective-permute-start | bytes 3145736 | tf_op jit(solution)/shard_map/ppermute | solution.py:30
  108.4 2.6 %collective-permute-start.24 = (bf16[2048,256]{1,0:T(8,128)(2,1)S(1)}, bf16[2048,256]{1,0:T(8,128)(2,1)S(1)}, u32[]{:S(2)}, u32[]{:S(2)}) collective-permute-start(bf16[2048,256]{1,0:T(8,128)(2,1)S(1)} %get-tuple-element.68), channel_id=1, source_target_pairs={{0,24},{1,97},{2,26},{3,99},{4,28},{5,101},{6,30},{7,103},{8,0},{9... | collective-permute-start | bytes 3145736 | tf_op jit(solution)/shard_map/ppermute | solution.py:30
  110.9 9.6 %collective-permute-done.26 = bf16[2048,256]{1,0:T(8,128)(2,1)S(1)} collective-permute-done((bf16[2048,256]{1,0:T(8,128)(2,1)S(1)}, bf16[2048,256]{1,0:T(8,128)(2,1)S(1)}, u32[]{:S(2)}, u32[]{:S(2)}) %collective-permute-start.26) | collective-permute-done | bytes 1048608 | tf_op jit(solution)/shard_map/ppermute | solution.py:30
  120.6 11.1 %collective-permute-done.25 = bf16[2048,256]{1,0:T(8,128)(2,1)S(1)} collective-permute-done((bf16[2048,256]{1,0:T(8,128)(2,1)S(1)}, bf16[2048,256]{1,0:T(8,128)(2,1)S(1)}, u32[]{:S(2)}, u32[]{:S(2)}) %collective-permute-start.25) | collective-permute-done | bytes 1048608 | tf_op jit(solution)/shard_map/ppermute | solution.py:30
  134.7 2.4 %collective-permute-start.27 = (bf16[512,256]{1,0:T(8,128)(2,1)S(1)}, bf16[512,256]{1,0:T(8,128)(2,1)S(1)}, u32[]{:S(2)}, u32[]{:S(2)}) collective-permute-start(bf16[512,256]{1,0:T(8,128)(2,1)S(1)} %get-tuple-element.71), channel_id=1, source_target_pairs={{0,96},{1,25},{2,98},{3,27},{4,100},{5,29},{6,102},{7,31},{8,104},... | collective-permute-start | bytes 786440 | tf_op jit(solution)/shard_map/ppermute | solution.py:30
  137.1 4.1 %collective-permute-done.29 = bf16[512,256]{1,0:T(8,128)(2,1)S(1)} collective-permute-done((bf16[512,256]{1,0:T(8,128)(2,1)S(1)}, bf16[512,256]{1,0:T(8,128)(2,1)S(1)}, u32[]{:S(2)}, u32[]{:S(2)}) %collective-permute-start.29) | collective-permute-done | bytes 262176 | tf_op jit(solution)/shard_map/ppermute | solution.py:30
  141.2 2.7 %collective-permute-done.28 = bf16[512,256]{1,0:T(8,128)(2,1)S(1)} collective-permute-done((bf16[512,256]{1,0:T(8,128)(2,1)S(1)}, bf16[512,256]{1,0:T(8,128)(2,1)S(1)}, u32[]{:S(2)}, u32[]{:S(2)}) %collective-permute-start.28) | collective-permute-done | bytes 262176 | tf_op jit(solution)/shard_map/ppermute | solution.py:30
  (94 shorter events, 38.0 us)
Async XLA Ops:
  3.6 25.2 %collective-permute-start.3 = (bf16[512,1024]{1,0:T(8,128)(2,1)}, bf16[512,1024]{1,0:T(8,128)(2,1)S(1)}, u32[]{:S(2)}, u32[]{:S(2)}) collective-permute-start(bf16[512,1024]{1,0:T(8,128)(2,1)} %get-tuple-element.41.refs_0_), channel_id=1, source_target_pairs={{0,2},{1,3},{2,4},{3,5},{4,6},{5,7},{6,0},{7,1},{8,10},{9,11},{10,... | collective-permute-start | bytes 3145736 | tf_op jit(solution)/shard_map/ppermute | solution.py:43
  4.9 24.8 %collective-permute-start.4 = (bf16[512,1024]{1,0:T(8,128)(2,1)}, bf16[512,1024]{1,0:T(8,128)(2,1)S(1)}, u32[]{:S(2)}, u32[]{:S(2)}) collective-permute-start(bf16[512,1024]{1,0:T(8,128)(2,1)} %get-tuple-element.41.refs_0_), channel_id=1, source_target_pairs={{0,6},{1,7},{2,0},{3,1},{4,2},{5,3},{6,4},{7,5},{8,14},{9,15},{10,... | collective-permute-start | bytes 3145736 | tf_op jit(solution)/shard_map/ppermute | solution.py:43
  10.4 10.8 %collective-permute-start.2 = (bf16[512,256]{1,0:T(8,128)(2,1)S(1)}, bf16[512,256]{1,0:T(8,128)(2,1)S(1)}, u32[]{:S(2)}, u32[]{:S(2)}) collective-permute-start(bf16[512,256]{1,0:T(8,128)(2,1)S(1)} %get-tuple-element.38), channel_id=1, source_target_pairs={{0,96},{1,25},{2,98},{3,27},{4,100},{5,29},{6,102},{7,31},{8,104},... | collective-permute-start | bytes 786440 | tf_op jit(solution)/shard_map/ppermute | solution.py:30
  14.5 8.0 %collective-permute-start.1 = (bf16[512,256]{1,0:T(8,128)(2,1)S(1)}, bf16[512,256]{1,0:T(8,128)(2,1)S(1)}, u32[]{:S(2)}, u32[]{:S(2)}) collective-permute-start(bf16[512,256]{1,0:T(8,128)(2,1)S(1)} %get-tuple-element.38), channel_id=1, source_target_pairs={{0,64},{1,17},{2,66},{3,19},{4,68},{5,21},{6,70},{7,23},{8,72},{9,... | collective-permute-start | bytes 786440 | tf_op jit(solution)/shard_map/ppermute | solution.py:30
  14.6 10.4 %collective-permute-start = (bf16[512,256]{1,0:T(8,128)(2,1)S(1)}, bf16[512,256]{1,0:T(8,128)(2,1)S(1)}, u32[]{:S(2)}, u32[]{:S(2)}) collective-permute-start(bf16[512,256]{1,0:T(8,128)(2,1)S(1)} %get-tuple-element.38), channel_id=1, source_target_pairs={{0,32},{1,9},{2,34},{3,11},{4,36},{5,13},{6,38},{7,15},{8,40},{9,1... | collective-permute-start | bytes 786440 | tf_op jit(solution)/shard_map/ppermute | solution.py:30
  29.7 21.8 %collective-permute-start.7 = (bf16[2048,256]{1,0:T(8,128)(2,1)S(1)}, bf16[2048,256]{1,0:T(8,128)(2,1)S(1)}, u32[]{:S(2)}, u32[]{:S(2)}) collective-permute-start(bf16[2048,256]{1,0:T(8,128)(2,1)S(1)} %pad_maximum_fusion.refs_0_), channel_id=1, source_target_pairs={{0,8},{1,33},{2,10},{3,35},{4,12},{5,37},{6,14},{7,39},{8,16},{9,4... | collective-permute-start | bytes 3145736 | tf_op jit(solution)/shard_map/ppermute | solution.py:30
  31.3 26.9 %collective-permute-start.8 = (bf16[2048,256]{1,0:T(8,128)(2,1)S(1)}, bf16[2048,256]{1,0:T(8,128)(2,1)S(1)}, u32[]{:S(2)}, u32[]{:S(2)}) collective-permute-start(bf16[2048,256]{1,0:T(8,128)(2,1)S(1)} %pad_maximum_fusion.refs_0_), channel_id=1, source_target_pairs={{0,16},{1,65},{2,18},{3,67},{4,20},{5,69},{6,22},{7,71},{8,24},{9,... | collective-permute-start | bytes 3145736 | tf_op jit(solution)/shard_map/ppermute | solution.py:30
  34.2 24.0 %collective-permute-start.9 = (bf16[2048,256]{1,0:T(8,128)(2,1)S(1)}, bf16[2048,256]{1,0:T(8,128)(2,1)S(1)}, u32[]{:S(2)}, u32[]{:S(2)}) collective-permute-start(bf16[2048,256]{1,0:T(8,128)(2,1)S(1)} %pad_maximum_fusion.refs_0_), channel_id=1, source_target_pairs={{0,24},{1,97},{2,26},{3,99},{4,28},{5,101},{6,30},{7,103},{8,0},{9... | collective-permute-start | bytes 3145736 | tf_op jit(solution)/shard_map/ppermute | solution.py:30
  35.5 12.4 %collective-permute-start.5 = (bf16[256,1024]{1,0:T(8,128)(2,1)S(1)}, bf16[256,1024]{1,0:T(8,128)(2,1)S(1)}, u32[]{:S(2)}, u32[]{:S(2)}) collective-permute-start(bf16[256,1024]{1,0:T(8,128)(2,1)S(1)} %slice.65), channel_id=1, source_target_pairs={{0,2},{1,3},{2,4},{3,5},{4,6},{5,7},{6,0},{7,1},{8,10},{9,11},{10,... | collective-permute-start | bytes 1572872 | tf_op jit(solution)/shard_map/ppermute | solution.py:43
  37.3 12.1 %collective-permute-start.6 = (bf16[256,1024]{1,0:T(8,128)(2,1)S(1)}, bf16[256,1024]{1,0:T(8,128)(2,1)S(1)}, u32[]{:S(2)}, u32[]{:S(2)}) collective-permute-start(bf16[256,1024]{1,0:T(8,128)(2,1)S(1)} %slice.66), channel_id=1, source_target_pairs={{0,6},{1,7},{2,0},{3,1},{4,2},{5,3},{6,4},{7,5},{8,14},{9,15},{10,... | collective-permute-start | bytes 1572872 | tf_op jit(solution)/shard_map/ppermute | solution.py:43
  49.5 22.3 %collective-permute-start.14 = (bf16[512,1024]{1,0:T(8,128)(2,1)S(1)}, bf16[512,1024]{1,0:T(8,128)(2,1)S(1)}, u32[]{:S(2)}, u32[]{:S(2)}) collective-permute-start(bf16[512,1024]{1,0:T(8,128)(2,1)S(1)} %get-tuple-element.51.refs_8_), channel_id=1, source_target_pairs={{0,2},{1,3},{2,4},{3,5},{4,6},{5,7},{6,0},{7,1},{8,10},{9,11},{10,... | collective-permute-start | bytes 3145736 | tf_op jit(solution)/shard_map/ppermute | solution.py:43
  51.3 22.4 %collective-permute-start.15 = (bf16[512,1024]{1,0:T(8,128)(2,1)S(1)}, bf16[512,1024]{1,0:T(8,128)(2,1)S(1)}, u32[]{:S(2)}, u32[]{:S(2)}) collective-permute-start(bf16[512,1024]{1,0:T(8,128)(2,1)S(1)} %get-tuple-element.51.refs_8_), channel_id=1, source_target_pairs={{0,6},{1,7},{2,0},{3,1},{4,2},{5,3},{6,4},{7,5},{8,14},{9,15},{10,... | collective-permute-start | bytes 3145736 | tf_op jit(solution)/shard_map/ppermute | solution.py:43
  51.5 10.0 %collective-permute-start.10 = (bf16[512,1024]{1,0:T(8,128)(2,1)S(1)}, bf16[512,1024]{1,0:T(8,128)(2,1)S(1)}, u32[]{:S(2)}, u32[]{:S(2)}) collective-permute-start(bf16[512,1024]{1,0:T(8,128)(2,1)S(1)} %copy-done.1), channel_id=1, source_target_pairs={{0,1},{1,0},{2,3},{3,2},{4,5},{5,4},{6,7},{7,6},{8,9},{9,8},{10,11... | collective-permute-start | bytes 3145736 | tf_op jit(solution)/shard_map/ppermute | solution.py:47
  65.8 10.6 %collective-permute-start.17 = (bf16[512,256]{1,0:T(8,128)(2,1)S(1)}, bf16[512,256]{1,0:T(8,128)(2,1)S(1)}, u32[]{:S(2)}, u32[]{:S(2)}) collective-permute-start(bf16[512,256]{1,0:T(8,128)(2,1)S(1)} %shard_map.132.kv_ref), channel_id=1, source_target_pairs={{0,64},{8,72},{16,80},{24,88},{32,96},{40,104},{48,112},{56,120},{... | collective-permute-start | bytes 786440 | tf_op jit(solution)/shard_map/ppermute | solution.py:17
  73.7 10.6 %collective-permute-start.21 = (bf16[256,1024]{1,0:T(8,128)(2,1)S(1)}, bf16[256,1024]{1,0:T(8,128)(2,1)S(1)}, u32[]{:S(2)}, u32[]{:S(2)}) collective-permute-start(bf16[256,1024]{1,0:T(8,128)(2,1)S(1)} %slice.75), channel_id=1, source_target_pairs={{0,2},{1,3},{2,4},{3,5},{4,6},{5,7},{6,0},{7,1},{8,10},{9,11},{10,... | collective-permute-start | bytes 1572872 | tf_op jit(solution)/shard_map/ppermute | solution.py:43
  75.5 10.4 %collective-permute-start.22 = (bf16[256,1024]{1,0:T(8,128)(2,1)S(1)}, bf16[256,1024]{1,0:T(8,128)(2,1)S(1)}, u32[]{:S(2)}, u32[]{:S(2)}) collective-permute-start(bf16[256,1024]{1,0:T(8,128)(2,1)S(1)} %slice.76), channel_id=1, source_target_pairs={{0,6},{1,7},{2,0},{3,1},{4,2},{5,3},{6,4},{7,5},{8,14},{9,15},{10,... | collective-permute-start | bytes 1572872 | tf_op jit(solution)/shard_map/ppermute | solution.py:43
  75.9 14.3 %collective-permute-start.16 = (bf16[512,1024]{1,0:T(8,128)(2,1)S(1)}, bf16[512,1024]{1,0:T(8,128)(2,1)S(1)}, u32[]{:S(2)}, u32[]{:S(2)}) collective-permute-start(bf16[512,1024]{1,0:T(8,128)(2,1)S(1)} %get-tuple-element.51.refs_8_), channel_id=1, source_target_pairs={{0,1},{1,0},{2,3},{3,2},{4,5},{5,4},{6,7},{7,6},{8,9},{9,8},{10,11... | collective-permute-start | bytes 3145736 | tf_op jit(solution)/shard_map/ppermute | solution.py:47
  79.8 9.7 %collective-permute-start.20 = (bf16[512,256]{1,0:T(8,128)(2,1)S(1)}, bf16[512,256]{1,0:T(8,128)(2,1)S(1)}, u32[]{:S(2)}, u32[]{:S(2)}) collective-permute-start(bf16[512,256]{1,0:T(8,128)(2,1)S(1)} %get-tuple-element.57.refs_17_), channel_id=1, source_target_pairs={{0,64},{8,72},{16,80},{24,88},{32,96},{40,104},{48,112},{56,120},{... | collective-permute-start | bytes 786440 | tf_op jit(solution)/shard_map/ppermute | solution.py:17
  102.5 18.1 %collective-permute-start.26 = (bf16[2048,256]{1,0:T(8,128)(2,1)S(1)}, bf16[2048,256]{1,0:T(8,128)(2,1)S(1)}, u32[]{:S(2)}, u32[]{:S(2)}) collective-permute-start(bf16[2048,256]{1,0:T(8,128)(2,1)S(1)} %get-tuple-element.69), channel_id=1, source_target_pairs={{0,16},{1,65},{2,18},{3,67},{4,20},{5,69},{6,22},{7,71},{8,24},{9,... | collective-permute-start | bytes 3145736 | tf_op jit(solution)/shard_map/ppermute | solution.py:30
  107.7 24.0 %collective-permute-start.25 = (bf16[2048,256]{1,0:T(8,128)(2,1)S(1)}, bf16[2048,256]{1,0:T(8,128)(2,1)S(1)}, u32[]{:S(2)}, u32[]{:S(2)}) collective-permute-start(bf16[2048,256]{1,0:T(8,128)(2,1)S(1)} %get-tuple-element.70), channel_id=1, source_target_pairs={{0,8},{1,33},{2,10},{3,35},{4,12},{5,37},{6,14},{7,39},{8,16},{9,4... | collective-permute-start | bytes 3145736 | tf_op jit(solution)/shard_map/ppermute | solution.py:30
  108.4 24.1 %collective-permute-start.24 = (bf16[2048,256]{1,0:T(8,128)(2,1)S(1)}, bf16[2048,256]{1,0:T(8,128)(2,1)S(1)}, u32[]{:S(2)}, u32[]{:S(2)}) collective-permute-start(bf16[2048,256]{1,0:T(8,128)(2,1)S(1)} %get-tuple-element.68), channel_id=1, source_target_pairs={{0,24},{1,97},{2,26},{3,99},{4,28},{5,101},{6,30},{7,103},{8,0},{9... | collective-permute-start | bytes 3145736 | tf_op jit(solution)/shard_map/ppermute | solution.py:30
  133.1 8.1 %collective-permute-start.29 = (bf16[512,256]{1,0:T(8,128)(2,1)S(1)}, bf16[512,256]{1,0:T(8,128)(2,1)S(1)}, u32[]{:S(2)}, u32[]{:S(2)}) collective-permute-start(bf16[512,256]{1,0:T(8,128)(2,1)S(1)} %get-tuple-element.72), channel_id=1, source_target_pairs={{0,64},{1,17},{2,66},{3,19},{4,68},{5,21},{6,70},{7,23},{8,72},{9,... | collective-permute-start | bytes 786440 | tf_op jit(solution)/shard_map/ppermute | solution.py:30
  133.5 10.4 %collective-permute-start.28 = (bf16[512,256]{1,0:T(8,128)(2,1)S(1)}, bf16[512,256]{1,0:T(8,128)(2,1)S(1)}, u32[]{:S(2)}, u32[]{:S(2)}) collective-permute-start(bf16[512,256]{1,0:T(8,128)(2,1)S(1)} %get-tuple-element.73), channel_id=1, source_target_pairs={{0,32},{1,9},{2,34},{3,11},{4,36},{5,13},{6,38},{7,15},{8,40},{9,1... | collective-permute-start | bytes 786440 | tf_op jit(solution)/shard_map/ppermute | solution.py:30
  134.7 9.2 %collective-permute-start.27 = (bf16[512,256]{1,0:T(8,128)(2,1)S(1)}, bf16[512,256]{1,0:T(8,128)(2,1)S(1)}, u32[]{:S(2)}, u32[]{:S(2)}) collective-permute-start(bf16[512,256]{1,0:T(8,128)(2,1)S(1)} %get-tuple-element.71), channel_id=1, source_target_pairs={{0,96},{1,25},{2,98},{3,27},{4,100},{5,29},{6,102},{7,31},{8,104},... | collective-permute-start | bytes 786440 | tf_op jit(solution)/shard_map/ppermute | solution.py:30
  (16 other events, 171.4 us)
